TPU v7x, 32 devices: a whole 2x2x4 slice. The times are simulated.
32 devices in a mesh: dp: 2 (over core), frames: 4 (over y, x), rows: 4 (over z).
Axes of the slice: x: 2, y: 2, z: 4, core: 2. Of those that a mesh axis runs over, the one named last changes fastest.
Arguments:
- acts_fine: bfloat16 [2, 8, 16, 16, 512], P('dp', 'frames', 'rows'), may hold values from -120 to 120
- acts_coarse: bfloat16 [2, 8, 8, 8, 512], P('dp', 'frames', 'rows'), may hold values from -120 to 120
- grad_coarse: bfloat16 [2, 8, 8, 8, 512], P('dp', 'frames', 'rows'), may hold values from -20 to 20
- gain_fine: float32 [512], replicated, may hold values from 0.5 to 1.5
- bias_fine: float32 [512], replicated, may hold values from -1 to 1
- kernel_fine: bfloat16 [27, 512, 512], P(None, 'rows'), may hold values from -0.0546875 to 0.0546875
- gain_coarse: float32 [512], replicated, may hold values from 0.5 to 1.5
- bias_coarse: float32 [512], replicated, may hold values from -1 to 1
- kernel_coarse: bfloat16 [27, 512, 512], P(None, 'rows'), may hold values from -0.0546875 to 0.0546875
Outputs:
- grad_fine: bfloat16 [2, 8, 16, 16, 512], P('dp', 'frames', 'rows')
- gain_grad_fine: float32 [512], replicated
- bias_grad_fine: float32 [512], replicated
- gain_grad_coarse: float32 [512], replicated
- bias_grad_coarse: float32 [512], replicated
All inputs are finite; a program needn't handle non-finite values.
Results may differ from a plain program's by a relative error of at most 0.0048.
Values may be sent and summed in bfloat16 or wider, within the bound.
No kernel may reach another device: no remote copies, remote signals or barrier semaphores. Data moves between devices by JAX's collectives and lax.ppermute only.
A program may use at most 64 MiB of HBM per device.

v0:
```python
import jax
import jax.numpy as jnp
from jax import lax
from jax.sharding import PartitionSpec as P

GROUPS = 32


EPSILON = 1e-06


def passed_along(block, axis, distance):
    devices = range(lax.axis_size(axis))
    route = [(i - distance, i) for i in devices if i - distance in devices]
    return lax.ppermute(block, axis, route)


def conv_back(source, kernel, frames_out, plan):
    frame_total, rows_all, col_count, channels = source.shape
    slice_width = kernel.shape[1]
    padded = jnp.pad(source, ((0, 0), (1, 1), (1, 1), (0, 0)))
    width_pad = col_count + 2
    flat_len = (rows_all + 2) * width_pad
    flattened = padded.reshape(frame_total, flat_len, channels)
    blocks = kernel.reshape(3, 9 * slice_width, channels)
    margin = width_pad + 1
    accumulated = jnp.zeros((slice_width, frames_out, flat_len + 2 * margin), jnp.float32)
    for tap_depth, source_start, frame_count, target_start in plan:
        products = lax.dot_general(
            blocks[tap_depth],
            flattened[source_start : source_start + frame_count],
            (((1,), (2,)), ((), ())),
            preferred_element_type=jnp.float32,
        )
        products = products.reshape(9, slice_width, frame_count, flat_len)
        for spatial in range(9):
            placed = margin + (spatial // 3 - 1) * width_pad + (spatial % 3 - 1)
            accumulated = accumulated.at[
                :, target_start : target_start + frame_count, placed : placed + flat_len
            ].add(products[spatial])
    interior = accumulated[:, :, margin : margin + flat_len].reshape(
        slice_width, frames_out, rows_all + 2, width_pad
    )
    return interior[:, :, 1:-1, 1:-1].reshape(slice_width, frames_out, rows_all * col_count)


def doubled(field):
    return jnp.repeat(jnp.repeat(field, 2, axis=1), 2, axis=2)


def channel_grad(outgoing, kernel, fine_level):
    frame_num = outgoing.shape[0]
    if fine_level:
        following = passed_along(outgoing, "frames", -1)
        gathered = doubled(
            lax.all_gather(jnp.concatenate([outgoing, following], 0), "rows", axis=1, tiled=True)
        )
    else:
        following = passed_along(outgoing, "frames", -1)
        gathered = lax.all_gather(
            jnp.concatenate([outgoing, following], 0), "rows", axis=1, tiled=True
        )
    plan = [(tap_depth, 2 - tap_depth, frame_num, 0) for tap_depth in range(3)]
    channel_part = conv_back(gathered, kernel, frame_num, plan)
    if fine_level:
        return lax.all_to_all(
            channel_part.astype(jnp.bfloat16), "rows", split_axis=2, concat_axis=0, tiled=True
        ).astype(channel_part.dtype)
    return lax.all_to_all(channel_part, "rows", split_axis=2, concat_axis=0, tiled=True)


def level_grad(acts, cotangent, outgoing, gain, bias, kernel, fine_level):
    frame_num, row_count, col_count, channels = acts.shape
    returned = channel_grad(outgoing, kernel, fine_level)
    conv_grad = returned.reshape(channels, frame_num, row_count, col_count).transpose(1, 2, 3, 0)
    values = acts.astype(jnp.float32)
    group_width = channels // GROUPS
    entries = (
        frame_num
        * lax.axis_size("frames")
        * row_count
        * lax.axis_size("rows")
        * col_count
        * group_width
    )
    channel_sum = jnp.sum(values, axis=(0, 1, 2))
    channel_square = jnp.sum(values * values, axis=(0, 1, 2))
    group_sum = jnp.sum(channel_sum.reshape(GROUPS, group_width), axis=1)
    group_square = jnp.sum(channel_square.reshape(GROUPS, group_width), axis=1)
    if fine_level:
        total_sum, total_square = lax.psum((group_sum, group_square), ("frames", "rows"))
    else:
        total_sum, total_square = lax.psum((group_sum, group_square), ("frames", "rows"))
    group_mean = total_sum / entries
    inv_std = lax.rsqrt(total_square / entries - group_mean * group_mean + EPSILON)
    mean_chan = jnp.repeat(group_mean, group_width)
    inv_chan = jnp.repeat(inv_std, group_width)
    normed = (values - mean_chan) * inv_chan
    preact = gain * normed + bias
    squash = jax.nn.sigmoid(preact)
    pre_grad = conv_grad * squash * (1.0 + preact * (1.0 - squash))
    local_one = jnp.sum(pre_grad, axis=(0, 1, 2))
    local_two = jnp.sum(pre_grad * normed, axis=(0, 1, 2))
    if fine_level:
        param_one, param_two = lax.psum((local_one, local_two), ("frames", "rows"))
    else:
        param_one, param_two = lax.psum((local_one, local_two), ("frames", "rows"))
    group_one = jnp.sum((gain * param_one).reshape(GROUPS, group_width), axis=1)
    group_two = jnp.sum((gain * param_two).reshape(GROUPS, group_width), axis=1)
    group_one = group_one / entries
    group_two = group_two / entries
    result_grad = cotangent.astype(jnp.float32) + inv_chan * (
        gain * pre_grad
        - jnp.repeat(group_one, group_width)
        - normed * jnp.repeat(group_two, group_width)
    )
    return (result_grad, param_one, param_two)


def shards(
    acts_fine,
    acts_coarse,
    grad_coarse,
    gain_fine,
    bias_fine,
    kernel_fine,
    gain_coarse,
    bias_coarse,
    kernel_coarse,
):
    coarse_input_grad, coarse_one, coarse_two = level_grad(
        acts_coarse[0],
        grad_coarse[0],
        grad_coarse[0],
        gain_coarse,
        bias_coarse,
        kernel_coarse,
        False,
    )
    quartered = (coarse_input_grad * 0.25).astype(jnp.bfloat16)
    upsampled = doubled(quartered)
    fine_grad, fine_one, fine_two = level_grad(
        acts_fine[0], upsampled, quartered, gain_fine, bias_fine, kernel_fine, True
    )
    totals = lax.psum((fine_one, fine_two, coarse_one, coarse_two), "dp")
    cells_fine = (
        lax.axis_size("dp")
        * acts_fine.shape[1]
        * lax.axis_size("frames")
        * acts_fine.shape[2]
        * lax.axis_size("rows")
        * acts_fine.shape[3]
    )
    cells_coarse = (
        lax.axis_size("dp")
        * acts_coarse.shape[1]
        * lax.axis_size("frames")
        * acts_coarse.shape[2]
        * lax.axis_size("rows")
        * acts_coarse.shape[3]
    )
    scale_fine = 1.0 / jnp.sqrt(jnp.float32(cells_fine))
    scale_coarse = 1.0 / jnp.sqrt(jnp.float32(cells_coarse))
    return (
        fine_grad.astype(jnp.bfloat16)[None],
        totals[1] * scale_fine,
        totals[0] * scale_fine,
        totals[3] * scale_coarse,
        totals[2] * scale_coarse,
    )


def solution(mesh):
    in_specs = (
        P("dp", "frames", "rows", None, None),
        P("dp", "frames", "rows", None, None),
        P("dp", "frames", "rows", None, None),
        P(),
        P(),
        P(None, "rows", None),
        P(),
        P(),
        P(None, "rows", None),
    )
    out_specs = (P("dp", "frames", "rows", None, None), P(), P(), P(), P())
    return jax.shard_map(shards, mesh=mesh, in_specs=in_specs, out_specs=out_specs, check_vma=False)
```

profile of v0, /device:TPU:0, one launch (start us, length us, event | category | flops | bytes accessed | tf_op | source)
XLA Modules:
  0.0 283.2 jit_solution(14137824121968831923)
XLA Ops:
  0.6 1.3 collective-permute-start
  3.5 3.4 %fusion.53 = (bf16[9,128,512]{2,1,0:T(8,128)(2,1)S(1)}, bf16[9,128,512]{2,1,0:T(8,128)(2,1)}, bf16[9,128,512]{2,1,0:T(8,128)(2,1)S(1)}) fusion(bf16[27,128,512]{2,1,0:T(8,128)(2,1)} %param.125), kind=kLoop, calls=%fused_computation.137 | loop fusion | bytes 7077888 | tf_op jit(solution)/shard_map/slice | solution.py:30
  7.3 44.8 %all-reduce.6 = (f32[32]{0:T(128)S(1)}, f32[32]{0:T(128)S(1)}) all-reduce(f32[32]{0:T(128)S(1)} %reduce_sum.147, f32[32]{0:T(128)S(1)} %reduce_sum.145), channel_id=1, replica_groups=mesh['dp'=2,'frames'=4,'rows'=4] {'frames','rows'}, use_global_device_ids=true, to_apply=%region_5.6 | all-reduce | flops 64 | bytes 512 | tf_op jit(solution)/shard_map/psum | solution.py:93
  54.4 13.9 %all_gather.6 = bf16[4,8,8,512]{3,2,1,0:T(8,128)(2,1)S(1)} all-gather(bf16[4,2,8,512]{3,2,1,0:T(8,128)(2,1)S(1)} %pad_maximum_fusion), channel_id=1, replica_groups=mesh['dp'=2,'frames'=4,'rows'=4] {'rows'}, dimensions={1}, use_global_device_ids=true | all-gather | bytes 327680 | tf_op jit(solution)/shard_map/all_gather | solution.py:60
  68.3 1.0 pad_slice_fusion.3
  73.0 1.9 copy.46
  75.2 1.5 convolution_bitcast_fusion.4
  85.6 3.3 %all-to-all-start = ((f32[128,2,64]{0,1,2:T(2,128)}), f32[128,2,64]{0,1,2:T(2,128)S(1)}, u32[]{:S(2)}, u32[]{:S(2)}) async-start(f32[128,2,64]{0,1,2:T(2,128)} %bitcast.15), calls=%async_computation | async-start | bytes 131072 | tf_op jit(solution)/shard_map/all_to_all | solution.py:69
  89.1 5.5 %all-to-all-done = f32[128,2,64]{0,1,2:T(2,128)S(1)} async-done(((f32[128,2,64]{0,1,2:T(2,128)}), f32[128,2,64]{0,1,2:T(2,128)S(1)}, u32[]{:S(2)}, u32[]{:S(2)}) %all-to-all-start) | async-done | bytes 65568 | tf_op jit(solution)/shard_map/all_to_all | solution.py:69
  94.8 38.4 %all-reduce.5 = (f32[512]{0:T(512)S(1)}, f32[512]{0:T(512)S(1)}, f32[32]{0:T(128)S(1)}, f32[32]{0:T(128)S(1)}) all-reduce(f32[512]{0:T(512)S(1)} %get-tuple-element.656, f32[512]{0:T(512)S(1)} %get-tuple-element.655, f32[32]{0:T(128)S(1)} %reduce_sum.155, ...), channel_id=1, replica_groups=mesh['dp'=2,'frames'=4,'rows'=4] {'frames','rows'}, use_global_device_ids=true, to_apply=%region_10.11 | all-reduce | flops 1088 | bytes 8704 | tf_op jit(solution)/shard_map/psum | solution.py:107
  133.9 1.3 collective-permute-start.1
  135.2 3.7 %fusion.52 = (bf16[9,128,512]{2,1,0:T(8,128)(2,1)}, bf16[9,128,512]{2,1,0:T(8,128)(2,1)S(1)}, bf16[9,128,512]{2,1,0:T(8,128)(2,1)}) fusion(bf16[27,128,512]{2,1,0:T(8,128)(2,1)} %param.122), kind=kLoop, calls=%fused_computation.136 | loop fusion | bytes 7077888 | tf_op jit(solution)/shard_map/slice | solution.py:30
  139.0 0.8 collective-permute-done.1
  139.8 14.0 %all_gather.7 = bf16[4,8,8,512]{3,2,1,0:T(8,128)(2,1)S(1)} all-gather(bf16[4,2,8,512]{3,2,1,0:T(8,128)(2,1)S(1)} %pad_maximum_fusion.1), channel_id=1, replica_groups=mesh['dp'=2,'frames'=4,'rows'=4] {'rows'}, dimensions={1}, use_global_device_ids=true | all-gather | bytes 327680 | tf_op jit(solution)/shard_map/all_gather | solution.py:56
  154.5 2.3 pad_slice_fusion
  156.9 1.1 convolution_bitcast_fusion.2
  158.8 1.8 scatter-add.226
  161.3 1.7 scatter-add.229
  163.8 1.7 scatter-add.230
  166.3 1.7 scatter-add.231
  168.8 1.7 scatter-add.234
  171.3 1.7 scatter-add.235
  173.7 1.7 scatter-add.236
  176.2 1.7 scatter-add.239
  177.9 2.5 convolution_bitcast_fusion.1
  181.2 1.7 scatter-add.240
  183.7 1.7 scatter-add.241
  186.2 1.7 scatter-add.244
  188.8 1.7 scatter-add.245
  191.2 1.7 scatter-add.246
  193.7 1.7 scatter-add.249
  196.2 1.7 scatter-add.250
  198.7 1.7 scatter-add.251
  201.2 1.7 scatter-add.254
  202.9 2.5 convolution_bitcast_fusion
  206.2 1.7 scatter-add.255
  208.7 1.7 scatter-add.256
  211.2 1.7 scatter-add.259
  213.7 1.7 scatter-add.260
  216.2 1.7 scatter-add.261
  218.7 1.7 scatter-add.264
  221.2 1.7 scatter-add.265
  223.7 1.7 scatter-add.266
  226.1 1.7 scatter-add.269
  228.8 3.3 %all-to-all-start.1 = ((bf16[128,2,256]{0,1,2:T(2,128)(2,1)}), bf16[128,2,256]{0,1,2:T(2,128)(2,1)S(1)}, u32[]{:S(2)}, u32[]{:S(2)}) async-start(bf16[128,2,256]{0,1,2:T(2,128)(2,1)} %bitcast.36), calls=%async_computation.1 | async-start | bytes 262144 | tf_op jit(solution)/shard_map/all_to_all | solution.py:66
  233.5 4.5 %all-to-all-done.1 = bf16[128,2,256]{0,1,2:T(2,128)(2,1)S(1)} async-done(((bf16[128,2,256]{0,1,2:T(2,128)(2,1)}), bf16[128,2,256]{0,1,2:T(2,128)(2,1)S(1)}, u32[]{:S(2)}, u32[]{:S(2)}) %all-to-all-start.1) | async-done | bytes 131104 | tf_op jit(solution)/shard_map/all_to_all | solution.py:66
  238.6 39.5 %all-reduce.4 = (f32[512]{0:T(512)S(1)}, f32[512]{0:T(512)S(1)}) all-reduce(f32[512]{0:T(512)S(1)} %get-tuple-element.654, f32[512]{0:T(512)S(1)} %get-tuple-element.653), channel_id=1, replica_groups=mesh['dp'=2,'frames'=4,'rows'=4] {'frames','rows'}, use_global_device_ids=true, to_apply=%region_22.23 | all-reduce | flops 1024 | bytes 8192 | tf_op jit(solution)/shard_map/psum | solution.py:105
  278.0 2.5 all-reduce.7
  (188 shorter events, 43.7 us)
Async XLA Ops:
  0.6 53.7 %collective-permute-start = (bf16[2,2,8,512]{3,2,1,0:T(8,128)(2,1)}, bf16[2,2,8,512]{3,2,1,0:T(8,128)(2,1)S(1)}, u32[]{:S(2)}, u32[]{:S(2)}) collective-permute-start(bf16[2,2,8,512]{3,2,1,0:T(8,128)(2,1)} %bitcast.187), channel_id=1, source_target_pairs={{4,0},{8,4},{12,8},{5,1},{9,5},{13,9},{6,2},{10,6},{14,10},{7,3},{... | collective-permute-start | bytes 98312 | tf_op jit(solution)/shard_map/ppermute | solution.py:15
  3.5 48.6 %copy-start.1 = (bf16[1,2,4,16,512]{4,3,2,1,0:T(8,128)(2,1)S(1)}, bf16[1,2,4,16,512]{4,3,2,1,0:T(8,128)(2,1)}, u32[]{:S(2)}) copy-start(bf16[1,2,4,16,512]{4,3,2,1,0:T(8,128)(2,1)} %param.117) | copy-start | bytes 393220
  3.5 50.9 %copy-start.6 = (bf16[1,2,2,8,512]{4,3,2,1,0:T(8,128)(2,1)S(1)}, bf16[1,2,2,8,512]{4,3,2,1,0:T(8,128)(2,1)}, u32[]{:S(2)}) copy-start(bf16[1,2,2,8,512]{4,3,2,1,0:T(8,128)(2,1)} %param.119) | copy-start | bytes 98308
  54.4 15.2 %copy-start = (bf16[9,128,512]{2,1,0:T(8,128)(2,1)S(1)}, bf16[9,128,512]{2,1,0:T(8,128)(2,1)}, u32[]{:S(2)}) copy-start(bf16[9,128,512]{2,1,0:T(8,128)(2,1)} %get-tuple-element.675) | copy-start | bytes 3538948
  76.6 3.7 %copy-start.3 = (bf16[2,10,10,512]{3,2,1,0:T(8,128)(2,1)S(1)}, bf16[2,10,10,512]{3,2,1,0:T(8,128)(2,1)}, u32[]{:S(2)}) copy-start(bf16[2,10,10,512]{3,2,1,0:T(8,128)(2,1)} %get-tuple-element.680) | copy-start | bytes 614404
  81.1 7.8 %copy-start.2 = (bf16[1,2,4,16,512]{4,3,2,1,0:T(8,128)(2,1)S(1)}, bf16[1,2,4,16,512]{4,3,2,1,0:T(8,128)(2,1)}, u32[]{:S(2)}) copy-start(bf16[1,2,4,16,512]{4,3,2,1,0:T(8,128)(2,1)} %param.117) | copy-start | bytes 393220
  81.1 13.5 %copy-start.4 = (bf16[1,2,2,8,512]{4,3,2,1,0:T(8,128)(2,1)S(1)}, bf16[1,2,2,8,512]{4,3,2,1,0:T(8,128)(2,1)}, u32[]{:S(2)}) copy-start(bf16[1,2,2,8,512]{4,3,2,1,0:T(8,128)(2,1)} %param.118) | copy-start | bytes 98308
  81.1 13.5 %copy-start.8 = (f32[512]{0:T(512)S(1)}, f32[512]{0:T(512)}, u32[]{:S(2)}) copy-start(f32[512]{0:T(512)} %param.123) | copy-start | bytes 6148
  81.1 13.5 %copy-start.10 = (f32[512]{0:T(512)S(1)}, f32[512]{0:T(512)}, u32[]{:S(2)}) copy-start(f32[512]{0:T(512)} %mul.148) | copy-start | bytes 6148
  81.1 13.5 %copy-start.11 = (f32[512]{0:T(512)S(1)}, f32[512]{0:T(512)}, u32[]{:S(2)}) copy-start(f32[512]{0:T(512)} %sub.59) | copy-start | bytes 6148
  81.1 13.5 %copy-start.12 = (f32[512]{0:T(512)S(1)}, f32[512]{0:T(512)}, u32[]{:S(2)}) copy-start(f32[512]{0:T(512)} %param.124) | copy-start | bytes 6148
  81.2 13.6 %copy-start.14 = (f32[32]{0:T(128)S(1)}, f32[32]{0:T(128)}, u32[]{:S(2)}) copy-start(f32[32]{0:T(128)} %reduce_sum.153) | copy-start | bytes 388
  81.2 52.7 %copy-start.7 = (bf16[1,2,2,8,512]{4,3,2,1,0:T(8,128)(2,1)S(1)}, bf16[1,2,2,8,512]{4,3,2,1,0:T(8,128)(2,1)}, u32[]{:S(2)}) copy-start(bf16[1,2,2,8,512]{4,3,2,1,0:T(8,128)(2,1)} %param.119) | copy-start | bytes 98308
  85.6 9.0 %all-to-all-start = ((f32[128,2,64]{0,1,2:T(2,128)}), f32[128,2,64]{0,1,2:T(2,128)S(1)}, u32[]{:S(2)}, u32[]{:S(2)}) async-start(f32[128,2,64]{0,1,2:T(2,128)} %bitcast.15), calls=%async_computation | async-start | bytes 131072 | tf_op jit(solution)/shard_map/all_to_all | solution.py:69
  133.9 5.8 %copy-start.5 = (bf16[2,2,8,512]{3,2,1,0:T(8,128)(2,1)}, bf16[2,2,8,512]{3,2,1,0:T(8,128)(2,1)S(1)}, u32[]{:S(2)}) copy-start(bf16[2,2,8,512]{3,2,1,0:T(8,128)(2,1)S(1)} %fusion.47) | copy-start | bytes 98308
  133.9 5.8 %collective-permute-start.1 = (bf16[2,2,8,512]{3,2,1,0:T(8,128)(2,1)S(1)}, bf16[2,2,8,512]{3,2,1,0:T(8,128)(2,1)S(1)}, u32[]{:S(2)}, u32[]{:S(2)}) collective-permute-start(bf16[2,2,8,512]{3,2,1,0:T(8,128)(2,1)S(1)} %fusion.47), channel_id=1, source_target_pairs={{4,0},{8,4},{12,8},{5,1},{9,5},{13,9},{6,2},{10,6},{14,10},{7,3},{... | collective-permute-start | bytes 98312 | tf_op jit(solution)/shard_map/ppermute | solution.py:15
  225.4 13.0 %copy-start.9 = (f32[512]{0:T(512)S(1)}, f32[512]{0:T(512)}, u32[]{:S(2)}) copy-start(f32[512]{0:T(512)} %param.120) | copy-start | bytes 6148
  225.4 13.0 %copy-start.13 = (f32[512]{0:T(512)S(1)}, f32[512]{0:T(512)}, u32[]{:S(2)}) copy-start(f32[512]{0:T(512)} %param.121) | copy-start | bytes 6148
  228.8 9.2 %all-to-all-start.1 = ((bf16[128,2,256]{0,1,2:T(2,128)(2,1)}), bf16[128,2,256]{0,1,2:T(2,128)(2,1)S(1)}, u32[]{:S(2)}, u32[]{:S(2)}) async-start(bf16[128,2,256]{0,1,2:T(2,128)(2,1)} %bitcast.36), calls=%async_computation.1 | async-start | bytes 262144 | tf_op jit(solution)/shard_map/all_to_all | solution.py:66
where the time goes:
time: 284 us; the launch traced here: 283 us
  blocking collectives  153 us (54%)
  local copies, waits for them, and re-layouts  74.2 us (26%)
  other arithmetic  25.5 us (9%)
  waiting for transfers between devices  10.8 us (4%)
  starting transfers between devices  9.19 us (3%)
  matrix products  8.72 us (3%)
    psum x2, blocking collectives, level_grad(): param_one, param_two = lax.psum((local_one, local_two), ('frames', 'rows'))  77.8 us
    scatter-add x54, local copies, waits for them, and re-layouts, conv_back(): accumulated = accumulated.at[:, target_start:target_start + frame_count,...  54.5 us
    psum x1, blocking collectives, level_grad(): lax.psum((group_sum, group_square), ('frames', 'rows'))  44.8 us
    all_gather x2, blocking collectives, channel_grad(): lax.all_gather(jnp.concatenate([outgoing, following], 0), 'rows', axis=1,...  27.9 us
    add x52, other arithmetic, conv_back(): accumulated = accumulated.at[:, target_start:target_start + frame_count,...  20.1 us
    dot_general x6, matrix products, conv_back(): lax.dot_general(blocks[tap_depth], flattened[source_start:source_start +...  8.72 us
    slice x2, local copies, waits for them, and re-layouts, conv_back(): blocks[tap_depth]  7.11 us
  transfers between devices with their start and end apart: 4, of which 3 were waited for; matrix products, arithmetic and copies ran while one was open for 5% of the time, Pallas kernels for 0%

commit v1 on v0

v1 whole, which is shorter than its diff:
```python
import jax
import jax.numpy as jnp
from jax import lax
from jax.sharding import PartitionSpec as P

GROUPS = 32
EPSILON = 1e-06
BLOCK = ("frames", "rows")


def to_everyone(block, count):
    copies = jnp.broadcast_to(block[None], (count,) + block.shape)
    return lax.all_to_all(copies, BLOCK, 0, 0)


def ahead(field, axis, distance):
    size = field.shape[axis]
    if distance == 0:
        return field
    widths = [(0, 0)] * field.ndim
    if distance > 0:
        widths[axis] = (0, distance)
        kept = lax.slice_in_dim(field, distance, size, axis=axis)
    else:
        widths[axis] = (-distance, 0)
        kept = lax.slice_in_dim(field, 0, size + distance, axis=axis)
    return jnp.pad(kept, widths)


def tap_products(source, kernel):
    sub = kernel.shape[1]
    frames, rows, cols, channels = source.shape
    products = lax.dot_general(
        kernel.reshape(27 * sub, channels),
        source.reshape(frames * rows * cols, channels),
        (((1,), (1,)), ((), ())),
        preferred_element_type=jnp.float32,
    ).reshape(3, 3, 3, sub, frames, rows, cols)
    return sum(ahead(products[depth], 3, 2 - depth) for depth in range(3))


def coarse_conv(source, kernel):
    spatial = tap_products(source, kernel)
    total = 0.0
    for row in range(3):
        part = sum(ahead(spatial[row, col], 3, 1 - col) for col in range(3))
        total = total + ahead(part, 2, 1 - row)
    return total


def fine_conv(source, kernel):
    spatial = tap_products(source, kernel)
    result = []
    for p in range(2):
        rows_of = []
        for q in range(2):
            total = 0.0
            for row in range(3):
                part = sum(ahead(spatial[row, col], 3, (q + 1 - col) // 2) for col in range(3))
                total = total + ahead(part, 2, (p + 1 - row) // 2)
            rows_of.append(total)
        result.append(jnp.stack(rows_of, 1))
    return jnp.stack(result, 1)


def group_total(sums, group_width):
    sub = sums.shape[-1]
    if sub % group_width == 0:
        grouped = jnp.sum(sums.reshape(-1, sub // group_width, group_width), axis=-1)
        return jnp.repeat(grouped, group_width, axis=-1)
    spread = jnp.moveaxis(lax.all_gather(sums, "frames"), 0, 1).reshape(sums.shape[0], -1, group_width)
    mine = lax.axis_index("frames") * sub // group_width
    grouped = lax.dynamic_index_in_dim(jnp.sum(spread, -1), mine, 1)
    return jnp.broadcast_to(grouped, sums.shape)


def level(acts, conv_grad, cotangent, gain, bias, group_width):
    sub = acts.shape[0]
    places = acts.size // sub
    values = acts.astype(jnp.float32).reshape(sub, places)
    conv_grad = conv_grad.reshape(sub, places)
    entries = places * group_width
    moments = group_total(
        jnp.stack([jnp.sum(values, 1), jnp.sum(values * values, 1)]), group_width
    ) / entries
    mean = moments[0]
    inv_std = lax.rsqrt(moments[1] - mean * mean + EPSILON)
    normed = (values - mean[:, None]) * inv_std[:, None]
    preact = gain[:, None] * normed + bias[:, None]
    squash = jax.nn.sigmoid(preact)
    pre_grad = conv_grad * squash * (1.0 + preact * (1.0 - squash))
    sums = jnp.stack([jnp.sum(pre_grad, 1), jnp.sum(pre_grad * normed, 1)])
    terms = group_total(sums * gain, group_width) / entries
    grad = cotangent.reshape(sub, places) + inv_std[:, None] * (
        gain[:, None] * pre_grad - terms[0][:, None] - normed * terms[1][:, None]
    )
    return grad, sums


def shards(
    acts_fine,
    acts_coarse,
    grad_coarse,
    gain_fine,
    bias_fine,
    kernel_fine,
    gain_coarse,
    bias_coarse,
    kernel_coarse,
):
    nf, nr, nd = lax.axis_size("frames"), lax.axis_size("rows"), lax.axis_size("dp")
    count = nf * nr
    channels = acts_fine.shape[-1]
    slice_width = kernel_fine.shape[1]
    sub = slice_width // nf
    group_width = channels // GROUPS
    tl, hl, w = acts_coarse.shape[1:4]
    frames, rows = tl * nf, hl * nr
    f, r = lax.axis_index("frames"), lax.axis_index("rows")

    gathered = to_everyone(grad_coarse[0], count)
    source = (
        gathered.reshape(nf, nr, tl, hl, w, channels)
        .transpose(0, 2, 1, 3, 4, 5)
        .reshape(frames, rows, w, channels)
    )
    coarse_in = acts_coarse[0].reshape(tl, hl, w, nr, nf, sub).transpose(4, 3, 5, 0, 1, 2)
    coarse_in = lax.all_to_all(coarse_in.reshape(count, sub, tl * hl * w), BLOCK, 0, 0)
    fine_in = acts_fine[0].reshape(tl, hl, 2, w, 2, nr, nf, sub).transpose(6, 5, 7, 2, 4, 0, 1, 3)
    fine_in = lax.all_to_all(fine_in.reshape(count, sub, 4 * tl * hl * w), BLOCK, 0, 0)

    def mine(vector):
        return lax.dynamic_slice_in_dim(vector, r * slice_width + f * sub, sub)

    def own(kernel):
        return lax.dynamic_slice_in_dim(kernel, f * sub, sub, axis=1)

    coarse_vals = (
        coarse_in.reshape(nf, nr, sub, tl, hl, w).transpose(2, 0, 3, 1, 4, 5).reshape(sub, frames, rows, w)
    )
    cot = lax.dynamic_slice_in_dim(source, r * slice_width + f * sub, sub, axis=3)
    cot = cot.astype(jnp.float32).transpose(3, 0, 1, 2)
    conv = coarse_conv(source, own(kernel_coarse))
    coarse_grad, coarse_sums = level(
        coarse_vals, conv, cot, mine(gain_coarse), mine(bias_coarse), group_width
    )
    quartered = (coarse_grad * 0.25).astype(jnp.bfloat16)
    spread = to_everyone(quartered, count)
    source_fine = (
        spread.reshape(nf, nr, sub, frames, rows, w)
        .transpose(3, 4, 5, 1, 0, 2)
        .reshape(frames, rows, w, channels)
    )
    conv = fine_conv(source_fine, own(kernel_fine))
    fine_vals = (
        fine_in.reshape(nf, nr, sub, 2, 2, tl, hl, w)
        .transpose(2, 3, 4, 0, 5, 1, 6, 7)
        .reshape(sub, 2, 2, frames, rows, w)
    )
    cot = jnp.broadcast_to(
        quartered.astype(jnp.float32).reshape(sub, 1, 1, frames, rows, w), conv.shape
    )
    fine_grad, fine_sums = level(
        fine_vals, conv, cot, mine(gain_fine), mine(bias_fine), group_width
    )
    back = (
        fine_grad.astype(jnp.bfloat16)
        .reshape(sub, 2, 2, nf, tl, nr, hl, w)
        .transpose(3, 5, 0, 1, 2, 4, 6, 7)
        .reshape(count, sub, 4 * tl * hl * w)
    )
    sums = to_everyone(jnp.concatenate([fine_sums, coarse_sums]), count)
    back = lax.all_to_all(back, BLOCK, 0, 0)
    out = (
        back.reshape(nf, nr, sub, 2, 2, tl, hl, w)
        .transpose(5, 6, 3, 7, 4, 1, 0, 2)
        .reshape(1, tl, 2 * hl, 2 * w, channels)
    )
    sums = sums.reshape(nf, nr, 4, sub).transpose(2, 1, 0, 3).reshape(4, channels)
    totals = lax.psum(sums, "dp")
    cells = nd * frames * rows * w
    scale_fine = 1.0 / jnp.sqrt(jnp.float32(4 * cells))
    scale_coarse = 1.0 / jnp.sqrt(jnp.float32(cells))
    return (
        out,
        totals[1] * scale_fine,
        totals[0] * scale_fine,
        totals[3] * scale_coarse,
        totals[2] * scale_coarse,
    )


def solution(mesh):
    in_specs = (
        P("dp", "frames", "rows", None, None),
        P("dp", "frames", "rows", None, None),
        P("dp", "frames", "rows", None, None),
        P(),
        P(),
        P(None, "rows", None),
        P(),
        P(),
        P(None, "rows", None),
    )
    out_specs = (P("dp", "frames", "rows", None, None), P(), P(), P(), P())
    return jax.shard_map(shards, mesh=mesh, in_specs=in_specs, out_specs=out_specs, check_vma=False)
```

time: 284 us -> 164 us (0.58)
  blocking collectives: 153 us -> 2.47 us
  waiting for transfers between devices: 10.8 us -> 32.8 us
  starting transfers between devices: 9.19 us -> 30.4 us
  other arithmetic: 25.5 us -> 15.5 us
  matrix products: 8.72 us -> 1.3 us
  local copies, waits for them, and re-layouts: 74.2 us -> 78.3 us
    psum x4 -> x1, blocking collectives: 125 us -> 2.47 us  [shards(): totals = lax.psum(sums, 'dp')]
    scatter-add x54 -> x0, local copies, waits for them, and re-layouts: 54.5 us -> none  [conv_back(): accumulated = accumulated.at[:, target_start:target_start + frame_count,...]
    all_gather x2 -> x0, blocking collectives: 27.9 us -> none  [channel_grad(): lax.all_gather(jnp.concatenate([outgoing, following], 0), 'rows', axis=1,...]
    all_to_all x2 -> x6, starting transfers between devices: 6.61 us -> 30.4 us  [the longest x3 10.7 us: to_everyone(): return lax.all_to_all(copies, BLOCK, 0, 0)]
    all_to_all x2 -> x6, waiting for transfers between devices: 9.97 us -> 32.8 us  [the longest x3 27.2 us: to_everyone(): return lax.all_to_all(copies, BLOCK, 0, 0)]
    squeeze x0 -> x12, local copies, waits for them, and re-layouts: none -> 18.2 us  [the longest x6 17.6 us: tap_products(): return sum((ahead(products[depth], 3, 2 - depth) for depth in range(3)))]
    add x52 -> x8, other arithmetic: 20.1 us -> 6.42 us  [the longest x2 5.72 us: tap_products(): return sum((ahead(products[depth], 3, 2 - depth) for depth in range(3)))]
    unnamed x30 -> x40, local copies, waits for them, and re-layouts: 0.09 us -> 11.1 us
  transfers between devices with their start and end apart: 4 -> 6, of which waited for: 3 -> 6; matrix products, arithmetic and copies ran while one was open for 5% -> 15% of each run, Pallas kernels for 0% -> 0%
where the time goes in v1:
time: 164 us; the launch traced here: 162 us
  local copies, waits for them, and re-layouts  78.3 us (48%)
  waiting for transfers between devices  32.8 us (20%)
  starting transfers between devices  30.4 us (19%)
  other arithmetic  15.5 us (9%)
  blocking collectives  2.47 us (2%)
    all_to_all x3, waiting for transfers between devices, to_everyone(): return lax.all_to_all(copies, BLOCK, 0, 0)  27.2 us
    squeeze x6, local copies, waits for them, and re-layouts, tap_products(): return sum((ahead(products[depth], 3, 2 - depth) for depth in range(3)))  17.6 us
    unnamed x40, local copies, waits for them, and re-layouts  11.1 us
    all_to_all x3, starting transfers between devices, to_everyone(): return lax.all_to_all(copies, BLOCK, 0, 0)  10.7 us
    slice x8, local copies, waits for them, and re-layouts, tap_products(): return sum((ahead(products[depth], 3, 2 - depth) for depth in range(3)))  9.39 us
    all_to_all x1, starting transfers between devices, shards(): lax.all_to_all(coarse_in.reshape(count, sub, tl * hl * w), BLOCK, 0, 0)  8.36 us
    all_to_all x1, starting transfers between devices, shards(): lax.all_to_all(fine_in.reshape(count, sub, 4 * tl * hl * w), BLOCK, 0, 0)  5.92 us
    add x2, other arithmetic, tap_products(): return sum((ahead(products[depth], 3, 2 - depth) for depth in range(3)))  5.72 us
  transfers between devices with their start and end apart: 6, of which 6 were waited for; matrix products, arithmetic and copies ran while one was open for 15% of the time, Pallas kernels for 0%

profile of v1, /device:TPU:0, one launch (start us, length us, event | category | flops | bytes accessed | tf_op | source)
XLA Modules:
  0.0 162.0 jit_solution(3546953004766062033)
XLA Ops:
  0.6 1.7 %reshape_squeeze.6 = bf16[2,2,8,4,4,32]{5,4,3,2,1,0:T(4,128)(2,1)} reshape(bf16[1,2,2,8,512]{4,3,2,1,0:T(8,128)(2,1)} %param.10) | data formatting | bytes 65536 | tf_op jit(solution)/shard_map/reshape;squeeze | solution.py:127
  2.4 1.6 copy.112
  3.9 1.7 %reshape.563 = bf16[16,2,512]{2,1,0:T(2,128)(2,1)} reshape(bf16[16,32,32]{2,1,0:T(8,128)(2,1)} %bitcast.237) | data formatting | bytes 65536
  5.6 8.4 %all-to-all-start.1 = ((bf16[16,2,512]{2,1,0:T(2,128)(2,1)}), bf16[16,2,512]{2,1,0:T(2,128)(2,1)}, u32[]{:S(2)}, u32[]{:S(2)}) async-start(bf16[16,2,512]{2,1,0:T(2,128)(2,1)} %reshape.563), calls=%async_computation.1 | async-start | bytes 65536 | tf_op jit(solution)/shard_map/all_to_all | solution.py:128
  14.0 1.0 constant_dynamic-slice_fusion.1
  18.1 1.2 reshape_squeeze.7
  20.5 0.9 all-to-all-done.1
  21.4 5.9 %all-to-all-start.2 = ((bf16[16,32,128]{2,1,0:T(8,128)(2,1)}), bf16[16,32,128]{2,1,0:T(8,128)(2,1)S(1)}, u32[]{:S(2)}, u32[]{:S(2)}) async-start(bf16[16,32,128]{2,1,0:T(8,128)(2,1)} %copy.123), calls=%async_computation.2 | async-start | bytes 262144 | tf_op jit(solution)/shard_map/all_to_all | solution.py:130
  27.3 2.2 %constant_dynamic-slice_fusion = bf16[27,32,512]{2,1,0:T(8,128)(2,1)} fusion(bf16[27,128,512]{2,1,0:T(8,128)(2,1)} %param.14, s32[]{:T(128)S(6)} %select_n.5), kind=kLoop, calls=%fused_computation.74 | loop fusion | bytes 1769476 | tf_op jit(solution)/shard_map/dynamic_slice | solution.py:136
  30.8 4.1 %all-to-all-done.2 = bf16[16,32,128]{2,1,0:T(8,128)(2,1)S(1)} async-done(((bf16[16,32,128]{2,1,0:T(8,128)(2,1)}), bf16[16,32,128]{2,1,0:T(8,128)(2,1)S(1)}, u32[]{:S(2)}, u32[]{:S(2)}) %all-to-all-start.2) | async-done | bytes 131104 | tf_op jit(solution)/shard_map/all_to_all | solution.py:130
  35.8 3.6 %all-to-all-start = ((bf16[16,2,2,8,512]{4,3,2,1,0:T(8,128)(2,1)}), bf16[16,2,2,8,512]{4,3,2,1,0:T(8,128)(2,1)S(1)}, u32[]{:S(2)}, u32[]{:S(2)}) async-start(bf16[16,2,2,8,512]{4,3,2,1,0:T(8,128)(2,1)} %broadcast_in_dim.61), calls=%async_computation | async-start | bytes 1048576 | tf_op jit(solution)/shard_map/all_to_all | solution.py:13
  40.2 1.2 multiply_reduce_fusion
  41.5 12.4 %all-to-all-done = bf16[16,2,2,8,512]{4,3,2,1,0:T(8,128)(2,1)S(1)} async-done(((bf16[16,2,2,8,512]{4,3,2,1,0:T(8,128)(2,1)}), bf16[16,2,2,8,512]{4,3,2,1,0:T(8,128)(2,1)S(1)}, u32[]{:S(2)}, u32[]{:S(2)}) %all-to-all-start) | async-done | bytes 524320 | tf_op jit(solution)/shard_map/all_to_all | solution.py:13
  54.7 1.2 fusion.20
  55.9 1.2 copy.116
  57.0 2.9 %squeeze.118 = f32[3,3,32,8,8,8]{2,1,0,5,4,3:T(4,128)S(1)} reshape(f32[288,512]{0,1:T(8,128)} %copy.116) | data formatting | bytes 1179648 | tf_op jit(solution)/shard_map/squeeze | solution.py:39
  60.6 1.6 copy.150
  62.2 1.2 copy.114
  63.4 2.9 %squeeze.58 = f32[3,3,32,8,8,8]{2,1,0,5,4,3:T(4,128)S(1)} reshape(f32[288,512]{0,1:T(8,128)} %copy.114) | data formatting | bytes 1179648 | tf_op jit(solution)/shard_map/squeeze | solution.py:39
  66.7 1.5 copy.149
  68.2 1.2 copy.118
  69.4 2.9 %squeeze.119 = f32[3,3,32,8,8,8]{2,1,0,5,4,3:T(4,128)S(1)} reshape(f32[288,512]{0,1:T(8,128)} %copy.118) | data formatting | bytes 1179648 | tf_op jit(solution)/shard_map/squeeze | solution.py:39
  72.3 2.9 %copy_add_fusion.1 = f32[3,3,32,8,8,8]{2,5,4,3,1,0:T(8,128)S(1)} fusion(f32[3,3,32,8,8,8]{2,1,0,5,4,3:T(4,128)S(1)} %squeeze.119, f32[3,3,32,7,8,8]{2,5,4,3,1,0:T(8,128)} %copy.150, f32[3,3,32,6,8,8]{2,5,4,3,1,0:T(8,128)} %copy.149), kind=kLoop, calls=%fused_computation.1 | loop fusion | flops 294912 | bytes 2138112 | tf_op jit(solution)/shard_map/add | solution.py:39
  77.7 3.8 %all-to-all-start.3 = ((bf16[16,32,512]{2,1,0:T(8,128)(2,1)}), bf16[16,32,512]{2,1,0:T(8,128)(2,1)S(1)}, u32[]{:S(2)}, u32[]{:S(2)}) async-start(bf16[16,32,512]{2,1,0:T(8,128)(2,1)} %broadcast_in_dim.71), calls=%async_computation.3 | async-start | bytes 1048576 | tf_op jit(solution)/shard_map/all_to_all | solution.py:13
  83.1 13.3 %all-to-all-done.3 = bf16[16,32,512]{2,1,0:T(8,128)(2,1)S(1)} async-done(((bf16[16,32,512]{2,1,0:T(8,128)(2,1)}), bf16[16,32,512]{2,1,0:T(8,128)(2,1)S(1)}, u32[]{:S(2)}, u32[]{:S(2)}) %all-to-all-start.3) | async-done | bytes 524320 | tf_op jit(solution)/shard_map/all_to_all | solution.py:13
  96.3 1.0 copy.129
  97.4 4.0 %copy.130 = bf16[8,8,8,4,4,32]{5,4,3,2,1,0:T(4,128)(2,1)} copy(bf16[8,8,8,4,4,32]{5,2,1,0,3,4:T(8,128)(2,1)S(1)} %bitcast.209) | data formatting | bytes 1048576 | tf_op jit(solution)/shard_map/transpose | solution.py:151
  101.4 4.9 %reshape_reshape.7 = bf16[512,512]{1,0:T(8,128)(2,1)S(1)} reshape(bf16[8,8,8,4,4,32]{5,4,3,2,1,0:T(4,128)(2,1)} %copy.130) | data formatting | bytes 1048576 | tf_op jit(solution)/shard_map/reshape;reshape | solution.py:35
  107.0 1.2 fusion.19
  108.2 1.2 copy.133
  109.3 2.9 %squeeze.132 = f32[3,3,32,8,8,8]{2,1,0,5,4,3:T(4,128)S(1)} reshape(f32[288,512]{0,1:T(8,128)} %copy.133) | data formatting | bytes 1179648 | tf_op jit(solution)/shard_map/squeeze | solution.py:39
  112.9 1.6 copy.152
  114.5 1.2 copy.131
  115.7 2.9 %squeeze.131 = f32[3,3,32,8,8,8]{2,1,0,5,4,3:T(4,128)S(1)} reshape(f32[288,512]{0,1:T(8,128)} %copy.131) | data formatting | bytes 1179648 | tf_op jit(solution)/shard_map/squeeze | solution.py:39
  119.0 1.5 copy.151
  120.5 1.2 copy.135
  121.7 3.1 %squeeze.133 = f32[3,3,32,8,8,8]{2,1,0,5,4,3:T(4,128)S(1)} reshape(f32[288,512]{0,1:T(8,128)} %copy.135) | data formatting | bytes 1179648 | tf_op jit(solution)/shard_map/squeeze | solution.py:39
  124.8 2.9 %copy_add_fusion = f32[3,3,32,8,8,8]{2,5,4,3,1,0:T(8,128)S(1)} fusion(f32[3,3,32,8,8,8]{2,1,0,5,4,3:T(4,128)S(1)} %squeeze.133, f32[3,3,32,7,8,8]{2,5,4,3,1,0:T(8,128)} %copy.152, f32[3,3,32,6,8,8]{2,5,4,3,1,0:T(8,128)} %copy.151), kind=kLoop, calls=%fused_computation | loop fusion | flops 294912 | bytes 2138112 | tf_op jit(solution)/shard_map/add | solution.py:39
  129.5 1.6 %fusion.15 = (f32[32]{0:T(128)S(1)}, f32[32]{0:T(128)S(1)}, f32[32,2,2,4,2,4,2,8]{0,7,6,4,2,1,5,3:T(8,128)}) fusion(f32[32]{0:T(128)S(1)} %add_rsqrt_fusion, f32[4,4,32,2,2,2,2,8]{2,7,6,5,4,3,1,0:T(8,128)S(1)} %copy-done.2, f32[32]{0:T(128)S(1)} %squeeze.130, f32[32]{0:T(128)S(1)} %dynamic_slice.27, f32[32]{0:T(128)S(1)} %dynamic_slice.25, ...), kind=kLoop, calls=%fused_computation.90 | loop fusion | flops 1179584 | bytes 787200 | tf_op jit(solution)/shard_map/reduce_sum | solution.py:92
  132.0 3.4 %all-to-all-start.5 = ((f32[16,1,128]{2,1,0:T(1,128)}), f32[16,1,128]{2,1,0:T(1,128)S(1)}, u32[]{:S(2)}, u32[]{:S(2)}) async-start(f32[16,1,128]{2,1,0:T(1,128)} %reshape.565), calls=%async_computation.5 | async-start | bytes 16384 | tf_op jit(solution)/shard_map/all_to_all | solution.py:13
  136.3 2.9 %fusion.5 = bf16[32,2,2,4,2,4,2,8]{0,7,6,4,2,1,5,3:T(8,128)(2,1)} fusion(f32[32,2,2,4,2,4,2,8]{0,7,6,4,2,1,5,3:T(8,128)} %get-tuple-element.11, f32[4,4,32,2,2,2,2,8]{2,7,6,5,4,3,1,0:T(8,128)} %get-tuple-element.13, f32[32]{0:T(128)S(1)} %mul.370, f32[32]{0:T(128)} %sub.133, f32[32]{0:T(128)S(1)} %add_rsqrt_fusion, f32[32]{0:T(128)} %copy-done.15, ...), kind=kLoop, calls=%fused_computation.11 | loop fusion | flops 589824 | bytes 688768 | tf_op jit(solution)/shard_map/convert_element_type | solution.py:167
  139.2 1.9 %copy.141 = bf16[16,32,128]{2,1,0:T(8,128)(2,1)} copy(bf16[16,32,128]{1,2,0:T(8,128)(2,1)} %bitcast.224) | data formatting | bytes 262144 | tf_op jit(solution)/shard_map/reshape | solution.py:170
  141.1 1.5 all-to-all-done.5
  142.6 5.4 %all-to-all-start.4 = ((bf16[16,32,128]{2,1,0:T(8,128)(2,1)}), bf16[16,32,128]{2,1,0:T(8,128)(2,1)}, u32[]{:S(2)}, u32[]{:S(2)}) async-start(bf16[16,32,128]{2,1,0:T(8,128)(2,1)} %copy.141), calls=%async_computation.4 | async-start | bytes 262144 | tf_op jit(solution)/shard_map/all_to_all | solution.py:173
  152.1 2.5 %psum.7 = f32[4,512]{1,0:T(4,128)S(1)} all-reduce(f32[4,512]{1,0:T(4,128)S(1)} %reshape.557), channel_id=1, replica_groups=mesh['dp'=2,'frames'=4,'rows'=4] {'dp'}, use_global_device_ids=true, to_apply=%region_12.13 | all-reduce | flops 2048 | bytes 16384 | tf_op jit(solution)/shard_map/psum | solution.py:180
  155.7 1.9 %copy.142 = bf16[16,32,128]{1,2,0:T(8,128)(2,1)} copy(bf16[16,32,128]{2,1,0:T(8,128)(2,1)} %all-to-all-done.4) | data formatting | bytes 262144 | tf_op jit(solution)/shard_map/all_to_all | solution.py:173
  157.6 2.2 %copy.143 = bf16[2,2,2,8,2,4,4,32]{7,6,5,4,3,2,1,0:T(4,128)(2,1)} copy(bf16[2,2,2,8,2,4,4,32]{7,3,1,0,4,2,5,6:T(8,128)(2,1)} %bitcast.222) | data formatting | bytes 262144 | tf_op jit(solution)/shard_map/transpose | solution.py:176
  159.9 2.2 %reshape.555 = bf16[1,2,4,16,512]{4,3,2,1,0:T(8,128)(2,1)} reshape(bf16[2,2,2,8,2,4,4,32]{7,6,5,4,3,2,1,0:T(4,128)(2,1)} %copy.143) | data formatting | bytes 262144 | tf_op jit(solution)/shard_map/reshape | solution.py:177
  (129 shorter events, 23.5 us)
Async XLA Ops:
  0.6 13.4 %copy-start = (bf16[27,128,512]{2,1,0:T(8,128)(2,1)S(1)}, bf16[27,128,512]{2,1,0:T(8,128)(2,1)}, u32[]{:S(2)}) copy-start(bf16[27,128,512]{2,1,0:T(8,128)(2,1)} %param.17) | copy-start | bytes 10616836
  5.6 15.8 %all-to-all-start.1 = ((bf16[16,2,512]{2,1,0:T(2,128)(2,1)}), bf16[16,2,512]{2,1,0:T(2,128)(2,1)}, u32[]{:S(2)}, u32[]{:S(2)}) async-start(bf16[16,2,512]{2,1,0:T(2,128)(2,1)} %reshape.563), calls=%async_computation.1 | async-start | bytes 65536 | tf_op jit(solution)/shard_map/all_to_all | solution.py:128
  15.0 20.0 %copy-start.13 = (bf16[1,2,2,8,512]{4,3,2,1,0:T(8,128)(2,1)S(1)}, bf16[1,2,2,8,512]{4,3,2,1,0:T(8,128)(2,1)}, u32[]{:S(2)}) copy-start(bf16[1,2,2,8,512]{4,3,2,1,0:T(8,128)(2,1)} %param.11) | copy-start | bytes 98308
  17.4 111.2 %copy-start.14 = (f32[32]{0:T(128)}, f32[32]{0:T(128)S(1)}, u32[]{:S(2)}) copy-start(f32[32]{0:T(128)S(1)} %dynamic_slice.25) | copy-start | bytes 388
  21.4 13.5 %all-to-all-start.2 = ((bf16[16,32,128]{2,1,0:T(8,128)(2,1)}), bf16[16,32,128]{2,1,0:T(8,128)(2,1)S(1)}, u32[]{:S(2)}, u32[]{:S(2)}) async-start(bf16[16,32,128]{2,1,0:T(8,128)(2,1)} %copy.123), calls=%async_computation.2 | async-start | bytes 262144 | tf_op jit(solution)/shard_map/all_to_all | solution.py:130
  35.8 18.1 %all-to-all-start = ((bf16[16,2,2,8,512]{4,3,2,1,0:T(8,128)(2,1)}), bf16[16,2,2,8,512]{4,3,2,1,0:T(8,128)(2,1)S(1)}, u32[]{:S(2)}, u32[]{:S(2)}) async-start(bf16[16,2,2,8,512]{4,3,2,1,0:T(8,128)(2,1)} %broadcast_in_dim.61), calls=%async_computation | async-start | bytes 1048576 | tf_op jit(solution)/shard_map/all_to_all | solution.py:13
  39.4 14.6 %copy-start.6 = (bf16[27,32,512]{2,1,0:T(8,128)(2,1)S(1)}, bf16[27,32,512]{2,1,0:T(8,128)(2,1)}, u32[]{:S(2)}) copy-start(bf16[27,32,512]{2,1,0:T(8,128)(2,1)} %constant_dynamic-slice_fusion.1) | copy-start | bytes 2654212
  40.2 14.5 %copy-start.3 = (bf16[16,32,128]{1,2,0:T(8,128)(2,1)}, bf16[16,32,128]{1,2,0:T(8,128)(2,1)S(1)}, u32[]{:S(2)}) copy-start(bf16[16,32,128]{1,2,0:T(8,128)(2,1)S(1)} %copy.124) | copy-start | bytes 393220
  54.0 1.9 %copy-start.7 = (bf16[4,2,4,2,8,512]{5,4,3,2,1,0:T(8,128)(2,1)}, bf16[4,2,4,2,8,512]{5,4,3,2,1,0:T(8,128)(2,1)S(1)}, u32[]{:S(2)}) copy-start(bf16[4,2,4,2,8,512]{5,4,3,2,1,0:T(8,128)(2,1)S(1)} %copy.111) | copy-start | bytes 1572868
  60.6 1.6 %copy-start.11 = (f32[288,512]{1,0:T(8,128)S(1)}, f32[288,512]{1,0:T(8,128)}, u32[]{:S(2)}) copy-start(f32[288,512]{1,0:T(8,128)} %get-tuple-element.39) | copy-start | bytes 1769476
  66.7 1.5 copy-start.9
  75.3 1.2 copy-start.8
  75.5 5.9 %copy-start.4 = (bf16[16,32,128]{1,2,0:T(8,128)(2,1)S(1)}, bf16[16,32,128]{1,2,0:T(8,128)(2,1)}, u32[]{:S(2)}) copy-start(bf16[16,32,128]{1,2,0:T(8,128)(2,1)} %copy-done.3) | copy-start | bytes 393220
  77.7 18.6 %all-to-all-start.3 = ((bf16[16,32,512]{2,1,0:T(8,128)(2,1)}), bf16[16,32,512]{2,1,0:T(8,128)(2,1)S(1)}, u32[]{:S(2)}, u32[]{:S(2)}) async-start(bf16[16,32,512]{2,1,0:T(8,128)(2,1)} %broadcast_in_dim.71), calls=%async_computation.3 | async-start | bytes 1048576 | tf_op jit(solution)/shard_map/all_to_all | solution.py:13
  82.1 46.5 %copy-start.15 = (f32[32]{0:T(128)}, f32[32]{0:T(128)S(1)}, u32[]{:S(2)}) copy-start(f32[32]{0:T(128)S(1)} %squeeze.130) | copy-start | bytes 388
  101.4 4.9 %copy-start.5 = (bf16[27,32,512]{2,1,0:T(8,128)(2,1)S(1)}, bf16[27,32,512]{2,1,0:T(8,128)(2,1)}, u32[]{:S(2)}) copy-start(bf16[27,32,512]{2,1,0:T(8,128)(2,1)} %constant_dynamic-slice_fusion) | copy-start | bytes 2654212
  112.9 1.6 %copy-start.12 = (f32[288,512]{1,0:T(8,128)S(1)}, f32[288,512]{1,0:T(8,128)}, u32[]{:S(2)}) copy-start(f32[288,512]{1,0:T(8,128)} %get-tuple-element.36) | copy-start | bytes 1769476
  119.0 1.5 copy-start.10
  128.3 1.2 copy-start.2
  132.0 10.6 %all-to-all-start.5 = ((f32[16,1,128]{2,1,0:T(1,128)}), f32[16,1,128]{2,1,0:T(1,128)S(1)}, u32[]{:S(2)}, u32[]{:S(2)}) async-start(f32[16,1,128]{2,1,0:T(1,128)} %reshape.565), calls=%async_computation.5 | async-start | bytes 16384 | tf_op jit(solution)/shard_map/all_to_all | solution.py:13
  136.3 25.7 %copy-start.1 = (bf16[27,128,512]{2,1,0:T(8,128)(2,1)S(1)}, bf16[27,128,512]{2,1,0:T(8,128)(2,1)}, u32[]{:S(2)}) copy-start(bf16[27,128,512]{2,1,0:T(8,128)(2,1)} %param.17) | copy-start | bytes 10616836
  142.6 13.1 %all-to-all-start.4 = ((bf16[16,32,128]{2,1,0:T(8,128)(2,1)}), bf16[16,32,128]{2,1,0:T(8,128)(2,1)}, u32[]{:S(2)}, u32[]{:S(2)}) async-start(bf16[16,32,128]{2,1,0:T(8,128)(2,1)} %copy.141), calls=%async_computation.4 | async-start | bytes 262144 | tf_op jit(solution)/shard_map/all_to_all | solution.py:173

commit v2 on v1

--- a/solution.py
+++ b/solution.py
@@ -1,6 +1,11 @@
+import functools
+import math
+
 import jax
 import jax.numpy as jnp
 from jax import lax
+from jax.experimental import pallas as pl
+from jax.experimental.pallas import tpu as pltpu
 from jax.sharding import PartitionSpec as P
 
 GROUPS = 32
@@ -97,7 +102,7 @@
     return grad, sums
 
 
-def shards(
+def plain_shards(
     acts_fine,
     acts_coarse,
     grad_coarse,
@@ -190,7 +195,428 @@
     )
 
 
+def lanes_at(shape, axis):
+    return lax.broadcasted_iota(jnp.int32, shape, axis)
+
+
+def pixel_order(tl, hl, w):
+    size = 4 * tl * hl * w
+    lane = lanes_at((size, size), 1)
+    j, i, t = lane % w, lane // w % hl, lane // (w * hl) % tl
+    q, p = lane // (w * hl * tl) % 2, lane // (2 * w * hl * tl)
+    pixel = (t * 2 * hl + 2 * i + p) * 2 * w + 2 * j + q
+    return (lanes_at((size, size), 0) == pixel).astype(jnp.float32).astype(jnp.bfloat16)
+
+
+def merged_order(nr, outer, tl, cells):
+    size = nr * outer * tl * cells
+    a = lanes_at((size, size), 0)
+    cell, t = a % cells, a // cells % tl
+    o, dev = a // (cells * tl) % outer, a // (cells * tl * outer)
+    target = ((o * tl + t) * nr + dev) * cells + cell
+    return (lanes_at((size, size), 1) == target).astype(jnp.float32).astype(jnp.bfloat16)
+
+
+def packed_order(nr, tl, cells, half):
+    shape = (nr * 128, nr * tl * cells)
+    a = lanes_at(shape, 0)
+    lane, dev = a % 128 - half * tl * cells, a // 128
+    target = (lane // cells * nr + dev) * cells + lane % cells
+    held = (lane >= 0) & (lane < tl * cells)
+    return (held & (lanes_at(shape, 1) == target)).astype(jnp.float32).astype(jnp.bfloat16)
+
+
+def one_hot_dot(a, b, dims):
+    return lax.dot_general(a, b, (dims, ((), ())), preferred_element_type=jnp.float32)
+
+
+def moved(field, distance, kept):
+    size = field.shape[1]
+    return jnp.where(kept, pltpu.roll(field, (-distance) % size, 1), 0.0)
+
+
+def own_column(row, base, sub):
+    shape = (sub, row.shape[1])
+    mine = lanes_at(shape, 1) == lanes_at(shape, 0) + base
+    return jnp.sum(jnp.where(mine, row, 0.0), axis=1, keepdims=True)
+
+
+def as_row(column):
+    shape = (column.shape[0], 128)
+    here = lanes_at(shape, 1) == lanes_at(shape, 0)
+    return jnp.sum(jnp.where(here, column, 0.0), axis=0, keepdims=True)
+
+
+def in_groups(column, group_width):
+    sub = column.shape[0]
+    grouped = jnp.sum(column.reshape(sub // group_width, group_width, 1), axis=1, keepdims=True)
+    return jnp.broadcast_to(grouped, (sub // group_width, group_width, 1)).reshape(sub, 1)
+
+
+def total(parts):
+    return sum(jnp.sum(part, axis=1, keepdims=True) for part in parts)
+
+
+def normalised(parts, gain, bias, entries, group_width):
+    mean = in_groups(total(parts), group_width) / entries
+    square = in_groups(total([part * part for part in parts]), group_width) / entries
+    inv_std = lax.rsqrt(square - mean * mean + EPSILON)
+    normed, slope = [], []
+    for part in parts:
+        unit = (part - mean) * inv_std
+        preact = gain * unit + bias
+        squash = jax.nn.sigmoid(preact)
+        normed.append(unit)
+        slope.append(squash * (1.0 + preact * (1.0 - squash)))
+    return normed, slope, inv_std
+
+
+def finished(convs, normed, slope, cots, gain, inv_std, entries, group_width):
+    pre = [conv * part for conv, part in zip(convs, slope)]
+    one = total(pre)
+    two = total([a * b for a, b in zip(pre, normed)])
+    group_one = in_groups(gain * one, group_width) / entries
+    group_two = in_groups(gain * two, group_width) / entries
+    grads = [
+        cot + inv_std * (gain * part - group_one - unit * group_two)
+        for cot, part, unit in zip(cots, pre, normed)
+    ]
+    return grads, one, two
+
+
+class Plan:
+    def __init__(self, mesh_sizes, acts_coarse, slice_width):
+        self.nf, self.nr = mesh_sizes
+        self.count = self.nf * self.nr
+        self.tl, self.hl, self.w, self.channels = acts_coarse
+        self.slice_width = slice_width
+        self.sub = slice_width // self.nf
+        self.cells = self.hl * self.w
+        self.local = self.tl * self.cells
+        self.image = self.cells * self.nr
+        self.frames = self.tl * self.nf
+        self.places = self.frames * self.image
+        self.group_width = self.channels // GROUPS
+        self.fits = (
+            self.sub == 32
+            and self.group_width == 16
+            and self.cells == 16
+            and self.tl == 2
+            and self.nr == 4
+            and self.channels % 128 == 0
+            and self.slice_width * self.nr == self.channels
+        )
+
+    def place_masks(self):
+        lane = lanes_at((1, self.places), 1)
+        col, row = lane % self.w, lane // self.w % (self.hl * self.nr)
+        last_row = self.hl * self.nr - 1
+        return (lane, col > 0, col < self.w - 1, row > 0, row < last_row)
+
+
+def pack_kernel(plan, g_ref, coarse_ref, fine_ref, out_ref):
+    sub, chunks = plan.sub, plan.channels // 128
+    order = pixel_order(plan.tl, plan.hl, plan.w)
+    fine = one_hot_dot(fine_ref[...], order, ((0,), (0,))).astype(jnp.bfloat16)
+    shape = (plan.local, 128)
+    low = (lanes_at(shape, 0) == lanes_at(shape, 1)).astype(jnp.float32).astype(jnp.bfloat16)
+    high = (lanes_at(shape, 0) + plan.local == lanes_at(shape, 1)).astype(jnp.float32).astype(jnp.bfloat16)
+    first = one_hot_dot(coarse_ref[...], low, ((0,), (0,)))
+    second = one_hot_dot(coarse_ref[...], high, ((0,), (0,)))
+    for f in range(plan.nf):
+        for r in range(plan.nr):
+            dest, c = f * plan.nr + r, r * plan.slice_width + f * sub
+            for k in range(chunks):
+                out_ref[dest, k * plan.local : (k + 1) * plan.local, :] = g_ref[:, k * 128 : (k + 1) * 128]
+            at = chunks * plan.local
+            out_ref[dest, at : at + sub, :] = fine[c : c + sub]
+            at += sub
+            half = sub // 2
+            out_ref[dest, at : at + half, :] = (first[c : c + half] + second[c + half : c + sub]).astype(jnp.bfloat16)
+
+
+def frame_sum(products_ref, tap, sub, lane, places, image):
+    near = products_ref[pl.ds((18 + tap) * sub, sub), :]
+    middle = products_ref[pl.ds((9 + tap) * sub, sub), :]
+    far = products_ref[pl.ds(tap * sub, sub), :]
+    return near + moved(middle, image, lane < places - image) + moved(far, 2 * image, lane < places - 2 * image)
+
+
+def coarse_kernel(plan, got_ref, gain_ref, bias_ref, kernel_ref, out_ref, sums_ref, weights, source, products, sem):
+    sub, nr, nf, cells, tl = plan.sub, plan.nr, plan.nf, plan.cells, plan.tl
+    f, r = lax.axis_index("frames"), lax.axis_index("rows")
+    base = r * plan.slice_width + f * sub
+    copy = pltpu.make_async_copy(
+        kernel_ref.at[:, pl.ds(pl.multiple_of(f * sub, sub), sub), :], weights.at[pl.ds(0, 27)], sem
+    )
+    copy.start()
+    chunks = plan.channels // 128
+    shape = (sub, plan.channels)
+    weights[27] = (lanes_at(shape, 1) == lanes_at(shape, 0) + base).astype(jnp.float32).astype(jnp.bfloat16)
+    for s_f in range(nf):
+        for s_r in range(nr):
+            for t in range(tl):
+                at = (s_f * tl + t) * plan.image + s_r * cells
+                for k in range(chunks):
+                    source[at : at + cells, k * 128 : (k + 1) * 128] = got_ref[
+                        s_f * nr + s_r, k * plan.local + t * cells : k * plan.local + (t + 1) * cells, :
+                    ]
+    at, half = chunks * plan.local + sub, sub // 2
+    stacked = jnp.concatenate(
+        [
+            jnp.concatenate([got_ref[s_f * nr + s_r, at : at + half, :] for s_r in range(nr)], axis=1)
+            for s_f in range(nf)
+        ],
+        axis=0,
+    )
+    halves = [one_hot_dot(stacked, packed_order(nr, tl, cells, h), ((1,), (0,))) for h in range(2)]
+    values = jnp.concatenate(
+        [
+            jnp.concatenate([part[s_f * half : (s_f + 1) * half] for s_f in range(nf)], axis=1)
+            for part in halves
+        ],
+        axis=0,
+    )
+    gain = own_column(gain_ref[...], base, sub)
+    bias = own_column(bias_ref[...], base, sub)
+    entries = plan.places * plan.group_width
+    normed, slope, inv_std = normalised([values], gain, bias, entries, plan.group_width)
+    copy.wait()
+    products[...] = lax.dot_general(
+        weights[...].reshape(28 * sub, plan.channels),
+        source[...],
+        (((1,), (1,)), ((), ())),
+        preferred_element_type=jnp.float32,
+    )
+    lane, has_left, has_right, has_up, has_down = plan.place_masks()
+    by_col = []
+    for col in range(3):
+        parts = [frame_sum(products, 3 * row + col, sub, lane, plan.places, plan.image) for row in range(3)]
+        by_col.append(parts[1] + moved(parts[0], plan.w, has_down) + moved(parts[2], -plan.w, has_up))
+    conv = by_col[1] + moved(by_col[0], 1, has_right) + moved(by_col[2], -1, has_left)
+    cot = products[pl.ds(27 * sub, sub), :]
+    grads, one, two = finished([conv], normed, slope, [cot], gain, inv_std, entries, plan.group_width)
+    quartered = (grads[0] * 0.25).astype(jnp.bfloat16)
+    for dest in range(plan.count):
+        out_ref[dest] = quartered
+    sums_ref[...] = jnp.concatenate([as_row(one), as_row(two)], axis=0)
+
+
+def unpack_kernel(plan, got_ref, gain_ref, bias_ref, normed_ref, slope_ref, inv_ref):
+    sub, nr, nf = plan.sub, plan.nr, plan.nf
+    base = lax.axis_index("rows") * plan.slice_width + lax.axis_index("frames") * sub
+    at = plan.channels // 128 * plan.local
+    stacked = jnp.concatenate(
+        [
+            jnp.concatenate([got_ref[s_f * nr + s_r, at : at + sub, :] for s_r in range(nr)], axis=1)
+            for s_f in range(nf)
+        ],
+        axis=0,
+    )
+    merged = one_hot_dot(stacked, merged_order(nr, 4, plan.tl, plan.cells), ((1,), (0,)))
+    width = plan.tl * plan.image
+    parts = [
+        jnp.concatenate(
+            [merged[s_f * sub : (s_f + 1) * sub, pq * width : (pq + 1) * width] for s_f in range(nf)], axis=1
+        )
+        for pq in range(4)
+    ]
+    gain = own_column(gain_ref[...], base, sub)
+    bias = own_column(bias_ref[...], base, sub)
+    entries = 4 * plan.places * plan.group_width
+    normed, slope, inv_std = normalised(parts, gain, bias, entries, plan.group_width)
+    for pq in range(4):
+        normed_ref[pq] = normed[pq]
+        slope_ref[pq] = slope[pq]
+    inv_ref[...] = jnp.broadcast_to(inv_std, (sub, 128))
+
+
+def fine_kernel(
+    plan, got_ref, normed_ref, slope_ref, inv_ref, gain_ref, sums_ref, kernel_ref, out_ref, weights, source, products, sem
+):
+    sub, nr, nf = plan.sub, plan.nr, plan.nf
+    f, r = lax.axis_index("frames"), lax.axis_index("rows")
+    base = r * plan.slice_width + f * sub
+    copy = pltpu.make_async_copy(
+        kernel_ref.at[:, pl.ds(pl.multiple_of(f * sub, sub), sub), :], weights, sem
+    )
+    copy.start()
+    for s_f in range(nf):
+        for s_r in range(nr):
+            c = s_r * plan.slice_width + s_f * sub
+            source[c : c + sub, :] = got_ref[s_f * nr + s_r]
+    gain = own_column(gain_ref[...], base, sub)
+    copy.wait()
+    products[...] = lax.dot_general(
+        weights[...].reshape(27 * sub, plan.channels),
+        source[...],
+        (((1,), (0,)), ((), ())),
+        preferred_element_type=jnp.float32,
+    )
+    lane, has_left, has_right, has_up, has_down = plan.place_masks()
+    by_row = []
+    for row in range(3):
+        a, b, c = [frame_sum(products, 3 * row + col, sub, lane, plan.places, plan.image) for col in range(3)]
+        by_row.append((a + b + moved(c, -1, has_left), moved(a, 1, has_right) + b + c))
+    convs = [by_row[0][q] + by_row[1][q] + moved(by_row[2][q], -plan.w, has_up) for q in range(2)]
+    convs += [moved(by_row[0][q], plan.w, has_down) + by_row[1][q] + by_row[2][q] for q in range(2)]
+    cot = got_ref[f * nr + r].astype(jnp.float32)
+    entries = 4 * plan.places * plan.group_width
+    grads, one, two = finished(
+        convs,
+        [normed_ref[pq] for pq in range(4)],
+        [slope_ref[pq] for pq in range(4)],
+        [cot] * 4,
+        gain,
+        inv_ref[:, 0:1],
+        entries,
+        plan.group_width,
+    )
+    width = plan.tl * plan.image
+    stacked = jnp.concatenate(
+        [
+            jnp.concatenate(
+                [grads[pq][:, s_f * width : (s_f + 1) * width].astype(jnp.bfloat16) for pq in range(4)], axis=1
+            )
+            for s_f in range(nf)
+        ],
+        axis=0,
+    )
+    sent = one_hot_dot(stacked, merged_order(nr, 4, plan.tl, plan.cells), ((1,), (1,))).astype(jnp.bfloat16)
+    sums = jnp.concatenate([as_row(one), as_row(two), sums_ref[...]], axis=0)
+    top = sums.astype(jnp.bfloat16).astype(jnp.float32)
+    middle = (sums - top).astype(jnp.bfloat16).astype(jnp.float32)
+    low = sums - top - middle
+    coded = jnp.concatenate([top, middle, low, jnp.zeros_like(top)], axis=0).astype(jnp.bfloat16)
+    for s_f in range(nf):
+        for s_r in range(nr):
+            out_ref[s_f * nr + s_r, 0:sub, :] = sent[s_f * sub : (s_f + 1) * sub, s_r * 128 : (s_r + 1) * 128]
+            out_ref[s_f * nr + s_r, sub : sub + 16, :] = coded
+
+
+def spread_kernel(plan, scales, got_ref, out_ref, *rest):
+    sum_refs, source = rest[:4], rest[4]
+    sub, nr, nf = plan.sub, plan.nr, plan.nf
+    for s_f in range(nf):
+        for s_r in range(nr):
+            c = s_r * plan.slice_width + s_f * sub
+            source[c : c + sub, :] = got_ref[s_f * nr + s_r, 0:sub, :]
+    order = pixel_order(plan.tl, plan.hl, plan.w)
+    out_ref[...] = one_hot_dot(order, source[...], ((1,), (1,))).astype(jnp.bfloat16)
+    columns = []
+    for s_r in range(nr):
+        held = 0.0
+        for s_f in range(nf):
+            coded = got_ref[s_f * nr + s_r, sub : sub + 16, :].astype(jnp.float32)
+            sums = coded[0:4] + coded[4:8] + coded[8:12]
+            held = held + (pltpu.roll(sums, s_f * sub, 1) if s_f else sums)
+        columns.append(held)
+    rows = jnp.concatenate(columns, axis=1)
+    for k in range(4):
+        sum_refs[k][...] = rows[k : k + 1] * scales[k]
+
+
+def in_vmem(count):
+    return [pl.BlockSpec(memory_space=pltpu.VMEM)] * count
+
+
+def shape_of(shape, kind):
+    return jax.ShapeDtypeStruct(shape, kind)
+
+
+LIMIT = pltpu.CompilerParams(vmem_limit_bytes=40 * 1024 * 1024)
+
+
+def fast_shards(
+    plan,
+    acts_fine,
+    acts_coarse,
+    grad_coarse,
+    gain_fine,
+    bias_fine,
+    kernel_fine,
+    gain_coarse,
+    bias_coarse,
+    kernel_coarse,
+):
+    nd = lax.axis_size("dp")
+    count, sub, channels, places, local = plan.count, plan.sub, plan.channels, plan.places, plan.local
+    chunks = channels // 128
+    packed_rows = chunks * local + sub + sub // 2
+    f32, bf16 = jnp.float32, jnp.bfloat16
+    packed = pl.pallas_call(
+        functools.partial(pack_kernel, plan),
+        out_shape=shape_of((count, packed_rows, 128), bf16),
+        in_specs=in_vmem(3),
+        out_specs=in_vmem(1)[0],
+        compiler_params=LIMIT,
+    )(
+        grad_coarse.reshape(local, channels),
+        acts_coarse.reshape(local, channels),
+        acts_fine.reshape(4 * local, channels),
+    )
+    got = lax.all_to_all(packed, BLOCK, 0, 0)
+    quartered, coarse_sums = pl.pallas_call(
+        functools.partial(coarse_kernel, plan),
+        out_shape=(shape_of((count, sub, places), bf16), shape_of((2, 128), f32)),
+        in_specs=in_vmem(3) + [pl.BlockSpec(memory_space=pl.ANY)],
+        out_specs=tuple(in_vmem(2)),
+        scratch_shapes=[
+            pltpu.VMEM((28, sub, channels), bf16),
+            pltpu.VMEM((places, channels), bf16),
+            pltpu.VMEM((28 * sub, places), f32),
+            pltpu.SemaphoreType.DMA,
+        ],
+        compiler_params=LIMIT,
+    )(got, gain_coarse.reshape(1, channels), bias_coarse.reshape(1, channels), kernel_coarse)
+    spread = lax.all_to_all(quartered, BLOCK, 0, 0)
+    normed, slope, inv_std = pl.pallas_call(
+        functools.partial(unpack_kernel, plan),
+        out_shape=(
+            shape_of((4, sub, places), f32),
+            shape_of((4, sub, places), f32),
+            shape_of((sub, 128), f32),
+        ),
+        in_specs=in_vmem(3),
+        out_specs=tuple(in_vmem(3)),
+        compiler_params=LIMIT,
+    )(got, gain_fine.reshape(1, channels), bias_fine.reshape(1, channels))
+    sent = pl.pallas_call(
+        functools.partial(fine_kernel, plan),
+        out_shape=shape_of((count, sub + 16, 128), bf16),
+        in_specs=in_vmem(6) + [pl.BlockSpec(memory_space=pl.ANY)],
+        out_specs=in_vmem(1)[0],
+        scratch_shapes=[
+            pltpu.VMEM((27, sub, channels), bf16),
+            pltpu.VMEM((channels, places), bf16),
+            pltpu.VMEM((27 * sub, places), f32),
+            pltpu.SemaphoreType.DMA,
+        ],
+        compiler_params=LIMIT,
+    )(spread, normed, slope, inv_std, gain_fine.reshape(1, channels), coarse_sums, kernel_fine)
+    back = lax.all_to_all(sent, BLOCK, 0, 0)
+    cells = nd * places
+    fine_scale, coarse_scale = 1.0 / math.sqrt(4 * cells), 1.0 / math.sqrt(cells)
+    out, *sums = pl.pallas_call(
+        functools.partial(spread_kernel, plan, (fine_scale, fine_scale, coarse_scale, coarse_scale)),
+        out_shape=(shape_of((4 * local, channels), bf16),) + (shape_of((1, channels), f32),) * 4,
+        in_specs=in_vmem(1),
+        out_specs=tuple(in_vmem(5)),
+        scratch_shapes=[pltpu.VMEM((channels, 4 * local), bf16)],
+        compiler_params=LIMIT,
+    )(back)
+    bias_f, gain_f, bias_c, gain_c = lax.psum(tuple(part.reshape(channels) for part in sums), "dp")
+    return out.reshape(acts_fine.shape), gain_f, bias_f, gain_c, bias_c
+
+
 def solution(mesh):
+    def shards(*arrays):
+        sizes = (lax.axis_size("frames"), lax.axis_size("rows"))
+        plan = Plan(sizes, arrays[1].shape[1:], arrays[5].shape[1])
+        if plan.fits:
+            return fast_shards(plan, *arrays)
+        return plain_shards(*arrays)
+
     in_specs = (
         P("dp", "frames", "rows", None, None),
         P("dp", "frames", "rows", None, None),

time: 164 us -> 76.1 us (0.46)
  local copies, waits for them, and re-layouts: 78.3 us -> 7.79 us
  blocking collectives: 2.47 us -> 42.8 us
  starting transfers between devices: 30.4 us -> 3.58 us
  waiting for transfers between devices: 32.8 us -> 15.1 us
  other arithmetic: 15.5 us -> 0 us
  Pallas kernels: 0 us -> 5.49 us
    all_to_all x0 -> x2, blocking collectives: none -> 39.8 us  [the longest x1 28.5 us: fast_shards(): got = lax.all_to_all(packed, BLOCK, 0, 0)]
    all_to_all x6 -> x1, starting transfers between devices: 30.4 us -> 3.58 us  [fast_shards(): spread = lax.all_to_all(quartered, BLOCK, 0, 0)]
    squeeze x12 -> x0, local copies, waits for them, and re-layouts: 18.2 us -> none  [the longest x6 17.6 us: tap_products(): return sum((ahead(products[depth], 3, 2 - depth) for depth in range(3)))]
    all_to_all x6 -> x1, waiting for transfers between devices: 32.8 us -> 15.1 us  [fast_shards(): spread = lax.all_to_all(quartered, BLOCK, 0, 0)]
    slice x26 -> x0, local copies, waits for them, and re-layouts: 11.8 us -> none  [the longest x8 9.39 us: tap_products(): return sum((ahead(products[depth], 3, 2 - depth) for depth in range(3)))]
    another operation x12 -> x0, local copies, waits for them, and re-layouts: 8.68 us -> none  [the longest x1 4.88 us: tap_products(): source.reshape(frames * rows * cols, channels)]
    transpose x5 -> x0, local copies, waits for them, and re-layouts: 8.49 us -> none  [the longest x1 4.03 us: shards(): source_fine = spread.reshape(nf, nr, sub, frames, rows, w).transpose(3, 4...]
    add x8 -> x0, other arithmetic: 6.42 us -> none  [the longest x2 5.72 us: tap_products(): return sum((ahead(products[depth], 3, 2 - depth) for depth in range(3)))]
  transfers between devices with their start and end apart: 6 -> 1, of which waited for: 6 -> 1; matrix products, arithmetic and copies ran while one was open for 15% -> 0% of each run, Pallas kernels for 0% -> 1%
where the time goes in v2:
time: 76.1 us; the launch traced here: 75.5 us
  blocking collectives  42.8 us (56%)
  waiting for transfers between devices  15.1 us (20%)
  local copies, waits for them, and re-layouts  7.79 us (10%)
  Pallas kernels  5.49 us (7%)
  starting transfers between devices  3.58 us (5%)
    all_to_all x1, blocking collectives, fast_shards(): got = lax.all_to_all(packed, BLOCK, 0, 0)  28.5 us
    all_to_all x1, waiting for transfers between devices, fast_shards(): spread = lax.all_to_all(quartered, BLOCK, 0, 0)  15.1 us
    all_to_all x1, blocking collectives, fast_shards(): back = lax.all_to_all(sent, BLOCK, 0, 0)  11.2 us
    unnamed x18, local copies, waits for them, and re-layouts  7.79 us
    all_to_all x1, starting transfers between devices, fast_shards(): spread = lax.all_to_all(quartered, BLOCK, 0, 0)  3.58 us
    psum x1, blocking collectives, fast_shards(): lax.psum(tuple((part.reshape(channels) for part in sums)), 'dp')  3.04 us
    pallas_call x1, Pallas kernels, fast_shards(): pl.pallas_call(functools.partial(coarse_kernel, plan), out_shape=(shape_o...  2.34 us
  transfers between devices with their start and end apart: 1, of which 1 were waited for; matrix products, arithmetic and copies ran while one was open for 0% of the time, Pallas kernels for 1%

profile of v2, /device:TPU:0, one launch (start us, length us, event | category | flops | bytes accessed | tf_op | source)
XLA Modules:
  0.0 75.5 jit_solution(1769861421450023967)
XLA Ops:
  0.6 0.0 copy-start.2
  0.6 0.9 %copy-done.2 = bf16[1,2,4,16,512]{4,3,2,1,0:T(8,128)(2,1)S(1)} copy-done((bf16[1,2,4,16,512]{4,3,2,1,0:T(8,128)(2,1)S(1)}, bf16[1,2,4,16,512]{4,3,2,1,0:T(8,128)(2,1)}, u32[]{:S(2)}) %copy-start.2) | copy-done | bytes 131096
  1.5 0.0 copy-start.3
  1.5 0.8 %copy-done.3 = bf16[1,2,2,8,512]{4,3,2,1,0:T(8,128)(2,1)S(1)} copy-done((bf16[1,2,2,8,512]{4,3,2,1,0:T(8,128)(2,1)S(1)}, bf16[1,2,2,8,512]{4,3,2,1,0:T(8,128)(2,1)}, u32[]{:S(2)}) %copy-start.3) | copy-done | bytes 32792
  2.3 0.0 copy-start.4
  2.3 0.8 %copy-done.4 = bf16[1,2,2,8,512]{4,3,2,1,0:T(8,128)(2,1)S(1)} copy-done((bf16[1,2,2,8,512]{4,3,2,1,0:T(8,128)(2,1)S(1)}, bf16[1,2,2,8,512]{4,3,2,1,0:T(8,128)(2,1)}, u32[]{:S(2)}) %copy-start.4) | copy-done | bytes 32792
  3.1 0.3 shard_map.128
  3.4 0.0 copy-start.5
  3.4 0.0 copy-start.8
  3.4 28.5 %all_to_all.15.got_ref = bf16[16,176,128]{2,1,0:T(8,128)(2,1)S(1)} all-to-all(bf16[16,176,128]{2,1,0:T(8,128)(2,1)S(1)} %shard_map.128), channel_id=1, replica_groups=mesh['dp'=2,'frames'=4,'rows'=4] {'frames','rows'}, dimensions={0} | all-to-all | bytes 1441792 | tf_op jit(solution)/shard_map/all_to_all | solution.py:558
  31.9 0.0 copy-start
  31.9 2.0 %copy-done = bf16[27,128,512]{2,1,0:T(8,128)(2,1)S(1)} copy-done((bf16[27,128,512]{2,1,0:T(8,128)(2,1)S(1)}, bf16[27,128,512]{2,1,0:T(8,128)(2,1)}, u32[]{:S(2)}) %copy-start) | copy-done | bytes 3538968
  33.9 0.0 copy-start.6
  33.9 0.7 copy-done.6
  34.6 0.0 copy-start.7
  34.6 0.7 copy-done.7
  35.3 2.3 %shard_map.129 = (bf16[16,32,512]{2,1,0:T(8,128)(2,1)}, f32[2,128]{1,0:T(2,128)S(1)}) custom-call(bf16[16,176,128]{2,1,0:T(8,128)(2,1)S(1)} %all_to_all.15.got_ref, f32[1,512]{1,0:T(1,128)S(1)} %bitcast.17, f32[1,512]{1,0:T(1,128)S(1)} %bitcast.18, bf16[27,128,512]{2,1,0:T(8,128)(2,1)S(1)} %copy-done), custom_call_target="tpu_custom_call" | custom-call | tf_op jit(solution)/shard_map/pallas_call | solution.py:559
  37.6 3.6 %all-to-all-start.1 = ((bf16[16,32,512]{2,1,0:T(8,128)(2,1)}), bf16[16,32,512]{2,1,0:T(8,128)(2,1)S(1)}, u32[]{:S(2)}, u32[]{:S(2)}) async-start(bf16[16,32,512]{2,1,0:T(8,128)(2,1)} %get-tuple-element.15), calls=%async_computation.1 | async-start | bytes 1048576 | tf_op jit(solution)/shard_map/all_to_all | solution.py:572
  41.2 0.0 copy-done.5
  41.2 0.0 copy-done.8
  41.2 0.5 shard_map.130
  41.8 15.1 %all-to-all-done.1.got_ref = bf16[16,32,512]{2,1,0:T(8,128)(2,1)S(1)} async-done(((bf16[16,32,512]{2,1,0:T(8,128)(2,1)}), bf16[16,32,512]{2,1,0:T(8,128)(2,1)S(1)}, u32[]{:S(2)}, u32[]{:S(2)}) %all-to-all-start.1) | async-done | bytes 524320 | tf_op jit(solution)/shard_map/all_to_all | solution.py:572
  56.9 0.0 copy-start.1
  56.9 2.0 %copy-done.1 = bf16[27,128,512]{2,1,0:T(8,128)(2,1)S(1)} copy-done((bf16[27,128,512]{2,1,0:T(8,128)(2,1)S(1)}, bf16[27,128,512]{2,1,0:T(8,128)(2,1)}, u32[]{:S(2)}) %copy-start.1) | copy-done | bytes 3538968
  58.9 1.4 %shard_map.131 = bf16[16,48,128]{2,1,0:T(8,128)(2,1)S(1)} custom-call(bf16[16,32,512]{2,1,0:T(8,128)(2,1)S(1)} %all-to-all-done.1.got_ref, f32[4,32,512]{2,1,0:T(8,128)S(1)} %get-tuple-element.16.normed_ref, f32[4,32,512]{2,1,0:T(8,128)S(1)} %get-tuple-element.17.slope_ref, f32[32,128]{1,0:T(8,128)S(1)} %get-tuple-element.18.inv_ref, f32[1,512]{1,0:T(1,128)S(1)} %bitcast.16, ...), custom_call_target="tpu_custom_call" | custom-call | tf_op jit(solution)/shard_map/pallas_call | solution.py:584
  60.3 11.2 %all_to_all.16.got_ref = bf16[16,48,128]{2,1,0:T(8,128)(2,1)S(1)} all-to-all(bf16[16,48,128]{2,1,0:T(8,128)(2,1)S(1)} %shard_map.131), channel_id=1, replica_groups=mesh['dp'=2,'frames'=4,'rows'=4] {'frames','rows'}, dimensions={0} | all-to-all | bytes 393216 | tf_op jit(solution)/shard_map/all_to_all | solution.py:597
  71.6 0.9 %shard_map.132 = (bf16[128,512]{1,0:T(8,128)(2,1)}, f32[1,512]{1,0:T(1,128)S(1)}, f32[1,512]{1,0:T(1,128)S(1)}, f32[1,512]{1,0:T(1,128)S(1)}, f32[1,512]{1,0:T(1,128)S(1)}) custom-call(bf16[16,48,128]{2,1,0:T(8,128)(2,1)S(1)} %all_to_all.16.got_ref), custom_call_target="tpu_custom_call" | custom-call | tf_op jit(solution)/shard_map/pallas_call | solution.py:600
  72.4 3.0 %all-reduce = (f32[512]{0:T(512)}, f32[512]{0:T(512)}, f32[512]{0:T(512)}, f32[512]{0:T(512)}) all-reduce(f32[512]{0:T(512)S(1)} %bitcast.21, f32[512]{0:T(512)S(1)} %bitcast.20, f32[512]{0:T(512)S(1)} %bitcast.23, f32[512]{0:T(512)S(1)} %bitcast.22), channel_id=1, replica_groups=mesh['dp'=2,'frames'=4,'rows'=4] {'dp'}, use_global_device_ids=true, to_apply=%region_0.0 | all-reduce | flops 2048 | bytes 16384 | tf_op jit(solution)/shard_map/psum | solution.py:608
Async XLA Ops:
  0.6 0.9 %copy-start.2 = (bf16[1,2,4,16,512]{4,3,2,1,0:T(8,128)(2,1)S(1)}, bf16[1,2,4,16,512]{4,3,2,1,0:T(8,128)(2,1)}, u32[]{:S(2)}) copy-start(bf16[1,2,4,16,512]{4,3,2,1,0:T(8,128)(2,1)} %param.9) | copy-start | bytes 393220
  1.5 0.8 %copy-start.3 = (bf16[1,2,2,8,512]{4,3,2,1,0:T(8,128)(2,1)S(1)}, bf16[1,2,2,8,512]{4,3,2,1,0:T(8,128)(2,1)}, u32[]{:S(2)}) copy-start(bf16[1,2,2,8,512]{4,3,2,1,0:T(8,128)(2,1)} %param.11) | copy-start | bytes 98308
  2.3 0.8 %copy-start.4 = (bf16[1,2,2,8,512]{4,3,2,1,0:T(8,128)(2,1)S(1)}, bf16[1,2,2,8,512]{4,3,2,1,0:T(8,128)(2,1)}, u32[]{:S(2)}) copy-start(bf16[1,2,2,8,512]{4,3,2,1,0:T(8,128)(2,1)} %param.10) | copy-start | bytes 98308
  3.4 37.9 %copy-start.5 = (f32[512]{0:T(512)S(1)}, f32[512]{0:T(512)}, u32[]{:S(2)}) copy-start(f32[512]{0:T(512)} %param.12) | copy-start | bytes 6148
  3.4 37.9 %copy-start.8 = (f32[512]{0:T(512)S(1)}, f32[512]{0:T(512)}, u32[]{:S(2)}) copy-start(f32[512]{0:T(512)} %param.13) | copy-start | bytes 6148
  31.9 2.0 %copy-start = (bf16[27,128,512]{2,1,0:T(8,128)(2,1)S(1)}, bf16[27,128,512]{2,1,0:T(8,128)(2,1)}, u32[]{:S(2)}) copy-start(bf16[27,128,512]{2,1,0:T(8,128)(2,1)} %kernel_ref.2) | copy-start | bytes 10616836
  33.9 0.7 copy-start.6
  34.6 0.7 copy-start.7
  37.6 19.2 %all-to-all-start.1 = ((bf16[16,32,512]{2,1,0:T(8,128)(2,1)}), bf16[16,32,512]{2,1,0:T(8,128)(2,1)S(1)}, u32[]{:S(2)}, u32[]{:S(2)}) async-start(bf16[16,32,512]{2,1,0:T(8,128)(2,1)} %get-tuple-element.15), calls=%async_computation.1 | async-start | bytes 1048576 | tf_op jit(solution)/shard_map/all_to_all | solution.py:572
  56.9 2.0 %copy-start.1 = (bf16[27,128,512]{2,1,0:T(8,128)(2,1)S(1)}, bf16[27,128,512]{2,1,0:T(8,128)(2,1)}, u32[]{:S(2)}) copy-start(bf16[27,128,512]{2,1,0:T(8,128)(2,1)} %kernel_ref.3) | copy-start | bytes 10616836

commit v3 on v2

--- a/solution.py
+++ b/solution.py
@@ -215,15 +215,6 @@
     o, dev = a // (cells * tl) % outer, a // (cells * tl * outer)
     target = ((o * tl + t) * nr + dev) * cells + cell
     return (lanes_at((size, size), 1) == target).astype(jnp.float32).astype(jnp.bfloat16)
-
-
-def packed_order(nr, tl, cells, half):
-    shape = (nr * 128, nr * tl * cells)
-    a = lanes_at(shape, 0)
-    lane, dev = a % 128 - half * tl * cells, a // 128
-    target = (lane // cells * nr + dev) * cells + lane % cells
-    held = (lane >= 0) & (lane < tl * cells)
-    return (held & (lanes_at(shape, 1) == target)).astype(jnp.float32).astype(jnp.bfloat16)
 
 
 def one_hot_dot(a, b, dims):
@@ -314,25 +305,92 @@
         return (lane, col > 0, col < self.w - 1, row > 0, row < last_row)
 
 
-def pack_kernel(plan, g_ref, coarse_ref, fine_ref, out_ref):
-    sub, chunks = plan.sub, plan.channels // 128
+def fetched(pairs, sems):
+    copies = [pltpu.make_async_copy(src, dst, sems.at[k]) for k, (src, dst) in enumerate(pairs)]
+    for copy in copies:
+        copy.start()
+    return copies
+
+
+def pack_kernel(plan, g_hbm, coarse_hbm, fine_hbm, out_ref, g_ref, coarse_ref, fine_ref, sems):
+    sub, chunks, local = plan.sub, plan.channels // 128, plan.local
+    copies = fetched(((fine_hbm, fine_ref), (coarse_hbm, coarse_ref), (g_hbm, g_ref)), sems)
     order = pixel_order(plan.tl, plan.hl, plan.w)
+    shape = (local, 128)
+    places = [
+        (lanes_at(shape, 0) + k * local == lanes_at(shape, 1)).astype(jnp.float32).astype(jnp.bfloat16)
+        for k in range(4)
+    ]
+    copies[0].wait()
     fine = one_hot_dot(fine_ref[...], order, ((0,), (0,))).astype(jnp.bfloat16)
-    shape = (plan.local, 128)
-    low = (lanes_at(shape, 0) == lanes_at(shape, 1)).astype(jnp.float32).astype(jnp.bfloat16)
-    high = (lanes_at(shape, 0) + plan.local == lanes_at(shape, 1)).astype(jnp.float32).astype(jnp.bfloat16)
-    first = one_hot_dot(coarse_ref[...], low, ((0,), (0,)))
-    second = one_hot_dot(coarse_ref[...], high, ((0,), (0,)))
+    copies[1].wait()
+    quarters = [one_hot_dot(coarse_ref[...], place, ((0,), (0,))) for place in places]
+    copies[2].wait()
     for f in range(plan.nf):
         for r in range(plan.nr):
             dest, c = f * plan.nr + r, r * plan.slice_width + f * sub
             for k in range(chunks):
-                out_ref[dest, k * plan.local : (k + 1) * plan.local, :] = g_ref[:, k * 128 : (k + 1) * 128]
-            at = chunks * plan.local
+                out_ref[dest, k * local : (k + 1) * local, :] = g_ref[:, k * 128 : (k + 1) * 128]
+            at = chunks * local
             out_ref[dest, at : at + sub, :] = fine[c : c + sub]
-            at += sub
-            half = sub // 2
-            out_ref[dest, at : at + half, :] = (first[c : c + half] + second[c + half : c + sub]).astype(jnp.bfloat16)
+            coarse = sum(quarters[k][c + 8 * k : c + 8 * k + 8] for k in range(4))
+            out_ref[dest, at + sub : at + sub + 8, :] = coarse.astype(jnp.bfloat16)
+
+
+def stage_kernel(
+    plan,
+    kernel_c,
+    kernel_f,
+    gain_c,
+    bias_c,
+    gain_f,
+    bias_f,
+    weights_c,
+    weights_f,
+    columns,
+    order,
+    rows,
+    sems,
+):
+    sub = plan.sub
+    f, r = lax.axis_index("frames"), lax.axis_index("rows")
+    base = r * plan.slice_width + f * sub
+    own = pl.ds(pl.multiple_of(f * sub, sub), sub)
+    copies = fetched(
+        [(row, rows.at[k]) for k, row in enumerate((gain_c, bias_c, gain_f, bias_f))]
+        + [(kernel_c.at[:, own, :], weights_c.at[pl.ds(0, 27)]), (kernel_f.at[:, own, :], weights_f)],
+        sems,
+    )
+    shape = (sub, plan.channels)
+    weights_c[27] = (lanes_at(shape, 1) == lanes_at(shape, 0) + base).astype(jnp.float32).astype(jnp.bfloat16)
+    order[...] = merged_order(plan.nr, 4, plan.tl, plan.cells)
+    for copy in copies:
+        copy.wait()
+    for k in range(4):
+        columns[k] = jnp.broadcast_to(own_column(rows[k], base, sub), (sub, 128))
+
+
+def by_frame_device(plan, got_ref, at, height):
+    return jnp.concatenate(
+        [
+            jnp.concatenate(
+                [got_ref[f * plan.nr + r, at : at + height, :] for r in range(plan.nr)], axis=1
+            )
+            for f in range(plan.nf)
+        ],
+        axis=0,
+    )
+
+
+def in_places(plan, merged, height):
+    width = plan.tl * plan.image
+    return [
+        jnp.concatenate(
+            [merged[f * height : (f + 1) * height, k * width : (k + 1) * width] for f in range(plan.nf)],
+            axis=1,
+        )
+        for k in range(4)
+    ]
 
 
 def frame_sum(products_ref, tap, sub, lane, places, image):
@@ -342,52 +400,29 @@
     return near + moved(middle, image, lane < places - image) + moved(far, 2 * image, lane < places - 2 * image)
 
 
-def coarse_kernel(plan, got_ref, gain_ref, bias_ref, kernel_ref, out_ref, sums_ref, weights, source, products, sem):
-    sub, nr, nf, cells, tl = plan.sub, plan.nr, plan.nf, plan.cells, plan.tl
-    f, r = lax.axis_index("frames"), lax.axis_index("rows")
-    base = r * plan.slice_width + f * sub
-    copy = pltpu.make_async_copy(
-        kernel_ref.at[:, pl.ds(pl.multiple_of(f * sub, sub), sub), :], weights.at[pl.ds(0, 27)], sem
-    )
-    copy.start()
+def coarse_kernel(plan, got_ref, weights, columns, order, out_ref, sums_ref, source, products):
+    sub, nr, nf, cells, tl, local = plan.sub, plan.nr, plan.nf, plan.cells, plan.tl, plan.local
     chunks = plan.channels // 128
-    shape = (sub, plan.channels)
-    weights[27] = (lanes_at(shape, 1) == lanes_at(shape, 0) + base).astype(jnp.float32).astype(jnp.bfloat16)
     for s_f in range(nf):
         for s_r in range(nr):
             for t in range(tl):
                 at = (s_f * tl + t) * plan.image + s_r * cells
                 for k in range(chunks):
                     source[at : at + cells, k * 128 : (k + 1) * 128] = got_ref[
-                        s_f * nr + s_r, k * plan.local + t * cells : k * plan.local + (t + 1) * cells, :
+                        s_f * nr + s_r, k * local + t * cells : k * local + (t + 1) * cells, :
                     ]
-    at, half = chunks * plan.local + sub, sub // 2
-    stacked = jnp.concatenate(
-        [
-            jnp.concatenate([got_ref[s_f * nr + s_r, at : at + half, :] for s_r in range(nr)], axis=1)
-            for s_f in range(nf)
-        ],
-        axis=0,
-    )
-    halves = [one_hot_dot(stacked, packed_order(nr, tl, cells, h), ((1,), (0,))) for h in range(2)]
-    values = jnp.concatenate(
-        [
-            jnp.concatenate([part[s_f * half : (s_f + 1) * half] for s_f in range(nf)], axis=1)
-            for part in halves
-        ],
-        axis=0,
-    )
-    gain = own_column(gain_ref[...], base, sub)
-    bias = own_column(bias_ref[...], base, sub)
-    entries = plan.places * plan.group_width
-    normed, slope, inv_std = normalised([values], gain, bias, entries, plan.group_width)
-    copy.wait()
     products[...] = lax.dot_general(
         weights[...].reshape(28 * sub, plan.channels),
         source[...],
         (((1,), (1,)), ((), ())),
         preferred_element_type=jnp.float32,
     )
+    packed = by_frame_device(plan, got_ref, chunks * local + sub, 8)
+    merged = one_hot_dot(packed, order[...], ((1,), (0,)))
+    values = jnp.concatenate(in_places(plan, merged, 8), axis=0)
+    gain, bias = columns[0][:, 0:1], columns[1][:, 0:1]
+    entries = plan.places * plan.group_width
+    normed, slope, inv_std = normalised([values], gain, bias, entries, plan.group_width)
     lane, has_left, has_right, has_up, has_down = plan.place_masks()
     by_col = []
     for col in range(3):
@@ -402,27 +437,11 @@
     sums_ref[...] = jnp.concatenate([as_row(one), as_row(two)], axis=0)
 
 
-def unpack_kernel(plan, got_ref, gain_ref, bias_ref, normed_ref, slope_ref, inv_ref):
-    sub, nr, nf = plan.sub, plan.nr, plan.nf
-    base = lax.axis_index("rows") * plan.slice_width + lax.axis_index("frames") * sub
-    at = plan.channels // 128 * plan.local
-    stacked = jnp.concatenate(
-        [
-            jnp.concatenate([got_ref[s_f * nr + s_r, at : at + sub, :] for s_r in range(nr)], axis=1)
-            for s_f in range(nf)
-        ],
-        axis=0,
-    )
-    merged = one_hot_dot(stacked, merged_order(nr, 4, plan.tl, plan.cells), ((1,), (0,)))
-    width = plan.tl * plan.image
-    parts = [
-        jnp.concatenate(
-            [merged[s_f * sub : (s_f + 1) * sub, pq * width : (pq + 1) * width] for s_f in range(nf)], axis=1
-        )
-        for pq in range(4)
-    ]
-    gain = own_column(gain_ref[...], base, sub)
-    bias = own_column(bias_ref[...], base, sub)
+def unpack_kernel(plan, got_ref, columns, order, normed_ref, slope_ref, inv_ref):
+    sub = plan.sub
+    packed = by_frame_device(plan, got_ref, plan.channels // 128 * plan.local, sub)
+    parts = in_places(plan, one_hot_dot(packed, order[...], ((1,), (0,))), sub)
+    gain, bias = columns[2][:, 0:1], columns[3][:, 0:1]
     entries = 4 * plan.places * plan.group_width
     normed, slope, inv_std = normalised(parts, gain, bias, entries, plan.group_width)
     for pq in range(4):
@@ -432,21 +451,15 @@
 
 
 def fine_kernel(
-    plan, got_ref, normed_ref, slope_ref, inv_ref, gain_ref, sums_ref, kernel_ref, out_ref, weights, source, products, sem
+    plan, got_ref, normed_ref, slope_ref, inv_ref, columns, order, sums_ref, weights, out_ref, source, products
 ):
     sub, nr, nf = plan.sub, plan.nr, plan.nf
     f, r = lax.axis_index("frames"), lax.axis_index("rows")
-    base = r * plan.slice_width + f * sub
-    copy = pltpu.make_async_copy(
-        kernel_ref.at[:, pl.ds(pl.multiple_of(f * sub, sub), sub), :], weights, sem
-    )
-    copy.start()
     for s_f in range(nf):
         for s_r in range(nr):
             c = s_r * plan.slice_width + s_f * sub
             source[c : c + sub, :] = got_ref[s_f * nr + s_r]
-    gain = own_column(gain_ref[...], base, sub)
-    copy.wait()
+    gain = columns[2][:, 0:1]
     products[...] = lax.dot_general(
         weights[...].reshape(27 * sub, plan.channels),
         source[...],
@@ -482,16 +495,14 @@
         ],
         axis=0,
     )
-    sent = one_hot_dot(stacked, merged_order(nr, 4, plan.tl, plan.cells), ((1,), (1,))).astype(jnp.bfloat16)
+    sent = one_hot_dot(stacked, order[...], ((1,), (1,))).astype(jnp.bfloat16)
     sums = jnp.concatenate([as_row(one), as_row(two), sums_ref[...]], axis=0)
     top = sums.astype(jnp.bfloat16).astype(jnp.float32)
-    middle = (sums - top).astype(jnp.bfloat16).astype(jnp.float32)
-    low = sums - top - middle
-    coded = jnp.concatenate([top, middle, low, jnp.zeros_like(top)], axis=0).astype(jnp.bfloat16)
+    coded = jnp.concatenate([top, sums - top], axis=0).astype(jnp.bfloat16)
     for s_f in range(nf):
         for s_r in range(nr):
             out_ref[s_f * nr + s_r, 0:sub, :] = sent[s_f * sub : (s_f + 1) * sub, s_r * 128 : (s_r + 1) * 128]
-            out_ref[s_f * nr + s_r, sub : sub + 16, :] = coded
+            out_ref[s_f * nr + s_r, sub : sub + 8, :] = coded
 
 
 def spread_kernel(plan, scales, got_ref, out_ref, *rest):
@@ -507,8 +518,8 @@
     for s_r in range(nr):
         held = 0.0
         for s_f in range(nf):
-            coded = got_ref[s_f * nr + s_r, sub : sub + 16, :].astype(jnp.float32)
-            sums = coded[0:4] + coded[4:8] + coded[8:12]
+            coded = got_ref[s_f * nr + s_r, sub : sub + 8, :].astype(jnp.float32)
+            sums = coded[0:4] + coded[4:8]
             held = held + (pltpu.roll(sums, s_f * sub, 1) if s_f else sums)
         columns.append(held)
     rows = jnp.concatenate(columns, axis=1)
@@ -518,6 +529,10 @@
 
 def in_vmem(count):
     return [pl.BlockSpec(memory_space=pltpu.VMEM)] * count
+
+
+def in_hbm(count):
+    return [pl.BlockSpec(memory_space=pltpu.HBM)] * count
 
 
 def shape_of(shape, kind):
@@ -542,13 +557,18 @@
     nd = lax.axis_size("dp")
     count, sub, channels, places, local = plan.count, plan.sub, plan.channels, plan.places, plan.local
     chunks = channels // 128
-    packed_rows = chunks * local + sub + sub // 2
     f32, bf16 = jnp.float32, jnp.bfloat16
     packed = pl.pallas_call(
         functools.partial(pack_kernel, plan),
-        out_shape=shape_of((count, packed_rows, 128), bf16),
-        in_specs=in_vmem(3),
+        out_shape=shape_of((count, chunks * local + sub + 8, 128), bf16),
+        in_specs=in_hbm(3),
         out_specs=in_vmem(1)[0],
+        scratch_shapes=[
+            pltpu.VMEM((local, channels), bf16),
+            pltpu.VMEM((local, channels), bf16),
+            pltpu.VMEM((4 * local, channels), bf16),
+            pltpu.SemaphoreType.DMA((3,)),
+        ],
         compiler_params=LIMIT,
     )(
         grad_coarse.reshape(local, channels),
@@ -556,19 +576,28 @@
         acts_fine.reshape(4 * local, channels),
     )
     got = lax.all_to_all(packed, BLOCK, 0, 0)
+    rows = [part.reshape(1, channels) for part in (gain_coarse, bias_coarse, gain_fine, bias_fine)]
+    weights_c, weights_f, columns, order = pl.pallas_call(
+        functools.partial(stage_kernel, plan),
+        out_shape=(
+            shape_of((28, sub, channels), bf16),
+            shape_of((27, sub, channels), bf16),
+            shape_of((4, sub, 128), f32),
+            shape_of((4 * plan.nr * local, 4 * plan.nr * local), bf16),
+        ),
+        in_specs=in_hbm(6),
+        out_specs=tuple(in_vmem(4)),
+        scratch_shapes=[pltpu.VMEM((4, 1, channels), f32), pltpu.SemaphoreType.DMA((6,))],
+        compiler_params=LIMIT,
+    )(kernel_coarse, kernel_fine, *rows)
     quartered, coarse_sums = pl.pallas_call(
         functools.partial(coarse_kernel, plan),
         out_shape=(shape_of((count, sub, places), bf16), shape_of((2, 128), f32)),
-        in_specs=in_vmem(3) + [pl.BlockSpec(memory_space=pl.ANY)],
+        in_specs=in_vmem(4),
         out_specs=tuple(in_vmem(2)),
-        scratch_shapes=[
-            pltpu.VMEM((28, sub, channels), bf16),
-            pltpu.VMEM((places, channels), bf16),
-            pltpu.VMEM((28 * sub, places), f32),
-            pltpu.SemaphoreType.DMA,
-        ],
+        scratch_shapes=[pltpu.VMEM((places, channels), bf16), pltpu.VMEM((28 * sub, places), f32)],
         compiler_params=LIMIT,
-    )(got, gain_coarse.reshape(1, channels), bias_coarse.reshape(1, channels), kernel_coarse)
+    )(got, weights_c, columns, order)
     spread = lax.all_to_all(quartered, BLOCK, 0, 0)
     normed, slope, inv_std = pl.pallas_call(
         functools.partial(unpack_kernel, plan),
@@ -580,20 +609,15 @@
         in_specs=in_vmem(3),
         out_specs=tuple(in_vmem(3)),
         compiler_params=LIMIT,
-    )(got, gain_fine.reshape(1, channels), bias_fine.reshape(1, channels))
+    )(got, columns, order)
     sent = pl.pallas_call(
         functools.partial(fine_kernel, plan),
-        out_shape=shape_of((count, sub + 16, 128), bf16),
-        in_specs=in_vmem(6) + [pl.BlockSpec(memory_space=pl.ANY)],
+        out_shape=shape_of((count, sub + 8, 128), bf16),
+        in_specs=in_vmem(8),
         out_specs=in_vmem(1)[0],
-        scratch_shapes=[
-            pltpu.VMEM((27, sub, channels), bf16),
-            pltpu.VMEM((channels, places), bf16),
-            pltpu.VMEM((27 * sub, places), f32),
-            pltpu.SemaphoreType.DMA,
-        ],
+        scratch_shapes=[pltpu.VMEM((channels, places), bf16), pltpu.VMEM((27 * sub, places), f32)],
         compiler_params=LIMIT,
-    )(spread, normed, slope, inv_std, gain_fine.reshape(1, channels), coarse_sums, kernel_fine)
+    )(spread, normed, slope, inv_std, columns, order, coarse_sums, weights_f)
     back = lax.all_to_all(sent, BLOCK, 0, 0)
     cells = nd * places
     fine_scale, coarse_scale = 1.0 / math.sqrt(4 * cells), 1.0 / math.sqrt(cells)

time: 76.1 us -> 70.6 us (0.928)
  blocking collectives: 42.8 us -> 13.6 us
  waiting for transfers between devices: 15.1 us -> 27.7 us
  starting transfers between devices: 3.58 us -> 11.9 us
  local copies, waits for them, and re-layouts: 7.79 us -> 9.92 us
    all_to_all x1 -> x0, blocking collectives: 28.5 us -> none  [fast_shards(): got = lax.all_to_all(packed, BLOCK, 0, 0)]
    all_to_all x0 -> x1, waiting for transfers between devices: none -> 12.4 us  [fast_shards(): got = lax.all_to_all(packed, BLOCK, 0, 0)]
    all_to_all x0 -> x1, starting transfers between devices: none -> 8.33 us  [fast_shards(): got = lax.all_to_all(packed, BLOCK, 0, 0)]
    unnamed x18 -> x20, local copies, waits for them, and re-layouts: 7.79 us -> 9.92 us
    pallas_call x1, Pallas kernels: 0.31 us -> 1.81 us  [fast_shards(): pl.pallas_call(functools.partial(pack_kernel, plan), out_shape=shape_of((...]
    pallas_call x1, Pallas kernels: 2.34 us -> 1.19 us  [fast_shards(): pl.pallas_call(functools.partial(coarse_kernel, plan), out_shape=(shape_o...]
  transfers between devices with their start and end apart: 1 -> 2, of which waited for: 1 -> 2; matrix products, arithmetic and copies ran while one was open for 0% -> 0% of each run, Pallas kernels for 1% -> 1%
where the time goes in v3:
time: 70.6 us; the launch traced here: 69.9 us
  waiting for transfers between devices  27.7 us (39%)
  blocking collectives  13.6 us (19%)
  starting transfers between devices  11.9 us (17%)
  local copies, waits for them, and re-layouts  9.92 us (14%)
  Pallas kernels  6.1 us (9%)
  between operations  0.72 us (1%)
    all_to_all x1, waiting for transfers between devices, fast_shards(): spread = lax.all_to_all(quartered, BLOCK, 0, 0)  15.2 us
    all_to_all x1, waiting for transfers between devices, fast_shards(): got = lax.all_to_all(packed, BLOCK, 0, 0)  12.4 us
    all_to_all x1, blocking collectives, fast_shards(): back = lax.all_to_all(sent, BLOCK, 0, 0)  10.6 us
    unnamed x20, local copies, waits for them, and re-layouts  9.92 us
    all_to_all x1, starting transfers between devices, fast_shards(): got = lax.all_to_all(packed, BLOCK, 0, 0)  8.33 us
    all_to_all x1, starting transfers between devices, fast_shards(): spread = lax.all_to_all(quartered, BLOCK, 0, 0)  3.57 us
    psum x1, blocking collectives, fast_shards(): lax.psum(tuple((part.reshape(channels) for part in sums)), 'dp')  3.04 us
    pallas_call x1, Pallas kernels, fast_shards(): pl.pallas_call(functools.partial(pack_kernel, plan), out_shape=shape_of((...  1.81 us
  transfers between devices with their start and end apart: 2, of which 2 were waited for; matrix products, arithmetic and copies ran while one was open for 0% of the time, Pallas kernels for 1%

profile of v3, /device:TPU:0, one launch (start us, length us, event | category | flops | bytes accessed | tf_op | source)
XLA Modules:
  0.0 69.9 jit_solution(14771227454910302085)
XLA Ops:
  0.6 0.0 copy-start.3
  0.6 0.9 %copy-done.3 = bf16[1,2,4,16,512]{4,3,2,1,0:T(8,128)(2,1)S(1)} copy-done((bf16[1,2,4,16,512]{4,3,2,1,0:T(8,128)(2,1)S(1)}, bf16[1,2,4,16,512]{4,3,2,1,0:T(8,128)(2,1)}, u32[]{:S(2)}) %copy-start.3) | copy-done | bytes 131096
  1.5 0.0 copy-start.4
  1.5 0.8 %copy-done.4 = bf16[1,2,2,8,512]{4,3,2,1,0:T(8,128)(2,1)S(1)} copy-done((bf16[1,2,2,8,512]{4,3,2,1,0:T(8,128)(2,1)S(1)}, bf16[1,2,2,8,512]{4,3,2,1,0:T(8,128)(2,1)}, u32[]{:S(2)}) %copy-start.4) | copy-done | bytes 32792
  2.3 0.0 copy-start.5
  2.3 0.8 %copy-done.5 = bf16[1,2,2,8,512]{4,3,2,1,0:T(8,128)(2,1)S(1)} copy-done((bf16[1,2,2,8,512]{4,3,2,1,0:T(8,128)(2,1)S(1)}, bf16[1,2,2,8,512]{4,3,2,1,0:T(8,128)(2,1)}, u32[]{:S(2)}) %copy-start.5) | copy-done | bytes 32792
  3.1 1.8 %shard_map.128 = bf16[16,168,128]{2,1,0:T(8,128)(2,1)} custom-call(bf16[32,512]{1,0:T(8,128)(2,1)S(1)} %bitcast.13, bf16[32,512]{1,0:T(8,128)(2,1)S(1)} %bitcast.14, bf16[128,512]{1,0:T(8,128)(2,1)S(1)} %bitcast.12), custom_call_target="tpu_custom_call" | custom-call | tf_op jit(solution)/shard_map/pallas_call | solution.py:561
  4.9 8.3 %all-to-all-start = ((bf16[16,168,128]{2,1,0:T(8,128)(2,1)}), bf16[16,168,128]{2,1,0:T(8,128)(2,1)S(1)}, u32[]{:S(2)}, u32[]{:S(2)}) async-start(bf16[16,168,128]{2,1,0:T(8,128)(2,1)} %shard_map.128), calls=%async_computation | async-start | bytes 1376256 | tf_op jit(solution)/shard_map/all_to_all | solution.py:578
  13.2 0.0 copy-start
  13.2 2.0 %copy-done = bf16[27,128,512]{2,1,0:T(8,128)(2,1)S(1)} copy-done((bf16[27,128,512]{2,1,0:T(8,128)(2,1)S(1)}, bf16[27,128,512]{2,1,0:T(8,128)(2,1)}, u32[]{:S(2)}) %copy-start) | copy-done | bytes 3538968
  15.2 0.0 copy-start.1
  15.2 2.0 %copy-done.1 = bf16[27,128,512]{2,1,0:T(8,128)(2,1)S(1)} copy-done((bf16[27,128,512]{2,1,0:T(8,128)(2,1)S(1)}, bf16[27,128,512]{2,1,0:T(8,128)(2,1)}, u32[]{:S(2)}) %copy-start.1) | copy-done | bytes 3538968
  17.2 0.0 copy-start.6
  17.2 0.7 copy-done.6
  17.9 0.0 copy-start.7
  17.9 0.7 copy-done.7
  18.6 0.0 copy-start.8
  18.6 0.7 copy-done.8
  19.3 0.0 copy-start.9
  19.3 0.7 copy-done.9
  19.9 0.5 shard_map.129
  20.5 12.4 %all-to-all-done.got_ref = bf16[16,168,128]{2,1,0:T(8,128)(2,1)S(1)} async-done(((bf16[16,168,128]{2,1,0:T(8,128)(2,1)}), bf16[16,168,128]{2,1,0:T(8,128)(2,1)S(1)}, u32[]{:S(2)}, u32[]{:S(2)}) %all-to-all-start) | async-done | bytes 688160 | tf_op jit(solution)/shard_map/all_to_all | solution.py:578
  32.9 1.2 %shard_map.130 = (bf16[16,32,512]{2,1,0:T(8,128)(2,1)S(1)}, f32[2,128]{1,0:T(2,128)S(1)}) custom-call(bf16[16,168,128]{2,1,0:T(8,128)(2,1)S(1)} %all-to-all-done.got_ref, bf16[28,32,512]{2,1,0:T(8,128)(2,1)S(1)} %get-tuple-element.19.weights, f32[4,32,128]{2,1,0:T(8,128)S(1)} %get-tuple-element.20.columns, bf16[512,512]{1,0:T(8,128)(2,1)S(1)} %get-tuple-element.21.order), custom_call_target="tpu_custom_call" | custom-call | tf_op jit(solution)/shard_map/pallas_call | solution.py:593
  34.1 0.0 copy-start.2
  34.1 0.8 %copy-done.2 = bf16[16,32,512]{2,1,0:T(8,128)(2,1)} copy-done((bf16[16,32,512]{2,1,0:T(8,128)(2,1)}, bf16[16,32,512]{2,1,0:T(8,128)(2,1)S(1)}, u32[]{:S(2)}) %copy-start.2) | copy-done | bytes 524312
  34.9 3.6 %all-to-all-start.1 = ((bf16[16,32,512]{2,1,0:T(8,128)(2,1)}), bf16[16,32,512]{2,1,0:T(8,128)(2,1)S(1)}, u32[]{:S(2)}, u32[]{:S(2)}) async-start(bf16[16,32,512]{2,1,0:T(8,128)(2,1)} %copy-done.2), calls=%async_computation.1 | async-start | bytes 1048576 | tf_op jit(solution)/shard_map/all_to_all | solution.py:601
  38.5 0.4 shard_map.131
  38.9 15.2 %all-to-all-done.1.got_ref = bf16[16,32,512]{2,1,0:T(8,128)(2,1)S(1)} async-done(((bf16[16,32,512]{2,1,0:T(8,128)(2,1)}), bf16[16,32,512]{2,1,0:T(8,128)(2,1)S(1)}, u32[]{:S(2)}, u32[]{:S(2)}) %all-to-all-start.1) | async-done | bytes 524320 | tf_op jit(solution)/shard_map/all_to_all | solution.py:601
  54.2 1.3 %shard_map.132 = bf16[16,40,128]{2,1,0:T(8,128)(2,1)S(1)} custom-call(bf16[16,32,512]{2,1,0:T(8,128)(2,1)S(1)} %all-to-all-done.1.got_ref, f32[4,32,512]{2,1,0:T(8,128)S(1)} %get-tuple-element.23.normed_ref, f32[4,32,512]{2,1,0:T(8,128)S(1)} %get-tuple-element.24.slope_ref, f32[32,128]{1,0:T(8,128)S(1)} %get-tuple-element.25.inv_ref, ...), custom_call_target="tpu_custom_call" | custom-call | tf_op jit(solution)/shard_map/pallas_call | solution.py:613
  55.5 10.6 %all_to_all.15.got_ref = bf16[16,40,128]{2,1,0:T(8,128)(2,1)S(1)} all-to-all(bf16[16,40,128]{2,1,0:T(8,128)(2,1)S(1)} %shard_map.132), channel_id=1, replica_groups=mesh['dp'=2,'frames'=4,'rows'=4] {'frames','rows'}, dimensions={0} | all-to-all | bytes 327680 | tf_op jit(solution)/shard_map/all_to_all | solution.py:621
  66.1 0.9 %shard_map.133 = (bf16[128,512]{1,0:T(8,128)(2,1)}, f32[1,512]{1,0:T(1,128)S(1)}, f32[1,512]{1,0:T(1,128)S(1)}, f32[1,512]{1,0:T(1,128)S(1)}, f32[1,512]{1,0:T(1,128)S(1)}) custom-call(bf16[16,40,128]{2,1,0:T(8,128)(2,1)S(1)} %all_to_all.15.got_ref), custom_call_target="tpu_custom_call" | custom-call | tf_op jit(solution)/shard_map/pallas_call | solution.py:624
  66.9 3.0 %all-reduce = (f32[512]{0:T(512)}, f32[512]{0:T(512)}, f32[512]{0:T(512)}, f32[512]{0:T(512)}) all-reduce(f32[512]{0:T(512)S(1)} %bitcast.16, f32[512]{0:T(512)S(1)} %bitcast.15, f32[512]{0:T(512)S(1)} %bitcast.18, f32[512]{0:T(512)S(1)} %bitcast.17), channel_id=1, replica_groups=mesh['dp'=2,'frames'=4,'rows'=4] {'dp'}, use_global_device_ids=true, to_apply=%region_0.0 | all-reduce | flops 2048 | bytes 16384 | tf_op jit(solution)/shard_map/psum | solution.py:632
Async XLA Ops:
  0.6 0.9 %copy-start.3 = (bf16[1,2,4,16,512]{4,3,2,1,0:T(8,128)(2,1)S(1)}, bf16[1,2,4,16,512]{4,3,2,1,0:T(8,128)(2,1)}, u32[]{:S(2)}) copy-start(bf16[1,2,4,16,512]{4,3,2,1,0:T(8,128)(2,1)} %param.9) | copy-start | bytes 393220
  1.5 0.8 %copy-start.4 = (bf16[1,2,2,8,512]{4,3,2,1,0:T(8,128)(2,1)S(1)}, bf16[1,2,2,8,512]{4,3,2,1,0:T(8,128)(2,1)}, u32[]{:S(2)}) copy-start(bf16[1,2,2,8,512]{4,3,2,1,0:T(8,128)(2,1)} %param.11) | copy-start | bytes 98308
  2.3 0.8 %copy-start.5 = (bf16[1,2,2,8,512]{4,3,2,1,0:T(8,128)(2,1)S(1)}, bf16[1,2,2,8,512]{4,3,2,1,0:T(8,128)(2,1)}, u32[]{:S(2)}) copy-start(bf16[1,2,2,8,512]{4,3,2,1,0:T(8,128)(2,1)} %param.10) | copy-start | bytes 98308
  4.9 28.0 %all-to-all-start = ((bf16[16,168,128]{2,1,0:T(8,128)(2,1)}), bf16[16,168,128]{2,1,0:T(8,128)(2,1)S(1)}, u32[]{:S(2)}, u32[]{:S(2)}) async-start(bf16[16,168,128]{2,1,0:T(8,128)(2,1)} %shard_map.128), calls=%async_computation | async-start | bytes 1376256 | tf_op jit(solution)/shard_map/all_to_all | solution.py:578
  13.2 2.0 %copy-start = (bf16[27,128,512]{2,1,0:T(8,128)(2,1)S(1)}, bf16[27,128,512]{2,1,0:T(8,128)(2,1)}, u32[]{:S(2)}) copy-start(bf16[27,128,512]{2,1,0:T(8,128)(2,1)} %kernel_c.1) | copy-start | bytes 10616836
  15.2 2.0 %copy-start.1 = (bf16[27,128,512]{2,1,0:T(8,128)(2,1)S(1)}, bf16[27,128,512]{2,1,0:T(8,128)(2,1)}, u32[]{:S(2)}) copy-start(bf16[27,128,512]{2,1,0:T(8,128)(2,1)} %kernel_f.1) | copy-start | bytes 10616836
  17.2 0.7 copy-start.6
  17.9 0.7 copy-start.7
  18.6 0.7 copy-start.8
  19.3 0.7 copy-start.9
  34.1 0.8 %copy-start.2 = (bf16[16,32,512]{2,1,0:T(8,128)(2,1)}, bf16[16,32,512]{2,1,0:T(8,128)(2,1)S(1)}, u32[]{:S(2)}) copy-start(bf16[16,32,512]{2,1,0:T(8,128)(2,1)S(1)} %get-tuple-element.22) | copy-start | bytes 1572868
  34.9 19.3 %all-to-all-start.1 = ((bf16[16,32,512]{2,1,0:T(8,128)(2,1)}), bf16[16,32,512]{2,1,0:T(8,128)(2,1)S(1)}, u32[]{:S(2)}, u32[]{:S(2)}) async-start(bf16[16,32,512]{2,1,0:T(8,128)(2,1)} %copy-done.2), calls=%async_computation.1 | async-start | bytes 1048576 | tf_op jit(solution)/shard_map/all_to_all | solution.py:601

commit v4 on v3

--- a/solution.py
+++ b/solution.py
@@ -312,8 +312,9 @@
     return copies
 
 
-def pack_kernel(plan, g_hbm, coarse_hbm, fine_hbm, out_ref, g_ref, coarse_ref, fine_ref, sems):
+def pack_kernel(plan, g_hbm, coarse_hbm, fine_hbm, out_hbm, out_ref, g_ref, coarse_ref, fine_ref, sems, out_sems):
     sub, chunks, local = plan.sub, plan.channels // 128, plan.local
+    sent = []
     copies = fetched(((fine_hbm, fine_ref), (coarse_hbm, coarse_ref), (g_hbm, g_ref)), sems)
     order = pixel_order(plan.tl, plan.hl, plan.w)
     shape = (local, 128)
@@ -335,6 +336,10 @@
             out_ref[dest, at : at + sub, :] = fine[c : c + sub]
             coarse = sum(quarters[k][c + 8 * k : c + 8 * k + 8] for k in range(4))
             out_ref[dest, at + sub : at + sub + 8, :] = coarse.astype(jnp.bfloat16)
+            sent.append(pltpu.make_async_copy(out_ref.at[dest], out_hbm.at[dest], out_sems.at[dest]))
+            sent[-1].start()
+    for copy in sent:
+        copy.wait()
 
 
 def stage_kernel(
@@ -400,7 +405,7 @@
     return near + moved(middle, image, lane < places - image) + moved(far, 2 * image, lane < places - 2 * image)
 
 
-def coarse_kernel(plan, got_ref, weights, columns, order, out_ref, sums_ref, source, products):
+def coarse_kernel(plan, got_ref, weights, columns, order, out_hbm, sums_ref, source, products, out_ref, sems):
     sub, nr, nf, cells, tl, local = plan.sub, plan.nr, plan.nf, plan.cells, plan.tl, plan.local
     chunks = plan.channels // 128
     for s_f in range(nf):
@@ -431,10 +436,11 @@
     conv = by_col[1] + moved(by_col[0], 1, has_right) + moved(by_col[2], -1, has_left)
     cot = products[pl.ds(27 * sub, sub), :]
     grads, one, two = finished([conv], normed, slope, [cot], gain, inv_std, entries, plan.group_width)
-    quartered = (grads[0] * 0.25).astype(jnp.bfloat16)
-    for dest in range(plan.count):
-        out_ref[dest] = quartered
+    out_ref[...] = (grads[0] * 0.25).astype(jnp.bfloat16)
+    copies = fetched([(out_ref, out_hbm.at[dest]) for dest in range(plan.count)], sems)
     sums_ref[...] = jnp.concatenate([as_row(one), as_row(two)], axis=0)
+    for copy in copies:
+        copy.wait()
 
 
 def unpack_kernel(plan, got_ref, columns, order, normed_ref, slope_ref, inv_ref):
@@ -535,6 +541,10 @@
     return [pl.BlockSpec(memory_space=pltpu.HBM)] * count
 
 
+def kept(array):
+    return pltpu.with_memory_space_constraint(array, pltpu.HBM)
+
+
 def shape_of(shape, kind):
     return jax.ShapeDtypeStruct(shape, kind)
 
@@ -560,23 +570,25 @@
     f32, bf16 = jnp.float32, jnp.bfloat16
     packed = pl.pallas_call(
         functools.partial(pack_kernel, plan),
-        out_shape=shape_of((count, chunks * local + sub + 8, 128), bf16),
+        out_shape=pltpu.HBM((count, chunks * local + sub + 8, 128), bf16),
         in_specs=in_hbm(3),
-        out_specs=in_vmem(1)[0],
+        out_specs=in_hbm(1)[0],
         scratch_shapes=[
+            pltpu.VMEM((count, chunks * local + sub + 8, 128), bf16),
             pltpu.VMEM((local, channels), bf16),
             pltpu.VMEM((local, channels), bf16),
             pltpu.VMEM((4 * local, channels), bf16),
             pltpu.SemaphoreType.DMA((3,)),
+            pltpu.SemaphoreType.DMA((count,)),
         ],
         compiler_params=LIMIT,
     )(
-        grad_coarse.reshape(local, channels),
-        acts_coarse.reshape(local, channels),
-        acts_fine.reshape(4 * local, channels),
+        kept(grad_coarse.reshape(local, channels)),
+        kept(acts_coarse.reshape(local, channels)),
+        kept(acts_fine.reshape(4 * local, channels)),
     )
     got = lax.all_to_all(packed, BLOCK, 0, 0)
-    rows = [part.reshape(1, channels) for part in (gain_coarse, bias_coarse, gain_fine, bias_fine)]
+    rows = [kept(part.reshape(1, channels)) for part in (gain_coarse, bias_coarse, gain_fine, bias_fine)]
     weights_c, weights_f, columns, order = pl.pallas_call(
         functools.partial(stage_kernel, plan),
         out_shape=(
@@ -589,13 +601,18 @@
         out_specs=tuple(in_vmem(4)),
         scratch_shapes=[pltpu.VMEM((4, 1, channels), f32), pltpu.SemaphoreType.DMA((6,))],
         compiler_params=LIMIT,
-    )(kernel_coarse, kernel_fine, *rows)
+    )(kept(kernel_coarse), kept(kernel_fine), *rows)
     quartered, coarse_sums = pl.pallas_call(
         functools.partial(coarse_kernel, plan),
-        out_shape=(shape_of((count, sub, places), bf16), shape_of((2, 128), f32)),
+        out_shape=(pltpu.HBM((count, sub, places), bf16), shape_of((2, 128), f32)),
         in_specs=in_vmem(4),
-        out_specs=tuple(in_vmem(2)),
-        scratch_shapes=[pltpu.VMEM((places, channels), bf16), pltpu.VMEM((28 * sub, places), f32)],
+        out_specs=tuple(in_hbm(1) + in_vmem(1)),
+        scratch_shapes=[
+            pltpu.VMEM((places, channels), bf16),
+            pltpu.VMEM((28 * sub, places), f32),
+            pltpu.VMEM((sub, places), bf16),
+            pltpu.SemaphoreType.DMA((count,)),
+        ],
         compiler_params=LIMIT,
     )(got, weights_c, columns, order)
     spread = lax.all_to_all(quartered, BLOCK, 0, 0)

time: 70.6 us -> 69.8 us (0.989)
  local copies, waits for them, and re-layouts: 9.92 us -> 1.65 us
  waiting for transfers between devices: 27.7 us -> 32.6 us
  Pallas kernels: 6.1 us -> 8.92 us
    unnamed x20 -> x4, local copies, waits for them, and re-layouts: 9.92 us -> 1.65 us
    all_to_all x1, waiting for transfers between devices: 12.4 us -> 18 us  [fast_shards(): got = lax.all_to_all(packed, BLOCK, 0, 0)]
    pallas_call x2, Pallas kernels: 3.01 us -> 4.67 us  [the longest x1 2.55 us: fast_shards(): pl.pallas_call(functools.partial(pack_kernel, plan), out_shape=pltpu.HBM(...]
    pallas_call x1, Pallas kernels: 0.52 us -> 1.65 us  [fast_shards(): pl.pallas_call(functools.partial(stage_kernel, plan), out_shape=(shape_of...]
    all_to_all x1, waiting for transfers between devices: 15.2 us -> 14.5 us  [fast_shards(): spread = lax.all_to_all(quartered, BLOCK, 0, 0)]
  transfers between devices with their start and end apart: 2 -> 2, of which waited for: 2 -> 2; matrix products, arithmetic and copies ran while one was open for 0% -> 0% of each run, Pallas kernels for 1% -> 3%
where the time goes in v4:
time: 69.8 us; the launch traced here: 69.4 us
  waiting for transfers between devices  32.6 us (47%)
  blocking collectives  13.6 us (19%)
  starting transfers between devices  11.9 us (17%)
  Pallas kernels  8.92 us (13%)
  local copies, waits for them, and re-layouts  1.65 us (2%)
  between operations  0.7 us (1%)
    all_to_all x1, waiting for transfers between devices, fast_shards(): got = lax.all_to_all(packed, BLOCK, 0, 0)  18 us
    all_to_all x1, waiting for transfers between devices, fast_shards(): spread = lax.all_to_all(quartered, BLOCK, 0, 0)  14.5 us
    all_to_all x1, blocking collectives, fast_shards(): back = lax.all_to_all(sent, BLOCK, 0, 0)  10.6 us
    all_to_all x1, starting transfers between devices, fast_shards(): got = lax.all_to_all(packed, BLOCK, 0, 0)  8.33 us
    all_to_all x1, starting transfers between devices, fast_shards(): spread = lax.all_to_all(quartered, BLOCK, 0, 0)  3.58 us
    psum x1, blocking collectives, fast_shards(): lax.psum(tuple((part.reshape(channels) for part in sums)), 'dp')  3.04 us
    pallas_call x1, Pallas kernels, fast_shards(): pl.pallas_call(functools.partial(pack_kernel, plan), out_shape=pltpu.HBM(...  2.55 us
    pallas_call x1, Pallas kernels, fast_shards(): pl.pallas_call(functools.partial(coarse_kernel, plan), out_shape=(pltpu.H...  2.12 us
  transfers between devices with their start and end apart: 2, of which 2 were waited for; matrix products, arithmetic and copies ran while one was open for 0% of the time, Pallas kernels for 3%

profile of v4, /device:TPU:0, one launch (start us, length us, event | category | flops | bytes accessed | tf_op | source)
XLA Modules:
  0.0 69.4 jit_solution(124440648716696087)
XLA Ops:
  0.6 2.6 %shard_map.128 = bf16[16,168,128]{2,1,0:T(8,128)(2,1)} custom-call(bf16[32,512]{1,0:T(8,128)(2,1)} %bitcast.17, bf16[32,512]{1,0:T(8,128)(2,1)} %bitcast.18, bf16[128,512]{1,0:T(8,128)(2,1)} %bitcast.16), custom_call_target="tpu_custom_call" | custom-call | tf_op jit(solution)/shard_map/pallas_call | solution.py:571
  3.2 8.3 %all-to-all-start = ((bf16[16,168,128]{2,1,0:T(8,128)(2,1)}), bf16[16,168,128]{2,1,0:T(8,128)(2,1)S(1)}, u32[]{:S(2)}, u32[]{:S(2)}) async-start(bf16[16,168,128]{2,1,0:T(8,128)(2,1)} %shard_map.128), calls=%async_computation | async-start | bytes 1376256 | tf_op jit(solution)/shard_map/all_to_all | solution.py:590
  11.5 1.7 %shard_map.129 = (bf16[28,32,512]{2,1,0:T(8,128)(2,1)S(1)}, bf16[27,32,512]{2,1,0:T(8,128)(2,1)S(1)}, f32[4,32,128]{2,1,0:T(8,128)S(1)}, bf16[512,512]{1,0:T(8,128)(2,1)S(1)}) custom-call(bf16[27,128,512]{2,1,0:T(8,128)(2,1)} %kernel_c.1, bf16[27,128,512]{2,1,0:T(8,128)(2,1)} %kernel_f.1, f32[1,512]{1,0:T(1,128)} %bitcast.19, f32[1,512]{1,0:T(1,128)} %bitcast.20, ...), custom_call_target="tpu_custom_call" | custom-call | tf_op jit(solution)/shard_map/pallas_call | solution.py:592
  13.2 18.0 %all-to-all-done.got_ref = bf16[16,168,128]{2,1,0:T(8,128)(2,1)S(1)} async-done(((bf16[16,168,128]{2,1,0:T(8,128)(2,1)}), bf16[16,168,128]{2,1,0:T(8,128)(2,1)S(1)}, u32[]{:S(2)}, u32[]{:S(2)}) %all-to-all-start) | async-done | bytes 688160 | tf_op jit(solution)/shard_map/all_to_all | solution.py:590
  31.2 2.1 %shard_map.130 = (bf16[16,32,512]{2,1,0:T(8,128)(2,1)}, f32[2,128]{1,0:T(2,128)S(1)}) custom-call(bf16[16,168,128]{2,1,0:T(8,128)(2,1)S(1)} %all-to-all-done.got_ref, bf16[28,32,512]{2,1,0:T(8,128)(2,1)S(1)} %get-tuple-element.19.weights, f32[4,32,128]{2,1,0:T(8,128)S(1)} %get-tuple-element.20.columns, bf16[512,512]{1,0:T(8,128)(2,1)S(1)} %get-tuple-element.21.order), custom_call_target="tpu_custom_call" | custom-call | tf_op jit(solution)/shard_map/pallas_call | solution.py:605
  33.4 3.6 %all-to-all-start.1 = ((bf16[16,32,512]{2,1,0:T(8,128)(2,1)}), bf16[16,32,512]{2,1,0:T(8,128)(2,1)S(1)}, u32[]{:S(2)}, u32[]{:S(2)}) async-start(bf16[16,32,512]{2,1,0:T(8,128)(2,1)} %get-tuple-element.22), calls=%async_computation.1 | async-start | bytes 1048576 | tf_op jit(solution)/shard_map/all_to_all | solution.py:618
  36.9 0.4 shard_map.131
  37.4 0.0 copy-start
  37.4 0.7 %copy-done = f32[4,32,512]{2,1,0:T(8,128)} copy-done((f32[4,32,512]{2,1,0:T(8,128)}, f32[4,32,512]{2,1,0:T(8,128)S(1)}, u32[]{:S(2)}) %copy-start) | copy-done | bytes 262168
  38.1 14.5 %all-to-all-done.1.got_ref = bf16[16,32,512]{2,1,0:T(8,128)(2,1)S(1)} async-done(((bf16[16,32,512]{2,1,0:T(8,128)(2,1)}), bf16[16,32,512]{2,1,0:T(8,128)(2,1)S(1)}, u32[]{:S(2)}, u32[]{:S(2)}) %all-to-all-start.1) | async-done | bytes 524320 | tf_op jit(solution)/shard_map/all_to_all | solution.py:618
  52.6 0.0 copy-start.1
  52.6 0.9 %copy-done.1 = f32[4,32,512]{2,1,0:T(8,128)S(1)} copy-done((f32[4,32,512]{2,1,0:T(8,128)S(1)}, f32[4,32,512]{2,1,0:T(8,128)}, u32[]{:S(2)}) %copy-start.1) | copy-done | bytes 262168
  53.6 1.3 %shard_map.132 = bf16[16,40,128]{2,1,0:T(8,128)(2,1)S(1)} custom-call(bf16[16,32,512]{2,1,0:T(8,128)(2,1)S(1)} %all-to-all-done.1.got_ref, f32[4,32,512]{2,1,0:T(8,128)S(1)} %get-tuple-element.23.normed_ref, f32[4,32,512]{2,1,0:T(8,128)S(1)} %copy-done.1, f32[32,128]{1,0:T(8,128)S(1)} %get-tuple-element.25.inv_ref, ...), custom_call_target="tpu_custom_call" | custom-call | tf_op jit(solution)/shard_map/pallas_call | solution.py:630
  54.9 10.6 %all_to_all.15.got_ref = bf16[16,40,128]{2,1,0:T(8,128)(2,1)S(1)} all-to-all(bf16[16,40,128]{2,1,0:T(8,128)(2,1)S(1)} %shard_map.132), channel_id=1, replica_groups=mesh['dp'=2,'frames'=4,'rows'=4] {'frames','rows'}, dimensions={0} | all-to-all | bytes 327680 | tf_op jit(solution)/shard_map/all_to_all | solution.py:638
  65.5 0.9 %shard_map.133 = (bf16[128,512]{1,0:T(8,128)(2,1)}, f32[1,512]{1,0:T(1,128)S(1)}, f32[1,512]{1,0:T(1,128)S(1)}, f32[1,512]{1,0:T(1,128)S(1)}, f32[1,512]{1,0:T(1,128)S(1)}) custom-call(bf16[16,40,128]{2,1,0:T(8,128)(2,1)S(1)} %all_to_all.15.got_ref), custom_call_target="tpu_custom_call" | custom-call | tf_op jit(solution)/shard_map/pallas_call | solution.py:641
  66.3 3.0 %all-reduce = (f32[512]{0:T(512)}, f32[512]{0:T(512)}, f32[512]{0:T(512)}, f32[512]{0:T(512)}) all-reduce(f32[512]{0:T(512)S(1)} %bitcast.13, f32[512]{0:T(512)S(1)} %bitcast.12, f32[512]{0:T(512)S(1)} %bitcast.15, f32[512]{0:T(512)S(1)} %bitcast.14), channel_id=1, replica_groups=mesh['dp'=2,'frames'=4,'rows'=4] {'dp'}, use_global_device_ids=true, to_apply=%region_0.0 | all-reduce | flops 2048 | bytes 16384 | tf_op jit(solution)/shard_map/psum | solution.py:649
Async XLA Ops:
  3.2 28.0 %all-to-all-start = ((bf16[16,168,128]{2,1,0:T(8,128)(2,1)}), bf16[16,168,128]{2,1,0:T(8,128)(2,1)S(1)}, u32[]{:S(2)}, u32[]{:S(2)}) async-start(bf16[16,168,128]{2,1,0:T(8,128)(2,1)} %shard_map.128), calls=%async_computation | async-start | bytes 1376256 | tf_op jit(solution)/shard_map/all_to_all | solution.py:590
  33.4 19.3 %all-to-all-start.1 = ((bf16[16,32,512]{2,1,0:T(8,128)(2,1)}), bf16[16,32,512]{2,1,0:T(8,128)(2,1)S(1)}, u32[]{:S(2)}, u32[]{:S(2)}) async-start(bf16[16,32,512]{2,1,0:T(8,128)(2,1)} %get-tuple-element.22), calls=%async_computation.1 | async-start | bytes 1048576 | tf_op jit(solution)/shard_map/all_to_all | solution.py:618
  37.4 0.7 %copy-start = (f32[4,32,512]{2,1,0:T(8,128)}, f32[4,32,512]{2,1,0:T(8,128)S(1)}, u32[]{:S(2)}) copy-start(f32[4,32,512]{2,1,0:T(8,128)S(1)} %get-tuple-element.24.slope_ref) | copy-start | bytes 786436
  52.6 1.0 %copy-start.1 = (f32[4,32,512]{2,1,0:T(8,128)S(1)}, f32[4,32,512]{2,1,0:T(8,128)}, u32[]{:S(2)}) copy-start(f32[4,32,512]{2,1,0:T(8,128)} %copy-done) | copy-start | bytes 786436

commit v5 on v4

--- a/solution.py
+++ b/solution.py
@@ -405,7 +405,7 @@
     return near + moved(middle, image, lane < places - image) + moved(far, 2 * image, lane < places - 2 * image)
 
 
-def coarse_kernel(plan, got_ref, weights, columns, order, out_hbm, sums_ref, source, products, out_ref, sems):
+def coarse_kernel(plan, got_ref, weights, columns, order, out_ref, sums_ref, source, products):
     sub, nr, nf, cells, tl, local = plan.sub, plan.nr, plan.nf, plan.cells, plan.tl, plan.local
     chunks = plan.channels // 128
     for s_f in range(nf):
@@ -437,10 +437,7 @@
     cot = products[pl.ds(27 * sub, sub), :]
     grads, one, two = finished([conv], normed, slope, [cot], gain, inv_std, entries, plan.group_width)
     out_ref[...] = (grads[0] * 0.25).astype(jnp.bfloat16)
-    copies = fetched([(out_ref, out_hbm.at[dest]) for dest in range(plan.count)], sems)
     sums_ref[...] = jnp.concatenate([as_row(one), as_row(two)], axis=0)
-    for copy in copies:
-        copy.wait()
 
 
 def unpack_kernel(plan, got_ref, columns, order, normed_ref, slope_ref, inv_ref):
@@ -604,18 +601,13 @@
     )(kept(kernel_coarse), kept(kernel_fine), *rows)
     quartered, coarse_sums = pl.pallas_call(
         functools.partial(coarse_kernel, plan),
-        out_shape=(pltpu.HBM((count, sub, places), bf16), shape_of((2, 128), f32)),
+        out_shape=(shape_of((sub, places), bf16), shape_of((2, 128), f32)),
         in_specs=in_vmem(4),
-        out_specs=tuple(in_hbm(1) + in_vmem(1)),
-        scratch_shapes=[
-            pltpu.VMEM((places, channels), bf16),
-            pltpu.VMEM((28 * sub, places), f32),
-            pltpu.VMEM((sub, places), bf16),
-            pltpu.SemaphoreType.DMA((count,)),
-        ],
+        out_specs=tuple(in_vmem(2)),
+        scratch_shapes=[pltpu.VMEM((places, channels), bf16), pltpu.VMEM((28 * sub, places), f32)],
         compiler_params=LIMIT,
     )(got, weights_c, columns, order)
-    spread = lax.all_to_all(quartered, BLOCK, 0, 0)
+    spread = lax.all_gather(quartered, BLOCK)
     normed, slope, inv_std = pl.pallas_call(
         functools.partial(unpack_kernel, plan),
         out_shape=(

time: 69.8 us -> 90.4 us (1.30)
  blocking collectives: 13.6 us -> 55.1 us
  waiting for transfers between devices: 32.6 us -> 18 us
  starting transfers between devices: 11.9 us -> 8.33 us
  local copies, waits for them, and re-layouts: 1.65 us -> 0 us
  Pallas kernels: 8.92 us -> 7.96 us
    all_gather x0 -> x1, blocking collectives: none -> 41.7 us  [fast_shards(): spread = lax.all_gather(quartered, BLOCK)]
    all_to_all x1 -> x0, waiting for transfers between devices: 14.5 us -> none  [fast_shards(): spread = lax.all_to_all(quartered, BLOCK, 0, 0)]
    all_to_all x1 -> x0, starting transfers between devices: 3.58 us -> none  [fast_shards(): spread = lax.all_to_all(quartered, BLOCK, 0, 0)]
    unnamed x4 -> x0, local copies, waits for them, and re-layouts: 1.65 us -> none
    pallas_call x1, Pallas kernels: 2.12 us -> 1.17 us  [fast_shards(): pl.pallas_call(functools.partial(coarse_kernel, plan), out_shape=(shape_o...]
  transfers between devices with their start and end apart: 2 -> 1, of which waited for: 2 -> 1; matrix products, arithmetic and copies ran while one was open for 0% -> 0% of each run, Pallas kernels for 3% -> 2%
where the time goes in v5:
time: 90.4 us; the launch traced here: 90.1 us
  blocking collectives  55.1 us (61%)
  waiting for transfers between devices  18 us (20%)
  starting transfers between devices  8.33 us (9%)
  Pallas kernels  7.96 us (9%)
    all_gather x1, blocking collectives, fast_shards(): spread = lax.all_gather(quartered, BLOCK)  41.7 us
    all_to_all x1, waiting for transfers between devices, fast_shards(): got = lax.all_to_all(packed, BLOCK, 0, 0)  18 us
    all_to_all x1, blocking collectives, fast_shards(): back = lax.all_to_all(sent, BLOCK, 0, 0)  10.3 us
    all_to_all x1, starting transfers between devices, fast_shards(): got = lax.all_to_all(packed, BLOCK, 0, 0)  8.33 us
    psum x1, blocking collectives, fast_shards(): lax.psum(tuple((part.reshape(channels) for part in sums)), 'dp')  3.04 us
    pallas_call x1, Pallas kernels, fast_shards(): pl.pallas_call(functools.partial(pack_kernel, plan), out_shape=pltpu.HBM(...  2.54 us
  transfers between devices with their start and end apart: 1, of which 1 were waited for; matrix products, arithmetic and copies ran while one was open for 0% of the time, Pallas kernels for 2%

profile of v5, /device:TPU:0, one launch (start us, length us, event | category | flops | bytes accessed | tf_op | source)
XLA Modules:
  0.0 90.1 jit_solution(7840674334713442823)
XLA Ops:
  0.6 2.5 %shard_map.128 = bf16[16,168,128]{2,1,0:T(8,128)(2,1)} custom-call(bf16[32,512]{1,0:T(8,128)(2,1)} %bitcast.19, bf16[32,512]{1,0:T(8,128)(2,1)} %bitcast.20, bf16[128,512]{1,0:T(8,128)(2,1)} %bitcast.18), custom_call_target="tpu_custom_call" | custom-call | tf_op jit(solution)/shard_map/pallas_call | solution.py:568
  3.2 8.3 %all-to-all-start = ((bf16[16,168,128]{2,1,0:T(8,128)(2,1)}), bf16[16,168,128]{2,1,0:T(8,128)(2,1)S(1)}, u32[]{:S(2)}, u32[]{:S(2)}) async-start(bf16[16,168,128]{2,1,0:T(8,128)(2,1)} %shard_map.128), calls=%async_computation | async-start | bytes 1376256 | tf_op jit(solution)/shard_map/all_to_all | solution.py:587
  11.5 1.7 %shard_map.129 = (bf16[28,32,512]{2,1,0:T(8,128)(2,1)S(1)}, bf16[27,32,512]{2,1,0:T(8,128)(2,1)S(1)}, f32[4,32,128]{2,1,0:T(8,128)S(1)}, bf16[512,512]{1,0:T(8,128)(2,1)S(1)}) custom-call(bf16[27,128,512]{2,1,0:T(8,128)(2,1)} %kernel_c.1, bf16[27,128,512]{2,1,0:T(8,128)(2,1)} %kernel_f.1, f32[1,512]{1,0:T(1,128)} %bitcast.21, f32[1,512]{1,0:T(1,128)} %bitcast.22, ...), custom_call_target="tpu_custom_call" | custom-call | tf_op jit(solution)/shard_map/pallas_call | solution.py:589
  13.2 18.0 %all-to-all-done.got_ref = bf16[16,168,128]{2,1,0:T(8,128)(2,1)S(1)} async-done(((bf16[16,168,128]{2,1,0:T(8,128)(2,1)}), bf16[16,168,128]{2,1,0:T(8,128)(2,1)S(1)}, u32[]{:S(2)}, u32[]{:S(2)}) %all-to-all-start) | async-done | bytes 688160 | tf_op jit(solution)/shard_map/all_to_all | solution.py:587
  31.2 1.2 %shard_map.130 = (bf16[32,512]{1,0:T(8,128)(2,1)S(1)}, f32[2,128]{1,0:T(2,128)S(1)}) custom-call(bf16[16,168,128]{2,1,0:T(8,128)(2,1)S(1)} %all-to-all-done.got_ref, bf16[28,32,512]{2,1,0:T(8,128)(2,1)S(1)} %get-tuple-element.19.weights, f32[4,32,128]{2,1,0:T(8,128)S(1)} %get-tuple-element.20.columns, bf16[512,512]{1,0:T(8,128)(2,1)S(1)} %get-tuple-element.21.order), custom_call_target="tpu_custom_call" | custom-call | tf_op jit(solution)/shard_map/pallas_call | solution.py:602
  32.4 41.7 %all-gather = bf16[512,512]{1,0:T(8,128)(2,1)S(1)} all-gather(bf16[32,512]{1,0:T(8,128)(2,1)S(1)} %get-tuple-element.22), channel_id=2, replica_groups=mesh['dp'=2,'frames'=4,'rows'=4] {'frames','rows'}, dimensions={0}, use_global_device_ids=true | all-gather | bytes 557056 | tf_op jit(solution)/shard_map/all_gather | solution.py:610
  74.1 0.4 shard_map.131
  74.5 1.3 %shard_map.132 = bf16[16,40,128]{2,1,0:T(8,128)(2,1)S(1)} custom-call(bf16[16,32,512]{2,1,0:T(8,128)(2,1)S(1)} %bitcast.13, f32[4,32,512]{2,1,0:T(8,128)S(1)} %get-tuple-element.23.normed_ref, f32[4,32,512]{2,1,0:T(8,128)S(1)} %get-tuple-element.24.slope_ref, f32[32,128]{1,0:T(8,128)S(1)} %get-tuple-element.25.inv_ref, ...), custom_call_target="tpu_custom_call" | custom-call | tf_op jit(solution)/shard_map/pallas_call | solution.py:622
  75.9 10.3 %all_to_all.10.got_ref = bf16[16,40,128]{2,1,0:T(8,128)(2,1)S(1)} all-to-all(bf16[16,40,128]{2,1,0:T(8,128)(2,1)S(1)} %shard_map.132), channel_id=1, replica_groups=mesh['dp'=2,'frames'=4,'rows'=4] {'frames','rows'}, dimensions={0} | all-to-all | bytes 327680 | tf_op jit(solution)/shard_map/all_to_all | solution.py:630
  86.2 0.9 shard_map.133
  87.0 3.0 %all-reduce = (f32[512]{0:T(512)}, f32[512]{0:T(512)}, f32[512]{0:T(512)}, f32[512]{0:T(512)}) all-reduce(f32[512]{0:T(512)S(1)} %bitcast.15, f32[512]{0:T(512)S(1)} %bitcast.14, f32[512]{0:T(512)S(1)} %bitcast.17, f32[512]{0:T(512)S(1)} %bitcast.16), channel_id=1, replica_groups=mesh['dp'=2,'frames'=4,'rows'=4] {'dp'}, use_global_device_ids=true, to_apply=%region_0.0 | all-reduce | flops 2048 | bytes 16384 | tf_op jit(solution)/shard_map/psum | solution.py:641
Async XLA Ops:
  3.2 28.0 %all-to-all-start = ((bf16[16,168,128]{2,1,0:T(8,128)(2,1)}), bf16[16,168,128]{2,1,0:T(8,128)(2,1)S(1)}, u32[]{:S(2)}, u32[]{:S(2)}) async-start(bf16[16,168,128]{2,1,0:T(8,128)(2,1)} %shard_map.128), calls=%async_computation | async-start | bytes 1376256 | tf_op jit(solution)/shard_map/all_to_all | solution.py:587

commit v6 on v3

--- a/solution.py
+++ b/solution.py
@@ -312,62 +312,67 @@
     return copies
 
 
-def pack_kernel(plan, g_hbm, coarse_hbm, fine_hbm, out_ref, g_ref, coarse_ref, fine_ref, sems):
+def pack_kernel(
+    plan,
+    g_hbm,
+    coarse_hbm,
+    fine_hbm,
+    kernel_c,
+    kernel_f,
+    gain_c,
+    bias_c,
+    gain_f,
+    bias_f,
+    out_ref,
+    weights_c,
+    weights_f,
+    columns,
+    order,
+    g_ref,
+    coarse_ref,
+    fine_ref,
+    rows,
+    sems,
+):
     sub, chunks, local = plan.sub, plan.channels // 128, plan.local
-    copies = fetched(((fine_hbm, fine_ref), (coarse_hbm, coarse_ref), (g_hbm, g_ref)), sems)
-    order = pixel_order(plan.tl, plan.hl, plan.w)
+    f, r = lax.axis_index("frames"), lax.axis_index("rows")
+    base = r * plan.slice_width + f * sub
+    own = pl.ds(pl.multiple_of(f * sub, sub), sub)
+    copies = fetched(
+        [(fine_hbm, fine_ref), (coarse_hbm, coarse_ref), (g_hbm, g_ref)]
+        + [(row, rows.at[k]) for k, row in enumerate((gain_c, bias_c, gain_f, bias_f))]
+        + [(kernel_c.at[:, own, :], weights_c.at[pl.ds(0, 27)]), (kernel_f.at[:, own, :], weights_f)],
+        sems,
+    )
+    shape = (sub, plan.channels)
+    weights_c[27] = (lanes_at(shape, 1) == lanes_at(shape, 0) + base).astype(jnp.float32).astype(jnp.bfloat16)
+    order[...] = merged_order(plan.nr, 4, plan.tl, plan.cells)
+    pixels = pixel_order(plan.tl, plan.hl, plan.w)
     shape = (local, 128)
     places = [
         (lanes_at(shape, 0) + k * local == lanes_at(shape, 1)).astype(jnp.float32).astype(jnp.bfloat16)
         for k in range(4)
     ]
     copies[0].wait()
-    fine = one_hot_dot(fine_ref[...], order, ((0,), (0,))).astype(jnp.bfloat16)
+    fine = one_hot_dot(fine_ref[...], pixels, ((0,), (0,))).astype(jnp.bfloat16)
     copies[1].wait()
     quarters = [one_hot_dot(coarse_ref[...], place, ((0,), (0,))) for place in places]
     copies[2].wait()
-    for f in range(plan.nf):
-        for r in range(plan.nr):
-            dest, c = f * plan.nr + r, r * plan.slice_width + f * sub
+    for s_f in range(plan.nf):
+        for s_r in range(plan.nr):
+            dest, c = s_f * plan.nr + s_r, s_r * plan.slice_width + s_f * sub
             for k in range(chunks):
                 out_ref[dest, k * local : (k + 1) * local, :] = g_ref[:, k * 128 : (k + 1) * 128]
             at = chunks * local
             out_ref[dest, at : at + sub, :] = fine[c : c + sub]
             coarse = sum(quarters[k][c + 8 * k : c + 8 * k + 8] for k in range(4))
             out_ref[dest, at + sub : at + sub + 8, :] = coarse.astype(jnp.bfloat16)
-
-
-def stage_kernel(
-    plan,
-    kernel_c,
-    kernel_f,
-    gain_c,
-    bias_c,
-    gain_f,
-    bias_f,
-    weights_c,
-    weights_f,
-    columns,
-    order,
-    rows,
-    sems,
-):
-    sub = plan.sub
-    f, r = lax.axis_index("frames"), lax.axis_index("rows")
-    base = r * plan.slice_width + f * sub
-    own = pl.ds(pl.multiple_of(f * sub, sub), sub)
-    copies = fetched(
-        [(row, rows.at[k]) for k, row in enumerate((gain_c, bias_c, gain_f, bias_f))]
-        + [(kernel_c.at[:, own, :], weights_c.at[pl.ds(0, 27)]), (kernel_f.at[:, own, :], weights_f)],
-        sems,
-    )
-    shape = (sub, plan.channels)
-    weights_c[27] = (lanes_at(shape, 1) == lanes_at(shape, 0) + base).astype(jnp.float32).astype(jnp.bfloat16)
-    order[...] = merged_order(plan.nr, 4, plan.tl, plan.cells)
-    for copy in copies:
+    for copy in copies[3:7]:
         copy.wait()
     for k in range(4):
         columns[k] = jnp.broadcast_to(own_column(rows[k], base, sub), (sub, 128))
+    for copy in copies[7:]:
+        copy.wait()
 
 
 def by_frame_device(plan, got_ref, at, height):
@@ -437,35 +442,24 @@
     sums_ref[...] = jnp.concatenate([as_row(one), as_row(two)], axis=0)
 
 
-def unpack_kernel(plan, got_ref, columns, order, normed_ref, slope_ref, inv_ref):
-    sub = plan.sub
-    packed = by_frame_device(plan, got_ref, plan.channels // 128 * plan.local, sub)
-    parts = in_places(plan, one_hot_dot(packed, order[...], ((1,), (0,))), sub)
-    gain, bias = columns[2][:, 0:1], columns[3][:, 0:1]
-    entries = 4 * plan.places * plan.group_width
-    normed, slope, inv_std = normalised(parts, gain, bias, entries, plan.group_width)
-    for pq in range(4):
-        normed_ref[pq] = normed[pq]
-        slope_ref[pq] = slope[pq]
-    inv_ref[...] = jnp.broadcast_to(inv_std, (sub, 128))
-
-
-def fine_kernel(
-    plan, got_ref, normed_ref, slope_ref, inv_ref, columns, order, sums_ref, weights, out_ref, source, products
-):
+def fine_kernel(plan, got_ref, acts_ref, columns, order, sums_ref, weights, out_ref, source, products):
     sub, nr, nf = plan.sub, plan.nr, plan.nf
     f, r = lax.axis_index("frames"), lax.axis_index("rows")
     for s_f in range(nf):
         for s_r in range(nr):
             c = s_r * plan.slice_width + s_f * sub
             source[c : c + sub, :] = got_ref[s_f * nr + s_r]
-    gain = columns[2][:, 0:1]
     products[...] = lax.dot_general(
         weights[...].reshape(27 * sub, plan.channels),
         source[...],
         (((1,), (0,)), ((), ())),
         preferred_element_type=jnp.float32,
     )
+    packed = by_frame_device(plan, acts_ref, plan.channels // 128 * plan.local, sub)
+    parts = in_places(plan, one_hot_dot(packed, order[...], ((1,), (0,))), sub)
+    gain, bias = columns[2][:, 0:1], columns[3][:, 0:1]
+    entries = 4 * plan.places * plan.group_width
+    normed, slope, inv_std = normalised(parts, gain, bias, entries, plan.group_width)
     lane, has_left, has_right, has_up, has_down = plan.place_masks()
     by_row = []
     for row in range(3):
@@ -474,17 +468,7 @@
     convs = [by_row[0][q] + by_row[1][q] + moved(by_row[2][q], -plan.w, has_up) for q in range(2)]
     convs += [moved(by_row[0][q], plan.w, has_down) + by_row[1][q] + by_row[2][q] for q in range(2)]
     cot = got_ref[f * nr + r].astype(jnp.float32)
-    entries = 4 * plan.places * plan.group_width
-    grads, one, two = finished(
-        convs,
-        [normed_ref[pq] for pq in range(4)],
-        [slope_ref[pq] for pq in range(4)],
-        [cot] * 4,
-        gain,
-        inv_ref[:, 0:1],
-        entries,
-        plan.group_width,
-    )
+    grads, one, two = finished(convs, normed, slope, [cot] * 4, gain, inv_std, entries, plan.group_width)
     width = plan.tl * plan.image
     stacked = jnp.concatenate(
         [
@@ -535,6 +519,10 @@
     return [pl.BlockSpec(memory_space=pltpu.HBM)] * count
 
 
+def kept(array):
+    return pltpu.with_memory_space_constraint(array, pltpu.HBM)
+
+
 def shape_of(shape, kind):
     return jax.ShapeDtypeStruct(shape, kind)
 
@@ -558,38 +546,35 @@
     count, sub, channels, places, local = plan.count, plan.sub, plan.channels, plan.places, plan.local
     chunks = channels // 128
     f32, bf16 = jnp.float32, jnp.bfloat16
-    packed = pl.pallas_call(
+    rows = [part.reshape(1, channels) for part in (gain_coarse, bias_coarse, gain_fine, bias_fine)]
+    packed, weights_c, weights_f, columns, order = pl.pallas_call(
         functools.partial(pack_kernel, plan),
-        out_shape=shape_of((count, chunks * local + sub + 8, 128), bf16),
-        in_specs=in_hbm(3),
-        out_specs=in_vmem(1)[0],
-        scratch_shapes=[
-            pltpu.VMEM((local, channels), bf16),
-            pltpu.VMEM((local, channels), bf16),
-            pltpu.VMEM((4 * local, channels), bf16),
-            pltpu.SemaphoreType.DMA((3,)),
-        ],
-        compiler_params=LIMIT,
-    )(
-        grad_coarse.reshape(local, channels),
-        acts_coarse.reshape(local, channels),
-        acts_fine.reshape(4 * local, channels),
-    )
-    got = lax.all_to_all(packed, BLOCK, 0, 0)
-    rows = [part.reshape(1, channels) for part in (gain_coarse, bias_coarse, gain_fine, bias_fine)]
-    weights_c, weights_f, columns, order = pl.pallas_call(
-        functools.partial(stage_kernel, plan),
         out_shape=(
+            shape_of((count, chunks * local + sub + 8, 128), bf16),
             shape_of((28, sub, channels), bf16),
             shape_of((27, sub, channels), bf16),
             shape_of((4, sub, 128), f32),
             shape_of((4 * plan.nr * local, 4 * plan.nr * local), bf16),
         ),
-        in_specs=in_hbm(6),
-        out_specs=tuple(in_vmem(4)),
-        scratch_shapes=[pltpu.VMEM((4, 1, channels), f32), pltpu.SemaphoreType.DMA((6,))],
+        in_specs=in_hbm(9),
+        out_specs=tuple(in_vmem(5)),
+        scratch_shapes=[
+            pltpu.VMEM((local, channels), bf16),
+            pltpu.VMEM((local, channels), bf16),
+            pltpu.VMEM((4 * local, channels), bf16),
+            pltpu.VMEM((4, 1, channels), f32),
+            pltpu.SemaphoreType.DMA((9,)),
+        ],
         compiler_params=LIMIT,
-    )(kernel_coarse, kernel_fine, *rows)
+    )(
+        kept(grad_coarse.reshape(local, channels)),
+        kept(acts_coarse.reshape(local, channels)),
+        kept(acts_fine.reshape(4 * local, channels)),
+        kept(kernel_coarse),
+        kept(kernel_fine),
+        *[kept(row) for row in rows],
+    )
+    got = lax.all_to_all(packed, BLOCK, 0, 0)
     quartered, coarse_sums = pl.pallas_call(
         functools.partial(coarse_kernel, plan),
         out_shape=(shape_of((count, sub, places), bf16), shape_of((2, 128), f32)),
@@ -599,25 +584,14 @@
         compiler_params=LIMIT,
     )(got, weights_c, columns, order)
     spread = lax.all_to_all(quartered, BLOCK, 0, 0)
-    normed, slope, inv_std = pl.pallas_call(
-        functools.partial(unpack_kernel, plan),
-        out_shape=(
-            shape_of((4, sub, places), f32),
-            shape_of((4, sub, places), f32),
-            shape_of((sub, 128), f32),
-        ),
-        in_specs=in_vmem(3),
-        out_specs=tuple(in_vmem(3)),
-        compiler_params=LIMIT,
-    )(got, columns, order)
     sent = pl.pallas_call(
         functools.partial(fine_kernel, plan),
         out_shape=shape_of((count, sub + 8, 128), bf16),
-        in_specs=in_vmem(8),
+        in_specs=in_vmem(6),
         out_specs=in_vmem(1)[0],
         scratch_shapes=[pltpu.VMEM((channels, places), bf16), pltpu.VMEM((27 * sub, places), f32)],
         compiler_params=LIMIT,
-    )(spread, normed, slope, inv_std, columns, order, coarse_sums, weights_f)
+    )(spread, got, columns, order, coarse_sums, weights_f)
     back = lax.all_to_all(sent, BLOCK, 0, 0)
     cells = nd * places
     fine_scale, coarse_scale = 1.0 / math.sqrt(4 * cells), 1.0 / math.sqrt(cells)

time: 70.6 us -> 66.1 us (0.936)
  blocking collectives: 13.6 us -> 59.9 us
  waiting for transfers between devices: 27.7 us -> 0 us
  starting transfers between devices: 11.9 us -> 0 us
  local copies, waits for them, and re-layouts: 9.92 us -> 0 us
  Pallas kernels: 6.1 us -> 5.28 us
    all_to_all x0 -> x2, blocking collectives: none -> 46.2 us  [the longest x1 27.8 us: fast_shards(): got = lax.all_to_all(packed, BLOCK, 0, 0)]
    all_to_all x2 -> x0, waiting for transfers between devices: 27.7 us -> none  [the longest x1 15.2 us: fast_shards(): spread = lax.all_to_all(quartered, BLOCK, 0, 0)]
    all_to_all x2 -> x0, starting transfers between devices: 11.9 us -> none  [the longest x1 8.33 us: fast_shards(): got = lax.all_to_all(packed, BLOCK, 0, 0)]
    unnamed x20 -> x0, local copies, waits for them, and re-layouts: 9.92 us -> none
    pallas_call x3 -> x1, Pallas kernels: 2.77 us -> 1.79 us  [fast_shards(): pl.pallas_call(functools.partial(pack_kernel, plan), out_shape=(shape_of(...]
  transfers between devices with their start and end apart: 2 -> 0, of which waited for: 2 -> 0; matrix products, arithmetic and copies ran while one was open for 0% -> 0% of each run, Pallas kernels for 1% -> 0%
where the time goes in v6:
time: 66.1 us; the launch traced here: 65.8 us
  blocking collectives  59.9 us (91%)
  Pallas kernels  5.28 us (8%)
    all_to_all x1, blocking collectives, fast_shards(): got = lax.all_to_all(packed, BLOCK, 0, 0)  27.8 us
    all_to_all x1, blocking collectives, fast_shards(): spread = lax.all_to_all(quartered, BLOCK, 0, 0)  18.4 us
    all_to_all x1, blocking collectives, fast_shards(): back = lax.all_to_all(sent, BLOCK, 0, 0)  10.6 us
    psum x1, blocking collectives, fast_shards(): lax.psum(tuple((part.reshape(channels) for part in sums)), 'dp')  3.04 us
    pallas_call x1, Pallas kernels, fast_shards(): pl.pallas_call(functools.partial(pack_kernel, plan), out_shape=(shape_of(...  1.79 us
    pallas_call x1, Pallas kernels, fast_shards(): pl.pallas_call(functools.partial(fine_kernel, plan), out_shape=shape_of((...  1.43 us

profile of v6, /device:TPU:0, one launch (start us, length us, event | category | flops | bytes accessed | tf_op | source)
XLA Modules:
  0.0 65.8 jit_solution(17646859421003517214)
XLA Ops:
  0.6 1.8 %shard_map.128 = (bf16[16,168,128]{2,1,0:T(8,128)(2,1)S(1)}, bf16[28,32,512]{2,1,0:T(8,128)(2,1)S(1)}, bf16[27,32,512]{2,1,0:T(8,128)(2,1)S(1)}, f32[4,32,128]{2,1,0:T(8,128)S(1)}, bf16[512,512]{1,0:T(8,128)(2,1)S(1)}) custom-call(bf16[32,512]{1,0:T(8,128)(2,1)} %bitcast.17, bf16[32,512]{1,0:T(8,128)(2,1)} %bitcast.18, bf16[128,512]{1,0:T(8,128)(2,1)} %bitcast.16, ...), custom_call_target="tpu_custom_call" | custom-call | tf_op jit(solution)/shard_map/pallas_call | solution.py:550
  2.4 27.8 %all_to_all.15.got_ref.acts_ref = bf16[16,168,128]{2,1,0:T(8,128)(2,1)S(1)} all-to-all(bf16[16,168,128]{2,1,0:T(8,128)(2,1)S(1)} %get-tuple-element.17), channel_id=1, replica_groups=mesh['dp'=2,'frames'=4,'rows'=4] {'frames','rows'}, dimensions={0} | all-to-all | bytes 1376256 | tf_op jit(solution)/shard_map/all_to_all | solution.py:577
  30.2 1.2 %shard_map.129 = (bf16[16,32,512]{2,1,0:T(8,128)(2,1)S(1)}, f32[2,128]{1,0:T(2,128)S(1)}) custom-call(bf16[16,168,128]{2,1,0:T(8,128)(2,1)S(1)} %all_to_all.15.got_ref.acts_ref, bf16[28,32,512]{2,1,0:T(8,128)(2,1)S(1)} %get-tuple-element.18.weights, f32[4,32,128]{2,1,0:T(8,128)S(1)} %get-tuple-element.19.columns, bf16[512,512]{1,0:T(8,128)(2,1)S(1)} %get-tuple-element.20.order), custom_call_target="tpu_custom_call" | custom-call | tf_op jit(solution)/shard_map/pallas_call | solution.py:578
  31.5 18.4 %all_to_all.16.got_ref = bf16[16,32,512]{2,1,0:T(8,128)(2,1)S(1)} all-to-all(bf16[16,32,512]{2,1,0:T(8,128)(2,1)S(1)} %get-tuple-element.21), channel_id=1, replica_groups=mesh['dp'=2,'frames'=4,'rows'=4] {'frames','rows'}, dimensions={0} | all-to-all | bytes 1048576 | tf_op jit(solution)/shard_map/all_to_all | solution.py:586
  49.9 1.4 %shard_map.130 = bf16[16,40,128]{2,1,0:T(8,128)(2,1)S(1)} custom-call(bf16[16,32,512]{2,1,0:T(8,128)(2,1)S(1)} %all_to_all.16.got_ref, bf16[16,168,128]{2,1,0:T(8,128)(2,1)S(1)} %all_to_all.15.got_ref.acts_ref, f32[4,32,128]{2,1,0:T(8,128)S(1)} %get-tuple-element.19.columns, bf16[512,512]{1,0:T(8,128)(2,1)S(1)} %get-tuple-element.20.order, ...), custom_call_target="tpu_custom_call" | custom-call | tf_op jit(solution)/shard_map/pallas_call | solution.py:587
  51.3 10.6 %all_to_all.17.got_ref = bf16[16,40,128]{2,1,0:T(8,128)(2,1)S(1)} all-to-all(bf16[16,40,128]{2,1,0:T(8,128)(2,1)S(1)} %shard_map.130), channel_id=1, replica_groups=mesh['dp'=2,'frames'=4,'rows'=4] {'frames','rows'}, dimensions={0} | all-to-all | bytes 327680 | tf_op jit(solution)/shard_map/all_to_all | solution.py:595
  61.9 0.9 %shard_map.131 = (bf16[128,512]{1,0:T(8,128)(2,1)}, f32[1,512]{1,0:T(1,128)S(1)}, f32[1,512]{1,0:T(1,128)S(1)}, f32[1,512]{1,0:T(1,128)S(1)}, f32[1,512]{1,0:T(1,128)S(1)}) custom-call(bf16[16,40,128]{2,1,0:T(8,128)(2,1)S(1)} %all_to_all.17.got_ref), custom_call_target="tpu_custom_call" | custom-call | tf_op jit(solution)/shard_map/pallas_call | solution.py:598
  62.8 3.0 %all-reduce = (f32[512]{0:T(512)}, f32[512]{0:T(512)}, f32[512]{0:T(512)}, f32[512]{0:T(512)}) all-reduce(f32[512]{0:T(512)S(1)} %bitcast.13, f32[512]{0:T(512)S(1)} %bitcast.12, f32[512]{0:T(512)S(1)} %bitcast.15, f32[512]{0:T(512)S(1)} %bitcast.14), channel_id=1, replica_groups=mesh['dp'=2,'frames'=4,'rows'=4] {'dp'}, use_global_device_ids=true, to_apply=%region_0.0 | all-reduce | flops 2048 | bytes 16384 | tf_op jit(solution)/shard_map/psum | solution.py:606

commit v7 on v6

--- a/solution.py
+++ b/solution.py
@@ -10,12 +10,13 @@
 
 GROUPS = 32
 EPSILON = 1e-06
-BLOCK = ("frames", "rows")
-
-
-def to_everyone(block, count):
+BLOCK = ("rows", "frames")
+PLAIN_BLOCK = ("frames", "rows")
+
+
+def plain_everyone(block, count):
     copies = jnp.broadcast_to(block[None], (count,) + block.shape)
-    return lax.all_to_all(copies, BLOCK, 0, 0)
+    return lax.all_to_all(copies, PLAIN_BLOCK, 0, 0)
 
 
 def ahead(field, axis, distance):
@@ -123,16 +124,16 @@
     frames, rows = tl * nf, hl * nr
     f, r = lax.axis_index("frames"), lax.axis_index("rows")
 
-    gathered = to_everyone(grad_coarse[0], count)
+    gathered = plain_everyone(grad_coarse[0], count)
     source = (
         gathered.reshape(nf, nr, tl, hl, w, channels)
         .transpose(0, 2, 1, 3, 4, 5)
         .reshape(frames, rows, w, channels)
     )
     coarse_in = acts_coarse[0].reshape(tl, hl, w, nr, nf, sub).transpose(4, 3, 5, 0, 1, 2)
-    coarse_in = lax.all_to_all(coarse_in.reshape(count, sub, tl * hl * w), BLOCK, 0, 0)
+    coarse_in = lax.all_to_all(coarse_in.reshape(count, sub, tl * hl * w), PLAIN_BLOCK, 0, 0)
     fine_in = acts_fine[0].reshape(tl, hl, 2, w, 2, nr, nf, sub).transpose(6, 5, 7, 2, 4, 0, 1, 3)
-    fine_in = lax.all_to_all(fine_in.reshape(count, sub, 4 * tl * hl * w), BLOCK, 0, 0)
+    fine_in = lax.all_to_all(fine_in.reshape(count, sub, 4 * tl * hl * w), PLAIN_BLOCK, 0, 0)
 
     def mine(vector):
         return lax.dynamic_slice_in_dim(vector, r * slice_width + f * sub, sub)
@@ -150,7 +151,7 @@
         coarse_vals, conv, cot, mine(gain_coarse), mine(bias_coarse), group_width
     )
     quartered = (coarse_grad * 0.25).astype(jnp.bfloat16)
-    spread = to_everyone(quartered, count)
+    spread = plain_everyone(quartered, count)
     source_fine = (
         spread.reshape(nf, nr, sub, frames, rows, w)
         .transpose(3, 4, 5, 1, 0, 2)
@@ -174,8 +175,8 @@
         .transpose(3, 5, 0, 1, 2, 4, 6, 7)
         .reshape(count, sub, 4 * tl * hl * w)
     )
-    sums = to_everyone(jnp.concatenate([fine_sums, coarse_sums]), count)
-    back = lax.all_to_all(back, BLOCK, 0, 0)
+    sums = plain_everyone(jnp.concatenate([fine_sums, coarse_sums]), count)
+    back = lax.all_to_all(back, PLAIN_BLOCK, 0, 0)
     out = (
         back.reshape(nf, nr, sub, 2, 2, tl, hl, w)
         .transpose(5, 6, 3, 7, 4, 1, 0, 2)
@@ -318,14 +319,12 @@
     coarse_hbm,
     fine_hbm,
     kernel_c,
-    kernel_f,
     gain_c,
     bias_c,
     gain_f,
     bias_f,
     out_ref,
     weights_c,
-    weights_f,
     columns,
     order,
     g_ref,
@@ -341,7 +340,7 @@
     copies = fetched(
         [(fine_hbm, fine_ref), (coarse_hbm, coarse_ref), (g_hbm, g_ref)]
         + [(row, rows.at[k]) for k, row in enumerate((gain_c, bias_c, gain_f, bias_f))]
-        + [(kernel_c.at[:, own, :], weights_c.at[pl.ds(0, 27)]), (kernel_f.at[:, own, :], weights_f)],
+        + [(kernel_c.at[:, own, :], weights_c.at[pl.ds(0, 27)])],
         sems,
     )
     shape = (sub, plan.channels)
@@ -360,7 +359,7 @@
     copies[2].wait()
     for s_f in range(plan.nf):
         for s_r in range(plan.nr):
-            dest, c = s_f * plan.nr + s_r, s_r * plan.slice_width + s_f * sub
+            dest, c = s_r * plan.nf + s_f, s_r * plan.slice_width + s_f * sub
             for k in range(chunks):
                 out_ref[dest, k * local : (k + 1) * local, :] = g_ref[:, k * 128 : (k + 1) * 128]
             at = chunks * local
@@ -379,7 +378,7 @@
     return jnp.concatenate(
         [
             jnp.concatenate(
-                [got_ref[f * plan.nr + r, at : at + height, :] for r in range(plan.nr)], axis=1
+                [got_ref[r * plan.nf + f, at : at + height, :] for r in range(plan.nr)], axis=1
             )
             for f in range(plan.nf)
         ],
@@ -405,7 +404,12 @@
     return near + moved(middle, image, lane < places - image) + moved(far, 2 * image, lane < places - 2 * image)
 
 
-def coarse_kernel(plan, got_ref, weights, columns, order, out_ref, sums_ref, source, products):
+def coarse_kernel(
+    plan, got_ref, weights, columns, order, kernel_f, out_ref, sums_ref, weights_f, source, products, sem
+):
+    own = pl.ds(pl.multiple_of(lax.axis_index("frames") * plan.sub, plan.sub), plan.sub)
+    copy = pltpu.make_async_copy(kernel_f.at[:, own, :], weights_f, sem)
+    copy.start()
     sub, nr, nf, cells, tl, local = plan.sub, plan.nr, plan.nf, plan.cells, plan.tl, plan.local
     chunks = plan.channels // 128
     for s_f in range(nf):
@@ -414,7 +418,7 @@
                 at = (s_f * tl + t) * plan.image + s_r * cells
                 for k in range(chunks):
                     source[at : at + cells, k * 128 : (k + 1) * 128] = got_ref[
-                        s_f * nr + s_r, k * local + t * cells : k * local + (t + 1) * cells, :
+                        s_r * nf + s_f, k * local + t * cells : k * local + (t + 1) * cells, :
                     ]
     products[...] = lax.dot_general(
         weights[...].reshape(28 * sub, plan.channels),
@@ -440,18 +444,15 @@
     for dest in range(plan.count):
         out_ref[dest] = quartered
     sums_ref[...] = jnp.concatenate([as_row(one), as_row(two)], axis=0)
-
-
-def fine_kernel(plan, got_ref, acts_ref, columns, order, sums_ref, weights, out_ref, source, products):
+    copy.wait()
+
+
+def fine_kernel(plan, got_ref, acts_ref, columns, order, sums_ref, weights, out_ref, products):
     sub, nr, nf = plan.sub, plan.nr, plan.nf
     f, r = lax.axis_index("frames"), lax.axis_index("rows")
-    for s_f in range(nf):
-        for s_r in range(nr):
-            c = s_r * plan.slice_width + s_f * sub
-            source[c : c + sub, :] = got_ref[s_f * nr + s_r]
     products[...] = lax.dot_general(
         weights[...].reshape(27 * sub, plan.channels),
-        source[...],
+        got_ref[...].reshape(plan.channels, plan.places),
         (((1,), (0,)), ((), ())),
         preferred_element_type=jnp.float32,
     )
@@ -467,7 +468,7 @@
         by_row.append((a + b + moved(c, -1, has_left), moved(a, 1, has_right) + b + c))
     convs = [by_row[0][q] + by_row[1][q] + moved(by_row[2][q], -plan.w, has_up) for q in range(2)]
     convs += [moved(by_row[0][q], plan.w, has_down) + by_row[1][q] + by_row[2][q] for q in range(2)]
-    cot = got_ref[f * nr + r].astype(jnp.float32)
+    cot = got_ref[r * nf + f].astype(jnp.float32)
     grads, one, two = finished(convs, normed, slope, [cot] * 4, gain, inv_std, entries, plan.group_width)
     width = plan.tl * plan.image
     stacked = jnp.concatenate(
@@ -485,30 +486,31 @@
     coded = jnp.concatenate([top, sums - top], axis=0).astype(jnp.bfloat16)
     for s_f in range(nf):
         for s_r in range(nr):
-            out_ref[s_f * nr + s_r, 0:sub, :] = sent[s_f * sub : (s_f + 1) * sub, s_r * 128 : (s_r + 1) * 128]
-            out_ref[s_f * nr + s_r, sub : sub + 8, :] = coded
-
-
-def spread_kernel(plan, scales, got_ref, out_ref, *rest):
-    sum_refs, source = rest[:4], rest[4]
+            out_ref[s_r * nf + s_f, 0:sub, :] = sent[s_f * sub : (s_f + 1) * sub, s_r * 128 : (s_r + 1) * 128]
+            out_ref[s_r * nf + s_f, sub : sub + 8, :] = coded
+
+
+def spread_kernel(plan, got_ref, out_ref, sums_ref):
     sub, nr, nf = plan.sub, plan.nr, plan.nf
-    for s_f in range(nf):
-        for s_r in range(nr):
-            c = s_r * plan.slice_width + s_f * sub
-            source[c : c + sub, :] = got_ref[s_f * nr + s_r, 0:sub, :]
     order = pixel_order(plan.tl, plan.hl, plan.w)
-    out_ref[...] = one_hot_dot(order, source[...], ((1,), (1,))).astype(jnp.bfloat16)
+    source = got_ref[:, 0:sub, :].reshape(plan.channels, 4 * plan.local)
+    out_ref[...] = one_hot_dot(order, source, ((1,), (1,))).astype(jnp.bfloat16)
     columns = []
     for s_r in range(nr):
         held = 0.0
         for s_f in range(nf):
-            coded = got_ref[s_f * nr + s_r, sub : sub + 8, :].astype(jnp.float32)
+            coded = got_ref[s_r * nf + s_f, sub : sub + 8, :].astype(jnp.float32)
             sums = coded[0:4] + coded[4:8]
             held = held + (pltpu.roll(sums, s_f * sub, 1) if s_f else sums)
         columns.append(held)
     rows = jnp.concatenate(columns, axis=1)
+    sums_ref[...] = jnp.concatenate([rows, jnp.zeros_like(rows)], axis=0)
+
+
+def total_kernel(scales, both_ref, *out_refs):
+    rows = sum(both_ref[k] for k in range(both_ref.shape[0]))
     for k in range(4):
-        sum_refs[k][...] = rows[k : k + 1] * scales[k]
+        out_refs[k][...] = rows[k : k + 1] * scales[k]
 
 
 def in_vmem(count):
@@ -547,23 +549,22 @@
     chunks = channels // 128
     f32, bf16 = jnp.float32, jnp.bfloat16
     rows = [part.reshape(1, channels) for part in (gain_coarse, bias_coarse, gain_fine, bias_fine)]
-    packed, weights_c, weights_f, columns, order = pl.pallas_call(
+    packed, weights_c, columns, order = pl.pallas_call(
         functools.partial(pack_kernel, plan),
         out_shape=(
             shape_of((count, chunks * local + sub + 8, 128), bf16),
             shape_of((28, sub, channels), bf16),
-            shape_of((27, sub, channels), bf16),
             shape_of((4, sub, 128), f32),
             shape_of((4 * plan.nr * local, 4 * plan.nr * local), bf16),
         ),
-        in_specs=in_hbm(9),
-        out_specs=tuple(in_vmem(5)),
+        in_specs=in_hbm(8),
+        out_specs=tuple(in_vmem(4)),
         scratch_shapes=[
             pltpu.VMEM((local, channels), bf16),
             pltpu.VMEM((local, channels), bf16),
             pltpu.VMEM((4 * local, channels), bf16),
             pltpu.VMEM((4, 1, channels), f32),
-            pltpu.SemaphoreType.DMA((9,)),
+            pltpu.SemaphoreType.DMA((8,)),
         ],
         compiler_params=LIMIT,
     )(
@@ -571,39 +572,53 @@
         kept(acts_coarse.reshape(local, channels)),
         kept(acts_fine.reshape(4 * local, channels)),
         kept(kernel_coarse),
-        kept(kernel_fine),
         *[kept(row) for row in rows],
     )
     got = lax.all_to_all(packed, BLOCK, 0, 0)
-    quartered, coarse_sums = pl.pallas_call(
+    quartered, coarse_sums, weights_f = pl.pallas_call(
         functools.partial(coarse_kernel, plan),
-        out_shape=(shape_of((count, sub, places), bf16), shape_of((2, 128), f32)),
-        in_specs=in_vmem(4),
-        out_specs=tuple(in_vmem(2)),
-        scratch_shapes=[pltpu.VMEM((places, channels), bf16), pltpu.VMEM((28 * sub, places), f32)],
+        out_shape=(
+            shape_of((count, sub, places), bf16),
+            shape_of((2, 128), f32),
+            shape_of((27, sub, channels), bf16),
+        ),
+        in_specs=in_vmem(4) + in_hbm(1),
+        out_specs=tuple(in_vmem(3)),
+        scratch_shapes=[
+            pltpu.VMEM((places, channels), bf16),
+            pltpu.VMEM((28 * sub, places), f32),
+            pltpu.SemaphoreType.DMA,
+        ],
         compiler_params=LIMIT,
-    )(got, weights_c, columns, order)
+    )(got, weights_c, columns, order, kept(kernel_fine))
     spread = lax.all_to_all(quartered, BLOCK, 0, 0)
     sent = pl.pallas_call(
         functools.partial(fine_kernel, plan),
         out_shape=shape_of((count, sub + 8, 128), bf16),
         in_specs=in_vmem(6),
         out_specs=in_vmem(1)[0],
-        scratch_shapes=[pltpu.VMEM((channels, places), bf16), pltpu.VMEM((27 * sub, places), f32)],
+        scratch_shapes=[pltpu.VMEM((27 * sub, places), f32)],
         compiler_params=LIMIT,
     )(spread, got, columns, order, coarse_sums, weights_f)
     back = lax.all_to_all(sent, BLOCK, 0, 0)
     cells = nd * places
     fine_scale, coarse_scale = 1.0 / math.sqrt(4 * cells), 1.0 / math.sqrt(cells)
-    out, *sums = pl.pallas_call(
-        functools.partial(spread_kernel, plan, (fine_scale, fine_scale, coarse_scale, coarse_scale)),
-        out_shape=(shape_of((4 * local, channels), bf16),) + (shape_of((1, channels), f32),) * 4,
+    out, sums = pl.pallas_call(
+        functools.partial(spread_kernel, plan),
+        out_shape=(pltpu.VMEM((4 * local, channels), bf16), shape_of((8, channels), f32)),
         in_specs=in_vmem(1),
-        out_specs=tuple(in_vmem(5)),
-        scratch_shapes=[pltpu.VMEM((channels, 4 * local), bf16)],
+        out_specs=tuple(in_vmem(2)),
         compiler_params=LIMIT,
     )(back)
-    bias_f, gain_f, bias_c, gain_c = lax.psum(tuple(part.reshape(channels) for part in sums), "dp")
+    both = lax.all_gather(sums, "dp")
+    sums = pl.pallas_call(
+        functools.partial(total_kernel, (fine_scale, fine_scale, coarse_scale, coarse_scale)),
+        out_shape=(shape_of((1, channels), f32),) * 4,
+        in_specs=in_vmem(1),
+        out_specs=tuple(in_vmem(4)),
+        compiler_params=LIMIT,
+    )(both)
+    bias_f, gain_f, bias_c, gain_c = [part.reshape(channels) for part in sums]
     return out.reshape(acts_fine.shape), gain_f, bias_f, gain_c, bias_c
 
 

time: 66.1 us -> 66.3 us (level)
  blocking collectives: 59.9 us -> 58.4 us
  Pallas kernels: 5.28 us -> 6.26 us
    psum x1 -> x0, blocking collectives: 3.04 us -> none  [fast_shards(): lax.psum(tuple((part.reshape(channels) for part in sums)), 'dp')]
    all_gather x0 -> x1, blocking collectives: none -> 1.82 us  [fast_shards(): both = lax.all_gather(sums, 'dp')]
    pallas_call x1, Pallas kernels: 1.21 us -> 2.27 us  [fast_shards(): pl.pallas_call(functools.partial(coarse_kernel, plan), out_shape=(shape_o...]
    all_to_all x1, blocking collectives: 10.6 us -> 11.6 us  [fast_shards(): back = lax.all_to_all(sent, BLOCK, 0, 0)]
    all_to_all x1, blocking collectives: 18.4 us -> 17.5 us  [fast_shards(): spread = lax.all_to_all(quartered, BLOCK, 0, 0)]
where the time goes in v7:
time: 66.3 us; the launch traced here: 66 us
  blocking collectives  58.4 us (88%)
  Pallas kernels  6.26 us (9%)
  between operations  0.67 us (1%)
    all_to_all x1, blocking collectives, fast_shards(): got = lax.all_to_all(packed, BLOCK, 0, 0)  27.5 us
    all_to_all x1, blocking collectives, fast_shards(): spread = lax.all_to_all(quartered, BLOCK, 0, 0)  17.5 us
    all_to_all x1, blocking collectives, fast_shards(): back = lax.all_to_all(sent, BLOCK, 0, 0)  11.6 us
    pallas_call x1, Pallas kernels, fast_shards(): pl.pallas_call(functools.partial(coarse_kernel, plan), out_shape=(shape_o...  2.27 us
    all_gather x1, blocking collectives, fast_shards(): both = lax.all_gather(sums, 'dp')  1.82 us
    pallas_call x1, Pallas kernels, fast_shards(): pl.pallas_call(functools.partial(pack_kernel, plan), out_shape=(shape_of(...  1.78 us
    pallas_call x1, Pallas kernels, fast_shards(): pl.pallas_call(functools.partial(fine_kernel, plan), out_shape=shape_of((...  1.43 us

profile of v7, /device:TPU:0, one launch (start us, length us, event | category | flops | bytes accessed | tf_op | source)
XLA Modules:
  0.0 66.0 jit_solution(2286567301266474051)
XLA Ops:
  0.6 1.8 %shard_map.128 = (bf16[16,168,128]{2,1,0:T(8,128)(2,1)S(1)}, bf16[28,32,512]{2,1,0:T(8,128)(2,1)S(1)}, f32[4,32,128]{2,1,0:T(8,128)S(1)}, bf16[512,512]{1,0:T(8,128)(2,1)S(1)}) custom-call(bf16[32,512]{1,0:T(8,128)(2,1)} %bitcast.16, bf16[32,512]{1,0:T(8,128)(2,1)} %bitcast.17, bf16[128,512]{1,0:T(8,128)(2,1)} %bitcast.15, bf16[27,128,512]{2,1,0:T(8,128)(2,1)} %kernel_c.1, ...), custom_call_target="tpu_custom_call" | custom-call | tf_op jit(solution)/shard_map/pallas_call | solution.py:552
  2.4 27.5 %all_to_all.15.got_ref.acts_ref = bf16[16,168,128]{2,1,0:T(8,128)(2,1)S(1)} all-to-all(bf16[16,168,128]{2,1,0:T(8,128)(2,1)S(1)} %get-tuple-element.18), channel_id=1, replica_groups=mesh['dp'=2,'frames'=4,'rows'=4] {'rows','frames'}, dimensions={0} | all-to-all | bytes 1376256 | tf_op jit(solution)/shard_map/all_to_all | solution.py:577
  29.9 2.3 %shard_map.129 = (bf16[16,32,512]{2,1,0:T(8,128)(2,1)S(1)}, f32[2,128]{1,0:T(2,128)S(1)}, bf16[27,32,512]{2,1,0:T(8,128)(2,1)S(1)}) custom-call(bf16[16,168,128]{2,1,0:T(8,128)(2,1)S(1)} %all_to_all.15.got_ref.acts_ref, bf16[28,32,512]{2,1,0:T(8,128)(2,1)S(1)} %get-tuple-element.19.weights, f32[4,32,128]{2,1,0:T(8,128)S(1)} %get-tuple-element.20.columns, ...), custom_call_target="tpu_custom_call" | custom-call | tf_op jit(solution)/shard_map/pallas_call | solution.py:578
  32.2 17.5 %all_to_all.16.got_ref = bf16[16,32,512]{2,1,0:T(8,128)(2,1)S(1)} all-to-all(bf16[16,32,512]{2,1,0:T(8,128)(2,1)S(1)} %get-tuple-element.22), channel_id=1, replica_groups=mesh['dp'=2,'frames'=4,'rows'=4] {'rows','frames'}, dimensions={0} | all-to-all | bytes 1048576 | tf_op jit(solution)/shard_map/all_to_all | solution.py:594
  49.7 1.4 %shard_map.130 = bf16[16,40,128]{2,1,0:T(8,128)(2,1)S(1)} custom-call(bf16[16,32,512]{2,1,0:T(8,128)(2,1)S(1)} %all_to_all.16.got_ref, bf16[16,168,128]{2,1,0:T(8,128)(2,1)S(1)} %all_to_all.15.got_ref.acts_ref, f32[4,32,128]{2,1,0:T(8,128)S(1)} %get-tuple-element.20.columns, bf16[512,512]{1,0:T(8,128)(2,1)S(1)} %get-tuple-element.21.order, ...), custom_call_target="tpu_custom_call" | custom-call | tf_op jit(solution)/shard_map/pallas_call | solution.py:595
  51.1 11.6 %all_to_all.17.got_ref = bf16[16,40,128]{2,1,0:T(8,128)(2,1)S(1)} all-to-all(bf16[16,40,128]{2,1,0:T(8,128)(2,1)S(1)} %shard_map.130), channel_id=1, replica_groups=mesh['dp'=2,'frames'=4,'rows'=4] {'rows','frames'}, dimensions={0} | all-to-all | bytes 327680 | tf_op jit(solution)/shard_map/all_to_all | solution.py:603
  62.7 0.2 shard_map.131
  62.9 0.7 copy.14
  63.6 1.8 %all-gather = f32[16,512]{1,0:T(8,128)S(1)} all-gather(f32[8,512]{1,0:T(8,128)S(1)} %get-tuple-element.26), channel_id=2, replica_groups=mesh['dp'=2,'frames'=4,'rows'=4] {'dp'}, dimensions={0}, use_global_device_ids=true | all-gather | bytes 49152 | tf_op jit(solution)/shard_map/all_gather | solution.py:613
  65.4 0.6 shard_map.132

commit v8 on v7

--- a/solution.py
+++ b/solution.py
@@ -319,12 +319,14 @@
     coarse_hbm,
     fine_hbm,
     kernel_c,
+    kernel_f,
     gain_c,
     bias_c,
     gain_f,
     bias_f,
     out_ref,
     weights_c,
+    weights_f,
     columns,
     order,
     g_ref,
@@ -340,7 +342,7 @@
     copies = fetched(
         [(fine_hbm, fine_ref), (coarse_hbm, coarse_ref), (g_hbm, g_ref)]
         + [(row, rows.at[k]) for k, row in enumerate((gain_c, bias_c, gain_f, bias_f))]
-        + [(kernel_c.at[:, own, :], weights_c.at[pl.ds(0, 27)])],
+        + [(kernel_c.at[:, own, :], weights_c.at[pl.ds(0, 27)]), (kernel_f.at[:, own, :], weights_f)],
         sems,
     )
     shape = (sub, plan.channels)
@@ -404,12 +406,7 @@
     return near + moved(middle, image, lane < places - image) + moved(far, 2 * image, lane < places - 2 * image)
 
 
-def coarse_kernel(
-    plan, got_ref, weights, columns, order, kernel_f, out_ref, sums_ref, weights_f, source, products, sem
-):
-    own = pl.ds(pl.multiple_of(lax.axis_index("frames") * plan.sub, plan.sub), plan.sub)
-    copy = pltpu.make_async_copy(kernel_f.at[:, own, :], weights_f, sem)
-    copy.start()
+def coarse_kernel(plan, got_ref, weights, columns, order, out_ref, sums_ref, source, products):
     sub, nr, nf, cells, tl, local = plan.sub, plan.nr, plan.nf, plan.cells, plan.tl, plan.local
     chunks = plan.channels // 128
     for s_f in range(nf):
@@ -444,7 +441,6 @@
     for dest in range(plan.count):
         out_ref[dest] = quartered
     sums_ref[...] = jnp.concatenate([as_row(one), as_row(two)], axis=0)
-    copy.wait()
 
 
 def fine_kernel(plan, got_ref, acts_ref, columns, order, sums_ref, weights, out_ref, products):
@@ -507,10 +503,16 @@
     sums_ref[...] = jnp.concatenate([rows, jnp.zeros_like(rows)], axis=0)
 
 
-def total_kernel(scales, both_ref, *out_refs):
+def total_kernel(scales, both_ref, result_ref, result_hbm, out_hbms, rows_ref, sems):
+    copies = fetched([(result_ref, result_hbm)], sems)
     rows = sum(both_ref[k] for k in range(both_ref.shape[0]))
     for k in range(4):
-        out_refs[k][...] = rows[k : k + 1] * scales[k]
+        rows_ref[k] = rows[k : k + 1] * scales[k]
+    for k in range(4):
+        copies.append(pltpu.make_async_copy(rows_ref.at[k], out_hbms[k], sems.at[k + 1]))
+        copies[-1].start()
+    for copy in copies:
+        copy.wait()
 
 
 def in_vmem(count):
@@ -549,22 +551,23 @@
     chunks = channels // 128
     f32, bf16 = jnp.float32, jnp.bfloat16
     rows = [part.reshape(1, channels) for part in (gain_coarse, bias_coarse, gain_fine, bias_fine)]
-    packed, weights_c, columns, order = pl.pallas_call(
+    packed, weights_c, weights_f, columns, order = pl.pallas_call(
         functools.partial(pack_kernel, plan),
         out_shape=(
             shape_of((count, chunks * local + sub + 8, 128), bf16),
             shape_of((28, sub, channels), bf16),
+            shape_of((27, sub, channels), bf16),
             shape_of((4, sub, 128), f32),
             shape_of((4 * plan.nr * local, 4 * plan.nr * local), bf16),
         ),
-        in_specs=in_hbm(8),
-        out_specs=tuple(in_vmem(4)),
+        in_specs=in_hbm(9),
+        out_specs=tuple(in_vmem(5)),
         scratch_shapes=[
             pltpu.VMEM((local, channels), bf16),
             pltpu.VMEM((local, channels), bf16),
             pltpu.VMEM((4 * local, channels), bf16),
             pltpu.VMEM((4, 1, channels), f32),
-            pltpu.SemaphoreType.DMA((8,)),
+            pltpu.SemaphoreType.DMA((9,)),
         ],
         compiler_params=LIMIT,
     )(
@@ -572,25 +575,18 @@
         kept(acts_coarse.reshape(local, channels)),
         kept(acts_fine.reshape(4 * local, channels)),
         kept(kernel_coarse),
+        kept(kernel_fine),
         *[kept(row) for row in rows],
     )
     got = lax.all_to_all(packed, BLOCK, 0, 0)
-    quartered, coarse_sums, weights_f = pl.pallas_call(
+    quartered, coarse_sums = pl.pallas_call(
         functools.partial(coarse_kernel, plan),
-        out_shape=(
-            shape_of((count, sub, places), bf16),
-            shape_of((2, 128), f32),
-            shape_of((27, sub, channels), bf16),
-        ),
-        in_specs=in_vmem(4) + in_hbm(1),
-        out_specs=tuple(in_vmem(3)),
-        scratch_shapes=[
-            pltpu.VMEM((places, channels), bf16),
-            pltpu.VMEM((28 * sub, places), f32),
-            pltpu.SemaphoreType.DMA,
-        ],
+        out_shape=(shape_of((count, sub, places), bf16), shape_of((2, 128), f32)),
+        in_specs=in_vmem(4),
+        out_specs=tuple(in_vmem(2)),
+        scratch_shapes=[pltpu.VMEM((places, channels), bf16), pltpu.VMEM((28 * sub, places), f32)],
         compiler_params=LIMIT,
-    )(got, weights_c, columns, order, kept(kernel_fine))
+    )(got, weights_c, columns, order)
     spread = lax.all_to_all(quartered, BLOCK, 0, 0)
     sent = pl.pallas_call(
         functools.partial(fine_kernel, plan),
@@ -611,13 +607,14 @@
         compiler_params=LIMIT,
     )(back)
     both = lax.all_gather(sums, "dp")
-    sums = pl.pallas_call(
+    out, sums = pl.pallas_call(
         functools.partial(total_kernel, (fine_scale, fine_scale, coarse_scale, coarse_scale)),
-        out_shape=(shape_of((1, channels), f32),) * 4,
-        in_specs=in_vmem(1),
-        out_specs=tuple(in_vmem(4)),
+        out_shape=(pltpu.HBM((4 * local, channels), bf16), (pltpu.HBM((1, channels), f32),) * 4),
+        in_specs=in_vmem(2),
+        out_specs=(in_hbm(1)[0], tuple(in_hbm(4))),
+        scratch_shapes=[pltpu.VMEM((4, 1, channels), f32), pltpu.SemaphoreType.DMA((5,))],
         compiler_params=LIMIT,
-    )(both)
+    )(both, out)
     bias_f, gain_f, bias_c, gain_c = [part.reshape(channels) for part in sums]
     return out.reshape(acts_fine.shape), gain_f, bias_f, gain_c, bias_c
 

time: 66.3 us -> 64.7 us (0.976)
  Pallas kernels: 6.26 us -> 5.32 us
    pallas_call x1, Pallas kernels: 2.27 us -> 1.21 us  [fast_shards(): pl.pallas_call(functools.partial(coarse_kernel, plan), out_shape=(shape_o...]
where the time goes in v8:
time: 64.7 us; the launch traced here: 64.4 us
  blocking collectives  58.4 us (90%)
  Pallas kernels  5.32 us (8%)
  between operations  0.67 us (1%)
    all_to_all x1, blocking collectives, fast_shards(): got = lax.all_to_all(packed, BLOCK, 0, 0)  27.5 us
    all_to_all x1, blocking collectives, fast_shards(): spread = lax.all_to_all(quartered, BLOCK, 0, 0)  17.5 us
    all_to_all x1, blocking collectives, fast_shards(): back = lax.all_to_all(sent, BLOCK, 0, 0)  11.6 us
    all_gather x1, blocking collectives, fast_shards(): both = lax.all_gather(sums, 'dp')  1.83 us
    pallas_call x1, Pallas kernels, fast_shards(): pl.pallas_call(functools.partial(pack_kernel, plan), out_shape=(shape_of(...  1.79 us
    pallas_call x1, Pallas kernels, fast_shards(): pl.pallas_call(functools.partial(fine_kernel, plan), out_shape=shape_of((...  1.43 us

profile of v8, /device:TPU:0, one launch (start us, length us, event | category | flops | bytes accessed | tf_op | source)
XLA Modules:
  0.0 64.4 jit_solution(6851711716279549356)
XLA Ops:
  0.6 1.8 %shard_map.128 = (bf16[16,168,128]{2,1,0:T(8,128)(2,1)S(1)}, bf16[28,32,512]{2,1,0:T(8,128)(2,1)S(1)}, bf16[27,32,512]{2,1,0:T(8,128)(2,1)S(1)}, f32[4,32,128]{2,1,0:T(8,128)S(1)}, bf16[512,512]{1,0:T(8,128)(2,1)S(1)}) custom-call(bf16[32,512]{1,0:T(8,128)(2,1)} %bitcast.15, bf16[32,512]{1,0:T(8,128)(2,1)} %bitcast.16, bf16[128,512]{1,0:T(8,128)(2,1)} %bitcast.14, ...), custom_call_target="tpu_custom_call" | custom-call | tf_op jit(solution)/shard_map/pallas_call | solution.py:554
  2.4 27.5 %all_to_all.15.got_ref.acts_ref = bf16[16,168,128]{2,1,0:T(8,128)(2,1)S(1)} all-to-all(bf16[16,168,128]{2,1,0:T(8,128)(2,1)S(1)} %get-tuple-element.19), channel_id=1, replica_groups=mesh['dp'=2,'frames'=4,'rows'=4] {'rows','frames'}, dimensions={0} | all-to-all | bytes 1376256 | tf_op jit(solution)/shard_map/all_to_all | solution.py:581
  29.9 1.2 %shard_map.129 = (bf16[16,32,512]{2,1,0:T(8,128)(2,1)S(1)}, f32[2,128]{1,0:T(2,128)S(1)}) custom-call(bf16[16,168,128]{2,1,0:T(8,128)(2,1)S(1)} %all_to_all.15.got_ref.acts_ref, bf16[28,32,512]{2,1,0:T(8,128)(2,1)S(1)} %get-tuple-element.20.weights, f32[4,32,128]{2,1,0:T(8,128)S(1)} %get-tuple-element.21.columns, bf16[512,512]{1,0:T(8,128)(2,1)S(1)} %get-tuple-element.22.order), custom_call_target="tpu_custom_call" | custom-call | tf_op jit(solution)/shard_map/pallas_call | solution.py:582
  31.1 17.5 %all_to_all.16.got_ref = bf16[16,32,512]{2,1,0:T(8,128)(2,1)S(1)} all-to-all(bf16[16,32,512]{2,1,0:T(8,128)(2,1)S(1)} %get-tuple-element.23), channel_id=1, replica_groups=mesh['dp'=2,'frames'=4,'rows'=4] {'rows','frames'}, dimensions={0} | all-to-all | bytes 1048576 | tf_op jit(solution)/shard_map/all_to_all | solution.py:590
  48.6 1.4 %shard_map.130 = bf16[16,40,128]{2,1,0:T(8,128)(2,1)S(1)} custom-call(bf16[16,32,512]{2,1,0:T(8,128)(2,1)S(1)} %all_to_all.16.got_ref, bf16[16,168,128]{2,1,0:T(8,128)(2,1)S(1)} %all_to_all.15.got_ref.acts_ref, f32[4,32,128]{2,1,0:T(8,128)S(1)} %get-tuple-element.21.columns, bf16[512,512]{1,0:T(8,128)(2,1)S(1)} %get-tuple-element.22.order, ...), custom_call_target="tpu_custom_call" | custom-call | tf_op jit(solution)/shard_map/pallas_call | solution.py:591
  50.1 11.6 %all_to_all.17.got_ref = bf16[16,40,128]{2,1,0:T(8,128)(2,1)S(1)} all-to-all(bf16[16,40,128]{2,1,0:T(8,128)(2,1)S(1)} %shard_map.130), channel_id=1, replica_groups=mesh['dp'=2,'frames'=4,'rows'=4] {'rows','frames'}, dimensions={0} | all-to-all | bytes 327680 | tf_op jit(solution)/shard_map/all_to_all | solution.py:599
  61.7 0.2 shard_map.131
  61.9 1.8 %all-gather = f32[16,512]{1,0:T(8,128)S(1)} all-gather(f32[8,512]{1,0:T(8,128)S(1)} %get-tuple-element.26), channel_id=2, replica_groups=mesh['dp'=2,'frames'=4,'rows'=4] {'dp'}, dimensions={0}, use_global_device_ids=true | all-gather | bytes 49152 | tf_op jit(solution)/shard_map/all_gather | solution.py:609
  63.7 0.7 %shard_map.132 = (bf16[128,512]{1,0:T(8,128)(2,1)}, f32[1,512]{1,0:T(1,128)}, f32[1,512]{1,0:T(1,128)}, f32[1,512]{1,0:T(1,128)}, f32[1,512]{1,0:T(1,128)}) custom-call(f32[2,8,512]{2,1,0:T(8,128)S(1)} %bitcast.13, bf16[128,512]{1,0:T(8,128)(2,1)S(1)} %get-tuple-element.27.result_ref), custom_call_target="tpu_custom_call" | custom-call | tf_op jit(solution)/shard_map/pallas_call | solution.py:610

commit v9 on v8

--- a/solution.py
+++ b/solution.py
@@ -10,7 +10,7 @@
 
 GROUPS = 32
 EPSILON = 1e-06
-BLOCK = ("rows", "frames")
+BLOCK = ("rows", "pairs", "member")
 PLAIN_BLOCK = ("frames", "rows")
 
 
@@ -200,13 +200,21 @@
     return lax.broadcasted_iota(jnp.int32, shape, axis)
 
 
-def pixel_order(tl, hl, w):
-    size = 4 * tl * hl * w
+def one_hot(found):
+    return found.astype(jnp.float32).astype(jnp.bfloat16)
+
+
+def pixel_order(plan, swapped):
+    tl, hl, w = plan.tl, plan.hl, plan.w // 2
+    size = 4 * plan.local
     lane = lanes_at((size, size), 1)
     j, i, t = lane % w, lane // w % hl, lane // (w * hl) % tl
-    q, p = lane // (w * hl * tl) % 2, lane // (2 * w * hl * tl)
-    pixel = (t * 2 * hl + 2 * i + p) * 2 * w + 2 * j + q
-    return (lanes_at((size, size), 0) == pixel).astype(jnp.float32).astype(jnp.bfloat16)
+    q, p = lane // (w * hl * tl) % 2, lane // (2 * w * hl * tl) % 2
+    half = lane // (4 * w * hl * tl)
+    if swapped:
+        half = 1 - half
+    pixel = (t * 2 * hl + 2 * i + p) * 4 * w + 2 * (half * w + j) + q
+    return one_hot(lanes_at((size, size), 0) == pixel)
 
 
 def merged_order(nr, outer, tl, cells):
@@ -215,7 +223,20 @@
     cell, t = a % cells, a // cells % tl
     o, dev = a // (cells * tl) % outer, a // (cells * tl * outer)
     target = ((o * tl + t) * nr + dev) * cells + cell
-    return (lanes_at((size, size), 1) == target).astype(jnp.float32).astype(jnp.bfloat16)
+    return one_hot(lanes_at((size, size), 1) == target)
+
+
+def column_order(plan):
+    w = plan.w // 2
+    lines = plan.places // plan.w
+    lane = lanes_at((1, 4 * lines * w + 4 * lines), 1)
+    inner = lane % (lines * w)
+    place = inner // w * plan.w + lane // (lines * w) * w + inner % w
+    past = lane - 2 * lines * w
+    border = past % lines * plan.w + jnp.where(past < 2 * lines, w, w - 1)
+    wanted = jnp.where(past >= 0, border, place)
+    shape = (plan.places, 2 * lines * w + 4 * lines)
+    return one_hot(lanes_at(shape, 0) == wanted[:, : shape[1]])
 
 
 def one_hot_dot(a, b, dims):
@@ -239,20 +260,42 @@
     return jnp.sum(jnp.where(here, column, 0.0), axis=0, keepdims=True)
 
 
+def terms(value, count):
+    found = []
+    for _ in range(count):
+        found.append(value.astype(jnp.bfloat16).astype(jnp.float32))
+        value = value - found[-1]
+    return found
+
+
 def in_groups(column, group_width):
     sub = column.shape[0]
     grouped = jnp.sum(column.reshape(sub // group_width, group_width, 1), axis=1, keepdims=True)
     return jnp.broadcast_to(grouped, (sub // group_width, group_width, 1)).reshape(sub, 1)
 
 
+def in_lane_groups(row, group_width):
+    lane = lanes_at(row.shape, 1)
+    size = row.shape[1]
+    step = 1
+    while step < group_width:
+        up, down = pltpu.roll(row, size - step, 1), pltpu.roll(row, step, 1)
+        row = row + jnp.where(lane // step % 2 == 0, up, down)
+        step *= 2
+    return row
+
+
 def total(parts):
     return sum(jnp.sum(part, axis=1, keepdims=True) for part in parts)
 
 
-def normalised(parts, gain, bias, entries, group_width):
-    mean = in_groups(total(parts), group_width) / entries
-    square = in_groups(total([part * part for part in parts]), group_width) / entries
-    inv_std = lax.rsqrt(square - mean * mean + EPSILON)
+def statistics(one, two, entries, group_width):
+    mean = in_groups(one, group_width) / entries
+    square = in_groups(two, group_width) / entries
+    return mean, lax.rsqrt(square - mean * mean + EPSILON)
+
+
+def normalised(parts, gain, bias, mean, inv_std):
     normed, slope = [], []
     for part in parts:
         unit = (part - mean) * inv_std
@@ -260,20 +303,7 @@
         squash = jax.nn.sigmoid(preact)
         normed.append(unit)
         slope.append(squash * (1.0 + preact * (1.0 - squash)))
-    return normed, slope, inv_std
-
-
-def finished(convs, normed, slope, cots, gain, inv_std, entries, group_width):
-    pre = [conv * part for conv, part in zip(convs, slope)]
-    one = total(pre)
-    two = total([a * b for a, b in zip(pre, normed)])
-    group_one = in_groups(gain * one, group_width) / entries
-    group_two = in_groups(gain * two, group_width) / entries
-    grads = [
-        cot + inv_std * (gain * part - group_one - unit * group_two)
-        for cot, part, unit in zip(cots, pre, normed)
-    ]
-    return grads, one, two
+    return normed, slope
 
 
 class Plan:
@@ -289,21 +319,28 @@
         self.frames = self.tl * self.nf
         self.places = self.frames * self.image
         self.group_width = self.channels // GROUPS
+        self.chunks = self.channels // 128
+        self.acts_at = self.chunks * self.local
+        self.packed_at = self.acts_at + self.sub
+        self.stats_at = self.packed_at + 8
+        self.block_rows = self.stats_at + 8
         self.fits = (
             self.sub == 32
+            and self.slice_width == 128
             and self.group_width == 16
             and self.cells == 16
+            and self.w == 8
             and self.tl == 2
             and self.nr == 4
-            and self.channels % 128 == 0
+            and self.nf == 4
             and self.slice_width * self.nr == self.channels
         )
 
-    def place_masks(self):
-        lane = lanes_at((1, self.places), 1)
-        col, row = lane % self.w, lane // self.w % (self.hl * self.nr)
+    def place_masks(self, w):
+        lane = lanes_at((1, self.places // self.w * w), 1)
+        col, row = lane % w, lane // w % (self.hl * self.nr)
         last_row = self.hl * self.nr - 1
-        return (lane, col > 0, col < self.w - 1, row > 0, row < last_row)
+        return (lane, col > 0, col < w - 1, row > 0, row < last_row)
 
 
 def fetched(pairs, sems):
@@ -311,6 +348,11 @@
     for copy in copies:
         copy.start()
     return copies
+
+
+def own_place(plan):
+    pair, member, r = lax.axis_index("pairs"), lax.axis_index("member"), lax.axis_index("rows")
+    return pair, member, r, r * plan.slice_width + (2 * pair + member) * plan.sub
 
 
 def pack_kernel(
@@ -325,53 +367,65 @@
     gain_f,
     bias_f,
     out_ref,
+    fine_ref,
     weights_c,
     weights_f,
     columns,
     order,
+    fine_order,
+    by_column,
+    rows,
     g_ref,
     coarse_ref,
-    fine_ref,
-    rows,
     sems,
 ):
-    sub, chunks, local = plan.sub, plan.channels // 128, plan.local
-    f, r = lax.axis_index("frames"), lax.axis_index("rows")
-    base = r * plan.slice_width + f * sub
-    own = pl.ds(pl.multiple_of(f * sub, sub), sub)
+    sub, chunks, local = plan.sub, plan.chunks, plan.local
+    pair, member, r, base = own_place(plan)
+    own = pl.ds(pl.multiple_of((2 * pair + member) * sub, sub), sub)
+    both = pl.ds(pl.multiple_of(2 * pair * sub, 2 * sub), 2 * sub)
     copies = fetched(
         [(fine_hbm, fine_ref), (coarse_hbm, coarse_ref), (g_hbm, g_ref)]
         + [(row, rows.at[k]) for k, row in enumerate((gain_c, bias_c, gain_f, bias_f))]
-        + [(kernel_c.at[:, own, :], weights_c.at[pl.ds(0, 27)]), (kernel_f.at[:, own, :], weights_f)],
+        + [(kernel_c.at[:, own, :], weights_c.at[pl.ds(0, 27)]), (kernel_f.at[:, both, :], weights_f)],
         sems,
     )
     shape = (sub, plan.channels)
-    weights_c[27] = (lanes_at(shape, 1) == lanes_at(shape, 0) + base).astype(jnp.float32).astype(jnp.bfloat16)
+    weights_c[27] = one_hot(lanes_at(shape, 1) == lanes_at(shape, 0) + base)
     order[...] = merged_order(plan.nr, 4, plan.tl, plan.cells)
-    pixels = pixel_order(plan.tl, plan.hl, plan.w)
+    fine_order[...] = merged_order(plan.nr, 8, plan.tl, plan.cells // 2)
+    by_column[...] = column_order(plan)
     shape = (local, 128)
-    places = [
-        (lanes_at(shape, 0) + k * local == lanes_at(shape, 1)).astype(jnp.float32).astype(jnp.bfloat16)
-        for k in range(4)
-    ]
+    places = [one_hot(lanes_at(shape, 0) + k * local == lanes_at(shape, 1)) for k in range(4)]
+    orders = [pixel_order(plan, swapped) for swapped in (False, True)]
     copies[0].wait()
-    fine = one_hot_dot(fine_ref[...], pixels, ((0,), (0,))).astype(jnp.bfloat16)
+    acts = fine_ref[...]
+    halves = [one_hot_dot(acts, order_of, ((0,), (0,))).astype(jnp.bfloat16) for order_of in orders]
+    values = acts.astype(jnp.float32)
+    one = jnp.sum(values, axis=0, keepdims=True)
+    two = jnp.sum(values * values, axis=0, keepdims=True)
+    stats = terms(one, 3) + terms(two, 3)
+    stats = jnp.concatenate(stats + [jnp.zeros_like(one)] * 2, axis=0).astype(jnp.bfloat16)
     copies[1].wait()
     quarters = [one_hot_dot(coarse_ref[...], place, ((0,), (0,))) for place in places]
     copies[2].wait()
-    for s_f in range(plan.nf):
-        for s_r in range(plan.nr):
+    low = lanes_at((sub, 128), 1) < 64
+    for s_r in range(plan.nr):
+        for s_f in range(plan.nf):
             dest, c = s_r * plan.nf + s_f, s_r * plan.slice_width + s_f * sub
             for k in range(chunks):
                 out_ref[dest, k * local : (k + 1) * local, :] = g_ref[:, k * 128 : (k + 1) * 128]
-            at = chunks * local
-            out_ref[dest, at : at + sub, :] = fine[c : c + sub]
+            first, half = s_r * plan.slice_width + s_f // 2 * 2 * sub, s_f % 2
+            upper, lower = halves[half][first : first + sub], halves[1 - half][first + sub : first + 2 * sub]
+            out_ref[dest, plan.acts_at : plan.packed_at, :] = jnp.where(low, upper, lower)
             coarse = sum(quarters[k][c + 8 * k : c + 8 * k + 8] for k in range(4))
-            out_ref[dest, at + sub : at + sub + 8, :] = coarse.astype(jnp.bfloat16)
+            out_ref[dest, plan.packed_at : plan.stats_at, :] = coarse.astype(jnp.bfloat16)
+            out_ref[dest, plan.stats_at : plan.block_rows, :] = stats[:, s_r * 128 : (s_r + 1) * 128]
     for copy in copies[3:7]:
         copy.wait()
-    for k in range(4):
-        columns[k] = jnp.broadcast_to(own_column(rows[k], base, sub), (sub, 128))
+    first = r * plan.slice_width + 2 * pair * sub
+    for k in range(2):
+        columns[k, 0:sub, :] = jnp.broadcast_to(own_column(rows[k], base, sub), (sub, 128))
+        columns[2 + k] = jnp.broadcast_to(own_column(rows[2 + k], first, 2 * sub), (2 * sub, 128))
     for copy in copies[7:]:
         copy.wait()
 
@@ -399,21 +453,18 @@
     ]
 
 
-def frame_sum(products_ref, tap, sub, lane, places, image):
-    near = products_ref[pl.ds((18 + tap) * sub, sub), :]
-    middle = products_ref[pl.ds((9 + tap) * sub, sub), :]
-    far = products_ref[pl.ds(tap * sub, sub), :]
+def frame_sum(products_ref, taps, sub, lane, places, image):
+    near, middle, far = [products_ref[pl.ds(tap * sub, sub), :] for tap in reversed(taps)]
     return near + moved(middle, image, lane < places - image) + moved(far, 2 * image, lane < places - 2 * image)
 
 
-def coarse_kernel(plan, got_ref, weights, columns, order, out_ref, sums_ref, source, products):
+def coarse_kernel(plan, got_ref, weights, columns, order, by_column, out_ref, sums_ref, source, products):
     sub, nr, nf, cells, tl, local = plan.sub, plan.nr, plan.nf, plan.cells, plan.tl, plan.local
-    chunks = plan.channels // 128
     for s_f in range(nf):
         for s_r in range(nr):
             for t in range(tl):
                 at = (s_f * tl + t) * plan.image + s_r * cells
-                for k in range(chunks):
+                for k in range(plan.chunks):
                     source[at : at + cells, k * 128 : (k + 1) * 128] = got_ref[
                         s_r * nf + s_f, k * local + t * cells : k * local + (t + 1) * cells, :
                     ]
@@ -423,84 +474,194 @@
         (((1,), (1,)), ((), ())),
         preferred_element_type=jnp.float32,
     )
-    packed = by_frame_device(plan, got_ref, chunks * local + sub, 8)
+    packed = by_frame_device(plan, got_ref, plan.packed_at, 8)
     merged = one_hot_dot(packed, order[...], ((1,), (0,)))
     values = jnp.concatenate(in_places(plan, merged, 8), axis=0)
-    gain, bias = columns[0][:, 0:1], columns[1][:, 0:1]
+    gain, bias = columns[0][0:sub, 0:1], columns[1][0:sub, 0:1]
     entries = plan.places * plan.group_width
-    normed, slope, inv_std = normalised([values], gain, bias, entries, plan.group_width)
-    lane, has_left, has_right, has_up, has_down = plan.place_masks()
+    mean, inv_std = statistics(total([values]), total([values * values]), entries, plan.group_width)
+    (normed,), (slope,) = normalised([values], gain, bias, mean, inv_std)
+    lane, has_left, has_right, has_up, has_down = plan.place_masks(plan.w)
     by_col = []
     for col in range(3):
-        parts = [frame_sum(products, 3 * row + col, sub, lane, plan.places, plan.image) for row in range(3)]
+        parts = [
+            frame_sum(products, [9 * depth + 3 * row + col for depth in range(3)], sub, lane, plan.places, plan.image)
+            for row in range(3)
+        ]
         by_col.append(parts[1] + moved(parts[0], plan.w, has_down) + moved(parts[2], -plan.w, has_up))
     conv = by_col[1] + moved(by_col[0], 1, has_right) + moved(by_col[2], -1, has_left)
     cot = products[pl.ds(27 * sub, sub), :]
-    grads, one, two = finished([conv], normed, slope, [cot], gain, inv_std, entries, plan.group_width)
-    quartered = (grads[0] * 0.25).astype(jnp.bfloat16)
-    for dest in range(plan.count):
-        out_ref[dest] = quartered
+    pre = conv * slope
+    one, two = total([pre]), total([pre * normed])
+    group_one = in_groups(gain * one, plan.group_width) / entries
+    group_two = in_groups(gain * two, plan.group_width) / entries
+    grad = cot + inv_std * (gain * pre - group_one - normed * group_two)
+    quartered = (grad * 0.25).astype(jnp.bfloat16)
+    sent = one_hot_dot(quartered, by_column[...], ((1,), (0,))).astype(jnp.bfloat16)
+    low = lanes_at((sub // 2, 128), 1) < 64
+    for half in range(2):
+        at = half * 256
+        border = sent[:, 512 + half * 128 : 640 + half * 128]
+        border = jnp.where(low, border[: sub // 2], border[sub // 2 :])
+        for dest in range(half, plan.count, 2):
+            out_ref[dest, 0:sub, :] = sent[:, at : at + 128]
+            out_ref[dest, sub : 2 * sub, :] = sent[:, at + 128 : at + 256]
+            out_ref[dest, 2 * sub : 2 * sub + sub // 2, :] = border
     sums_ref[...] = jnp.concatenate([as_row(one), as_row(two)], axis=0)
 
 
-def fine_kernel(plan, got_ref, acts_ref, columns, order, sums_ref, weights, out_ref, products):
-    sub, nr, nf = plan.sub, plan.nr, plan.nf
-    f, r = lax.axis_index("frames"), lax.axis_index("rows")
-    products[...] = lax.dot_general(
-        weights[...].reshape(27 * sub, plan.channels),
-        got_ref[...].reshape(plan.channels, plan.places),
-        (((1,), (0,)), ((), ())),
-        preferred_element_type=jnp.float32,
-    )
-    packed = by_frame_device(plan, acts_ref, plan.channels // 128 * plan.local, sub)
-    parts = in_places(plan, one_hot_dot(packed, order[...], ((1,), (0,))), sub)
+def halves_at(plan, merged):
+    sub = plan.sub
+    turned = jnp.concatenate([pltpu.roll(merged[:, k * 128 : (k + 1) * 128], 64, 1) for k in range(4)], axis=1)
+    low = lanes_at((sub, 128), 1) < 64
+    parts = []
+    for pq in range(4):
+        groups = []
+        for group in range(2):
+            e = 4 * group + pq
+            at = e // 2 * 128
+            strips = []
+            for m in range(plan.nf // 2):
+                first, second = slice(2 * m * sub, (2 * m + 1) * sub), slice((2 * m + 1) * sub, (2 * m + 2) * sub)
+                if e % 2 == 0:
+                    strips.append(jnp.where(low, merged[first, at : at + 128], turned[second, at : at + 128]))
+                else:
+                    strips.append(jnp.where(low, turned[first, at : at + 128], merged[second, at : at + 128]))
+            groups.append(jnp.concatenate(strips, axis=1))
+        parts.append(jnp.concatenate(groups, axis=0))
+    return parts
+
+
+def halves_from(plan, parts):
+    sub = plan.sub
+    low = lanes_at((sub, 128), 1) < 64
+    down = []
+    for f in range(plan.nf):
+        across = []
+        for v in range(4):
+            pair = []
+            for e in (2 * v, 2 * v + 1):
+                group, pq = e // 4, e % 4
+                strip = parts[pq][group * sub : (group + 1) * sub, f // 2 * 128 : (f // 2 + 1) * 128]
+                pair.append(strip if e % 2 == f % 2 else pltpu.roll(strip, 64, 1))
+            across.append(jnp.where(low, pair[0], pair[1]))
+        down.append(jnp.concatenate(across, axis=1))
+    return jnp.concatenate(down, axis=0)
+
+
+def fine_kernel(
+    plan, got_ref, acts_ref, columns, order, sums_ref, weights, out_ref, source, border, products, beyond
+):
+    sub, nr, nf, wide = plan.sub, plan.nr, plan.nf, 2 * plan.sub
+    pair, member, r, _ = own_place(plan)
+    w = plan.w // 2
+    lines = plan.places // plan.w
+    places = lines * w
+    for k in range(2):
+        source[:, k * 128 : (k + 1) * 128] = got_ref[:, k * sub : (k + 1) * sub, :].reshape(plan.channels, 128)
+    products[...] = one_hot_dot(weights[...].reshape(27 * wide, plan.channels), source[...], ((1,), (0,)))
+    packed = got_ref[:, wide : wide + sub // 2, :].reshape(plan.count * sub // 2, 128)
+    shape = (128, places)
+    beside = lanes_at(shape, 1) == lanes_at(shape, 0) % lines * w + (1 - member) * (w - 1)
+    for k in range(2):
+        here = one_hot(beside & (lanes_at(shape, 0) // lines == k))
+        found = one_hot_dot(packed, here, ((1,), (0,))).astype(jnp.bfloat16)
+        for s in range(plan.count):
+            border[s * sub + k * (sub // 2) : s * sub + (k + 1) * (sub // 2), :] = found[
+                s * (sub // 2) : (s + 1) * (sub // 2)
+            ]
+    facing = jnp.concatenate([weights[3 * k + 2 * member] for k in range(9)], axis=0)
+    beyond[...] = one_hot_dot(facing, border[...], ((1,), (0,)))
+    merged = one_hot_dot(by_frame_device(plan, acts_ref, plan.acts_at, sub), order[...], ((1,), (0,)))
+    parts = halves_at(plan, merged)
+    stats = sum(
+        acts_ref[s, plan.stats_at : plan.block_rows, :].astype(jnp.float32) for s in range(plan.count)
+    )
+    entries = 4 * plan.places * plan.group_width
+    one = own_column(stats[0:1] + stats[1:2] + stats[2:3], pair * wide, wide)
+    two = own_column(stats[3:4] + stats[4:5] + stats[5:6], pair * wide, wide)
+    mean, inv_std = statistics(one, two, entries, plan.group_width)
     gain, bias = columns[2][:, 0:1], columns[3][:, 0:1]
-    entries = 4 * plan.places * plan.group_width
-    normed, slope, inv_std = normalised(parts, gain, bias, entries, plan.group_width)
-    lane, has_left, has_right, has_up, has_down = plan.place_masks()
+    normed, slope = normalised(parts, gain, bias, mean, inv_std)
+    lane, has_left, has_right, has_up, has_down = plan.place_masks(w)
+    image = plan.image // 2
+    right, left = (1 - member).astype(jnp.float32), member.astype(jnp.float32)
     by_row = []
     for row in range(3):
-        a, b, c = [frame_sum(products, 3 * row + col, sub, lane, plan.places, plan.image) for col in range(3)]
-        by_row.append((a + b + moved(c, -1, has_left), moved(a, 1, has_right) + b + c))
-    convs = [by_row[0][q] + by_row[1][q] + moved(by_row[2][q], -plan.w, has_up) for q in range(2)]
-    convs += [moved(by_row[0][q], plan.w, has_down) + by_row[1][q] + by_row[2][q] for q in range(2)]
-    cot = got_ref[r * nf + f].astype(jnp.float32)
-    grads, one, two = finished(convs, normed, slope, [cot] * 4, gain, inv_std, entries, plan.group_width)
-    width = plan.tl * plan.image
-    stacked = jnp.concatenate(
-        [
-            jnp.concatenate(
-                [grads[pq][:, s_f * width : (s_f + 1) * width].astype(jnp.bfloat16) for pq in range(4)], axis=1
-            )
-            for s_f in range(nf)
-        ],
-        axis=0,
-    )
+        a, b, c = [
+            frame_sum(products, [9 * depth + 3 * row + col for depth in range(3)], wide, lane, places, image)
+            for col in range(3)
+        ]
+        extra = frame_sum(beyond, [3 * depth + row for depth in range(3)], wide, lane, places, image)
+        by_row.append(
+            (a + b + moved(c, -1, has_left) + left * extra, moved(a, 1, has_right) + b + c + right * extra)
+        )
+    convs = [by_row[0][q] + by_row[1][q] + moved(by_row[2][q], -w, has_up) for q in range(2)]
+    convs += [moved(by_row[0][q], w, has_down) + by_row[1][q] + by_row[2][q] for q in range(2)]
+    pre = [conv * part for conv, part in zip(convs, slope)]
+    one = total(pre)
+    two = total([a * b for a, b in zip(pre, normed)])
+    cot = source[pl.ds(pl.multiple_of(r * plan.slice_width + pair * wide, wide), wide), :].astype(jnp.float32)
+    scale = inv_std * gain
+    stacked = halves_from(plan, [cot + scale * part for part in pre]).astype(jnp.bfloat16)
     sent = one_hot_dot(stacked, order[...], ((1,), (1,))).astype(jnp.bfloat16)
-    sums = jnp.concatenate([as_row(one), as_row(two), sums_ref[...]], axis=0)
-    top = sums.astype(jnp.bfloat16).astype(jnp.float32)
-    coded = jnp.concatenate([top, sums - top], axis=0).astype(jnp.bfloat16)
-    for s_f in range(nf):
-        for s_r in range(nr):
+    coarse = sums_ref[0:1] + pltpu.roll(sums_ref[1:2], sub, 1)
+    coded = (
+        terms(as_row(one) + pltpu.roll(as_row(two), 64, 1), 2)
+        + terms(coarse, 2)
+        + terms(as_row(inv_std) + pltpu.roll(as_row(mean), 64, 1), 3)
+    )
+    coded = jnp.concatenate(coded + [jnp.zeros_like(coarse)], axis=0).astype(jnp.bfloat16)
+    for s_r in range(nr):
+        for s_f in range(nf):
             out_ref[s_r * nf + s_f, 0:sub, :] = sent[s_f * sub : (s_f + 1) * sub, s_r * 128 : (s_r + 1) * 128]
             out_ref[s_r * nf + s_f, sub : sub + 8, :] = coded
 
 
-def spread_kernel(plan, got_ref, out_ref, sums_ref):
+def spread_kernel(plan, got_ref, acts_ref, rows_ref, out_ref, sums_ref):
     sub, nr, nf = plan.sub, plan.nr, plan.nf
-    order = pixel_order(plan.tl, plan.hl, plan.w)
-    source = got_ref[:, 0:sub, :].reshape(plan.channels, 4 * plan.local)
-    out_ref[...] = one_hot_dot(order, source, ((1,), (1,))).astype(jnp.bfloat16)
-    columns = []
+    low = lanes_at((sub, 128), 1) < 64
+    low_row = lanes_at((1, 128), 1) < 64
+    first_row = lanes_at((1, 128), 1) < sub
+    source = []
+    fine, coarse, moments = [[], []], [[], []], [[], []]
     for s_r in range(nr):
-        held = 0.0
-        for s_f in range(nf):
-            coded = got_ref[s_r * nf + s_f, sub : sub + 8, :].astype(jnp.float32)
-            sums = coded[0:4] + coded[4:8]
-            held = held + (pltpu.roll(sums, s_f * sub, 1) if s_f else sums)
-        columns.append(held)
-    rows = jnp.concatenate(columns, axis=1)
-    sums_ref[...] = jnp.concatenate([rows, jnp.zeros_like(rows)], axis=0)
+        ones, twos, c_ones, c_twos, invs, means = [], [], 0.0, 0.0, [], []
+        for pair in range(nf // 2):
+            at = s_r * nf + 2 * pair
+            left, right = [got_ref[at + k, 0:sub, :].astype(jnp.float32) for k in range(2)]
+            source.append(jnp.where(low, left, pltpu.roll(right, 64, 1)))
+            source.append(jnp.where(low, pltpu.roll(left, 64, 1), right))
+            coded = [got_ref[at + k, sub : sub + 8, :].astype(jnp.float32) for k in range(2)]
+            sums = coded[0][0:1] + coded[0][1:2] + coded[1][0:1] + coded[1][1:2]
+            ones.append(sums if pair == 0 else pltpu.roll(sums, 64, 1))
+            twos.append(pltpu.roll(sums, 64, 1) if pair == 0 else sums)
+            both = coded[0][4:5] + coded[0][5:6] + coded[0][6:7]
+            invs.append(both if pair == 0 else pltpu.roll(both, 64, 1))
+            means.append(pltpu.roll(both, 64, 1) if pair == 0 else both)
+            for k in range(2):
+                sums = coded[k][2:3] + coded[k][3:4]
+                to = (2 * pair + k) * sub
+                c_one = jnp.where(first_row, sums, 0.0)
+                c_two = jnp.where(first_row, pltpu.roll(sums, 128 - sub, 1), 0.0)
+                c_ones = c_ones + (pltpu.roll(c_one, to, 1) if to else c_one)
+                c_twos = c_twos + (pltpu.roll(c_two, to, 1) if to else c_two)
+        fine[0].append(jnp.where(low_row, ones[0], ones[1]))
+        fine[1].append(jnp.where(low_row, twos[0], twos[1]))
+        moments[0].append(jnp.where(low_row, invs[0], invs[1]))
+        moments[1].append(jnp.where(low_row, means[0], means[1]))
+        coarse[0].append(c_ones)
+        coarse[1].append(c_twos)
+    one, two, inv_std, mean, c_one, c_two = [jnp.concatenate(part, axis=1) for part in fine + moments + coarse]
+    source = jnp.concatenate(source, axis=0).astype(jnp.bfloat16)
+    result = one_hot_dot(pixel_order(plan, False), source, ((1,), (1,)))
+    gain = rows_ref[2]
+    entries = 4 * plan.places * plan.group_width
+    group_one = in_lane_groups(gain * one, plan.group_width) / entries
+    group_two = in_lane_groups(gain * two, plan.group_width) / entries
+    normed = (acts_ref[...].astype(jnp.float32) - mean) * inv_std
+    out_ref[...] = (result - inv_std * (group_one + normed * group_two)).astype(jnp.bfloat16)
+    sums_ref[...] = jnp.concatenate([one, two, c_one, c_two] + [jnp.zeros_like(one)] * 4, axis=0)
 
 
 def total_kernel(scales, both_ref, result_ref, result_hbm, out_hbms, rows_ref, sems):
@@ -548,25 +709,26 @@
 ):
     nd = lax.axis_size("dp")
     count, sub, channels, places, local = plan.count, plan.sub, plan.channels, plan.places, plan.local
-    chunks = channels // 128
     f32, bf16 = jnp.float32, jnp.bfloat16
     rows = [part.reshape(1, channels) for part in (gain_coarse, bias_coarse, gain_fine, bias_fine)]
-    packed, weights_c, weights_f, columns, order = pl.pallas_call(
+    packed, acts, weights_c, weights_f, columns, order, fine_order, by_column, rows = pl.pallas_call(
         functools.partial(pack_kernel, plan),
         out_shape=(
-            shape_of((count, chunks * local + sub + 8, 128), bf16),
+            shape_of((count, plan.block_rows, 128), bf16),
+            shape_of((4 * local, channels), bf16),
             shape_of((28, sub, channels), bf16),
-            shape_of((27, sub, channels), bf16),
-            shape_of((4, sub, 128), f32),
+            shape_of((27, 2 * sub, channels), bf16),
+            shape_of((4, 2 * sub, 128), f32),
             shape_of((4 * plan.nr * local, 4 * plan.nr * local), bf16),
+            shape_of((4 * plan.nr * local, 4 * plan.nr * local), bf16),
+            shape_of((places, places + places // 2), bf16),
+            shape_of((4, 1, channels), f32),
         ),
         in_specs=in_hbm(9),
-        out_specs=tuple(in_vmem(5)),
+        out_specs=tuple(in_vmem(9)),
         scratch_shapes=[
             pltpu.VMEM((local, channels), bf16),
             pltpu.VMEM((local, channels), bf16),
-            pltpu.VMEM((4 * local, channels), bf16),
-            pltpu.VMEM((4, 1, channels), f32),
             pltpu.SemaphoreType.DMA((9,)),
         ],
         compiler_params=LIMIT,
@@ -581,31 +743,36 @@
     got = lax.all_to_all(packed, BLOCK, 0, 0)
     quartered, coarse_sums = pl.pallas_call(
         functools.partial(coarse_kernel, plan),
-        out_shape=(shape_of((count, sub, places), bf16), shape_of((2, 128), f32)),
-        in_specs=in_vmem(4),
+        out_shape=(shape_of((count, 2 * sub + sub // 2, 128), bf16), shape_of((2, 128), f32)),
+        in_specs=in_vmem(5),
         out_specs=tuple(in_vmem(2)),
         scratch_shapes=[pltpu.VMEM((places, channels), bf16), pltpu.VMEM((28 * sub, places), f32)],
         compiler_params=LIMIT,
-    )(got, weights_c, columns, order)
+    )(got, weights_c, columns, order, by_column)
     spread = lax.all_to_all(quartered, BLOCK, 0, 0)
     sent = pl.pallas_call(
         functools.partial(fine_kernel, plan),
         out_shape=shape_of((count, sub + 8, 128), bf16),
         in_specs=in_vmem(6),
         out_specs=in_vmem(1)[0],
-        scratch_shapes=[pltpu.VMEM((27 * sub, places), f32)],
+        scratch_shapes=[
+            pltpu.VMEM((channels, places // 2), bf16),
+            pltpu.VMEM((channels, places // 2), bf16),
+            pltpu.VMEM((54 * sub, places // 2), f32),
+            pltpu.VMEM((18 * sub, places // 2), f32),
+        ],
         compiler_params=LIMIT,
-    )(spread, got, columns, order, coarse_sums, weights_f)
+    )(spread, got, columns, fine_order, coarse_sums, weights_f)
     back = lax.all_to_all(sent, BLOCK, 0, 0)
     cells = nd * places
     fine_scale, coarse_scale = 1.0 / math.sqrt(4 * cells), 1.0 / math.sqrt(cells)
     out, sums = pl.pallas_call(
         functools.partial(spread_kernel, plan),
         out_shape=(pltpu.VMEM((4 * local, channels), bf16), shape_of((8, channels), f32)),
-        in_specs=in_vmem(1),
+        in_specs=in_vmem(3),
         out_specs=tuple(in_vmem(2)),
         compiler_params=LIMIT,
-    )(back)
+    )(back, acts, rows)
     both = lax.all_gather(sums, "dp")
     out, sums = pl.pallas_call(
         functools.partial(total_kernel, (fine_scale, fine_scale, coarse_scale, coarse_scale)),
@@ -620,23 +787,20 @@
 
 
 def solution(mesh):
-    def shards(*arrays):
-        sizes = (lax.axis_size("frames"), lax.axis_size("rows"))
-        plan = Plan(sizes, arrays[1].shape[1:], arrays[5].shape[1])
+    def function(*arrays):
+        local = [size // mesh.shape[axis] for size, axis in zip(arrays[1].shape, ("dp", "frames", "rows"))]
+        sizes = (mesh.shape["frames"], mesh.shape["rows"])
+        plan = Plan(sizes, (*local[1:], *arrays[1].shape[3:]), arrays[5].shape[1] // mesh.shape["rows"])
         if plan.fits:
-            return fast_shards(plan, *arrays)
-        return plain_shards(*arrays)
-
-    in_specs = (
-        P("dp", "frames", "rows", None, None),
-        P("dp", "frames", "rows", None, None),
-        P("dp", "frames", "rows", None, None),
-        P(),
-        P(),
-        P(None, "rows", None),
-        P(),
-        P(),
-        P(None, "rows", None),
-    )
-    out_specs = (P("dp", "frames", "rows", None, None), P(), P(), P(), P())
-    return jax.shard_map(shards, mesh=mesh, in_specs=in_specs, out_specs=out_specs, check_vma=False)
+            split = (mesh.shape["dp"], plan.nf // 2, 2, plan.nr)
+            used = jax.sharding.Mesh(mesh.devices.reshape(split), ("dp", "pairs", "member", "rows"))
+            shards, frames = functools.partial(fast_shards, plan), ("pairs", "member")
+        else:
+            used, shards, frames = mesh, plain_shards, "frames"
+        blocks, kernel = P("dp", frames, "rows", None, None), P(None, "rows", None)
+        in_specs = (blocks, blocks, blocks, P(), P(), kernel, P(), P(), kernel)
+        out_specs = (blocks, P(), P(), P(), P())
+        mapped = jax.shard_map(shards, mesh=used, in_specs=in_specs, out_specs=out_specs, check_vma=False)
+        return mapped(*arrays)
+
+    return function

time: 64.7 us -> 62.1 us (0.960)
  blocking collectives: 58.4 us -> 54.8 us
  Pallas kernels: 5.32 us -> 6.38 us
    all_to_all x1, blocking collectives: 17.5 us -> 13.6 us  [fast_shards(): spread = lax.all_to_all(quartered, BLOCK, 0, 0)]
where the time goes in v9:
time: 62.1 us; the launch traced here: 61.8 us
  blocking collectives  54.8 us (88%)
  Pallas kernels  6.38 us (10%)
  between operations  0.67 us (1%)
    all_to_all x1, blocking collectives, fast_shards(): got = lax.all_to_all(packed, BLOCK, 0, 0)  28.1 us
    all_to_all x1, blocking collectives, fast_shards(): spread = lax.all_to_all(quartered, BLOCK, 0, 0)  13.6 us
    all_to_all x1, blocking collectives, fast_shards(): back = lax.all_to_all(sent, BLOCK, 0, 0)  11.2 us
    pallas_call x1, Pallas kernels, fast_shards(): pl.pallas_call(functools.partial(pack_kernel, plan), out_shape=(shape_of(...  2.01 us
    all_gather x1, blocking collectives, fast_shards(): both = lax.all_gather(sums, 'dp')  1.83 us
    pallas_call x1, Pallas kernels, fast_shards(): pl.pallas_call(functools.partial(fine_kernel, plan), out_shape=shape_of((...  1.8 us
    pallas_call x1, Pallas kernels, fast_shards(): pl.pallas_call(functools.partial(coarse_kernel, plan), out_shape=(shape_o...  1.39 us

profile of v9, /device:TPU:0, one launch (start us, length us, event | category | flops | bytes accessed | tf_op | source)
XLA Modules:
  0.0 61.8 jit_solution(9898921570593802989)
XLA Ops:
  0.6 2.0 %shard_map.128 = (bf16[16,176,128]{2,1,0:T(8,128)(2,1)S(1)}, bf16[128,512]{1,0:T(8,128)(2,1)S(1)}, bf16[28,32,512]{2,1,0:T(8,128)(2,1)S(1)}, bf16[27,64,512]{2,1...) custom-call(bf16[32,512]{1,0:T(8,128)(2,1)} %bitcast.15, ...), custom_call_target="tpu_custom_call" | custom-call | tf_op jit(solution)/shard_map/pallas_call | solution.py:714
  2.7 28.1 %all_to_all.15.got_ref.acts_ref = bf16[16,176,128]{2,1,0:T(8,128)(2,1)S(1)} all-to-all(bf16[16,176,128]{2,1,0:T(8,128)(2,1)S(1)} %get-tuple-element.23), channel_id=1, replica_groups=mesh['dp'=2,'pairs'=2,'member'=2,'rows'=4] {'rows','pairs','member'}, dimensions={0} | all-to-all | bytes 1441792 | tf_op jit(solution)/shard_map/all_to_all | solution.py:743
  30.8 1.4 %shard_map.129 = (bf16[16,80,128]{2,1,0:T(8,128)(2,1)S(1)}, f32[2,128]{1,0:T(2,128)S(1)}) custom-call(bf16[16,176,128]{2,1,0:T(8,128)(2,1)S(1)} %all_to_all.15.got_ref.acts_ref, bf16[28,32,512]{2,1,0:T(8,128)(2,1)S(1)} %get-tuple-element.24.weights, f32[4,64,128]{2,1,0:T(8,128)S(1)} %get-tuple-element.25.columns, ...), custom_call_target="tpu_custom_call" | custom-call | tf_op jit(solution)/shard_map/pallas_call | solution.py:744
  32.2 13.6 %all_to_all.16.got_ref = bf16[16,80,128]{2,1,0:T(8,128)(2,1)S(1)} all-to-all(bf16[16,80,128]{2,1,0:T(8,128)(2,1)S(1)} %get-tuple-element.28), channel_id=1, replica_groups=mesh['dp'=2,'pairs'=2,'member'=2,'rows'=4] {'rows','pairs','member'}, dimensions={0} | all-to-all | bytes 655360 | tf_op jit(solution)/shard_map/all_to_all | solution.py:752
  45.8 1.8 %shard_map.130 = bf16[16,40,128]{2,1,0:T(8,128)(2,1)S(1)} custom-call(bf16[16,80,128]{2,1,0:T(8,128)(2,1)S(1)} %all_to_all.16.got_ref, bf16[16,176,128]{2,1,0:T(8,128)(2,1)S(1)} %all_to_all.15.got_ref.acts_ref, f32[4,64,128]{2,1,0:T(8,128)S(1)} %get-tuple-element.25.columns, bf16[512,512]{1,0:T(8,128)(2,1)S(1)} %get-tuple-element.29.order, ...), custom_call_target="tpu_custom_call" | custom-call | tf_op jit(solution)/shard_map/pallas_call | solution.py:753
  47.6 11.2 %all_to_all.17.got_ref = bf16[16,40,128]{2,1,0:T(8,128)(2,1)S(1)} all-to-all(bf16[16,40,128]{2,1,0:T(8,128)(2,1)S(1)} %shard_map.130), channel_id=1, replica_groups=mesh['dp'=2,'pairs'=2,'member'=2,'rows'=4] {'rows','pairs','member'}, dimensions={0} | all-to-all | bytes 327680 | tf_op jit(solution)/shard_map/all_to_all | solution.py:766
  58.8 0.5 shard_map.131
  59.3 1.8 %all-gather = f32[16,512]{1,0:T(8,128)S(1)} all-gather(f32[8,512]{1,0:T(8,128)S(1)} %get-tuple-element.34), channel_id=2, replica_groups=mesh['dp'=2,'pairs'=2,'member'=2,'rows'=4] {'dp'}, dimensions={0}, use_global_device_ids=true | all-gather | bytes 49152 | tf_op jit(solution)/shard_map/all_gather | solution.py:776
  61.1 0.7 %shard_map.132 = (bf16[128,512]{1,0:T(8,128)(2,1)}, f32[1,512]{1,0:T(1,128)}, f32[1,512]{1,0:T(1,128)}, f32[1,512]{1,0:T(1,128)}, f32[1,512]{1,0:T(1,128)}) custom-call(f32[2,8,512]{2,1,0:T(8,128)S(1)} %bitcast.13, bf16[128,512]{1,0:T(8,128)(2,1)S(1)} %get-tuple-element.35.result_ref), custom_call_target="tpu_custom_call" | custom-call | tf_op jit(solution)/shard_map/pallas_call | solution.py:777

commit v10 on v9

--- a/solution.py
+++ b/solution.py
@@ -207,7 +207,7 @@
 def pixel_order(plan, swapped):
     tl, hl, w = plan.tl, plan.hl, plan.w // 2
     size = 4 * plan.local
-    lane = lanes_at((size, size), 1)
+    lane = lanes_at((1, size), 1)
     j, i, t = lane % w, lane // w % hl, lane // (w * hl) % tl
     q, p = lane // (w * hl * tl) % 2, lane // (2 * w * hl * tl) % 2
     half = lane // (4 * w * hl * tl)
@@ -219,11 +219,10 @@
 
 def merged_order(nr, outer, tl, cells):
     size = nr * outer * tl * cells
-    a = lanes_at((size, size), 0)
-    cell, t = a % cells, a // cells % tl
-    o, dev = a // (cells * tl) % outer, a // (cells * tl * outer)
-    target = ((o * tl + t) * nr + dev) * cells + cell
-    return one_hot(lanes_at((size, size), 1) == target)
+    lane = lanes_at((1, size), 1)
+    cell, dev = lane % cells, lane // cells % nr
+    t, o = lane // (cells * nr) % tl, lane // (cells * nr * tl)
+    return one_hot(lanes_at((size, size), 0) == ((dev * outer + o) * tl + t) * cells + cell)
 
 
 def column_order(plan):
@@ -320,9 +319,10 @@
         self.places = self.frames * self.image
         self.group_width = self.channels // GROUPS
         self.chunks = self.channels // 128
-        self.acts_at = self.chunks * self.local
+        self.acts_at = self.chunks // 2 * self.local
         self.packed_at = self.acts_at + self.sub
-        self.stats_at = self.packed_at + 8
+        self.cot_at = self.packed_at + 8
+        self.stats_at = self.cot_at + 8
         self.block_rows = self.stats_at + 8
         self.fits = (
             self.sub == 32
@@ -381,16 +381,15 @@
 ):
     sub, chunks, local = plan.sub, plan.chunks, plan.local
     pair, member, r, base = own_place(plan)
-    own = pl.ds(pl.multiple_of((2 * pair + member) * sub, sub), sub)
+    depth = plan.channels // 2
+    half = pl.ds(pl.multiple_of(member * depth, depth), depth)
     both = pl.ds(pl.multiple_of(2 * pair * sub, 2 * sub), 2 * sub)
     copies = fetched(
         [(fine_hbm, fine_ref), (coarse_hbm, coarse_ref), (g_hbm, g_ref)]
         + [(row, rows.at[k]) for k, row in enumerate((gain_c, bias_c, gain_f, bias_f))]
-        + [(kernel_c.at[:, own, :], weights_c.at[pl.ds(0, 27)]), (kernel_f.at[:, both, :], weights_f)],
+        + [(kernel_c.at[:, both, half], weights_c), (kernel_f.at[:, both, :], weights_f)],
         sems,
     )
-    shape = (sub, plan.channels)
-    weights_c[27] = one_hot(lanes_at(shape, 1) == lanes_at(shape, 0) + base)
     order[...] = merged_order(plan.nr, 4, plan.tl, plan.cells)
     fine_order[...] = merged_order(plan.nr, 8, plan.tl, plan.cells // 2)
     by_column[...] = column_order(plan)
@@ -408,17 +407,20 @@
     copies[1].wait()
     quarters = [one_hot_dot(coarse_ref[...], place, ((0,), (0,))) for place in places]
     copies[2].wait()
+    cots = [one_hot_dot(g_ref[...], place, ((0,), (0,))) for place in places]
     low = lanes_at((sub, 128), 1) < 64
     for s_r in range(plan.nr):
         for s_f in range(plan.nf):
             dest, c = s_r * plan.nf + s_f, s_r * plan.slice_width + s_f * sub
-            for k in range(chunks):
-                out_ref[dest, k * local : (k + 1) * local, :] = g_ref[:, k * 128 : (k + 1) * 128]
             first, half = s_r * plan.slice_width + s_f // 2 * 2 * sub, s_f % 2
+            for k in range(chunks // 2):
+                at = (half * chunks // 2 + k) * 128
+                out_ref[dest, k * local : (k + 1) * local, :] = g_ref[:, at : at + 128]
             upper, lower = halves[half][first : first + sub], halves[1 - half][first + sub : first + 2 * sub]
             out_ref[dest, plan.acts_at : plan.packed_at, :] = jnp.where(low, upper, lower)
-            coarse = sum(quarters[k][c + 8 * k : c + 8 * k + 8] for k in range(4))
-            out_ref[dest, plan.packed_at : plan.stats_at, :] = coarse.astype(jnp.bfloat16)
+            for at, found in ((plan.packed_at, quarters), (plan.cot_at, cots)):
+                rows_of = sum(found[k][c + 8 * k : c + 8 * k + 8] for k in range(4))
+                out_ref[dest, at : at + 8, :] = rows_of.astype(jnp.bfloat16)
             out_ref[dest, plan.stats_at : plan.block_rows, :] = stats[:, s_r * 128 : (s_r + 1) * 128]
     for copy in copies[3:7]:
         copy.wait()
@@ -458,39 +460,52 @@
     return near + moved(middle, image, lane < places - image) + moved(far, 2 * image, lane < places - 2 * image)
 
 
-def coarse_kernel(plan, got_ref, weights, columns, order, by_column, out_ref, sums_ref, source, products):
+def coarse_kernel(
+    plan, got_ref, weights, columns, order, mine_ref, sent_ref, held_ref, inv_ref, source, products, conv_ref
+):
     sub, nr, nf, cells, tl, local = plan.sub, plan.nr, plan.nf, plan.cells, plan.tl, plan.local
+    wide, depth = 2 * sub, plan.channels // 2
+    _, member, _, _ = own_place(plan)
     for s_f in range(nf):
         for s_r in range(nr):
             for t in range(tl):
                 at = (s_f * tl + t) * plan.image + s_r * cells
-                for k in range(plan.chunks):
+                for k in range(plan.chunks // 2):
                     source[at : at + cells, k * 128 : (k + 1) * 128] = got_ref[
                         s_r * nf + s_f, k * local + t * cells : k * local + (t + 1) * cells, :
                     ]
-    products[...] = lax.dot_general(
-        weights[...].reshape(28 * sub, plan.channels),
-        source[...],
-        (((1,), (1,)), ((), ())),
-        preferred_element_type=jnp.float32,
-    )
-    packed = by_frame_device(plan, got_ref, plan.packed_at, 8)
-    merged = one_hot_dot(packed, order[...], ((1,), (0,)))
-    values = jnp.concatenate(in_places(plan, merged, 8), axis=0)
+    products[...] = one_hot_dot(weights[...].reshape(27 * wide, depth), source[...], ((1,), (1,)))
+    found = []
+    for at in (plan.packed_at, plan.cot_at):
+        merged = one_hot_dot(by_frame_device(plan, got_ref, at, 8), order[...], ((1,), (0,)))
+        found.append(jnp.concatenate(in_places(plan, merged, 8), axis=0))
+    values, cot = found
     gain, bias = columns[0][0:sub, 0:1], columns[1][0:sub, 0:1]
     entries = plan.places * plan.group_width
     mean, inv_std = statistics(total([values]), total([values * values]), entries, plan.group_width)
     (normed,), (slope,) = normalised([values], gain, bias, mean, inv_std)
+    held_ref[0], held_ref[1], held_ref[2] = normed, slope, cot
+    inv_ref[...] = jnp.broadcast_to(inv_std, (sub, 128))
     lane, has_left, has_right, has_up, has_down = plan.place_masks(plan.w)
     by_col = []
     for col in range(3):
         parts = [
-            frame_sum(products, [9 * depth + 3 * row + col for depth in range(3)], sub, lane, plan.places, plan.image)
+            frame_sum(products, [9 * k + 3 * row + col for k in range(3)], wide, lane, plan.places, plan.image)
             for row in range(3)
         ]
         by_col.append(parts[1] + moved(parts[0], plan.w, has_down) + moved(parts[2], -plan.w, has_up))
-    conv = by_col[1] + moved(by_col[0], 1, has_right) + moved(by_col[2], -1, has_left)
-    cot = products[pl.ds(27 * sub, sub), :]
+    conv_ref[...] = by_col[1] + moved(by_col[0], 1, has_right) + moved(by_col[2], -1, has_left)
+    mine_ref[...] = conv_ref[pl.ds(pl.multiple_of(member * sub, sub), sub), :]
+    sent_ref[...] = conv_ref[pl.ds(pl.multiple_of((1 - member) * sub, sub), sub), :].astype(jnp.bfloat16)
+
+
+def quarter_kernel(plan, mine_ref, both_ref, held_ref, inv_ref, columns, by_column, out_ref, sums_ref):
+    sub = plan.sub
+    _, member, _, _ = own_place(plan)
+    conv = mine_ref[...] + both_ref[1 - member].astype(jnp.float32)
+    normed, slope, cot = held_ref[0], held_ref[1], held_ref[2]
+    gain, inv_std = columns[0][0:sub, 0:1], inv_ref[:, 0:1]
+    entries = plan.places * plan.group_width
     pre = conv * slope
     one, two = total([pre]), total([pre * normed])
     group_one = in_groups(gain * one, plan.group_width) / entries
@@ -716,7 +731,7 @@
         out_shape=(
             shape_of((count, plan.block_rows, 128), bf16),
             shape_of((4 * local, channels), bf16),
-            shape_of((28, sub, channels), bf16),
+            shape_of((27, 2 * sub, channels // 2), bf16),
             shape_of((27, 2 * sub, channels), bf16),
             shape_of((4, 2 * sub, 128), f32),
             shape_of((4 * plan.nr * local, 4 * plan.nr * local), bf16),
@@ -741,14 +756,31 @@
         *[kept(row) for row in rows],
     )
     got = lax.all_to_all(packed, BLOCK, 0, 0)
+    mine, theirs, held, inv_std = pl.pallas_call(
+        functools.partial(coarse_kernel, plan),
+        out_shape=(
+            shape_of((sub, places), f32),
+            shape_of((sub, places), bf16),
+            shape_of((3, sub, places), f32),
+            shape_of((sub, 128), f32),
+        ),
+        in_specs=in_vmem(4),
+        out_specs=tuple(in_vmem(4)),
+        scratch_shapes=[
+            pltpu.VMEM((places, channels // 2), bf16),
+            pltpu.VMEM((54 * sub, places), f32),
+            pltpu.VMEM((2 * sub, places), f32),
+        ],
+        compiler_params=LIMIT,
+    )(got, weights_c, columns, order)
+    both = lax.all_gather(theirs, "member")
     quartered, coarse_sums = pl.pallas_call(
-        functools.partial(coarse_kernel, plan),
+        functools.partial(quarter_kernel, plan),
         out_shape=(shape_of((count, 2 * sub + sub // 2, 128), bf16), shape_of((2, 128), f32)),
-        in_specs=in_vmem(5),
+        in_specs=in_vmem(6),
         out_specs=tuple(in_vmem(2)),
-        scratch_shapes=[pltpu.VMEM((places, channels), bf16), pltpu.VMEM((28 * sub, places), f32)],
         compiler_params=LIMIT,
-    )(got, weights_c, columns, order, by_column)
+    )(mine, both, held, inv_std, columns, by_column)
     spread = lax.all_to_all(quartered, BLOCK, 0, 0)
     sent = pl.pallas_call(
         functools.partial(fine_kernel, plan),

time: 62.1 us -> 60.8 us (0.979)
  blocking collectives: 54.8 us -> 53.3 us
    all_to_all x1, blocking collectives: 28.1 us -> 22.6 us  [fast_shards(): got = lax.all_to_all(packed, BLOCK, 0, 0)]
    all_gather x0 -> x1, blocking collectives: none -> 4.59 us  [fast_shards(): both = lax.all_gather(theirs, 'member')]
    all_to_all x1, blocking collectives: 13.6 us -> 12.6 us  [fast_shards(): spread = lax.all_to_all(quartered, BLOCK, 0, 0)]
where the time goes in v10:
time: 60.8 us; the launch traced here: 60.5 us
  blocking collectives  53.3 us (88%)
  Pallas kernels  6.52 us (11%)
  between operations  0.68 us (1%)
    all_to_all x1, blocking collectives, fast_shards(): got = lax.all_to_all(packed, BLOCK, 0, 0)  22.6 us
    all_to_all x1, blocking collectives, fast_shards(): spread = lax.all_to_all(quartered, BLOCK, 0, 0)  12.6 us
    all_to_all x1, blocking collectives, fast_shards(): back = lax.all_to_all(sent, BLOCK, 0, 0)  11.7 us
    all_gather x1, blocking collectives, fast_shards(): both = lax.all_gather(theirs, 'member')  4.59 us
    pallas_call x1, Pallas kernels, fast_shards(): pl.pallas_call(functools.partial(pack_kernel, plan), out_shape=(shape_of(...  2.05 us
    all_gather x1, blocking collectives, fast_shards(): both = lax.all_gather(sums, 'dp')  1.83 us
    pallas_call x1, Pallas kernels, fast_shards(): pl.pallas_call(functools.partial(fine_kernel, plan), out_shape=shape_of((...  1.8 us

profile of v10, /device:TPU:0, one launch (start us, length us, event | category | flops | bytes accessed | tf_op | source)
XLA Modules:
  0.0 60.5 jit_solution(17926245511953691572)
XLA Ops:
  0.6 2.0 %shard_map.128 = (bf16[16,120,128]{2,1,0:T(8,128)(2,1)S(1)}, bf16[128,512]{1,0:T(8,128)(2,1)S(1)}, bf16[27,64,256]{2,1,0:T(8,128)(2,1)S(1)}, bf16[27,64,512]{2,1...) custom-call(bf16[32,512]{1,0:T(8,128)(2,1)} %bitcast.17, ...), custom_call_target="tpu_custom_call" | custom-call | tf_op jit(solution)/shard_map/pallas_call | solution.py:729
  2.7 22.6 %all_to_all.15.got_ref.acts_ref = bf16[16,120,128]{2,1,0:T(8,128)(2,1)S(1)} all-to-all(bf16[16,120,128]{2,1,0:T(8,128)(2,1)S(1)} %get-tuple-element.27), channel_id=1, replica_groups=mesh['dp'=2,'pairs'=2,'member'=2,'rows'=4] {'rows','pairs','member'}, dimensions={0} | all-to-all | bytes 983040 | tf_op jit(solution)/shard_map/all_to_all | solution.py:758
  25.3 1.1 %shard_map.129 = (f32[32,512]{1,0:T(8,128)S(1)}, bf16[32,512]{1,0:T(8,128)(2,1)S(1)}, f32[3,32,512]{2,1,0:T(8,128)S(1)}, f32[32,128]{1,0:T(8,128)S(1)}) custom-call(bf16[16,120,128]{2,1,0:T(8,128)(2,1)S(1)} %all_to_all.15.got_ref.acts_ref, bf16[27,64,256]{2,1,0:T(8,128)(2,1)S(1)} %get-tuple-element.28.weights, f32[4,64,128]{2,1,0:T(8,128)S(1)} %get-tuple-element.29.columns, ...), custom_call_target="tpu_custom_call" | custom-call | tf_op jit(solution)/shard_map/pallas_call | solution.py:759
  26.4 4.6 %all-gather = bf16[64,512]{1,0:T(8,128)(2,1)S(1)} all-gather(bf16[32,512]{1,0:T(8,128)(2,1)S(1)} %get-tuple-element.32), channel_id=2, replica_groups=mesh['dp'=2,'pairs'=2,'member'=2,'rows'=4] {'member'}, dimensions={0}, use_global_device_ids=true | all-gather | bytes 98304 | tf_op jit(solution)/shard_map/all_gather | solution.py:776
  31.0 0.4 shard_map.130
  31.4 12.6 %all_to_all.16.got_ref = bf16[16,80,128]{2,1,0:T(8,128)(2,1)S(1)} all-to-all(bf16[16,80,128]{2,1,0:T(8,128)(2,1)S(1)} %get-tuple-element.36), channel_id=1, replica_groups=mesh['dp'=2,'pairs'=2,'member'=2,'rows'=4] {'rows','pairs','member'}, dimensions={0} | all-to-all | bytes 655360 | tf_op jit(solution)/shard_map/all_to_all | solution.py:784
  44.0 1.8 %shard_map.131 = bf16[16,40,128]{2,1,0:T(8,128)(2,1)S(1)} custom-call(bf16[16,80,128]{2,1,0:T(8,128)(2,1)S(1)} %all_to_all.16.got_ref, bf16[16,120,128]{2,1,0:T(8,128)(2,1)S(1)} %all_to_all.15.got_ref.acts_ref, f32[4,64,128]{2,1,0:T(8,128)S(1)} %get-tuple-element.29.columns, bf16[512,512]{1,0:T(8,128)(2,1)S(1)} %get-tuple-element.37.order, ...), custom_call_target="tpu_custom_call" | custom-call | tf_op jit(solution)/shard_map/pallas_call | solution.py:785
  45.8 11.7 %all_to_all.17.got_ref = bf16[16,40,128]{2,1,0:T(8,128)(2,1)S(1)} all-to-all(bf16[16,40,128]{2,1,0:T(8,128)(2,1)S(1)} %shard_map.131), channel_id=1, replica_groups=mesh['dp'=2,'pairs'=2,'member'=2,'rows'=4] {'rows','pairs','member'}, dimensions={0} | all-to-all | bytes 327680 | tf_op jit(solution)/shard_map/all_to_all | solution.py:798
  57.5 0.5 shard_map.132
  58.0 1.8 %all-gather.1 = f32[16,512]{1,0:T(8,128)S(1)} all-gather(f32[8,512]{1,0:T(8,128)S(1)} %get-tuple-element.42), channel_id=3, replica_groups=mesh['dp'=2,'pairs'=2,'member'=2,'rows'=4] {'dp'}, dimensions={0}, use_global_device_ids=true | all-gather | bytes 49152 | tf_op jit(solution)/shard_map/all_gather | solution.py:808
  59.8 0.7 %shard_map.133 = (bf16[128,512]{1,0:T(8,128)(2,1)}, f32[1,512]{1,0:T(1,128)}, f32[1,512]{1,0:T(1,128)}, f32[1,512]{1,0:T(1,128)}, f32[1,512]{1,0:T(1,128)}) custom-call(f32[2,8,512]{2,1,0:T(8,128)S(1)} %bitcast.15, bf16[128,512]{1,0:T(8,128)(2,1)S(1)} %get-tuple-element.43.result_ref), custom_call_target="tpu_custom_call" | custom-call | tf_op jit(solution)/shard_map/pallas_call | solution.py:809

commit v11 on v10

--- a/solution.py
+++ b/solution.py
@@ -335,6 +335,9 @@
             and self.nf == 4
             and self.slice_width * self.nr == self.channels
         )
+
+    def holder(self, block):
+        return block % 2 * 2 + block // 2
 
     def place_masks(self, w):
         lane = lanes_at((1, self.places // self.w * w), 1)
@@ -387,27 +390,37 @@
     copies = fetched(
         [(fine_hbm, fine_ref), (coarse_hbm, coarse_ref), (g_hbm, g_ref)]
         + [(row, rows.at[k]) for k, row in enumerate((gain_c, bias_c, gain_f, bias_f))]
-        + [(kernel_c.at[:, both, half], weights_c), (kernel_f.at[:, both, :], weights_f)],
+        + [
+            pieces
+            for k in range(9)
+            for taps in (pl.ds(3 * k, 3),)
+            for pieces in (
+                (kernel_c.at[taps, both, half], weights_c.at[taps]),
+                (kernel_f.at[taps, both, :], weights_f.at[taps]),
+            )
+        ],
         sems,
     )
     order[...] = merged_order(plan.nr, 4, plan.tl, plan.cells)
     fine_order[...] = merged_order(plan.nr, 8, plan.tl, plan.cells // 2)
     by_column[...] = column_order(plan)
-    shape = (local, 128)
-    places = [one_hot(lanes_at(shape, 0) + k * local == lanes_at(shape, 1)) for k in range(4)]
-    orders = [pixel_order(plan, swapped) for swapped in (False, True)]
+    shape = (local, 4 * 128)
+    lane = lanes_at(shape, 1)
+    quarter = one_hot(lanes_at(shape, 0) + lane // 128 * local == lane % 128)
+    orders = jnp.concatenate([pixel_order(plan, swapped) for swapped in (False, True)], axis=1)
     copies[0].wait()
     acts = fine_ref[...]
-    halves = [one_hot_dot(acts, order_of, ((0,), (0,))).astype(jnp.bfloat16) for order_of in orders]
+    halves = one_hot_dot(acts, orders, ((0,), (0,))).astype(jnp.bfloat16)
+    halves = [halves[:, :128], halves[:, 128:]]
     values = acts.astype(jnp.float32)
     one = jnp.sum(values, axis=0, keepdims=True)
     two = jnp.sum(values * values, axis=0, keepdims=True)
     stats = terms(one, 3) + terms(two, 3)
     stats = jnp.concatenate(stats + [jnp.zeros_like(one)] * 2, axis=0).astype(jnp.bfloat16)
     copies[1].wait()
-    quarters = [one_hot_dot(coarse_ref[...], place, ((0,), (0,))) for place in places]
+    packed_acts = one_hot_dot(coarse_ref[...], quarter, ((0,), (0,)))
     copies[2].wait()
-    cots = [one_hot_dot(g_ref[...], place, ((0,), (0,))) for place in places]
+    packed_cot = one_hot_dot(g_ref[...], quarter, ((0,), (0,)))
     low = lanes_at((sub, 128), 1) < 64
     for s_r in range(plan.nr):
         for s_f in range(plan.nf):
@@ -418,8 +431,8 @@
                 out_ref[dest, k * local : (k + 1) * local, :] = g_ref[:, at : at + 128]
             upper, lower = halves[half][first : first + sub], halves[1 - half][first + sub : first + 2 * sub]
             out_ref[dest, plan.acts_at : plan.packed_at, :] = jnp.where(low, upper, lower)
-            for at, found in ((plan.packed_at, quarters), (plan.cot_at, cots)):
-                rows_of = sum(found[k][c + 8 * k : c + 8 * k + 8] for k in range(4))
+            for at, found in ((plan.packed_at, packed_acts), (plan.cot_at, packed_cot)):
+                rows_of = sum(found[c + 8 * k : c + 8 * k + 8, k * 128 : (k + 1) * 128] for k in range(4))
                 out_ref[dest, at : at + 8, :] = rows_of.astype(jnp.bfloat16)
             out_ref[dest, plan.stats_at : plan.block_rows, :] = stats[:, s_r * 128 : (s_r + 1) * 128]
     for copy in copies[3:7]:
@@ -436,7 +449,7 @@
     return jnp.concatenate(
         [
             jnp.concatenate(
-                [got_ref[r * plan.nf + f, at : at + height, :] for r in range(plan.nr)], axis=1
+                [got_ref[r * plan.nf + plan.holder(f), at : at + height, :] for r in range(plan.nr)], axis=1
             )
             for f in range(plan.nf)
         ],
@@ -455,11 +468,6 @@
     ]
 
 
-def frame_sum(products_ref, taps, sub, lane, places, image):
-    near, middle, far = [products_ref[pl.ds(tap * sub, sub), :] for tap in reversed(taps)]
-    return near + moved(middle, image, lane < places - image) + moved(far, 2 * image, lane < places - 2 * image)
-
-
 def coarse_kernel(
     plan, got_ref, weights, columns, order, mine_ref, sent_ref, held_ref, inv_ref, source, products, conv_ref
 ):
@@ -469,12 +477,20 @@
     for s_f in range(nf):
         for s_r in range(nr):
             for t in range(tl):
-                at = (s_f * tl + t) * plan.image + s_r * cells
+                at = (plan.holder(s_f) * tl + t) * plan.image + s_r * cells
                 for k in range(plan.chunks // 2):
                     source[at : at + cells, k * 128 : (k + 1) * 128] = got_ref[
                         s_r * nf + s_f, k * local + t * cells : k * local + (t + 1) * cells, :
                     ]
-    products[...] = one_hot_dot(weights[...].reshape(27 * wide, depth), source[...], ((1,), (1,)))
+    source[plan.places :, :] = jnp.zeros((2 * plan.image, depth), jnp.bfloat16)
+    products[...] = sum(
+        one_hot_dot(
+            weights[9 * k : 9 * k + 9].reshape(9 * wide, depth),
+            source[(2 - k) * plan.image : (2 - k) * plan.image + plan.places, :],
+            ((1,), (1,)),
+        )
+        for k in range(3)
+    )
     found = []
     for at in (plan.packed_at, plan.cot_at):
         merged = one_hot_dot(by_frame_device(plan, got_ref, at, 8), order[...], ((1,), (0,)))
@@ -489,10 +505,7 @@
     lane, has_left, has_right, has_up, has_down = plan.place_masks(plan.w)
     by_col = []
     for col in range(3):
-        parts = [
-            frame_sum(products, [9 * k + 3 * row + col for k in range(3)], wide, lane, plan.places, plan.image)
-            for row in range(3)
-        ]
+        parts = [products[pl.ds((3 * row + col) * wide, wide), :] for row in range(3)]
         by_col.append(parts[1] + moved(parts[0], plan.w, has_down) + moved(parts[2], -plan.w, has_up))
     conv_ref[...] = by_col[1] + moved(by_col[0], 1, has_right) + moved(by_col[2], -1, has_left)
     mine_ref[...] = conv_ref[pl.ds(pl.multiple_of(member * sub, sub), sub), :]
@@ -574,7 +587,6 @@
     places = lines * w
     for k in range(2):
         source[:, k * 128 : (k + 1) * 128] = got_ref[:, k * sub : (k + 1) * sub, :].reshape(plan.channels, 128)
-    products[...] = one_hot_dot(weights[...].reshape(27 * wide, plan.channels), source[...], ((1,), (0,)))
     packed = got_ref[:, wide : wide + sub // 2, :].reshape(plan.count * sub // 2, 128)
     shape = (128, places)
     beside = lanes_at(shape, 1) == lanes_at(shape, 0) % lines * w + (1 - member) * (w - 1)
@@ -585,8 +597,19 @@
             border[s * sub + k * (sub // 2) : s * sub + (k + 1) * (sub // 2), :] = found[
                 s * (sub // 2) : (s + 1) * (sub // 2)
             ]
-    facing = jnp.concatenate([weights[3 * k + 2 * member] for k in range(9)], axis=0)
-    beyond[...] = one_hot_dot(facing, border[...], ((1,), (0,)))
+    image, shape = plan.image // 2, (places, places)
+    sums, extras = 0.0, 0.0
+    for k in range(3):
+        here, beside = source[...], border[...]
+        if k < 2:
+            later = one_hot(lanes_at(shape, 0) == lanes_at(shape, 1) + (2 - k) * image)
+            here, beside = [one_hot_dot(part, later, ((1,), (0,))).astype(jnp.bfloat16) for part in (here, beside)]
+        sums = sums + one_hot_dot(
+            weights[9 * k : 9 * k + 9].reshape(9 * wide, plan.channels), here, ((1,), (0,))
+        )
+        facing = jnp.concatenate([weights[9 * k + 3 * row + 2 * member] for row in range(3)], axis=0)
+        extras = extras + one_hot_dot(facing, beside, ((1,), (0,)))
+    products[...], beyond[...] = sums, extras
     merged = one_hot_dot(by_frame_device(plan, acts_ref, plan.acts_at, sub), order[...], ((1,), (0,)))
     parts = halves_at(plan, merged)
     stats = sum(
@@ -599,15 +622,11 @@
     gain, bias = columns[2][:, 0:1], columns[3][:, 0:1]
     normed, slope = normalised(parts, gain, bias, mean, inv_std)
     lane, has_left, has_right, has_up, has_down = plan.place_masks(w)
-    image = plan.image // 2
     right, left = (1 - member).astype(jnp.float32), member.astype(jnp.float32)
     by_row = []
     for row in range(3):
-        a, b, c = [
-            frame_sum(products, [9 * depth + 3 * row + col for depth in range(3)], wide, lane, places, image)
-            for col in range(3)
-        ]
-        extra = frame_sum(beyond, [3 * depth + row for depth in range(3)], wide, lane, places, image)
+        a, b, c = [products[pl.ds((3 * row + col) * wide, wide), :] for col in range(3)]
+        extra = beyond[pl.ds(row * wide, wide), :]
         by_row.append(
             (a + b + moved(c, -1, has_left) + left * extra, moved(a, 1, has_right) + b + c + right * extra)
         )
@@ -629,8 +648,9 @@
     coded = jnp.concatenate(coded + [jnp.zeros_like(coarse)], axis=0).astype(jnp.bfloat16)
     for s_r in range(nr):
         for s_f in range(nf):
-            out_ref[s_r * nf + s_f, 0:sub, :] = sent[s_f * sub : (s_f + 1) * sub, s_r * 128 : (s_r + 1) * 128]
-            out_ref[s_r * nf + s_f, sub : sub + 8, :] = coded
+            dest = s_r * nf + plan.holder(s_f)
+            out_ref[dest, 0:sub, :] = sent[s_f * sub : (s_f + 1) * sub, s_r * 128 : (s_r + 1) * 128]
+            out_ref[dest, sub : sub + 8, :] = coded
 
 
 def spread_kernel(plan, got_ref, acts_ref, rows_ref, out_ref, sums_ref):
@@ -744,7 +764,7 @@
         scratch_shapes=[
             pltpu.VMEM((local, channels), bf16),
             pltpu.VMEM((local, channels), bf16),
-            pltpu.SemaphoreType.DMA((9,)),
+            pltpu.SemaphoreType.DMA((25,)),
         ],
         compiler_params=LIMIT,
     )(
@@ -767,8 +787,8 @@
         in_specs=in_vmem(4),
         out_specs=tuple(in_vmem(4)),
         scratch_shapes=[
-            pltpu.VMEM((places, channels // 2), bf16),
-            pltpu.VMEM((54 * sub, places), f32),
+            pltpu.VMEM((places + 2 * plan.image, channels // 2), bf16),
+            pltpu.VMEM((18 * sub, places), f32),
             pltpu.VMEM((2 * sub, places), f32),
         ],
         compiler_params=LIMIT,
@@ -790,8 +810,8 @@
         scratch_shapes=[
             pltpu.VMEM((channels, places // 2), bf16),
             pltpu.VMEM((channels, places // 2), bf16),
-            pltpu.VMEM((54 * sub, places // 2), f32),
             pltpu.VMEM((18 * sub, places // 2), f32),
+            pltpu.VMEM((6 * sub, places // 2), f32),
         ],
         compiler_params=LIMIT,
     )(spread, got, columns, fine_order, coarse_sums, weights_f)
@@ -824,9 +844,9 @@
         sizes = (mesh.shape["frames"], mesh.shape["rows"])
         plan = Plan(sizes, (*local[1:], *arrays[1].shape[3:]), arrays[5].shape[1] // mesh.shape["rows"])
         if plan.fits:
-            split = (mesh.shape["dp"], plan.nf // 2, 2, plan.nr)
-            used = jax.sharding.Mesh(mesh.devices.reshape(split), ("dp", "pairs", "member", "rows"))
-            shards, frames = functools.partial(fast_shards, plan), ("pairs", "member")
+            split = (mesh.shape["dp"], 2, plan.nf // 2, plan.nr)
+            used = jax.sharding.Mesh(mesh.devices.reshape(split), ("dp", "member", "pairs", "rows"))
+            shards, frames = functools.partial(fast_shards, plan), ("member", "pairs")
         else:
             used, shards, frames = mesh, plain_shards, "frames"
         blocks, kernel = P("dp", frames, "rows", None, None), P(None, "rows", None)

time: 60.8 us -> 61.1 us (level)
  no operation moved by 1% of the time
where the time goes in v11:
time: 61.1 us; the launch traced here: 60.8 us
  blocking collectives  53.3 us (87%)
  Pallas kernels  6.8 us (11%)
  between operations  0.67 us (1%)
    all_to_all x1, blocking collectives, fast_shards(): got = lax.all_to_all(packed, BLOCK, 0, 0)  22.6 us
    all_to_all x1, blocking collectives, fast_shards(): spread = lax.all_to_all(quartered, BLOCK, 0, 0)  12.6 us
    all_to_all x1, blocking collectives, fast_shards(): back = lax.all_to_all(sent, BLOCK, 0, 0)  11.7 us
    all_gather x1, blocking collectives, fast_shards(): both = lax.all_gather(theirs, 'member')  4.59 us
    pallas_call x1, Pallas kernels, fast_shards(): pl.pallas_call(functools.partial(pack_kernel, plan), out_shape=(shape_of(...  2.35 us
    pallas_call x1, Pallas kernels, fast_shards(): pl.pallas_call(functools.partial(fine_kernel, plan), out_shape=shape_of((...  1.94 us
    all_gather x1, blocking collectives, fast_shards(): both = lax.all_gather(sums, 'dp')  1.83 us

profile of v11, /device:TPU:0, one launch (start us, length us, event | category | flops | bytes accessed | tf_op | source)
XLA Modules:
  0.0 60.8 jit_solution(16170914004698271389)
XLA Ops:
  0.6 2.3 %shard_map.128 = (bf16[16,120,128]{2,1,0:T(8,128)(2,1)S(1)}, bf16[128,512]{1,0:T(8,128)(2,1)S(1)}, bf16[27,64,256]{2,1,0:T(8,128)(2,1)S(1)}, bf16[27,64,512]{2,1...) custom-call(bf16[32,512]{1,0:T(8,128)(2,1)} %bitcast.17, ...), custom_call_target="tpu_custom_call" | custom-call | tf_op jit(solution)/shard_map/pallas_call | solution.py:749
  3.0 22.6 %all_to_all.15.got_ref.acts_ref = bf16[16,120,128]{2,1,0:T(8,128)(2,1)S(1)} all-to-all(bf16[16,120,128]{2,1,0:T(8,128)(2,1)S(1)} %get-tuple-element.27), channel_id=1, replica_groups=mesh['dp'=2,'member'=2,'pairs'=2,'rows'=4] {'rows','pairs','member'}, dimensions={0} | all-to-all | bytes 983040 | tf_op jit(solution)/shard_map/all_to_all | solution.py:778
  25.6 0.9 %shard_map.129 = (f32[32,512]{1,0:T(8,128)S(1)}, bf16[32,512]{1,0:T(8,128)(2,1)S(1)}, f32[3,32,512]{2,1,0:T(8,128)S(1)}, f32[32,128]{1,0:T(8,128)S(1)}) custom-call(bf16[16,120,128]{2,1,0:T(8,128)(2,1)S(1)} %all_to_all.15.got_ref.acts_ref, bf16[27,64,256]{2,1,0:T(8,128)(2,1)S(1)} %get-tuple-element.28.weights, f32[4,64,128]{2,1,0:T(8,128)S(1)} %get-tuple-element.29.columns, ...), custom_call_target="tpu_custom_call" | custom-call | tf_op jit(solution)/shard_map/pallas_call | solution.py:779
  26.5 4.6 %all-gather = bf16[64,512]{1,0:T(8,128)(2,1)S(1)} all-gather(bf16[32,512]{1,0:T(8,128)(2,1)S(1)} %get-tuple-element.32), channel_id=2, replica_groups=mesh['dp'=2,'member'=2,'pairs'=2,'rows'=4] {'member'}, dimensions={0}, use_global_device_ids=true | all-gather | bytes 98304 | tf_op jit(solution)/shard_map/all_gather | solution.py:796
  31.1 0.4 shard_map.130
  31.5 12.6 %all_to_all.16.got_ref = bf16[16,80,128]{2,1,0:T(8,128)(2,1)S(1)} all-to-all(bf16[16,80,128]{2,1,0:T(8,128)(2,1)S(1)} %get-tuple-element.36), channel_id=1, replica_groups=mesh['dp'=2,'member'=2,'pairs'=2,'rows'=4] {'rows','pairs','member'}, dimensions={0} | all-to-all | bytes 655360 | tf_op jit(solution)/shard_map/all_to_all | solution.py:804
  44.2 1.9 %shard_map.131 = bf16[16,40,128]{2,1,0:T(8,128)(2,1)S(1)} custom-call(bf16[16,80,128]{2,1,0:T(8,128)(2,1)S(1)} %all_to_all.16.got_ref, bf16[16,120,128]{2,1,0:T(8,128)(2,1)S(1)} %all_to_all.15.got_ref.acts_ref, f32[4,64,128]{2,1,0:T(8,128)S(1)} %get-tuple-element.29.columns, bf16[512,512]{1,0:T(8,128)(2,1)S(1)} %get-tuple-element.37.order, ...), custom_call_target="tpu_custom_call" | custom-call | tf_op jit(solution)/shard_map/pallas_call | solution.py:805
  46.1 11.7 %all_to_all.17.got_ref = bf16[16,40,128]{2,1,0:T(8,128)(2,1)S(1)} all-to-all(bf16[16,40,128]{2,1,0:T(8,128)(2,1)S(1)} %shard_map.131), channel_id=1, replica_groups=mesh['dp'=2,'member'=2,'pairs'=2,'rows'=4] {'rows','pairs','member'}, dimensions={0} | all-to-all | bytes 327680 | tf_op jit(solution)/shard_map/all_to_all | solution.py:818
  57.8 0.5 shard_map.132
  58.3 1.8 %all-gather.1 = f32[16,512]{1,0:T(8,128)S(1)} all-gather(f32[8,512]{1,0:T(8,128)S(1)} %get-tuple-element.42), channel_id=3, replica_groups=mesh['dp'=2,'member'=2,'pairs'=2,'rows'=4] {'dp'}, dimensions={0}, use_global_device_ids=true | all-gather | bytes 49152 | tf_op jit(solution)/shard_map/all_gather | solution.py:828
  60.1 0.7 %shard_map.133 = (bf16[128,512]{1,0:T(8,128)(2,1)}, f32[1,512]{1,0:T(1,128)}, f32[1,512]{1,0:T(1,128)}, f32[1,512]{1,0:T(1,128)}, f32[1,512]{1,0:T(1,128)}) custom-call(f32[2,8,512]{2,1,0:T(8,128)S(1)} %bitcast.15, bf16[128,512]{1,0:T(8,128)(2,1)S(1)} %get-tuple-element.43.result_ref), custom_call_target="tpu_custom_call" | custom-call | tf_op jit(solution)/shard_map/pallas_call | solution.py:829

commit v12 on v10

--- a/solution.py
+++ b/solution.py
@@ -322,8 +322,7 @@
         self.acts_at = self.chunks // 2 * self.local
         self.packed_at = self.acts_at + self.sub
         self.cot_at = self.packed_at + 8
-        self.stats_at = self.cot_at + 8
-        self.block_rows = self.stats_at + 8
+        self.block_rows = self.cot_at + 8
         self.fits = (
             self.sub == 32
             and self.slice_width == 128
@@ -393,21 +392,18 @@
     order[...] = merged_order(plan.nr, 4, plan.tl, plan.cells)
     fine_order[...] = merged_order(plan.nr, 8, plan.tl, plan.cells // 2)
     by_column[...] = column_order(plan)
-    shape = (local, 128)
-    places = [one_hot(lanes_at(shape, 0) + k * local == lanes_at(shape, 1)) for k in range(4)]
-    orders = [pixel_order(plan, swapped) for swapped in (False, True)]
+    shape = (local, 4 * 128)
+    lane = lanes_at(shape, 1)
+    quarter = one_hot(lanes_at(shape, 0) + lane // 128 * local == lane % 128)
+    orders = jnp.concatenate([pixel_order(plan, swapped) for swapped in (False, True)], axis=1)
     copies[0].wait()
     acts = fine_ref[...]
-    halves = [one_hot_dot(acts, order_of, ((0,), (0,))).astype(jnp.bfloat16) for order_of in orders]
-    values = acts.astype(jnp.float32)
-    one = jnp.sum(values, axis=0, keepdims=True)
-    two = jnp.sum(values * values, axis=0, keepdims=True)
-    stats = terms(one, 3) + terms(two, 3)
-    stats = jnp.concatenate(stats + [jnp.zeros_like(one)] * 2, axis=0).astype(jnp.bfloat16)
+    halves = one_hot_dot(acts, orders, ((0,), (0,))).astype(jnp.bfloat16)
+    halves = [halves[:, :128], halves[:, 128:]]
     copies[1].wait()
-    quarters = [one_hot_dot(coarse_ref[...], place, ((0,), (0,))) for place in places]
+    packed_acts = one_hot_dot(coarse_ref[...], quarter, ((0,), (0,)))
     copies[2].wait()
-    cots = [one_hot_dot(g_ref[...], place, ((0,), (0,))) for place in places]
+    packed_cot = one_hot_dot(g_ref[...], quarter, ((0,), (0,)))
     low = lanes_at((sub, 128), 1) < 64
     for s_r in range(plan.nr):
         for s_f in range(plan.nf):
@@ -418,10 +414,9 @@
                 out_ref[dest, k * local : (k + 1) * local, :] = g_ref[:, at : at + 128]
             upper, lower = halves[half][first : first + sub], halves[1 - half][first + sub : first + 2 * sub]
             out_ref[dest, plan.acts_at : plan.packed_at, :] = jnp.where(low, upper, lower)
-            for at, found in ((plan.packed_at, quarters), (plan.cot_at, cots)):
-                rows_of = sum(found[k][c + 8 * k : c + 8 * k + 8] for k in range(4))
+            for at, found in ((plan.packed_at, packed_acts), (plan.cot_at, packed_cot)):
+                rows_of = sum(found[c + 8 * k : c + 8 * k + 8, k * 128 : (k + 1) * 128] for k in range(4))
                 out_ref[dest, at : at + 8, :] = rows_of.astype(jnp.bfloat16)
-            out_ref[dest, plan.stats_at : plan.block_rows, :] = stats[:, s_r * 128 : (s_r + 1) * 128]
     for copy in copies[3:7]:
         copy.wait()
     first = r * plan.slice_width + 2 * pair * sub
@@ -461,7 +456,20 @@
 
 
 def coarse_kernel(
-    plan, got_ref, weights, columns, order, mine_ref, sent_ref, held_ref, inv_ref, source, products, conv_ref
+    plan,
+    got_ref,
+    weights,
+    columns,
+    order,
+    fine_order,
+    mine_ref,
+    sent_ref,
+    held_ref,
+    inv_ref,
+    fine_ref,
+    source,
+    products,
+    conv_ref,
 ):
     sub, nr, nf, cells, tl, local = plan.sub, plan.nr, plan.nf, plan.cells, plan.tl, plan.local
     wide, depth = 2 * sub, plan.channels // 2
@@ -474,7 +482,22 @@
                     source[at : at + cells, k * 128 : (k + 1) * 128] = got_ref[
                         s_r * nf + s_f, k * local + t * cells : k * local + (t + 1) * cells, :
                     ]
-    products[...] = one_hot_dot(weights[...].reshape(27 * wide, depth), source[...], ((1,), (1,)))
+    source[plan.places :, :] = jnp.zeros((2 * plan.image, depth), jnp.bfloat16)
+    products[...] = sum(
+        one_hot_dot(
+            weights[9 * k : 9 * k + 9].reshape(9 * wide, depth),
+            source[(2 - k) * plan.image : (2 - k) * plan.image + plan.places, :],
+            ((1,), (1,)),
+        )
+        for k in range(3)
+    )
+    merged = one_hot_dot(by_frame_device(plan, got_ref, plan.acts_at, sub), fine_order[...], ((1,), (0,)))
+    parts = halves_at(plan, merged)
+    for pq in range(4):
+        fine_ref[pq] = parts[pq]
+    one, two = total(parts), total([part * part for part in parts])
+    stats = terms(as_row(one) + pltpu.roll(as_row(two), 64, 1), 3)
+    stats = jnp.concatenate(stats + [jnp.zeros_like(stats[0])] * 5, axis=0).astype(jnp.bfloat16)
     found = []
     for at in (plan.packed_at, plan.cot_at):
         merged = one_hot_dot(by_frame_device(plan, got_ref, at, 8), order[...], ((1,), (0,)))
@@ -489,20 +512,20 @@
     lane, has_left, has_right, has_up, has_down = plan.place_masks(plan.w)
     by_col = []
     for col in range(3):
-        parts = [
-            frame_sum(products, [9 * k + 3 * row + col for k in range(3)], wide, lane, plan.places, plan.image)
-            for row in range(3)
-        ]
+        parts = [products[pl.ds((3 * row + col) * wide, wide), :] for row in range(3)]
         by_col.append(parts[1] + moved(parts[0], plan.w, has_down) + moved(parts[2], -plan.w, has_up))
     conv_ref[...] = by_col[1] + moved(by_col[0], 1, has_right) + moved(by_col[2], -1, has_left)
     mine_ref[...] = conv_ref[pl.ds(pl.multiple_of(member * sub, sub), sub), :]
-    sent_ref[...] = conv_ref[pl.ds(pl.multiple_of((1 - member) * sub, sub), sub), :].astype(jnp.bfloat16)
+    theirs = conv_ref[pl.ds(pl.multiple_of((1 - member) * sub, sub), sub), :]
+    sent_ref[0:sub, :] = theirs.astype(jnp.bfloat16)
+    sent_ref[sub:, 0:128] = stats
+    sent_ref[sub:, 128:] = jnp.zeros((8, plan.places - 128), jnp.bfloat16)
 
 
 def quarter_kernel(plan, mine_ref, both_ref, held_ref, inv_ref, columns, by_column, out_ref, sums_ref):
     sub = plan.sub
     _, member, _, _ = own_place(plan)
-    conv = mine_ref[...] + both_ref[1 - member].astype(jnp.float32)
+    conv = mine_ref[...] + both_ref[1 - member, 0:sub, :].astype(jnp.float32)
     normed, slope, cot = held_ref[0], held_ref[1], held_ref[2]
     gain, inv_std = columns[0][0:sub, 0:1], inv_ref[:, 0:1]
     entries = plan.places * plan.group_width
@@ -565,7 +588,7 @@
 
 
 def fine_kernel(
-    plan, got_ref, acts_ref, columns, order, sums_ref, weights, out_ref, source, border, products, beyond
+    plan, got_ref, acts_ref, both_ref, columns, order, sums_ref, weights, out_ref, source, border, products, beyond
 ):
     sub, nr, nf, wide = plan.sub, plan.nr, plan.nf, 2 * plan.sub
     pair, member, r, _ = own_place(plan)
@@ -587,14 +610,11 @@
             ]
     facing = jnp.concatenate([weights[3 * k + 2 * member] for k in range(9)], axis=0)
     beyond[...] = one_hot_dot(facing, border[...], ((1,), (0,)))
-    merged = one_hot_dot(by_frame_device(plan, acts_ref, plan.acts_at, sub), order[...], ((1,), (0,)))
-    parts = halves_at(plan, merged)
-    stats = sum(
-        acts_ref[s, plan.stats_at : plan.block_rows, :].astype(jnp.float32) for s in range(plan.count)
-    )
+    parts = [acts_ref[pq] for pq in range(4)]
+    stats = sum(both_ref[k, sub : sub + 8, 0:128].astype(jnp.float32) for k in range(2))
+    stats = stats[0:1] + stats[1:2] + stats[2:3]
     entries = 4 * plan.places * plan.group_width
-    one = own_column(stats[0:1] + stats[1:2] + stats[2:3], pair * wide, wide)
-    two = own_column(stats[3:4] + stats[4:5] + stats[5:6], pair * wide, wide)
+    one, two = own_column(stats, 0, wide), own_column(stats, 64, wide)
     mean, inv_std = statistics(one, two, entries, plan.group_width)
     gain, bias = columns[2][:, 0:1], columns[3][:, 0:1]
     normed, slope = normalised(parts, gain, bias, mean, inv_std)
@@ -756,23 +776,24 @@
         *[kept(row) for row in rows],
     )
     got = lax.all_to_all(packed, BLOCK, 0, 0)
-    mine, theirs, held, inv_std = pl.pallas_call(
+    mine, theirs, held, inv_std, fine_acts = pl.pallas_call(
         functools.partial(coarse_kernel, plan),
         out_shape=(
             shape_of((sub, places), f32),
-            shape_of((sub, places), bf16),
+            shape_of((sub + 8, places), bf16),
             shape_of((3, sub, places), f32),
             shape_of((sub, 128), f32),
+            shape_of((4, 2 * sub, places // 2), f32),
         ),
-        in_specs=in_vmem(4),
-        out_specs=tuple(in_vmem(4)),
+        in_specs=in_vmem(5),
+        out_specs=tuple(in_vmem(5)),
         scratch_shapes=[
-            pltpu.VMEM((places, channels // 2), bf16),
-            pltpu.VMEM((54 * sub, places), f32),
+            pltpu.VMEM((places + 2 * plan.image, channels // 2), bf16),
+            pltpu.VMEM((18 * sub, places), f32),
             pltpu.VMEM((2 * sub, places), f32),
         ],
         compiler_params=LIMIT,
-    )(got, weights_c, columns, order)
+    )(got, weights_c, columns, order, fine_order)
     both = lax.all_gather(theirs, "member")
     quartered, coarse_sums = pl.pallas_call(
         functools.partial(quarter_kernel, plan),
@@ -785,7 +806,7 @@
     sent = pl.pallas_call(
         functools.partial(fine_kernel, plan),
         out_shape=shape_of((count, sub + 8, 128), bf16),
-        in_specs=in_vmem(6),
+        in_specs=in_vmem(7),
         out_specs=in_vmem(1)[0],
         scratch_shapes=[
             pltpu.VMEM((channels, places // 2), bf16),
@@ -794,7 +815,7 @@
             pltpu.VMEM((18 * sub, places // 2), f32),
         ],
         compiler_params=LIMIT,
-    )(spread, got, columns, fine_order, coarse_sums, weights_f)
+    )(spread, fine_acts, both, columns, fine_order, coarse_sums, weights_f)
     back = lax.all_to_all(sent, BLOCK, 0, 0)
     cells = nd * places
     fine_scale, coarse_scale = 1.0 / math.sqrt(4 * cells), 1.0 / math.sqrt(cells)

time: 60.8 us -> 60.3 us (level)
    all_to_all x1, blocking collectives: 22.6 us -> 22 us  [fast_shards(): got = lax.all_to_all(packed, BLOCK, 0, 0)]
where the time goes in v12:
time: 60.3 us; the launch traced here: 60 us
  blocking collectives  52.8 us (88%)
  Pallas kernels  6.59 us (11%)
  between operations  0.68 us (1%)
    all_to_all x1, blocking collectives, fast_shards(): got = lax.all_to_all(packed, BLOCK, 0, 0)  22 us
    all_to_all x1, blocking collectives, fast_shards(): spread = lax.all_to_all(quartered, BLOCK, 0, 0)  12.8 us
    all_to_all x1, blocking collectives, fast_shards(): back = lax.all_to_all(sent, BLOCK, 0, 0)  11.4 us
    all_gather x1, blocking collectives, fast_shards(): both = lax.all_gather(theirs, 'member')  4.68 us
    pallas_call x1, Pallas kernels, fast_shards(): pl.pallas_call(functools.partial(pack_kernel, plan), out_shape=(shape_of(...  2.17 us
    all_gather x1, blocking collectives, fast_shards(): both = lax.all_gather(sums, 'dp')  1.83 us
    pallas_call x1, Pallas kernels, fast_shards(): pl.pallas_call(functools.partial(fine_kernel, plan), out_shape=shape_of((...  1.68 us

profile of v12, /device:TPU:0, one launch (start us, length us, event | category | flops | bytes accessed | tf_op | source)
XLA Modules:
  0.0 60.0 jit_solution(14475068565690186374)
XLA Ops:
  0.6 2.2 %shard_map.128 = (bf16[16,112,128]{2,1,0:T(8,128)(2,1)S(1)}, bf16[128,512]{1,0:T(8,128)(2,1)S(1)}, bf16[27,64,256]{2,1,0:T(8,128)(2,1)S(1)}, bf16[27,64,512]{2,1...) custom-call(bf16[32,512]{1,0:T(8,128)(2,1)} %bitcast.18, ...), custom_call_target="tpu_custom_call" | custom-call | tf_op jit(solution)/shard_map/pallas_call | solution.py:749
  2.8 22.0 %all_to_all.15.got_ref = bf16[16,112,128]{2,1,0:T(8,128)(2,1)S(1)} all-to-all(bf16[16,112,128]{2,1,0:T(8,128)(2,1)S(1)} %get-tuple-element.28), channel_id=1, replica_groups=mesh['dp'=2,'pairs'=2,'member'=2,'rows'=4] {'rows','pairs','member'}, dimensions={0} | all-to-all | bytes 917504 | tf_op jit(solution)/shard_map/all_to_all | solution.py:778
  24.8 1.2 %shard_map.129 = (f32[32,512]{1,0:T(8,128)S(1)}, bf16[40,512]{1,0:T(8,128)(2,1)S(1)}, f32[3,32,512]{2,1,0:T(8,128)S(1)}, f32[32,128]{1,0:T(8,128)S(1)}, f32[4,64,256]{2,1,0:T(8,128)S(1)}) custom-call(bf16[16,112,128]{2,1,0:T(8,128)(2,1)S(1)} %all_to_all.15.got_ref, bf16[27,64,256]{2,1,0:T(8,128)(2,1)S(1)} %get-tuple-element.29.weights, ...), custom_call_target="tpu_custom_call" | custom-call | tf_op jit(solution)/shard_map/pallas_call | solution.py:779
  26.0 4.7 %all-gather = bf16[80,512]{1,0:T(8,128)(2,1)S(1)} all-gather(bf16[40,512]{1,0:T(8,128)(2,1)S(1)} %get-tuple-element.34), channel_id=2, replica_groups=mesh['dp'=2,'pairs'=2,'member'=2,'rows'=4] {'member'}, dimensions={0}, use_global_device_ids=true | all-gather | bytes 122880 | tf_op jit(solution)/shard_map/all_gather | solution.py:797
  30.6 0.4 shard_map.130
  31.0 12.8 %all_to_all.16.got_ref = bf16[16,80,128]{2,1,0:T(8,128)(2,1)S(1)} all-to-all(bf16[16,80,128]{2,1,0:T(8,128)(2,1)S(1)} %get-tuple-element.38), channel_id=1, replica_groups=mesh['dp'=2,'pairs'=2,'member'=2,'rows'=4] {'rows','pairs','member'}, dimensions={0} | all-to-all | bytes 655360 | tf_op jit(solution)/shard_map/all_to_all | solution.py:805
  43.9 1.7 %shard_map.131 = bf16[16,40,128]{2,1,0:T(8,128)(2,1)S(1)} custom-call(bf16[16,80,128]{2,1,0:T(8,128)(2,1)S(1)} %all_to_all.16.got_ref, f32[4,64,256]{2,1,0:T(8,128)S(1)} %get-tuple-element.39.acts_ref, bf16[2,40,512]{2,1,0:T(8,128)(2,1)S(1)} %bitcast.15, f32[4,64,128]{2,1,0:T(8,128)S(1)} %get-tuple-element.30.columns, ...), custom_call_target="tpu_custom_call" | custom-call | tf_op jit(solution)/shard_map/pallas_call | solution.py:806
  45.6 11.4 %all_to_all.17.got_ref = bf16[16,40,128]{2,1,0:T(8,128)(2,1)S(1)} all-to-all(bf16[16,40,128]{2,1,0:T(8,128)(2,1)S(1)} %shard_map.131), channel_id=1, replica_groups=mesh['dp'=2,'pairs'=2,'member'=2,'rows'=4] {'rows','pairs','member'}, dimensions={0} | all-to-all | bytes 327680 | tf_op jit(solution)/shard_map/all_to_all | solution.py:819
  57.0 0.5 shard_map.132
  57.5 1.8 %all-gather.1 = f32[16,512]{1,0:T(8,128)S(1)} all-gather(f32[8,512]{1,0:T(8,128)S(1)} %get-tuple-element.44), channel_id=3, replica_groups=mesh['dp'=2,'pairs'=2,'member'=2,'rows'=4] {'dp'}, dimensions={0}, use_global_device_ids=true | all-gather | bytes 49152 | tf_op jit(solution)/shard_map/all_gather | solution.py:829
  59.3 0.7 %shard_map.133 = (bf16[128,512]{1,0:T(8,128)(2,1)}, f32[1,512]{1,0:T(1,128)}, f32[1,512]{1,0:T(1,128)}, f32[1,512]{1,0:T(1,128)}, f32[1,512]{1,0:T(1,128)}) custom-call(f32[2,8,512]{2,1,0:T(8,128)S(1)} %bitcast.16, bf16[128,512]{1,0:T(8,128)(2,1)S(1)} %get-tuple-element.45.result_ref), custom_call_target="tpu_custom_call" | custom-call | tf_op jit(solution)/shard_map/pallas_call | solution.py:830

commit v13 on v12

--- a/solution.py
+++ b/solution.py
@@ -392,31 +392,32 @@
     order[...] = merged_order(plan.nr, 4, plan.tl, plan.cells)
     fine_order[...] = merged_order(plan.nr, 8, plan.tl, plan.cells // 2)
     by_column[...] = column_order(plan)
-    shape = (local, 4 * 128)
-    lane = lanes_at(shape, 1)
-    quarter = one_hot(lanes_at(shape, 0) + lane // 128 * local == lane % 128)
+    shape = (2 * local, 2 * 128)
+    lane = lanes_at((1, 2 * 128), 1)
+    repeated = one_hot(lanes_at(shape, 0) == lane % local + lane // 128 * local)
+    shape = (plan.channels, 128)
+    quarter = lanes_at(shape, 0) // 8 % 4 == lanes_at(shape, 1) // local
     orders = jnp.concatenate([pixel_order(plan, swapped) for swapped in (False, True)], axis=1)
     copies[0].wait()
     acts = fine_ref[...]
     halves = one_hot_dot(acts, orders, ((0,), (0,))).astype(jnp.bfloat16)
     halves = [halves[:, :128], halves[:, 128:]]
     copies[1].wait()
-    packed_acts = one_hot_dot(coarse_ref[...], quarter, ((0,), (0,)))
     copies[2].wait()
-    packed_cot = one_hot_dot(g_ref[...], quarter, ((0,), (0,)))
+    small = one_hot_dot(jnp.concatenate([coarse_ref[...], g_ref[...]], axis=0), repeated, ((0,), (0,)))
+    for k, at in enumerate((plan.packed_at, plan.cot_at)):
+        rows_of = jnp.where(quarter, small[:, k * 128 : (k + 1) * 128], 0.0).reshape(plan.count, 4, 8, 128)
+        out_ref[:, at : at + 8, :] = jnp.sum(rows_of, axis=1).astype(jnp.bfloat16)
     low = lanes_at((sub, 128), 1) < 64
     for s_r in range(plan.nr):
         for s_f in range(plan.nf):
-            dest, c = s_r * plan.nf + s_f, s_r * plan.slice_width + s_f * sub
+            dest = s_r * plan.nf + s_f
             first, half = s_r * plan.slice_width + s_f // 2 * 2 * sub, s_f % 2
             for k in range(chunks // 2):
                 at = (half * chunks // 2 + k) * 128
                 out_ref[dest, k * local : (k + 1) * local, :] = g_ref[:, at : at + 128]
             upper, lower = halves[half][first : first + sub], halves[1 - half][first + sub : first + 2 * sub]
             out_ref[dest, plan.acts_at : plan.packed_at, :] = jnp.where(low, upper, lower)
-            for at, found in ((plan.packed_at, packed_acts), (plan.cot_at, packed_cot)):
-                rows_of = sum(found[c + 8 * k : c + 8 * k + 8, k * 128 : (k + 1) * 128] for k in range(4))
-                out_ref[dest, at : at + 8, :] = rows_of.astype(jnp.bfloat16)
     for copy in copies[3:7]:
         copy.wait()
     first = r * plan.slice_width + 2 * pair * sub
@@ -448,11 +449,6 @@
         )
         for k in range(4)
     ]
-
-
-def frame_sum(products_ref, taps, sub, lane, places, image):
-    near, middle, far = [products_ref[pl.ds(tap * sub, sub), :] for tap in reversed(taps)]
-    return near + moved(middle, image, lane < places - image) + moved(far, 2 * image, lane < places - 2 * image)
 
 
 def coarse_kernel(
@@ -597,7 +593,6 @@
     places = lines * w
     for k in range(2):
         source[:, k * 128 : (k + 1) * 128] = got_ref[:, k * sub : (k + 1) * sub, :].reshape(plan.channels, 128)
-    products[...] = one_hot_dot(weights[...].reshape(27 * wide, plan.channels), source[...], ((1,), (0,)))
     packed = got_ref[:, wide : wide + sub // 2, :].reshape(plan.count * sub // 2, 128)
     shape = (128, places)
     beside = lanes_at(shape, 1) == lanes_at(shape, 0) % lines * w + (1 - member) * (w - 1)
@@ -608,8 +603,22 @@
             border[s * sub + k * (sub // 2) : s * sub + (k + 1) * (sub // 2), :] = found[
                 s * (sub // 2) : (s + 1) * (sub // 2)
             ]
-    facing = jnp.concatenate([weights[3 * k + 2 * member] for k in range(9)], axis=0)
-    beyond[...] = one_hot_dot(facing, border[...], ((1,), (0,)))
+    image = plan.image // 2
+    sums, extras = 0.0, 0.0
+    for k in (2, 1, 0):
+        here, beside = source[...], border[...]
+        if k < 2:
+            shift = (2 - k) * image
+            inside = lanes_at((1, places), 1) < places - shift
+            here, beside = [
+                jnp.where(inside, pltpu.roll(part, places - shift, 1), jnp.zeros_like(part)) for part in (here, beside)
+            ]
+        sums = sums + one_hot_dot(
+            weights[9 * k : 9 * k + 9].reshape(9 * wide, plan.channels), here, ((1,), (0,))
+        )
+        facing = jnp.concatenate([weights[9 * k + 3 * row + 2 * member] for row in range(3)], axis=0)
+        extras = extras + one_hot_dot(facing, beside, ((1,), (0,)))
+    products[...], beyond[...] = sums, extras
     parts = [acts_ref[pq] for pq in range(4)]
     stats = sum(both_ref[k, sub : sub + 8, 0:128].astype(jnp.float32) for k in range(2))
     stats = stats[0:1] + stats[1:2] + stats[2:3]
@@ -619,15 +628,11 @@
     gain, bias = columns[2][:, 0:1], columns[3][:, 0:1]
     normed, slope = normalised(parts, gain, bias, mean, inv_std)
     lane, has_left, has_right, has_up, has_down = plan.place_masks(w)
-    image = plan.image // 2
     right, left = (1 - member).astype(jnp.float32), member.astype(jnp.float32)
     by_row = []
     for row in range(3):
-        a, b, c = [
-            frame_sum(products, [9 * depth + 3 * row + col for depth in range(3)], wide, lane, places, image)
-            for col in range(3)
-        ]
-        extra = frame_sum(beyond, [3 * depth + row for depth in range(3)], wide, lane, places, image)
+        a, b, c = [products[pl.ds((3 * row + col) * wide, wide), :] for col in range(3)]
+        extra = beyond[pl.ds(row * wide, wide), :]
         by_row.append(
             (a + b + moved(c, -1, has_left) + left * extra, moved(a, 1, has_right) + b + c + right * extra)
         )
@@ -811,8 +816,8 @@
         scratch_shapes=[
             pltpu.VMEM((channels, places // 2), bf16),
             pltpu.VMEM((channels, places // 2), bf16),
-            pltpu.VMEM((54 * sub, places // 2), f32),
             pltpu.VMEM((18 * sub, places // 2), f32),
+            pltpu.VMEM((6 * sub, places // 2), f32),
         ],
         compiler_params=LIMIT,
     )(spread, fine_acts, both, columns, fine_order, coarse_sums, weights_f)

time: 60.3 us -> 60.1 us (level)
  no operation moved by 1% of the time
where the time goes in v13:
time: 60.1 us; the launch traced here: 59.8 us
  blocking collectives  52.8 us (88%)
  Pallas kernels  6.38 us (11%)
  between operations  0.68 us (1%)
    all_to_all x1, blocking collectives, fast_shards(): got = lax.all_to_all(packed, BLOCK, 0, 0)  22 us
    all_to_all x1, blocking collectives, fast_shards(): spread = lax.all_to_all(quartered, BLOCK, 0, 0)  12.8 us
    all_to_all x1, blocking collectives, fast_shards(): back = lax.all_to_all(sent, BLOCK, 0, 0)  11.4 us
    all_gather x1, blocking collectives, fast_shards(): both = lax.all_gather(theirs, 'member')  4.68 us
    pallas_call x1, Pallas kernels, fast_shards(): pl.pallas_call(functools.partial(pack_kernel, plan), out_shape=(shape_of(...  2.02 us
    all_gather x1, blocking collectives, fast_shards(): both = lax.all_gather(sums, 'dp')  1.83 us
    pallas_call x1, Pallas kernels, fast_shards(): pl.pallas_call(functools.partial(fine_kernel, plan), out_shape=shape_of((...  1.62 us

profile of v13, /device:TPU:0, one launch (start us, length us, event | category | flops | bytes accessed | tf_op | source)
XLA Modules:
  0.0 59.8 jit_solution(11815768965492802058)
XLA Ops:
  0.6 2.0 %shard_map.128 = (bf16[16,112,128]{2,1,0:T(8,128)(2,1)S(1)}, bf16[128,512]{1,0:T(8,128)(2,1)S(1)}, bf16[27,64,256]{2,1,0:T(8,128)(2,1)S(1)}, bf16[27,64,512]{2,1...) custom-call(bf16[32,512]{1,0:T(8,128)(2,1)} %bitcast.18, ...), custom_call_target="tpu_custom_call" | custom-call | tf_op jit(solution)/shard_map/pallas_call | solution.py:754
  2.7 22.0 %all_to_all.15.got_ref = bf16[16,112,128]{2,1,0:T(8,128)(2,1)S(1)} all-to-all(bf16[16,112,128]{2,1,0:T(8,128)(2,1)S(1)} %get-tuple-element.28), channel_id=1, replica_groups=mesh['dp'=2,'pairs'=2,'member'=2,'rows'=4] {'rows','pairs','member'}, dimensions={0} | all-to-all | bytes 917504 | tf_op jit(solution)/shard_map/all_to_all | solution.py:783
  24.6 1.2 %shard_map.129 = (f32[32,512]{1,0:T(8,128)S(1)}, bf16[40,512]{1,0:T(8,128)(2,1)S(1)}, f32[3,32,512]{2,1,0:T(8,128)S(1)}, f32[32,128]{1,0:T(8,128)S(1)}, f32[4,64,256]{2,1,0:T(8,128)S(1)}) custom-call(bf16[16,112,128]{2,1,0:T(8,128)(2,1)S(1)} %all_to_all.15.got_ref, bf16[27,64,256]{2,1,0:T(8,128)(2,1)S(1)} %get-tuple-element.29.weights, ...), custom_call_target="tpu_custom_call" | custom-call | tf_op jit(solution)/shard_map/pallas_call | solution.py:784
  25.8 4.7 %all-gather = bf16[80,512]{1,0:T(8,128)(2,1)S(1)} all-gather(bf16[40,512]{1,0:T(8,128)(2,1)S(1)} %get-tuple-element.34), channel_id=2, replica_groups=mesh['dp'=2,'pairs'=2,'member'=2,'rows'=4] {'member'}, dimensions={0}, use_global_device_ids=true | all-gather | bytes 122880 | tf_op jit(solution)/shard_map/all_gather | solution.py:802
  30.5 0.4 shard_map.130
  30.9 12.8 %all_to_all.16.got_ref = bf16[16,80,128]{2,1,0:T(8,128)(2,1)S(1)} all-to-all(bf16[16,80,128]{2,1,0:T(8,128)(2,1)S(1)} %get-tuple-element.38), channel_id=1, replica_groups=mesh['dp'=2,'pairs'=2,'member'=2,'rows'=4] {'rows','pairs','member'}, dimensions={0} | all-to-all | bytes 655360 | tf_op jit(solution)/shard_map/all_to_all | solution.py:810
  43.7 1.6 %shard_map.131 = bf16[16,40,128]{2,1,0:T(8,128)(2,1)S(1)} custom-call(bf16[16,80,128]{2,1,0:T(8,128)(2,1)S(1)} %all_to_all.16.got_ref, f32[4,64,256]{2,1,0:T(8,128)S(1)} %get-tuple-element.39.acts_ref, bf16[2,40,512]{2,1,0:T(8,128)(2,1)S(1)} %bitcast.15, f32[4,64,128]{2,1,0:T(8,128)S(1)} %get-tuple-element.30.columns, ...), custom_call_target="tpu_custom_call" | custom-call | tf_op jit(solution)/shard_map/pallas_call | solution.py:811
  45.4 11.4 %all_to_all.17.got_ref = bf16[16,40,128]{2,1,0:T(8,128)(2,1)S(1)} all-to-all(bf16[16,40,128]{2,1,0:T(8,128)(2,1)S(1)} %shard_map.131), channel_id=1, replica_groups=mesh['dp'=2,'pairs'=2,'member'=2,'rows'=4] {'rows','pairs','member'}, dimensions={0} | all-to-all | bytes 327680 | tf_op jit(solution)/shard_map/all_to_all | solution.py:824
  56.8 0.5 shard_map.132
  57.3 1.8 %all-gather.1 = f32[16,512]{1,0:T(8,128)S(1)} all-gather(f32[8,512]{1,0:T(8,128)S(1)} %get-tuple-element.44), channel_id=3, replica_groups=mesh['dp'=2,'pairs'=2,'member'=2,'rows'=4] {'dp'}, dimensions={0}, use_global_device_ids=true | all-gather | bytes 49152 | tf_op jit(solution)/shard_map/all_gather | solution.py:834
  59.1 0.7 %shard_map.133 = (bf16[128,512]{1,0:T(8,128)(2,1)}, f32[1,512]{1,0:T(1,128)}, f32[1,512]{1,0:T(1,128)}, f32[1,512]{1,0:T(1,128)}, f32[1,512]{1,0:T(1,128)}) custom-call(f32[2,8,512]{2,1,0:T(8,128)S(1)} %bitcast.16, bf16[128,512]{1,0:T(8,128)(2,1)S(1)} %get-tuple-element.45.result_ref), custom_call_target="tpu_custom_call" | custom-call | tf_op jit(solution)/shard_map/pallas_call | solution.py:835

commit v14 on v13

--- a/solution.py
+++ b/solution.py
@@ -344,8 +344,12 @@
 
 def fetched(pairs, sems):
     copies = [pltpu.make_async_copy(src, dst, sems.at[k]) for k, (src, dst) in enumerate(pairs)]
-    for copy in copies:
-        copy.start()
+
+    @pl.when(lax.axis_index("rows") >= 0)
+    def _():
+        for copy in copies:
+            copy.start()
+
     return copies
 
 
@@ -386,7 +390,7 @@
     copies = fetched(
         [(fine_hbm, fine_ref), (coarse_hbm, coarse_ref), (g_hbm, g_ref)]
         + [(row, rows.at[k]) for k, row in enumerate((gain_c, bias_c, gain_f, bias_f))]
-        + [(kernel_c.at[:, both, half], weights_c), (kernel_f.at[:, both, :], weights_f)],
+        + [(kernel_c.at[:, both, half], weights_c), (kernel_f.at[pl.ds(18, 9), both, :], weights_f)],
         sems,
     )
     order[...] = merged_order(plan.nr, 4, plan.tl, plan.cells)
@@ -458,18 +462,23 @@
     columns,
     order,
     fine_order,
+    kernel_f,
     mine_ref,
     sent_ref,
     held_ref,
     inv_ref,
     fine_ref,
+    weights_f,
     source,
     products,
     conv_ref,
+    sems,
 ):
     sub, nr, nf, cells, tl, local = plan.sub, plan.nr, plan.nf, plan.cells, plan.tl, plan.local
     wide, depth = 2 * sub, plan.channels // 2
-    _, member, _, _ = own_place(plan)
+    pair, member, _, _ = own_place(plan)
+    both = pl.ds(pl.multiple_of(pair * wide, wide), wide)
+    copies = fetched([(kernel_f.at[pl.ds(0, 18), both, :], weights_f)], sems)
     for s_f in range(nf):
         for s_r in range(nr):
             for t in range(tl):
@@ -516,6 +525,8 @@
     sent_ref[0:sub, :] = theirs.astype(jnp.bfloat16)
     sent_ref[sub:, 0:128] = stats
     sent_ref[sub:, 128:] = jnp.zeros((8, plan.places - 128), jnp.bfloat16)
+    for copy in copies:
+        copy.wait()
 
 
 def quarter_kernel(plan, mine_ref, both_ref, held_ref, inv_ref, columns, by_column, out_ref, sums_ref):
@@ -584,7 +595,7 @@
 
 
 def fine_kernel(
-    plan, got_ref, acts_ref, both_ref, columns, order, sums_ref, weights, out_ref, source, border, products, beyond
+    plan, got_ref, acts_ref, both_ref, columns, order, sums_ref, late, early, out_ref, source, border, products, beyond
 ):
     sub, nr, nf, wide = plan.sub, plan.nr, plan.nf, 2 * plan.sub
     pair, member, r, _ = own_place(plan)
@@ -613,10 +624,11 @@
             here, beside = [
                 jnp.where(inside, pltpu.roll(part, places - shift, 1), jnp.zeros_like(part)) for part in (here, beside)
             ]
+        weights, first = (late, 0) if k == 2 else (early, 9 * k)
         sums = sums + one_hot_dot(
-            weights[9 * k : 9 * k + 9].reshape(9 * wide, plan.channels), here, ((1,), (0,))
+            weights[first : first + 9].reshape(9 * wide, plan.channels), here, ((1,), (0,))
         )
-        facing = jnp.concatenate([weights[9 * k + 3 * row + 2 * member] for row in range(3)], axis=0)
+        facing = jnp.concatenate([weights[first + 3 * row + 2 * member] for row in range(3)], axis=0)
         extras = extras + one_hot_dot(facing, beside, ((1,), (0,)))
     products[...], beyond[...] = sums, extras
     parts = [acts_ref[pq] for pq in range(4)]
@@ -757,7 +769,7 @@
             shape_of((count, plan.block_rows, 128), bf16),
             shape_of((4 * local, channels), bf16),
             shape_of((27, 2 * sub, channels // 2), bf16),
-            shape_of((27, 2 * sub, channels), bf16),
+            shape_of((9, 2 * sub, channels), bf16),
             shape_of((4, 2 * sub, 128), f32),
             shape_of((4 * plan.nr * local, 4 * plan.nr * local), bf16),
             shape_of((4 * plan.nr * local, 4 * plan.nr * local), bf16),
@@ -781,7 +793,7 @@
         *[kept(row) for row in rows],
     )
     got = lax.all_to_all(packed, BLOCK, 0, 0)
-    mine, theirs, held, inv_std, fine_acts = pl.pallas_call(
+    mine, theirs, held, inv_std, fine_acts, early_f = pl.pallas_call(
         functools.partial(coarse_kernel, plan),
         out_shape=(
             shape_of((sub, places), f32),
@@ -789,16 +801,18 @@
             shape_of((3, sub, places), f32),
             shape_of((sub, 128), f32),
             shape_of((4, 2 * sub, places // 2), f32),
+            shape_of((18, 2 * sub, channels), bf16),
         ),
-        in_specs=in_vmem(5),
-        out_specs=tuple(in_vmem(5)),
+        in_specs=in_vmem(5) + in_hbm(1),
+        out_specs=tuple(in_vmem(6)),
         scratch_shapes=[
             pltpu.VMEM((places + 2 * plan.image, channels // 2), bf16),
             pltpu.VMEM((18 * sub, places), f32),
             pltpu.VMEM((2 * sub, places), f32),
+            pltpu.SemaphoreType.DMA((1,)),
         ],
         compiler_params=LIMIT,
-    )(got, weights_c, columns, order, fine_order)
+    )(got, weights_c, columns, order, fine_order, kept(kernel_fine))
     both = lax.all_gather(theirs, "member")
     quartered, coarse_sums = pl.pallas_call(
         functools.partial(quarter_kernel, plan),
@@ -811,7 +825,7 @@
     sent = pl.pallas_call(
         functools.partial(fine_kernel, plan),
         out_shape=shape_of((count, sub + 8, 128), bf16),
-        in_specs=in_vmem(7),
+        in_specs=in_vmem(8),
         out_specs=in_vmem(1)[0],
         scratch_shapes=[
             pltpu.VMEM((channels, places // 2), bf16),
@@ -820,7 +834,7 @@
             pltpu.VMEM((6 * sub, places // 2), f32),
         ],
         compiler_params=LIMIT,
-    )(spread, fine_acts, both, columns, fine_order, coarse_sums, weights_f)
+    )(spread, fine_acts, both, columns, fine_order, coarse_sums, weights_f, early_f)
     back = lax.all_to_all(sent, BLOCK, 0, 0)
     cells = nd * places
     fine_scale, coarse_scale = 1.0 / math.sqrt(4 * cells), 1.0 / math.sqrt(cells)

time: 60.1 us -> 61.1 us (1.017)
  Pallas kernels: 6.38 us -> 7.33 us
    pallas_call x1, Pallas kernels: 1.16 us -> 2.35 us  [fast_shards(): pl.pallas_call(functools.partial(coarse_kernel, plan), out_shape=(shape_o...]
where the time goes in v14:
time: 61.1 us; the launch traced here: 60.8 us
  blocking collectives  52.8 us (86%)
  Pallas kernels  7.33 us (12%)
  between operations  0.68 us (1%)
    all_to_all x1, blocking collectives, fast_shards(): got = lax.all_to_all(packed, BLOCK, 0, 0)  22 us
    all_to_all x1, blocking collectives, fast_shards(): spread = lax.all_to_all(quartered, BLOCK, 0, 0)  12.8 us
    all_to_all x1, blocking collectives, fast_shards(): back = lax.all_to_all(sent, BLOCK, 0, 0)  11.4 us
    all_gather x1, blocking collectives, fast_shards(): both = lax.all_gather(theirs, 'member')  4.68 us
    pallas_call x1, Pallas kernels, fast_shards(): pl.pallas_call(functools.partial(coarse_kernel, plan), out_shape=(shape_o...  2.35 us
    all_gather x1, blocking collectives, fast_shards(): both = lax.all_gather(sums, 'dp')  1.83 us
    pallas_call x1, Pallas kernels, fast_shards(): pl.pallas_call(functools.partial(pack_kernel, plan), out_shape=(shape_of(...  1.78 us
    pallas_call x1, Pallas kernels, fast_shards(): pl.pallas_call(functools.partial(fine_kernel, plan), out_shape=shape_of((...  1.61 us

profile of v14, /device:TPU:0, one launch (start us, length us, event | category | flops | bytes accessed | tf_op | source)
XLA Modules:
  0.0 60.8 jit_solution(9135172251625472614)
XLA Ops:
  0.6 1.8 %shard_map.128 = (bf16[16,112,128]{2,1,0:T(8,128)(2,1)S(1)}, bf16[128,512]{1,0:T(8,128)(2,1)S(1)}, bf16[27,64,256]{2,1,0:T(8,128)(2,1)S(1)}, bf16[9,64,512]{2,1,...) custom-call(bf16[32,512]{1,0:T(8,128)(2,1)} %bitcast.18, ...), custom_call_target="tpu_custom_call" | custom-call | tf_op jit(solution)/shard_map/pallas_call | solution.py:766
  2.4 22.0 %all_to_all.15.got_ref = bf16[16,112,128]{2,1,0:T(8,128)(2,1)S(1)} all-to-all(bf16[16,112,128]{2,1,0:T(8,128)(2,1)S(1)} %get-tuple-element.29), channel_id=1, replica_groups=mesh['dp'=2,'pairs'=2,'member'=2,'rows'=4] {'rows','pairs','member'}, dimensions={0} | all-to-all | bytes 917504 | tf_op jit(solution)/shard_map/all_to_all | solution.py:795
  24.4 2.3 %shard_map.129 = (f32[32,512]{1,0:T(8,128)S(1)}, bf16[40,512]{1,0:T(8,128)(2,1)S(1)}, f32[3,32,512]{2,1,0:T(8,128)S(1)}, f32[32,128]{1,0:T(8,128)S(1)}, f32[4,64...) custom-call(bf16[16,112,128]{2,1,0:T(8,128)(2,1)S(1)} %all_to_all.15.got_ref, ...), custom_call_target="tpu_custom_call" | custom-call | tf_op jit(solution)/shard_map/pallas_call | solution.py:796
  26.8 4.7 %all-gather = bf16[80,512]{1,0:T(8,128)(2,1)S(1)} all-gather(bf16[40,512]{1,0:T(8,128)(2,1)S(1)} %get-tuple-element.35), channel_id=2, replica_groups=mesh['dp'=2,'pairs'=2,'member'=2,'rows'=4] {'member'}, dimensions={0}, use_global_device_ids=true | all-gather | bytes 122880 | tf_op jit(solution)/shard_map/all_gather | solution.py:816
  31.4 0.4 shard_map.130
  31.8 12.8 %all_to_all.16.got_ref = bf16[16,80,128]{2,1,0:T(8,128)(2,1)S(1)} all-to-all(bf16[16,80,128]{2,1,0:T(8,128)(2,1)S(1)} %get-tuple-element.39), channel_id=1, replica_groups=mesh['dp'=2,'pairs'=2,'member'=2,'rows'=4] {'rows','pairs','member'}, dimensions={0} | all-to-all | bytes 655360 | tf_op jit(solution)/shard_map/all_to_all | solution.py:824
  44.7 1.6 %shard_map.131 = bf16[16,40,128]{2,1,0:T(8,128)(2,1)S(1)} custom-call(bf16[16,80,128]{2,1,0:T(8,128)(2,1)S(1)} %all_to_all.16.got_ref, f32[4,64,256]{2,1,0:T(8,128)S(1)} %get-tuple-element.40.acts_ref, bf16[2,40,512]{2,1,0:T(8,128)(2,1)S(1)} %bitcast.15, f32[4,64,128]{2,1,0:T(8,128)S(1)} %get-tuple-element.31.columns, ...), custom_call_target="tpu_custom_call" | custom-call | tf_op jit(solution)/shard_map/pallas_call | solution.py:825
  46.3 11.4 %all_to_all.17.got_ref = bf16[16,40,128]{2,1,0:T(8,128)(2,1)S(1)} all-to-all(bf16[16,40,128]{2,1,0:T(8,128)(2,1)S(1)} %shard_map.131), channel_id=1, replica_groups=mesh['dp'=2,'pairs'=2,'member'=2,'rows'=4] {'rows','pairs','member'}, dimensions={0} | all-to-all | bytes 327680 | tf_op jit(solution)/shard_map/all_to_all | solution.py:838
  57.7 0.5 shard_map.132
  58.2 1.8 %all-gather.1 = f32[16,512]{1,0:T(8,128)S(1)} all-gather(f32[8,512]{1,0:T(8,128)S(1)} %get-tuple-element.46), channel_id=3, replica_groups=mesh['dp'=2,'pairs'=2,'member'=2,'rows'=4] {'dp'}, dimensions={0}, use_global_device_ids=true | all-gather | bytes 49152 | tf_op jit(solution)/shard_map/all_gather | solution.py:848
  60.1 0.7 %shard_map.133 = (bf16[128,512]{1,0:T(8,128)(2,1)}, f32[1,512]{1,0:T(1,128)}, f32[1,512]{1,0:T(1,128)}, f32[1,512]{1,0:T(1,128)}, f32[1,512]{1,0:T(1,128)}) custom-call(f32[2,8,512]{2,1,0:T(8,128)S(1)} %bitcast.16, bf16[128,512]{1,0:T(8,128)(2,1)S(1)} %get-tuple-element.47.result_ref), custom_call_target="tpu_custom_call" | custom-call | tf_op jit(solution)/shard_map/pallas_call | solution.py:849

commit v15 on v13

--- a/solution.py
+++ b/solution.py
@@ -359,16 +359,12 @@
     g_hbm,
     coarse_hbm,
     fine_hbm,
-    kernel_c,
-    kernel_f,
     gain_c,
     bias_c,
     gain_f,
     bias_f,
     out_ref,
     fine_ref,
-    weights_c,
-    weights_f,
     columns,
     order,
     fine_order,
@@ -380,13 +376,9 @@
 ):
     sub, chunks, local = plan.sub, plan.chunks, plan.local
     pair, member, r, base = own_place(plan)
-    depth = plan.channels // 2
-    half = pl.ds(pl.multiple_of(member * depth, depth), depth)
-    both = pl.ds(pl.multiple_of(2 * pair * sub, 2 * sub), 2 * sub)
     copies = fetched(
         [(fine_hbm, fine_ref), (coarse_hbm, coarse_ref), (g_hbm, g_ref)]
-        + [(row, rows.at[k]) for k, row in enumerate((gain_c, bias_c, gain_f, bias_f))]
-        + [(kernel_c.at[:, both, half], weights_c), (kernel_f.at[:, both, :], weights_f)],
+        + [(row, rows.at[k]) for k, row in enumerate((gain_c, bias_c, gain_f, bias_f))],
         sems,
     )
     order[...] = merged_order(plan.nr, 4, plan.tl, plan.cells)
@@ -424,8 +416,6 @@
     for k in range(2):
         columns[k, 0:sub, :] = jnp.broadcast_to(own_column(rows[k], base, sub), (sub, 128))
         columns[2 + k] = jnp.broadcast_to(own_column(rows[2 + k], first, 2 * sub), (2 * sub, 128))
-    for copy in copies[7:]:
-        copy.wait()
 
 
 def by_frame_device(plan, got_ref, at, height):
@@ -469,7 +459,9 @@
 ):
     sub, nr, nf, cells, tl, local = plan.sub, plan.nr, plan.nf, plan.cells, plan.tl, plan.local
     wide, depth = 2 * sub, plan.channels // 2
-    _, member, _, _ = own_place(plan)
+    pair, member, _, _ = own_place(plan)
+    both = pl.ds(pl.multiple_of(pair * wide, wide), wide)
+    half = pl.ds(pl.multiple_of(member * depth, depth), depth)
     for s_f in range(nf):
         for s_r in range(nr):
             for t in range(tl):
@@ -481,7 +473,7 @@
     source[plan.places :, :] = jnp.zeros((2 * plan.image, depth), jnp.bfloat16)
     products[...] = sum(
         one_hot_dot(
-            weights[9 * k : 9 * k + 9].reshape(9 * wide, depth),
+            weights[9 * k : 9 * k + 9, both, half].reshape(9 * wide, depth),
             source[(2 - k) * plan.image : (2 - k) * plan.image + plan.places, :],
             ((1,), (1,)),
         )
@@ -588,6 +580,7 @@
 ):
     sub, nr, nf, wide = plan.sub, plan.nr, plan.nf, 2 * plan.sub
     pair, member, r, _ = own_place(plan)
+    both = pl.ds(pl.multiple_of(pair * wide, wide), wide)
     w = plan.w // 2
     lines = plan.places // plan.w
     places = lines * w
@@ -614,9 +607,9 @@
                 jnp.where(inside, pltpu.roll(part, places - shift, 1), jnp.zeros_like(part)) for part in (here, beside)
             ]
         sums = sums + one_hot_dot(
-            weights[9 * k : 9 * k + 9].reshape(9 * wide, plan.channels), here, ((1,), (0,))
+            weights[9 * k : 9 * k + 9, both, :].reshape(9 * wide, plan.channels), here, ((1,), (0,))
         )
-        facing = jnp.concatenate([weights[9 * k + 3 * row + 2 * member] for row in range(3)], axis=0)
+        facing = jnp.concatenate([weights[9 * k + 3 * row + 2 * member, both, :] for row in range(3)], axis=0)
         extras = extras + one_hot_dot(facing, beside, ((1,), (0,)))
     products[...], beyond[...] = sums, extras
     parts = [acts_ref[pq] for pq in range(4)]
@@ -733,6 +726,7 @@
 
 
 LIMIT = pltpu.CompilerParams(vmem_limit_bytes=40 * 1024 * 1024)
+COST = pl.CostEstimate(flops=2_000_000_000, bytes_accessed=4_000_000, transcendentals=0)
 
 
 def fast_shards(
@@ -751,33 +745,30 @@
     count, sub, channels, places, local = plan.count, plan.sub, plan.channels, plan.places, plan.local
     f32, bf16 = jnp.float32, jnp.bfloat16
     rows = [part.reshape(1, channels) for part in (gain_coarse, bias_coarse, gain_fine, bias_fine)]
-    packed, acts, weights_c, weights_f, columns, order, fine_order, by_column, rows = pl.pallas_call(
+    packed, acts, columns, order, fine_order, by_column, rows = pl.pallas_call(
         functools.partial(pack_kernel, plan),
         out_shape=(
             shape_of((count, plan.block_rows, 128), bf16),
             shape_of((4 * local, channels), bf16),
-            shape_of((27, 2 * sub, channels // 2), bf16),
-            shape_of((27, 2 * sub, channels), bf16),
             shape_of((4, 2 * sub, 128), f32),
             shape_of((4 * plan.nr * local, 4 * plan.nr * local), bf16),
             shape_of((4 * plan.nr * local, 4 * plan.nr * local), bf16),
             shape_of((places, places + places // 2), bf16),
             shape_of((4, 1, channels), f32),
         ),
-        in_specs=in_hbm(9),
-        out_specs=tuple(in_vmem(9)),
+        in_specs=in_hbm(7),
+        out_specs=tuple(in_vmem(7)),
         scratch_shapes=[
             pltpu.VMEM((local, channels), bf16),
             pltpu.VMEM((local, channels), bf16),
-            pltpu.SemaphoreType.DMA((9,)),
+            pltpu.SemaphoreType.DMA((7,)),
         ],
         compiler_params=LIMIT,
+        cost_estimate=COST,
     )(
         kept(grad_coarse.reshape(local, channels)),
         kept(acts_coarse.reshape(local, channels)),
         kept(acts_fine.reshape(4 * local, channels)),
-        kept(kernel_coarse),
-        kept(kernel_fine),
         *[kept(row) for row in rows],
     )
     got = lax.all_to_all(packed, BLOCK, 0, 0)
@@ -798,7 +789,8 @@
             pltpu.VMEM((2 * sub, places), f32),
         ],
         compiler_params=LIMIT,
-    )(got, weights_c, columns, order, fine_order)
+        cost_estimate=COST,
+    )(got, kernel_coarse, columns, order, fine_order)
     both = lax.all_gather(theirs, "member")
     quartered, coarse_sums = pl.pallas_call(
         functools.partial(quarter_kernel, plan),
@@ -806,6 +798,7 @@
         in_specs=in_vmem(6),
         out_specs=tuple(in_vmem(2)),
         compiler_params=LIMIT,
+        cost_estimate=COST,
     )(mine, both, held, inv_std, columns, by_column)
     spread = lax.all_to_all(quartered, BLOCK, 0, 0)
     sent = pl.pallas_call(
@@ -820,7 +813,8 @@
             pltpu.VMEM((6 * sub, places // 2), f32),
         ],
         compiler_params=LIMIT,
-    )(spread, fine_acts, both, columns, fine_order, coarse_sums, weights_f)
+        cost_estimate=COST,
+    )(spread, fine_acts, both, columns, fine_order, coarse_sums, kernel_fine)
     back = lax.all_to_all(sent, BLOCK, 0, 0)
     cells = nd * places
     fine_scale, coarse_scale = 1.0 / math.sqrt(4 * cells), 1.0 / math.sqrt(cells)
@@ -830,6 +824,7 @@
         in_specs=in_vmem(3),
         out_specs=tuple(in_vmem(2)),
         compiler_params=LIMIT,
+        cost_estimate=COST,
     )(back, acts, rows)
     both = lax.all_gather(sums, "dp")
     out, sums = pl.pallas_call(
@@ -839,6 +834,7 @@
         out_specs=(in_hbm(1)[0], tuple(in_hbm(4))),
         scratch_shapes=[pltpu.VMEM((4, 1, channels), f32), pltpu.SemaphoreType.DMA((5,))],
         compiler_params=LIMIT,
+        cost_estimate=COST,
     )(both, out)
     bias_f, gain_f, bias_c, gain_c = [part.reshape(channels) for part in sums]
     return out.reshape(acts_fine.shape), gain_f, bias_f, gain_c, bias_c

time: 60.1 us -> 60.1 us (level)
  no operation moved by 1% of the time
where the time goes in v15:
time: 60.1 us; the launch traced here: 59.8 us
  blocking collectives  52.9 us (88%)
  Pallas kernels  6.23 us (10%)
  between operations  0.69 us (1%)
    all_to_all x1, blocking collectives, fast_shards(): got = lax.all_to_all(packed, BLOCK, 0, 0)  22 us
    all_to_all x1, blocking collectives, fast_shards(): spread = lax.all_to_all(quartered, BLOCK, 0, 0)  13 us
    all_to_all x1, blocking collectives, fast_shards(): back = lax.all_to_all(sent, BLOCK, 0, 0)  11.4 us
    all_gather x1, blocking collectives, fast_shards(): both = lax.all_gather(theirs, 'member')  4.68 us
    pallas_call x1, Pallas kernels, fast_shards(): pl.pallas_call(functools.partial(pack_kernel, plan), out_shape=(shape_of(...  1.9 us
    all_gather x1, blocking collectives, fast_shards(): both = lax.all_gather(sums, 'dp')  1.83 us
    pallas_call x1, Pallas kernels, fast_shards(): pl.pallas_call(functools.partial(fine_kernel, plan), out_shape=shape_of((...  1.63 us

profile of v15, /device:TPU:0, one launch (start us, length us, event | category | flops | bytes accessed | tf_op | source)
XLA Modules:
  0.0 59.8 jit_solution(437008723017411873)
XLA Ops:
  0.6 0.0 copy-start
  0.6 1.9 %shard_map.128 = (bf16[16,112,128]{2,1,0:T(8,128)(2,1)S(1)}, bf16[128,512]{1,0:T(8,128)(2,1)S(1)}, f32[4,64,128]{2,1,0:T(8,128)S(1)}, bf16[512,512]{1,0:T(8,128)...) custom-call(bf16[32,512]{1,0:T(8,128)(2,1)} %bitcast.18, ...), custom_call_target="tpu_custom_call" | custom-call | flops 2000000000 | bytes 4000000 | tf_op jit(solution)/shard_map/pallas_call | solution.py:748
  2.6 22.0 %all_to_all.15.got_ref = bf16[16,112,128]{2,1,0:T(8,128)(2,1)S(1)} all-to-all(bf16[16,112,128]{2,1,0:T(8,128)(2,1)S(1)} %get-tuple-element.26), channel_id=1, replica_groups=mesh['dp'=2,'pairs'=2,'member'=2,'rows'=4] {'rows','pairs','member'}, dimensions={0} | all-to-all | bytes 917504 | tf_op jit(solution)/shard_map/all_to_all | solution.py:774
  24.5 0.0 copy-done
  24.5 1.1 %shard_map.129 = (f32[32,512]{1,0:T(8,128)S(1)}, bf16[40,512]{1,0:T(8,128)(2,1)S(1)}, f32[3,32,512]{2,1,0:T(8,128)S(1)}, f32[32,128]{1,0:T(8,128)S(1)}, f32[4,64,256]{2,1,0:T(8,128)S(1)}) custom-call(bf16[16,112,128]{2,1,0:T(8,128)(2,1)S(1)} %all_to_all.15.got_ref, bf16[27,128,512]{2,1,0:T(8,128)(2,1)S(1)} %copy-done, ...), custom_call_target="tpu_custom_call" | custom-call | flops 2000000000 | bytes 4000000 | tf_op jit(solution)/shard_map/pallas_call | solution.py:775
  25.7 4.7 %all-gather = bf16[80,512]{1,0:T(8,128)(2,1)S(1)} all-gather(bf16[40,512]{1,0:T(8,128)(2,1)S(1)} %get-tuple-element.31), channel_id=2, replica_groups=mesh['dp'=2,'pairs'=2,'member'=2,'rows'=4] {'member'}, dimensions={0}, use_global_device_ids=true | all-gather | bytes 122880 | tf_op jit(solution)/shard_map/all_gather | solution.py:794
  30.4 0.0 copy-start.1
  30.4 0.4 shard_map.130
  30.8 13.0 %all_to_all.16.got_ref = bf16[16,80,128]{2,1,0:T(8,128)(2,1)S(1)} all-to-all(bf16[16,80,128]{2,1,0:T(8,128)(2,1)S(1)} %get-tuple-element.35), channel_id=1, replica_groups=mesh['dp'=2,'pairs'=2,'member'=2,'rows'=4] {'rows','pairs','member'}, dimensions={0} | all-to-all | bytes 655360 | tf_op jit(solution)/shard_map/all_to_all | solution.py:803
  43.7 0.0 copy-done.1
  43.7 1.6 %shard_map.131 = bf16[16,40,128]{2,1,0:T(8,128)(2,1)S(1)} custom-call(bf16[16,80,128]{2,1,0:T(8,128)(2,1)S(1)} %all_to_all.16.got_ref, f32[4,64,256]{2,1,0:T(8,128)S(1)} %get-tuple-element.36.acts_ref, bf16[2,40,512]{2,1,0:T(8,128)(2,1)S(1)} %bitcast.15, f32[4,64,128]{2,1,0:T(8,128)S(1)} %get-tuple-element.27.columns, ...), custom_call_target="tpu_custom_call" | custom-call | flops 2000000000 | bytes 4000000 | tf_op jit(solution)/shard_map/pallas_call | solution.py:804
  45.4 11.4 %all_to_all.17.got_ref = bf16[16,40,128]{2,1,0:T(8,128)(2,1)S(1)} all-to-all(bf16[16,40,128]{2,1,0:T(8,128)(2,1)S(1)} %shard_map.131), channel_id=1, replica_groups=mesh['dp'=2,'pairs'=2,'member'=2,'rows'=4] {'rows','pairs','member'}, dimensions={0} | all-to-all | bytes 327680 | tf_op jit(solution)/shard_map/all_to_all | solution.py:818
  56.8 0.5 shard_map.132
  57.3 1.8 %all-gather.1 = f32[16,512]{1,0:T(8,128)S(1)} all-gather(f32[8,512]{1,0:T(8,128)S(1)} %get-tuple-element.40), channel_id=3, replica_groups=mesh['dp'=2,'pairs'=2,'member'=2,'rows'=4] {'dp'}, dimensions={0}, use_global_device_ids=true | all-gather | bytes 49152 | tf_op jit(solution)/shard_map/all_gather | solution.py:829
  59.1 0.7 %shard_map.133 = (bf16[128,512]{1,0:T(8,128)(2,1)}, f32[1,512]{1,0:T(1,128)}, f32[1,512]{1,0:T(1,128)}, f32[1,512]{1,0:T(1,128)}, f32[1,512]{1,0:T(1,128)}) custom-call(f32[2,8,512]{2,1,0:T(8,128)S(1)} %bitcast.16, bf16[128,512]{1,0:T(8,128)(2,1)S(1)} %get-tuple-element.41.result_ref), custom_call_target="tpu_custom_call" | custom-call | flops 2000000000 | bytes 4000000 | tf_op jit(solution)/shard_map/pallas_call | solution.py:830
Async XLA Ops:
  0.6 23.9 %copy-start = (bf16[27,128,512]{2,1,0:T(8,128)(2,1)S(1)}, bf16[27,128,512]{2,1,0:T(8,128)(2,1)}, u32[]{:S(2)}) copy-start(bf16[27,128,512]{2,1,0:T(8,128)(2,1)} %weights.2) | copy-start | bytes 10616836
  30.4 13.4 %copy-start.1 = (bf16[27,128,512]{2,1,0:T(8,128)(2,1)S(1)}, bf16[27,128,512]{2,1,0:T(8,128)(2,1)}, u32[]{:S(2)}) copy-start(bf16[27,128,512]{2,1,0:T(8,128)(2,1)} %weights.3) | copy-start | bytes 10616836

commit v16 on v15

--- a/solution.py
+++ b/solution.py
@@ -354,36 +354,9 @@
     return pair, member, r, r * plan.slice_width + (2 * pair + member) * plan.sub
 
 
-def pack_kernel(
-    plan,
-    g_hbm,
-    coarse_hbm,
-    fine_hbm,
-    gain_c,
-    bias_c,
-    gain_f,
-    bias_f,
-    out_ref,
-    fine_ref,
-    columns,
-    order,
-    fine_order,
-    by_column,
-    rows,
-    g_ref,
-    coarse_ref,
-    sems,
-):
+def pack_kernel(plan, g_hbm, coarse_hbm, fine_hbm, out_ref, fine_ref, g_ref, coarse_ref, sems):
     sub, chunks, local = plan.sub, plan.chunks, plan.local
-    pair, member, r, base = own_place(plan)
-    copies = fetched(
-        [(fine_hbm, fine_ref), (coarse_hbm, coarse_ref), (g_hbm, g_ref)]
-        + [(row, rows.at[k]) for k, row in enumerate((gain_c, bias_c, gain_f, bias_f))],
-        sems,
-    )
-    order[...] = merged_order(plan.nr, 4, plan.tl, plan.cells)
-    fine_order[...] = merged_order(plan.nr, 8, plan.tl, plan.cells // 2)
-    by_column[...] = column_order(plan)
+    copies = fetched([(fine_hbm, fine_ref), (coarse_hbm, coarse_ref), (g_hbm, g_ref)], sems)
     shape = (2 * local, 2 * 128)
     lane = lanes_at((1, 2 * 128), 1)
     repeated = one_hot(lanes_at(shape, 0) == lane % local + lane // 128 * local)
@@ -410,12 +383,6 @@
                 out_ref[dest, k * local : (k + 1) * local, :] = g_ref[:, at : at + 128]
             upper, lower = halves[half][first : first + sub], halves[1 - half][first + sub : first + 2 * sub]
             out_ref[dest, plan.acts_at : plan.packed_at, :] = jnp.where(low, upper, lower)
-    for copy in copies[3:7]:
-        copy.wait()
-    first = r * plan.slice_width + 2 * pair * sub
-    for k in range(2):
-        columns[k, 0:sub, :] = jnp.broadcast_to(own_column(rows[k], base, sub), (sub, 128))
-        columns[2 + k] = jnp.broadcast_to(own_column(rows[2 + k], first, 2 * sub), (2 * sub, 128))
 
 
 def by_frame_device(plan, got_ref, at, height):
@@ -445,21 +412,34 @@
     plan,
     got_ref,
     weights,
-    columns,
-    order,
-    fine_order,
+    gain_c,
+    bias_c,
+    gain_f,
+    bias_f,
     mine_ref,
     sent_ref,
     held_ref,
     inv_ref,
     fine_ref,
+    columns,
+    fine_order,
+    by_column,
+    order,
     source,
     products,
     conv_ref,
 ):
     sub, nr, nf, cells, tl, local = plan.sub, plan.nr, plan.nf, plan.cells, plan.tl, plan.local
     wide, depth = 2 * sub, plan.channels // 2
-    pair, member, _, _ = own_place(plan)
+    pair, member, r, base = own_place(plan)
+    first = r * plan.slice_width + pair * wide
+    columns[0, 0:sub, :] = jnp.broadcast_to(own_column(gain_c[...], base, sub), (sub, 128))
+    columns[1, 0:sub, :] = jnp.broadcast_to(own_column(bias_c[...], base, sub), (sub, 128))
+    columns[2] = jnp.broadcast_to(own_column(gain_f[...], first, wide), (wide, 128))
+    columns[3] = jnp.broadcast_to(own_column(bias_f[...], first, wide), (wide, 128))
+    order[...] = merged_order(plan.nr, 4, plan.tl, plan.cells)
+    fine_order[...] = merged_order(plan.nr, 8, plan.tl, plan.cells // 2)
+    by_column[...] = column_order(plan)
     both = pl.ds(pl.multiple_of(pair * wide, wide), wide)
     half = pl.ds(pl.multiple_of(member * depth, depth), depth)
     for s_f in range(nf):
@@ -651,7 +631,7 @@
             out_ref[s_r * nf + s_f, sub : sub + 8, :] = coded
 
 
-def spread_kernel(plan, got_ref, acts_ref, rows_ref, out_ref, sums_ref):
+def spread_kernel(plan, got_ref, acts_ref, gain_ref, out_ref, sums_ref):
     sub, nr, nf = plan.sub, plan.nr, plan.nf
     low = lanes_at((sub, 128), 1) < 64
     low_row = lanes_at((1, 128), 1) < 64
@@ -688,7 +668,7 @@
     one, two, inv_std, mean, c_one, c_two = [jnp.concatenate(part, axis=1) for part in fine + moments + coarse]
     source = jnp.concatenate(source, axis=0).astype(jnp.bfloat16)
     result = one_hot_dot(pixel_order(plan, False), source, ((1,), (1,)))
-    gain = rows_ref[2]
+    gain = gain_ref[...]
     entries = 4 * plan.places * plan.group_width
     group_one = in_lane_groups(gain * one, plan.group_width) / entries
     group_two = in_lane_groups(gain * two, plan.group_width) / entries
@@ -745,23 +725,18 @@
     count, sub, channels, places, local = plan.count, plan.sub, plan.channels, plan.places, plan.local
     f32, bf16 = jnp.float32, jnp.bfloat16
     rows = [part.reshape(1, channels) for part in (gain_coarse, bias_coarse, gain_fine, bias_fine)]
-    packed, acts, columns, order, fine_order, by_column, rows = pl.pallas_call(
+    packed, acts = pl.pallas_call(
         functools.partial(pack_kernel, plan),
         out_shape=(
             shape_of((count, plan.block_rows, 128), bf16),
             shape_of((4 * local, channels), bf16),
-            shape_of((4, 2 * sub, 128), f32),
-            shape_of((4 * plan.nr * local, 4 * plan.nr * local), bf16),
-            shape_of((4 * plan.nr * local, 4 * plan.nr * local), bf16),
-            shape_of((places, places + places // 2), bf16),
-            shape_of((4, 1, channels), f32),
         ),
-        in_specs=in_hbm(7),
-        out_specs=tuple(in_vmem(7)),
+        in_specs=in_hbm(3),
+        out_specs=tuple(in_vmem(2)),
         scratch_shapes=[
             pltpu.VMEM((local, channels), bf16),
             pltpu.VMEM((local, channels), bf16),
-            pltpu.SemaphoreType.DMA((7,)),
+            pltpu.SemaphoreType.DMA((3,)),
         ],
         compiler_params=LIMIT,
         cost_estimate=COST,
@@ -769,10 +744,10 @@
         kept(grad_coarse.reshape(local, channels)),
         kept(acts_coarse.reshape(local, channels)),
         kept(acts_fine.reshape(4 * local, channels)),
-        *[kept(row) for row in rows],
-    )
+    )
+    packed, kernel_coarse = lax.optimization_barrier((packed, kernel_coarse))
     got = lax.all_to_all(packed, BLOCK, 0, 0)
-    mine, theirs, held, inv_std, fine_acts = pl.pallas_call(
+    mine, theirs, held, inv_std, fine_acts, columns, fine_order, by_column = pl.pallas_call(
         functools.partial(coarse_kernel, plan),
         out_shape=(
             shape_of((sub, places), f32),
@@ -780,17 +755,21 @@
             shape_of((3, sub, places), f32),
             shape_of((sub, 128), f32),
             shape_of((4, 2 * sub, places // 2), f32),
+            shape_of((4, 2 * sub, 128), f32),
+            shape_of((4 * plan.nr * local, 4 * plan.nr * local), bf16),
+            shape_of((places, places + places // 2), bf16),
         ),
-        in_specs=in_vmem(5),
-        out_specs=tuple(in_vmem(5)),
+        in_specs=in_vmem(6),
+        out_specs=tuple(in_vmem(8)),
         scratch_shapes=[
+            pltpu.VMEM((4 * plan.nr * local, 4 * plan.nr * local), bf16),
             pltpu.VMEM((places + 2 * plan.image, channels // 2), bf16),
             pltpu.VMEM((18 * sub, places), f32),
             pltpu.VMEM((2 * sub, places), f32),
         ],
         compiler_params=LIMIT,
         cost_estimate=COST,
-    )(got, kernel_coarse, columns, order, fine_order)
+    )(got, kernel_coarse, *rows)
     both = lax.all_gather(theirs, "member")
     quartered, coarse_sums = pl.pallas_call(
         functools.partial(quarter_kernel, plan),
@@ -825,7 +804,7 @@
         out_specs=tuple(in_vmem(2)),
         compiler_params=LIMIT,
         cost_estimate=COST,
-    )(back, acts, rows)
+    )(back, acts, rows[2])
     both = lax.all_gather(sums, "dp")
     out, sums = pl.pallas_call(
         functools.partial(total_kernel, (fine_scale, fine_scale, coarse_scale, coarse_scale)),

time: 60.1 us -> 60.2 us (level)
  no operation moved by 1% of the time
where the time goes in v16:
time: 60.2 us; the launch traced here: 59.9 us
  blocking collectives  52.9 us (88%)
  Pallas kernels  6.26 us (10%)
  between operations  0.74 us (1%)
    all_to_all x1, blocking collectives, fast_shards(): got = lax.all_to_all(packed, BLOCK, 0, 0)  22 us
    all_to_all x1, blocking collectives, fast_shards(): spread = lax.all_to_all(quartered, BLOCK, 0, 0)  13 us
    all_to_all x1, blocking collectives, fast_shards(): back = lax.all_to_all(sent, BLOCK, 0, 0)  11.4 us
    all_gather x1, blocking collectives, fast_shards(): both = lax.all_gather(theirs, 'member')  4.68 us
    all_gather x1, blocking collectives, fast_shards(): both = lax.all_gather(sums, 'dp')  1.83 us
    pallas_call x1, Pallas kernels, fast_shards(): pl.pallas_call(functools.partial(pack_kernel, plan), out_shape=(shape_of(...  1.73 us
    pallas_call x1, Pallas kernels, fast_shards(): pl.pallas_call(functools.partial(fine_kernel, plan), out_shape=shape_of((...  1.64 us
    pallas_call x1, Pallas kernels, fast_shards(): pl.pallas_call(functools.partial(coarse_kernel, plan), out_shape=(shape_o...  1.32 us

profile of v16, /device:TPU:0, one launch (start us, length us, event | category | flops | bytes accessed | tf_op | source)
XLA Modules:
  0.0 59.9 jit_solution(12003227034355552123)
XLA Ops:
  0.6 0.0 copy-start
  0.6 0.0 copy-start.2
  0.7 0.0 copy-start.3
  0.7 0.0 copy-start.4
  0.7 0.0 copy-start.5
  0.7 1.7 %shard_map.128 = (bf16[16,112,128]{2,1,0:T(8,128)(2,1)S(1)}, bf16[128,512]{1,0:T(8,128)(2,1)S(1)}) custom-call(bf16[32,512]{1,0:T(8,128)(2,1)} %bitcast.23, bf16[32,512]{1,0:T(8,128)(2,1)} %bitcast.24, bf16[128,512]{1,0:T(8,128)(2,1)} %bitcast.22), custom_call_target="tpu_custom_call" | custom-call | flops 2000000000 | bytes 4000000 | tf_op jit(solution)/shard_map/pallas_call | solution.py:728
  2.4 22.0 %all_to_all.15.got_ref = bf16[16,112,128]{2,1,0:T(8,128)(2,1)S(1)} all-to-all(bf16[16,112,128]{2,1,0:T(8,128)(2,1)S(1)} %get-tuple-element.27), channel_id=1, replica_groups=mesh['dp'=2,'pairs'=2,'member'=2,'rows'=4] {'rows','pairs','member'}, dimensions={0} | all-to-all | bytes 917504 | tf_op jit(solution)/shard_map/all_to_all | solution.py:749
  24.4 0.0 copy-done
  24.4 0.0 copy-done.2
  24.4 0.0 copy-done.3
  24.4 0.0 copy-done.4
  24.4 0.0 copy-done.5
  24.4 1.3 %shard_map.129 = (f32[32,512]{1,0:T(8,128)S(1)}, bf16[40,512]{1,0:T(8,128)(2,1)S(1)}, f32[3,32,512]{2,1,0:T(8,128)S(1)}, f32[32,128]{1,0:T(8,128)S(1)}, f32[4,64...) custom-call(bf16[16,112,128]{2,1,0:T(8,128)(2,1)S(1)} %all_to_all.15, ...), custom_call_target="tpu_custom_call" | custom-call | flops 2000000000 | bytes 4000000 | tf_op jit(solution)/shard_map/pallas_call | solution.py:750
  25.8 4.7 %all-gather = bf16[80,512]{1,0:T(8,128)(2,1)S(1)} all-gather(bf16[40,512]{1,0:T(8,128)(2,1)S(1)} %get-tuple-element.30), channel_id=2, replica_groups=mesh['dp'=2,'pairs'=2,'member'=2,'rows'=4] {'member'}, dimensions={0}, use_global_device_ids=true | all-gather | bytes 122880 | tf_op jit(solution)/shard_map/all_gather | solution.py:773
  30.4 0.0 copy-start.1
  30.4 0.4 shard_map.130
  30.8 13.0 %all_to_all.16.got_ref = bf16[16,80,128]{2,1,0:T(8,128)(2,1)S(1)} all-to-all(bf16[16,80,128]{2,1,0:T(8,128)(2,1)S(1)} %get-tuple-element.35), channel_id=1, replica_groups=mesh['dp'=2,'pairs'=2,'member'=2,'rows'=4] {'rows','pairs','member'}, dimensions={0} | all-to-all | bytes 655360 | tf_op jit(solution)/shard_map/all_to_all | solution.py:782
  43.8 0.0 copy-done.1
  43.8 1.6 %shard_map.131 = bf16[16,40,128]{2,1,0:T(8,128)(2,1)S(1)} custom-call(bf16[16,80,128]{2,1,0:T(8,128)(2,1)S(1)} %all_to_all.16.got_ref, f32[4,64,256]{2,1,0:T(8,128)S(1)} %get-tuple-element.36.acts_ref, bf16[2,40,512]{2,1,0:T(8,128)(2,1)S(1)} %bitcast.15, f32[4,64,128]{2,1,0:T(8,128)S(1)} %get-tuple-element.33.columns, ...), custom_call_target="tpu_custom_call" | custom-call | flops 2000000000 | bytes 4000000 | tf_op jit(solution)/shard_map/pallas_call | solution.py:783
  45.5 11.4 %all_to_all.17.got_ref = bf16[16,40,128]{2,1,0:T(8,128)(2,1)S(1)} all-to-all(bf16[16,40,128]{2,1,0:T(8,128)(2,1)S(1)} %shard_map.131), channel_id=1, replica_groups=mesh['dp'=2,'pairs'=2,'member'=2,'rows'=4] {'rows','pairs','member'}, dimensions={0} | all-to-all | bytes 327680 | tf_op jit(solution)/shard_map/all_to_all | solution.py:797
  56.9 0.5 shard_map.132
  57.4 1.8 %all-gather.1 = f32[16,512]{1,0:T(8,128)S(1)} all-gather(f32[8,512]{1,0:T(8,128)S(1)} %get-tuple-element.40), channel_id=3, replica_groups=mesh['dp'=2,'pairs'=2,'member'=2,'rows'=4] {'dp'}, dimensions={0}, use_global_device_ids=true | all-gather | bytes 49152 | tf_op jit(solution)/shard_map/all_gather | solution.py:808
  59.2 0.7 %shard_map.133 = (bf16[128,512]{1,0:T(8,128)(2,1)}, f32[1,512]{1,0:T(1,128)}, f32[1,512]{1,0:T(1,128)}, f32[1,512]{1,0:T(1,128)}, f32[1,512]{1,0:T(1,128)}) custom-call(f32[2,8,512]{2,1,0:T(8,128)S(1)} %bitcast.16, bf16[128,512]{1,0:T(8,128)(2,1)S(1)} %get-tuple-element.41.result_ref), custom_call_target="tpu_custom_call" | custom-call | flops 2000000000 | bytes 4000000 | tf_op jit(solution)/shard_map/pallas_call | solution.py:809
Async XLA Ops:
  0.6 23.8 %copy-start = (bf16[27,128,512]{2,1,0:T(8,128)(2,1)S(1)}, bf16[27,128,512]{2,1,0:T(8,128)(2,1)}, u32[]{:S(2)}) copy-start(bf16[27,128,512]{2,1,0:T(8,128)(2,1)} %weights.1) | copy-start | bytes 10616836
  0.6 23.8 %copy-start.2 = (f32[512]{0:T(512)S(1)}, f32[512]{0:T(512)}, u32[]{:S(2)}) copy-start(f32[512]{0:T(512)} %param.15) | copy-start | bytes 6148
  0.7 23.8 %copy-start.3 = (f32[512]{0:T(512)S(1)}, f32[512]{0:T(512)}, u32[]{:S(2)}) copy-start(f32[512]{0:T(512)} %param.16) | copy-start | bytes 6148
  0.7 23.7 %copy-start.4 = (f32[512]{0:T(512)S(1)}, f32[512]{0:T(512)}, u32[]{:S(2)}) copy-start(f32[512]{0:T(512)} %param.13) | copy-start | bytes 6148
  0.7 23.7 %copy-start.5 = (f32[512]{0:T(512)S(1)}, f32[512]{0:T(512)}, u32[]{:S(2)}) copy-start(f32[512]{0:T(512)} %param.12) | copy-start | bytes 6148
  30.4 13.4 %copy-start.1 = (bf16[27,128,512]{2,1,0:T(8,128)(2,1)S(1)}, bf16[27,128,512]{2,1,0:T(8,128)(2,1)}, u32[]{:S(2)}) copy-start(bf16[27,128,512]{2,1,0:T(8,128)(2,1)} %weights.2) | copy-start | bytes 10616836

commit v17 on v16

--- a/solution.py
+++ b/solution.py
@@ -354,21 +354,22 @@
     return pair, member, r, r * plan.slice_width + (2 * pair + member) * plan.sub
 
 
-def pack_kernel(plan, g_hbm, coarse_hbm, fine_hbm, out_ref, fine_ref, g_ref, coarse_ref, sems):
+def fetch_kernel(g_hbm, coarse_hbm, fine_hbm, g_ref, coarse_ref, fine_ref, sems):
+    for copy in fetched([(fine_hbm, fine_ref), (coarse_hbm, coarse_ref), (g_hbm, g_ref)], sems):
+        copy.wait()
+
+
+def pack_kernel(plan, g_ref, coarse_ref, fine_ref, out_ref):
     sub, chunks, local = plan.sub, plan.chunks, plan.local
-    copies = fetched([(fine_hbm, fine_ref), (coarse_hbm, coarse_ref), (g_hbm, g_ref)], sems)
     shape = (2 * local, 2 * 128)
     lane = lanes_at((1, 2 * 128), 1)
     repeated = one_hot(lanes_at(shape, 0) == lane % local + lane // 128 * local)
     shape = (plan.channels, 128)
     quarter = lanes_at(shape, 0) // 8 % 4 == lanes_at(shape, 1) // local
     orders = jnp.concatenate([pixel_order(plan, swapped) for swapped in (False, True)], axis=1)
-    copies[0].wait()
     acts = fine_ref[...]
     halves = one_hot_dot(acts, orders, ((0,), (0,))).astype(jnp.bfloat16)
     halves = [halves[:, :128], halves[:, 128:]]
-    copies[1].wait()
-    copies[2].wait()
     small = one_hot_dot(jnp.concatenate([coarse_ref[...], g_ref[...]], axis=0), repeated, ((0,), (0,)))
     for k, at in enumerate((plan.packed_at, plan.cot_at)):
         rows_of = jnp.where(quarter, small[:, k * 128 : (k + 1) * 128], 0.0).reshape(plan.count, 4, 8, 128)
@@ -725,27 +726,24 @@
     count, sub, channels, places, local = plan.count, plan.sub, plan.channels, plan.places, plan.local
     f32, bf16 = jnp.float32, jnp.bfloat16
     rows = [part.reshape(1, channels) for part in (gain_coarse, bias_coarse, gain_fine, bias_fine)]
-    packed, acts = pl.pallas_call(
+    places_of = ((local, channels), (local, channels), (4 * local, channels))
+    fetched_of = pl.pallas_call(
+        fetch_kernel,
+        out_shape=tuple(pltpu.VMEM(shape, bf16) for shape in places_of),
+        in_specs=in_hbm(3),
+        out_specs=tuple(in_vmem(3)),
+        scratch_shapes=[pltpu.SemaphoreType.DMA((3,))],
+        compiler_params=LIMIT,
+    )(*[kept(part.reshape(shape)) for part, shape in zip((grad_coarse, acts_coarse, acts_fine), places_of)])
+    acts = fetched_of[2]
+    packed = pl.pallas_call(
         functools.partial(pack_kernel, plan),
-        out_shape=(
-            shape_of((count, plan.block_rows, 128), bf16),
-            shape_of((4 * local, channels), bf16),
-        ),
-        in_specs=in_hbm(3),
-        out_specs=tuple(in_vmem(2)),
-        scratch_shapes=[
-            pltpu.VMEM((local, channels), bf16),
-            pltpu.VMEM((local, channels), bf16),
-            pltpu.SemaphoreType.DMA((3,)),
-        ],
+        out_shape=shape_of((count, plan.block_rows, 128), bf16),
+        in_specs=in_vmem(3),
+        out_specs=in_vmem(1)[0],
         compiler_params=LIMIT,
         cost_estimate=COST,
-    )(
-        kept(grad_coarse.reshape(local, channels)),
-        kept(acts_coarse.reshape(local, channels)),
-        kept(acts_fine.reshape(4 * local, channels)),
-    )
-    packed, kernel_coarse = lax.optimization_barrier((packed, kernel_coarse))
+    )(*fetched_of)
     got = lax.all_to_all(packed, BLOCK, 0, 0)
     mine, theirs, held, inv_std, fine_acts, columns, fine_order, by_column = pl.pallas_call(
         functools.partial(coarse_kernel, plan),

time: 60.2 us -> 59.9 us (level)
    pallas_call x1 -> x2, Pallas kernels: 1.73 us -> 1.27 us  [the longest x1 0.94 us: fast_shards(): pl.pallas_call(fetch_kernel, out_shape=tuple((pltpu.VMEM(shape, bf16) for...]
where the time goes in v17:
time: 59.9 us; the launch traced here: 59.6 us
  blocking collectives  53 us (88%)
  Pallas kernels  5.79 us (10%)
  between operations  0.74 us (1%)
    all_to_all x1, blocking collectives, fast_shards(): got = lax.all_to_all(packed, BLOCK, 0, 0)  22.1 us
    all_to_all x1, blocking collectives, fast_shards(): spread = lax.all_to_all(quartered, BLOCK, 0, 0)  13 us
    all_to_all x1, blocking collectives, fast_shards(): back = lax.all_to_all(sent, BLOCK, 0, 0)  11.4 us
    all_gather x1, blocking collectives, fast_shards(): both = lax.all_gather(theirs, 'member')  4.68 us
    all_gather x1, blocking collectives, fast_shards(): both = lax.all_gather(sums, 'dp')  1.83 us
    pallas_call x1, Pallas kernels, fast_shards(): pl.pallas_call(functools.partial(fine_kernel, plan), out_shape=shape_of((...  1.64 us
    pallas_call x1, Pallas kernels, fast_shards(): pl.pallas_call(functools.partial(coarse_kernel, plan), out_shape=(shape_o...  1.31 us

profile of v17, /device:TPU:0, one launch (start us, length us, event | category | flops | bytes accessed | tf_op | source)
XLA Modules:
  0.0 59.6 jit_solution(4995049025249691295)
XLA Ops:
  0.6 0.9 %shard_map.128 = (bf16[32,512]{1,0:T(8,128)(2,1)S(1)}, bf16[32,512]{1,0:T(8,128)(2,1)S(1)}, bf16[128,512]{1,0:T(8,128)(2,1)S(1)}) custom-call(bf16[32,512]{1,0:T(8,128)(2,1)} %bitcast.23, bf16[32,512]{1,0:T(8,128)(2,1)} %bitcast.24, bf16[128,512]{1,0:T(8,128)(2,1)} %bitcast.22), custom_call_target="tpu_custom_call" | custom-call | tf_op jit(solution)/shard_map/pallas_call | solution.py:730
  1.6 0.0 copy-start
  1.6 0.0 copy-start.2
  1.6 0.0 copy-start.3
  1.6 0.0 copy-start.4
  1.6 0.0 copy-start.5
  1.6 0.3 shard_map.129
  2.0 22.1 %all_to_all.15.got_ref = bf16[16,112,128]{2,1,0:T(8,128)(2,1)S(1)} all-to-all(bf16[16,112,128]{2,1,0:T(8,128)(2,1)S(1)} %shard_map.129), channel_id=1, replica_groups=mesh['dp'=2,'pairs'=2,'member'=2,'rows'=4] {'rows','pairs','member'}, dimensions={0} | all-to-all | bytes 917504 | tf_op jit(solution)/shard_map/all_to_all | solution.py:747
  24.1 0.0 copy-done
  24.1 0.0 copy-done.2
  24.1 0.0 copy-done.3
  24.1 0.0 copy-done.4
  24.1 0.0 copy-done.5
  24.1 1.3 %shard_map.130 = (f32[32,512]{1,0:T(8,128)S(1)}, bf16[40,512]{1,0:T(8,128)(2,1)S(1)}, f32[3,32,512]{2,1,0:T(8,128)S(1)}, f32[32,128]{1,0:T(8,128)S(1)}, f32[4,64...) custom-call(bf16[16,112,128]{2,1,0:T(8,128)(2,1)S(1)} %all_to_all.15, ...), custom_call_target="tpu_custom_call" | custom-call | flops 2000000000 | bytes 4000000 | tf_op jit(solution)/shard_map/pallas_call | solution.py:748
  25.4 4.7 %all-gather = bf16[80,512]{1,0:T(8,128)(2,1)S(1)} all-gather(bf16[40,512]{1,0:T(8,128)(2,1)S(1)} %get-tuple-element.29), channel_id=2, replica_groups=mesh['dp'=2,'pairs'=2,'member'=2,'rows'=4] {'member'}, dimensions={0}, use_global_device_ids=true | all-gather | bytes 122880 | tf_op jit(solution)/shard_map/all_gather | solution.py:771
  30.1 0.0 copy-start.1
  30.1 0.4 shard_map.131
  30.5 13.0 %all_to_all.16.got_ref = bf16[16,80,128]{2,1,0:T(8,128)(2,1)S(1)} all-to-all(bf16[16,80,128]{2,1,0:T(8,128)(2,1)S(1)} %get-tuple-element.34), channel_id=1, replica_groups=mesh['dp'=2,'pairs'=2,'member'=2,'rows'=4] {'rows','pairs','member'}, dimensions={0} | all-to-all | bytes 655360 | tf_op jit(solution)/shard_map/all_to_all | solution.py:780
  43.5 0.0 copy-done.1
  43.5 1.6 %shard_map.132 = bf16[16,40,128]{2,1,0:T(8,128)(2,1)S(1)} custom-call(bf16[16,80,128]{2,1,0:T(8,128)(2,1)S(1)} %all_to_all.16.got_ref, f32[4,64,256]{2,1,0:T(8,128)S(1)} %get-tuple-element.35.acts_ref, bf16[2,40,512]{2,1,0:T(8,128)(2,1)S(1)} %bitcast.15, f32[4,64,128]{2,1,0:T(8,128)S(1)} %get-tuple-element.32.columns, ...), custom_call_target="tpu_custom_call" | custom-call | flops 2000000000 | bytes 4000000 | tf_op jit(solution)/shard_map/pallas_call | solution.py:781
  45.1 11.4 %all_to_all.17.got_ref = bf16[16,40,128]{2,1,0:T(8,128)(2,1)S(1)} all-to-all(bf16[16,40,128]{2,1,0:T(8,128)(2,1)S(1)} %shard_map.132), channel_id=1, replica_groups=mesh['dp'=2,'pairs'=2,'member'=2,'rows'=4] {'rows','pairs','member'}, dimensions={0} | all-to-all | bytes 327680 | tf_op jit(solution)/shard_map/all_to_all | solution.py:795
  56.6 0.5 shard_map.133
  57.1 1.8 %all-gather.1 = f32[16,512]{1,0:T(8,128)S(1)} all-gather(f32[8,512]{1,0:T(8,128)S(1)} %get-tuple-element.38), channel_id=3, replica_groups=mesh['dp'=2,'pairs'=2,'member'=2,'rows'=4] {'dp'}, dimensions={0}, use_global_device_ids=true | all-gather | bytes 49152 | tf_op jit(solution)/shard_map/all_gather | solution.py:806
  58.9 0.7 %shard_map.134 = (bf16[128,512]{1,0:T(8,128)(2,1)}, f32[1,512]{1,0:T(1,128)}, f32[1,512]{1,0:T(1,128)}, f32[1,512]{1,0:T(1,128)}, f32[1,512]{1,0:T(1,128)}) custom-call(f32[2,8,512]{2,1,0:T(8,128)S(1)} %bitcast.16, bf16[128,512]{1,0:T(8,128)(2,1)S(1)} %get-tuple-element.39.result_ref), custom_call_target="tpu_custom_call" | custom-call | flops 2000000000 | bytes 4000000 | tf_op jit(solution)/shard_map/pallas_call | solution.py:807
Async XLA Ops:
  1.6 22.5 %copy-start = (bf16[27,128,512]{2,1,0:T(8,128)(2,1)S(1)}, bf16[27,128,512]{2,1,0:T(8,128)(2,1)}, u32[]{:S(2)}) copy-start(bf16[27,128,512]{2,1,0:T(8,128)(2,1)} %weights.2) | copy-start | bytes 10616836
  1.6 22.5 %copy-start.2 = (f32[512]{0:T(512)S(1)}, f32[512]{0:T(512)}, u32[]{:S(2)}) copy-start(f32[512]{0:T(512)} %param.15) | copy-start | bytes 6148
  1.6 22.5 %copy-start.3 = (f32[512]{0:T(512)S(1)}, f32[512]{0:T(512)}, u32[]{:S(2)}) copy-start(f32[512]{0:T(512)} %param.16) | copy-start | bytes 6148
  1.6 22.5 %copy-start.4 = (f32[512]{0:T(512)S(1)}, f32[512]{0:T(512)}, u32[]{:S(2)}) copy-start(f32[512]{0:T(512)} %param.13) | copy-start | bytes 6148
  1.6 22.5 %copy-start.5 = (f32[512]{0:T(512)S(1)}, f32[512]{0:T(512)}, u32[]{:S(2)}) copy-start(f32[512]{0:T(512)} %param.12) | copy-start | bytes 6148
  30.1 13.4 %copy-start.1 = (bf16[27,128,512]{2,1,0:T(8,128)(2,1)S(1)}, bf16[27,128,512]{2,1,0:T(8,128)(2,1)}, u32[]{:S(2)}) copy-start(bf16[27,128,512]{2,1,0:T(8,128)(2,1)} %weights.3) | copy-start | bytes 10616836

commit v18 on v17

--- a/solution.py
+++ b/solution.py
@@ -11,6 +11,7 @@
 GROUPS = 32
 EPSILON = 1e-06
 BLOCK = ("rows", "pairs", "member")
+BACK_BLOCK = ("pairs", "member", "rows")
 PLAIN_BLOCK = ("frames", "rows")
 
 
@@ -628,8 +629,8 @@
     coded = jnp.concatenate(coded + [jnp.zeros_like(coarse)], axis=0).astype(jnp.bfloat16)
     for s_r in range(nr):
         for s_f in range(nf):
-            out_ref[s_r * nf + s_f, 0:sub, :] = sent[s_f * sub : (s_f + 1) * sub, s_r * 128 : (s_r + 1) * 128]
-            out_ref[s_r * nf + s_f, sub : sub + 8, :] = coded
+            out_ref[s_f * nr + s_r, 0:sub, :] = sent[s_f * sub : (s_f + 1) * sub, s_r * 128 : (s_r + 1) * 128]
+            out_ref[s_f * nr + s_r, sub : sub + 8, :] = coded
 
 
 def spread_kernel(plan, got_ref, acts_ref, gain_ref, out_ref, sums_ref):
@@ -642,11 +643,11 @@
     for s_r in range(nr):
         ones, twos, c_ones, c_twos, invs, means = [], [], 0.0, 0.0, [], []
         for pair in range(nf // 2):
-            at = s_r * nf + 2 * pair
-            left, right = [got_ref[at + k, 0:sub, :].astype(jnp.float32) for k in range(2)]
+            at = 2 * pair * nr + s_r
+            left, right = [got_ref[at + k * nr, 0:sub, :].astype(jnp.float32) for k in range(2)]
             source.append(jnp.where(low, left, pltpu.roll(right, 64, 1)))
             source.append(jnp.where(low, pltpu.roll(left, 64, 1), right))
-            coded = [got_ref[at + k, sub : sub + 8, :].astype(jnp.float32) for k in range(2)]
+            coded = [got_ref[at + k * nr, sub : sub + 8, :].astype(jnp.float32) for k in range(2)]
             sums = coded[0][0:1] + coded[0][1:2] + coded[1][0:1] + coded[1][1:2]
             ones.append(sums if pair == 0 else pltpu.roll(sums, 64, 1))
             twos.append(pltpu.roll(sums, 64, 1) if pair == 0 else sums)
@@ -792,7 +793,7 @@
         compiler_params=LIMIT,
         cost_estimate=COST,
     )(spread, fine_acts, both, columns, fine_order, coarse_sums, kernel_fine)
-    back = lax.all_to_all(sent, BLOCK, 0, 0)
+    back = lax.all_to_all(sent, BACK_BLOCK, 0, 0)
     cells = nd * places
     fine_scale, coarse_scale = 1.0 / math.sqrt(4 * cells), 1.0 / math.sqrt(cells)
     out, sums = pl.pallas_call(

time: 59.9 us -> 59.6 us (level)
  no operation moved by 1% of the time
where the time goes in v18:
time: 59.6 us; the launch traced here: 59.4 us
  blocking collectives  52.8 us (89%)
  Pallas kernels  5.79 us (10%)
  between operations  0.74 us (1%)
    all_to_all x1, blocking collectives, fast_shards(): got = lax.all_to_all(packed, BLOCK, 0, 0)  22.1 us
    all_to_all x1, blocking collectives, fast_shards(): spread = lax.all_to_all(quartered, BLOCK, 0, 0)  13 us
    all_to_all x1, blocking collectives, fast_shards(): back = lax.all_to_all(sent, BACK_BLOCK, 0, 0)  11.2 us
    all_gather x1, blocking collectives, fast_shards(): both = lax.all_gather(theirs, 'member')  4.68 us
    all_gather x1, blocking collectives, fast_shards(): both = lax.all_gather(sums, 'dp')  1.83 us
    pallas_call x1, Pallas kernels, fast_shards(): pl.pallas_call(functools.partial(fine_kernel, plan), out_shape=shape_of((...  1.64 us
    pallas_call x1, Pallas kernels, fast_shards(): pl.pallas_call(functools.partial(coarse_kernel, plan), out_shape=(shape_o...  1.31 us

profile of v18, /device:TPU:0, one launch (start us, length us, event | category | flops | bytes accessed | tf_op | source)
XLA Modules:
  0.0 59.4 jit_solution(1212856979607672412)
XLA Ops:
  0.6 0.9 %shard_map.128 = (bf16[32,512]{1,0:T(8,128)(2,1)S(1)}, bf16[32,512]{1,0:T(8,128)(2,1)S(1)}, bf16[128,512]{1,0:T(8,128)(2,1)S(1)}) custom-call(bf16[32,512]{1,0:T(8,128)(2,1)} %bitcast.23, bf16[32,512]{1,0:T(8,128)(2,1)} %bitcast.24, bf16[128,512]{1,0:T(8,128)(2,1)} %bitcast.22), custom_call_target="tpu_custom_call" | custom-call | tf_op jit(solution)/shard_map/pallas_call | solution.py:731
  1.6 0.0 copy-start
  1.6 0.0 copy-start.2
  1.6 0.0 copy-start.3
  1.6 0.0 copy-start.4
  1.6 0.0 copy-start.5
  1.6 0.3 shard_map.129
  2.0 22.1 %all_to_all.15.got_ref = bf16[16,112,128]{2,1,0:T(8,128)(2,1)S(1)} all-to-all(bf16[16,112,128]{2,1,0:T(8,128)(2,1)S(1)} %shard_map.129), channel_id=1, replica_groups=mesh['dp'=2,'pairs'=2,'member'=2,'rows'=4] {'rows','pairs','member'}, dimensions={0} | all-to-all | bytes 917504 | tf_op jit(solution)/shard_map/all_to_all | solution.py:748
  24.1 0.0 copy-done
  24.1 0.0 copy-done.2
  24.1 0.0 copy-done.3
  24.1 0.0 copy-done.4
  24.1 0.0 copy-done.5
  24.1 1.3 %shard_map.130 = (f32[32,512]{1,0:T(8,128)S(1)}, bf16[40,512]{1,0:T(8,128)(2,1)S(1)}, f32[3,32,512]{2,1,0:T(8,128)S(1)}, f32[32,128]{1,0:T(8,128)S(1)}, f32[4,64...) custom-call(bf16[16,112,128]{2,1,0:T(8,128)(2,1)S(1)} %all_to_all.15, ...), custom_call_target="tpu_custom_call" | custom-call | flops 2000000000 | bytes 4000000 | tf_op jit(solution)/shard_map/pallas_call | solution.py:749
  25.4 4.7 %all-gather = bf16[80,512]{1,0:T(8,128)(2,1)S(1)} all-gather(bf16[40,512]{1,0:T(8,128)(2,1)S(1)} %get-tuple-element.29), channel_id=2, replica_groups=mesh['dp'=2,'pairs'=2,'member'=2,'rows'=4] {'member'}, dimensions={0}, use_global_device_ids=true | all-gather | bytes 122880 | tf_op jit(solution)/shard_map/all_gather | solution.py:772
  30.1 0.0 copy-start.1
  30.1 0.4 shard_map.131
  30.5 13.0 %all_to_all.16.got_ref = bf16[16,80,128]{2,1,0:T(8,128)(2,1)S(1)} all-to-all(bf16[16,80,128]{2,1,0:T(8,128)(2,1)S(1)} %get-tuple-element.34), channel_id=1, replica_groups=mesh['dp'=2,'pairs'=2,'member'=2,'rows'=4] {'rows','pairs','member'}, dimensions={0} | all-to-all | bytes 655360 | tf_op jit(solution)/shard_map/all_to_all | solution.py:781
  43.5 0.0 copy-done.1
  43.5 1.6 %shard_map.132 = bf16[16,40,128]{2,1,0:T(8,128)(2,1)S(1)} custom-call(bf16[16,80,128]{2,1,0:T(8,128)(2,1)S(1)} %all_to_all.16.got_ref, f32[4,64,256]{2,1,0:T(8,128)S(1)} %get-tuple-element.35.acts_ref, bf16[2,40,512]{2,1,0:T(8,128)(2,1)S(1)} %bitcast.15, f32[4,64,128]{2,1,0:T(8,128)S(1)} %get-tuple-element.32.columns, ...), custom_call_target="tpu_custom_call" | custom-call | flops 2000000000 | bytes 4000000 | tf_op jit(solution)/shard_map/pallas_call | solution.py:782
  45.1 11.2 %all_to_all.17.got_ref = bf16[16,40,128]{2,1,0:T(8,128)(2,1)S(1)} all-to-all(bf16[16,40,128]{2,1,0:T(8,128)(2,1)S(1)} %shard_map.132), channel_id=1, replica_groups=mesh['dp'=2,'pairs'=2,'member'=2,'rows'=4] {'pairs','member','rows'}, dimensions={0} | all-to-all | bytes 327680 | tf_op jit(solution)/shard_map/all_to_all | solution.py:796
  56.4 0.5 shard_map.133
  56.8 1.8 %all-gather.1 = f32[16,512]{1,0:T(8,128)S(1)} all-gather(f32[8,512]{1,0:T(8,128)S(1)} %get-tuple-element.38), channel_id=3, replica_groups=mesh['dp'=2,'pairs'=2,'member'=2,'rows'=4] {'dp'}, dimensions={0}, use_global_device_ids=true | all-gather | bytes 49152 | tf_op jit(solution)/shard_map/all_gather | solution.py:807
  58.7 0.7 %shard_map.134 = (bf16[128,512]{1,0:T(8,128)(2,1)}, f32[1,512]{1,0:T(1,128)}, f32[1,512]{1,0:T(1,128)}, f32[1,512]{1,0:T(1,128)}, f32[1,512]{1,0:T(1,128)}) custom-call(f32[2,8,512]{2,1,0:T(8,128)S(1)} %bitcast.16, bf16[128,512]{1,0:T(8,128)(2,1)S(1)} %get-tuple-element.39.result_ref), custom_call_target="tpu_custom_call" | custom-call | flops 2000000000 | bytes 4000000 | tf_op jit(solution)/shard_map/pallas_call | solution.py:808
Async XLA Ops:
  1.6 22.5 %copy-start = (bf16[27,128,512]{2,1,0:T(8,128)(2,1)S(1)}, bf16[27,128,512]{2,1,0:T(8,128)(2,1)}, u32[]{:S(2)}) copy-start(bf16[27,128,512]{2,1,0:T(8,128)(2,1)} %weights.2) | copy-start | bytes 10616836
  1.6 22.5 %copy-start.2 = (f32[512]{0:T(512)S(1)}, f32[512]{0:T(512)}, u32[]{:S(2)}) copy-start(f32[512]{0:T(512)} %param.15) | copy-start | bytes 6148
  1.6 22.5 %copy-start.3 = (f32[512]{0:T(512)S(1)}, f32[512]{0:T(512)}, u32[]{:S(2)}) copy-start(f32[512]{0:T(512)} %param.16) | copy-start | bytes 6148
  1.6 22.5 %copy-start.4 = (f32[512]{0:T(512)S(1)}, f32[512]{0:T(512)}, u32[]{:S(2)}) copy-start(f32[512]{0:T(512)} %param.13) | copy-start | bytes 6148
  1.6 22.5 %copy-start.5 = (f32[512]{0:T(512)S(1)}, f32[512]{0:T(512)}, u32[]{:S(2)}) copy-start(f32[512]{0:T(512)} %param.12) | copy-start | bytes 6148
  30.1 13.4 %copy-start.1 = (bf16[27,128,512]{2,1,0:T(8,128)(2,1)S(1)}, bf16[27,128,512]{2,1,0:T(8,128)(2,1)}, u32[]{:S(2)}) copy-start(bf16[27,128,512]{2,1,0:T(8,128)(2,1)} %weights.3) | copy-start | bytes 10616836

commit v19 on v18

--- a/solution.py
+++ b/solution.py
@@ -300,7 +300,7 @@
     for part in parts:
         unit = (part - mean) * inv_std
         preact = gain * unit + bias
-        squash = jax.nn.sigmoid(preact)
+        squash = 0.5 + 0.5 * jnp.tanh(0.5 * preact)
         normed.append(unit)
         slope.append(squash * (1.0 + preact * (1.0 - squash)))
     return normed, slope
@@ -428,7 +428,6 @@
     by_column,
     order,
     source,
-    products,
     conv_ref,
 ):
     sub, nr, nf, cells, tl, local = plan.sub, plan.nr, plan.nf, plan.cells, plan.tl, plan.local
@@ -453,7 +452,7 @@
                         s_r * nf + s_f, k * local + t * cells : k * local + (t + 1) * cells, :
                     ]
     source[plan.places :, :] = jnp.zeros((2 * plan.image, depth), jnp.bfloat16)
-    products[...] = sum(
+    products = sum(
         one_hot_dot(
             weights[9 * k : 9 * k + 9, both, half].reshape(9 * wide, depth),
             source[(2 - k) * plan.image : (2 - k) * plan.image + plan.places, :],
@@ -468,11 +467,12 @@
     one, two = total(parts), total([part * part for part in parts])
     stats = terms(as_row(one) + pltpu.roll(as_row(two), 64, 1), 3)
     stats = jnp.concatenate(stats + [jnp.zeros_like(stats[0])] * 5, axis=0).astype(jnp.bfloat16)
-    found = []
-    for at in (plan.packed_at, plan.cot_at):
-        merged = one_hot_dot(by_frame_device(plan, got_ref, at, 8), order[...], ((1,), (0,)))
-        found.append(jnp.concatenate(in_places(plan, merged, 8), axis=0))
-    values, cot = found
+    small = [by_frame_device(plan, got_ref, at, 8) for at in (plan.packed_at, plan.cot_at)]
+    merged = one_hot_dot(jnp.concatenate(small, axis=0), order[...], ((1,), (0,)))
+    rows_of = 8 * nf
+    values, cot = [
+        jnp.concatenate(in_places(plan, merged[k * rows_of : (k + 1) * rows_of], 8), axis=0) for k in range(2)
+    ]
     gain, bias = columns[0][0:sub, 0:1], columns[1][0:sub, 0:1]
     entries = plan.places * plan.group_width
     mean, inv_std = statistics(total([values]), total([values * values]), entries, plan.group_width)
@@ -482,7 +482,7 @@
     lane, has_left, has_right, has_up, has_down = plan.place_masks(plan.w)
     by_col = []
     for col in range(3):
-        parts = [products[pl.ds((3 * row + col) * wide, wide), :] for row in range(3)]
+        parts = [products[(3 * row + col) * wide : (3 * row + col + 1) * wide] for row in range(3)]
         by_col.append(parts[1] + moved(parts[0], plan.w, has_down) + moved(parts[2], -plan.w, has_up))
     conv_ref[...] = by_col[1] + moved(by_col[0], 1, has_right) + moved(by_col[2], -1, has_left)
     mine_ref[...] = conv_ref[pl.ds(pl.multiple_of(member * sub, sub), sub), :]
@@ -558,7 +558,7 @@
 
 
 def fine_kernel(
-    plan, got_ref, acts_ref, both_ref, columns, order, sums_ref, weights, out_ref, source, border, products, beyond
+    plan, got_ref, acts_ref, both_ref, columns, order, sums_ref, weights, out_ref, source, border
 ):
     sub, nr, nf, wide = plan.sub, plan.nr, plan.nf, 2 * plan.sub
     pair, member, r, _ = own_place(plan)
@@ -593,7 +593,6 @@
         )
         facing = jnp.concatenate([weights[9 * k + 3 * row + 2 * member, both, :] for row in range(3)], axis=0)
         extras = extras + one_hot_dot(facing, beside, ((1,), (0,)))
-    products[...], beyond[...] = sums, extras
     parts = [acts_ref[pq] for pq in range(4)]
     stats = sum(both_ref[k, sub : sub + 8, 0:128].astype(jnp.float32) for k in range(2))
     stats = stats[0:1] + stats[1:2] + stats[2:3]
@@ -606,8 +605,8 @@
     right, left = (1 - member).astype(jnp.float32), member.astype(jnp.float32)
     by_row = []
     for row in range(3):
-        a, b, c = [products[pl.ds((3 * row + col) * wide, wide), :] for col in range(3)]
-        extra = beyond[pl.ds(row * wide, wide), :]
+        a, b, c = [sums[(3 * row + col) * wide : (3 * row + col + 1) * wide] for col in range(3)]
+        extra = extras[row * wide : (row + 1) * wide]
         by_row.append(
             (a + b + moved(c, -1, has_left) + left * extra, moved(a, 1, has_right) + b + c + right * extra)
         )
@@ -763,7 +762,6 @@
         scratch_shapes=[
             pltpu.VMEM((4 * plan.nr * local, 4 * plan.nr * local), bf16),
             pltpu.VMEM((places + 2 * plan.image, channels // 2), bf16),
-            pltpu.VMEM((18 * sub, places), f32),
             pltpu.VMEM((2 * sub, places), f32),
         ],
         compiler_params=LIMIT,
@@ -787,8 +785,6 @@
         scratch_shapes=[
             pltpu.VMEM((channels, places // 2), bf16),
             pltpu.VMEM((channels, places // 2), bf16),
-            pltpu.VMEM((18 * sub, places // 2), f32),
-            pltpu.VMEM((6 * sub, places // 2), f32),
         ],
         compiler_params=LIMIT,
         cost_estimate=COST,

time: 59.6 us -> 59.6 us (level)
  no operation moved by 1% of the time
where the time goes in v19:
time: 59.6 us; the launch traced here: 59.3 us
  blocking collectives  52.8 us (89%)
  Pallas kernels  5.71 us (10%)
  between operations  0.74 us (1%)
    all_to_all x1, blocking collectives, fast_shards(): got = lax.all_to_all(packed, BLOCK, 0, 0)  22.1 us
    all_to_all x1, blocking collectives, fast_shards(): spread = lax.all_to_all(quartered, BLOCK, 0, 0)  13 us
    all_to_all x1, blocking collectives, fast_shards(): back = lax.all_to_all(sent, BACK_BLOCK, 0, 0)  11.2 us
    all_gather x1, blocking collectives, fast_shards(): both = lax.all_gather(theirs, 'member')  4.68 us
    all_gather x1, blocking collectives, fast_shards(): both = lax.all_gather(sums, 'dp')  1.83 us
    pallas_call x1, Pallas kernels, fast_shards(): pl.pallas_call(functools.partial(fine_kernel, plan), out_shape=shape_of((...  1.64 us
    pallas_call x1, Pallas kernels, fast_shards(): pl.pallas_call(functools.partial(coarse_kernel, plan), out_shape=(shape_o...  1.24 us

profile of v19, /device:TPU:0, one launch (start us, length us, event | category | flops | bytes accessed | tf_op | source)
XLA Modules:
  0.0 59.3 jit_solution(5922532819233525279)
XLA Ops:
  0.6 0.9 %shard_map.128 = (bf16[32,512]{1,0:T(8,128)(2,1)S(1)}, bf16[32,512]{1,0:T(8,128)(2,1)S(1)}, bf16[128,512]{1,0:T(8,128)(2,1)S(1)}) custom-call(bf16[32,512]{1,0:T(8,128)(2,1)} %bitcast.23, bf16[32,512]{1,0:T(8,128)(2,1)} %bitcast.24, bf16[128,512]{1,0:T(8,128)(2,1)} %bitcast.22), custom_call_target="tpu_custom_call" | custom-call | tf_op jit(solution)/shard_map/pallas_call | solution.py:730
  1.6 0.0 copy-start
  1.6 0.0 copy-start.2
  1.6 0.0 copy-start.3
  1.6 0.0 copy-start.4
  1.6 0.0 copy-start.5
  1.6 0.3 shard_map.129
  2.0 22.1 %all_to_all.15.got_ref = bf16[16,112,128]{2,1,0:T(8,128)(2,1)S(1)} all-to-all(bf16[16,112,128]{2,1,0:T(8,128)(2,1)S(1)} %shard_map.129), channel_id=1, replica_groups=mesh['dp'=2,'pairs'=2,'member'=2,'rows'=4] {'rows','pairs','member'}, dimensions={0} | all-to-all | bytes 917504 | tf_op jit(solution)/shard_map/all_to_all | solution.py:747
  24.1 0.0 copy-done
  24.1 0.0 copy-done.2
  24.1 0.0 copy-done.3
  24.1 0.0 copy-done.4
  24.1 0.0 copy-done.5
  24.1 1.2 %shard_map.130 = (f32[32,512]{1,0:T(8,128)S(1)}, bf16[40,512]{1,0:T(8,128)(2,1)S(1)}, f32[3,32,512]{2,1,0:T(8,128)S(1)}, f32[32,128]{1,0:T(8,128)S(1)}, f32[4,64...) custom-call(bf16[16,112,128]{2,1,0:T(8,128)(2,1)S(1)} %all_to_all.15, ...), custom_call_target="tpu_custom_call" | custom-call | flops 2000000000 | bytes 4000000 | tf_op jit(solution)/shard_map/pallas_call | solution.py:748
  25.4 4.7 %all-gather = bf16[80,512]{1,0:T(8,128)(2,1)S(1)} all-gather(bf16[40,512]{1,0:T(8,128)(2,1)S(1)} %get-tuple-element.29), channel_id=2, replica_groups=mesh['dp'=2,'pairs'=2,'member'=2,'rows'=4] {'member'}, dimensions={0}, use_global_device_ids=true | all-gather | bytes 122880 | tf_op jit(solution)/shard_map/all_gather | solution.py:770
  30.0 0.0 copy-start.1
  30.0 0.4 shard_map.131
  30.4 13.0 %all_to_all.16.got_ref = bf16[16,80,128]{2,1,0:T(8,128)(2,1)S(1)} all-to-all(bf16[16,80,128]{2,1,0:T(8,128)(2,1)S(1)} %get-tuple-element.34), channel_id=1, replica_groups=mesh['dp'=2,'pairs'=2,'member'=2,'rows'=4] {'rows','pairs','member'}, dimensions={0} | all-to-all | bytes 655360 | tf_op jit(solution)/shard_map/all_to_all | solution.py:779
  43.4 0.0 copy-done.1
  43.4 1.6 %shard_map.132 = bf16[16,40,128]{2,1,0:T(8,128)(2,1)S(1)} custom-call(bf16[16,80,128]{2,1,0:T(8,128)(2,1)S(1)} %all_to_all.16.got_ref, f32[4,64,256]{2,1,0:T(8,128)S(1)} %get-tuple-element.35.acts_ref, bf16[2,40,512]{2,1,0:T(8,128)(2,1)S(1)} %bitcast.15, f32[4,64,128]{2,1,0:T(8,128)S(1)} %get-tuple-element.32.columns, ...), custom_call_target="tpu_custom_call" | custom-call | flops 2000000000 | bytes 4000000 | tf_op jit(solution)/shard_map/pallas_call | solution.py:780
  45.1 11.2 %all_to_all.17.got_ref = bf16[16,40,128]{2,1,0:T(8,128)(2,1)S(1)} all-to-all(bf16[16,40,128]{2,1,0:T(8,128)(2,1)S(1)} %shard_map.132), channel_id=1, replica_groups=mesh['dp'=2,'pairs'=2,'member'=2,'rows'=4] {'pairs','member','rows'}, dimensions={0} | all-to-all | bytes 327680 | tf_op jit(solution)/shard_map/all_to_all | solution.py:792
  56.3 0.5 shard_map.133
  56.8 1.8 %all-gather.1 = f32[16,512]{1,0:T(8,128)S(1)} all-gather(f32[8,512]{1,0:T(8,128)S(1)} %get-tuple-element.38), channel_id=3, replica_groups=mesh['dp'=2,'pairs'=2,'member'=2,'rows'=4] {'dp'}, dimensions={0}, use_global_device_ids=true | all-gather | bytes 49152 | tf_op jit(solution)/shard_map/all_gather | solution.py:803
  58.6 0.7 %shard_map.134 = (bf16[128,512]{1,0:T(8,128)(2,1)}, f32[1,512]{1,0:T(1,128)}, f32[1,512]{1,0:T(1,128)}, f32[1,512]{1,0:T(1,128)}, f32[1,512]{1,0:T(1,128)}) custom-call(f32[2,8,512]{2,1,0:T(8,128)S(1)} %bitcast.16, bf16[128,512]{1,0:T(8,128)(2,1)S(1)} %get-tuple-element.39.result_ref), custom_call_target="tpu_custom_call" | custom-call | flops 2000000000 | bytes 4000000 | tf_op jit(solution)/shard_map/pallas_call | solution.py:804
Async XLA Ops:
  1.6 22.5 %copy-start = (bf16[27,128,512]{2,1,0:T(8,128)(2,1)S(1)}, bf16[27,128,512]{2,1,0:T(8,128)(2,1)}, u32[]{:S(2)}) copy-start(bf16[27,128,512]{2,1,0:T(8,128)(2,1)} %weights.2) | copy-start | bytes 10616836
  1.6 22.5 %copy-start.2 = (f32[512]{0:T(512)S(1)}, f32[512]{0:T(512)}, u32[]{:S(2)}) copy-start(f32[512]{0:T(512)} %param.15) | copy-start | bytes 6148
  1.6 22.5 %copy-start.3 = (f32[512]{0:T(512)S(1)}, f32[512]{0:T(512)}, u32[]{:S(2)}) copy-start(f32[512]{0:T(512)} %param.16) | copy-start | bytes 6148
  1.6 22.5 %copy-start.4 = (f32[512]{0:T(512)S(1)}, f32[512]{0:T(512)}, u32[]{:S(2)}) copy-start(f32[512]{0:T(512)} %param.13) | copy-start | bytes 6148
  1.6 22.5 %copy-start.5 = (f32[512]{0:T(512)S(1)}, f32[512]{0:T(512)}, u32[]{:S(2)}) copy-start(f32[512]{0:T(512)} %param.12) | copy-start | bytes 6148
  30.0 13.4 %copy-start.1 = (bf16[27,128,512]{2,1,0:T(8,128)(2,1)S(1)}, bf16[27,128,512]{2,1,0:T(8,128)(2,1)}, u32[]{:S(2)}) copy-start(bf16[27,128,512]{2,1,0:T(8,128)(2,1)} %weights.3) | copy-start | bytes 10616836

commit v20 on v19

--- a/solution.py
+++ b/solution.py
@@ -511,7 +511,7 @@
         at = half * 256
         border = sent[:, 512 + half * 128 : 640 + half * 128]
         border = jnp.where(low, border[: sub // 2], border[sub // 2 :])
-        for dest in range(half, plan.count, 2):
+        for dest in [f * plan.nr + r for f in range(half, plan.nf, 2) for r in range(plan.nr)]:
             out_ref[dest, 0:sub, :] = sent[:, at : at + 128]
             out_ref[dest, sub : 2 * sub, :] = sent[:, at + 128 : at + 256]
             out_ref[dest, 2 * sub : 2 * sub + sub // 2, :] = border
@@ -566,16 +566,18 @@
     w = plan.w // 2
     lines = plan.places // plan.w
     places = lines * w
-    for k in range(2):
-        source[:, k * 128 : (k + 1) * 128] = got_ref[:, k * sub : (k + 1) * sub, :].reshape(plan.channels, 128)
+    starts = [s % nr * plan.slice_width + s // nr * sub for s in range(plan.count)]
+    for s, at in enumerate(starts):
+        for k in range(2):
+            source[at : at + sub, k * 128 : (k + 1) * 128] = got_ref[s, k * sub : (k + 1) * sub, :]
     packed = got_ref[:, wide : wide + sub // 2, :].reshape(plan.count * sub // 2, 128)
     shape = (128, places)
     beside = lanes_at(shape, 1) == lanes_at(shape, 0) % lines * w + (1 - member) * (w - 1)
     for k in range(2):
         here = one_hot(beside & (lanes_at(shape, 0) // lines == k))
         found = one_hot_dot(packed, here, ((1,), (0,))).astype(jnp.bfloat16)
-        for s in range(plan.count):
-            border[s * sub + k * (sub // 2) : s * sub + (k + 1) * (sub // 2), :] = found[
+        for s, at in enumerate(starts):
+            border[at + k * (sub // 2) : at + (k + 1) * (sub // 2), :] = found[
                 s * (sub // 2) : (s + 1) * (sub // 2)
             ]
     image = plan.image // 2
@@ -776,7 +778,7 @@
         compiler_params=LIMIT,
         cost_estimate=COST,
     )(mine, both, held, inv_std, columns, by_column)
-    spread = lax.all_to_all(quartered, BLOCK, 0, 0)
+    spread = lax.all_to_all(quartered, BACK_BLOCK, 0, 0)
     sent = pl.pallas_call(
         functools.partial(fine_kernel, plan),
         out_shape=shape_of((count, sub + 8, 128), bf16),

time: 59.6 us -> 59.6 us (level)
    all_to_all x1, blocking collectives: 13 us -> 13.8 us  [fast_shards(): spread = lax.all_to_all(quartered, BACK_BLOCK, 0, 0)]
    all_to_all x1, blocking collectives: 11.2 us -> 10.4 us  [fast_shards(): back = lax.all_to_all(sent, BACK_BLOCK, 0, 0)]
where the time goes in v20:
time: 59.6 us; the launch traced here: 59.4 us
  blocking collectives  52.9 us (89%)
  Pallas kernels  5.71 us (10%)
  between operations  0.74 us (1%)
    all_to_all x1, blocking collectives, fast_shards(): got = lax.all_to_all(packed, BLOCK, 0, 0)  22.1 us
    all_to_all x1, blocking collectives, fast_shards(): spread = lax.all_to_all(quartered, BACK_BLOCK, 0, 0)  13.8 us
    all_to_all x1, blocking collectives, fast_shards(): back = lax.all_to_all(sent, BACK_BLOCK, 0, 0)  10.4 us
    all_gather x1, blocking collectives, fast_shards(): both = lax.all_gather(theirs, 'member')  4.68 us
    all_gather x1, blocking collectives, fast_shards(): both = lax.all_gather(sums, 'dp')  1.83 us
    pallas_call x1, Pallas kernels, fast_shards(): pl.pallas_call(functools.partial(fine_kernel, plan), out_shape=shape_of((...  1.64 us
    pallas_call x1, Pallas kernels, fast_shards(): pl.pallas_call(functools.partial(coarse_kernel, plan), out_shape=(shape_o...  1.24 us

profile of v20, /device:TPU:0, one launch (start us, length us, event | category | flops | bytes accessed | tf_op | source)
XLA Modules:
  0.0 59.4 jit_solution(13487248322151043090)
XLA Ops:
  0.6 0.9 %shard_map.128 = (bf16[32,512]{1,0:T(8,128)(2,1)S(1)}, bf16[32,512]{1,0:T(8,128)(2,1)S(1)}, bf16[128,512]{1,0:T(8,128)(2,1)S(1)}) custom-call(bf16[32,512]{1,0:T(8,128)(2,1)} %bitcast.23, bf16[32,512]{1,0:T(8,128)(2,1)} %bitcast.24, bf16[128,512]{1,0:T(8,128)(2,1)} %bitcast.22), custom_call_target="tpu_custom_call" | custom-call | tf_op jit(solution)/shard_map/pallas_call | solution.py:732
  1.6 0.0 copy-start
  1.6 0.0 copy-start.2
  1.6 0.0 copy-start.3
  1.6 0.0 copy-start.4
  1.6 0.0 copy-start.5
  1.6 0.3 shard_map.129
  2.0 22.1 %all_to_all.15.got_ref = bf16[16,112,128]{2,1,0:T(8,128)(2,1)S(1)} all-to-all(bf16[16,112,128]{2,1,0:T(8,128)(2,1)S(1)} %shard_map.129), channel_id=1, replica_groups=mesh['dp'=2,'pairs'=2,'member'=2,'rows'=4] {'rows','pairs','member'}, dimensions={0} | all-to-all | bytes 917504 | tf_op jit(solution)/shard_map/all_to_all | solution.py:749
  24.1 0.0 copy-done
  24.1 0.0 copy-done.2
  24.1 0.0 copy-done.3
  24.1 0.0 copy-done.4
  24.1 0.0 copy-done.5
  24.1 1.2 %shard_map.130 = (f32[32,512]{1,0:T(8,128)S(1)}, bf16[40,512]{1,0:T(8,128)(2,1)S(1)}, f32[3,32,512]{2,1,0:T(8,128)S(1)}, f32[32,128]{1,0:T(8,128)S(1)}, f32[4,64...) custom-call(bf16[16,112,128]{2,1,0:T(8,128)(2,1)S(1)} %all_to_all.15, ...), custom_call_target="tpu_custom_call" | custom-call | flops 2000000000 | bytes 4000000 | tf_op jit(solution)/shard_map/pallas_call | solution.py:750
  25.4 4.7 %all-gather = bf16[80,512]{1,0:T(8,128)(2,1)S(1)} all-gather(bf16[40,512]{1,0:T(8,128)(2,1)S(1)} %get-tuple-element.29), channel_id=2, replica_groups=mesh['dp'=2,'pairs'=2,'member'=2,'rows'=4] {'member'}, dimensions={0}, use_global_device_ids=true | all-gather | bytes 122880 | tf_op jit(solution)/shard_map/all_gather | solution.py:772
  30.0 0.0 copy-start.1
  30.0 0.4 shard_map.131
  30.4 13.8 %all_to_all.16.got_ref = bf16[16,80,128]{2,1,0:T(8,128)(2,1)S(1)} all-to-all(bf16[16,80,128]{2,1,0:T(8,128)(2,1)S(1)} %get-tuple-element.34), channel_id=1, replica_groups=mesh['dp'=2,'pairs'=2,'member'=2,'rows'=4] {'pairs','member','rows'}, dimensions={0} | all-to-all | bytes 655360 | tf_op jit(solution)/shard_map/all_to_all | solution.py:781
  44.3 0.0 copy-done.1
  44.3 1.6 %shard_map.132 = bf16[16,40,128]{2,1,0:T(8,128)(2,1)S(1)} custom-call(bf16[16,80,128]{2,1,0:T(8,128)(2,1)S(1)} %all_to_all.16.got_ref, f32[4,64,256]{2,1,0:T(8,128)S(1)} %get-tuple-element.35.acts_ref, bf16[2,40,512]{2,1,0:T(8,128)(2,1)S(1)} %bitcast.15, f32[4,64,128]{2,1,0:T(8,128)S(1)} %get-tuple-element.32.columns, ...), custom_call_target="tpu_custom_call" | custom-call | flops 2000000000 | bytes 4000000 | tf_op jit(solution)/shard_map/pallas_call | solution.py:782
  45.9 10.4 %all_to_all.17.got_ref = bf16[16,40,128]{2,1,0:T(8,128)(2,1)S(1)} all-to-all(bf16[16,40,128]{2,1,0:T(8,128)(2,1)S(1)} %shard_map.132), channel_id=1, replica_groups=mesh['dp'=2,'pairs'=2,'member'=2,'rows'=4] {'pairs','member','rows'}, dimensions={0} | all-to-all | bytes 327680 | tf_op jit(solution)/shard_map/all_to_all | solution.py:794
  56.4 0.5 shard_map.133
  56.9 1.8 %all-gather.1 = f32[16,512]{1,0:T(8,128)S(1)} all-gather(f32[8,512]{1,0:T(8,128)S(1)} %get-tuple-element.38), channel_id=3, replica_groups=mesh['dp'=2,'pairs'=2,'member'=2,'rows'=4] {'dp'}, dimensions={0}, use_global_device_ids=true | all-gather | bytes 49152 | tf_op jit(solution)/shard_map/all_gather | solution.py:805
  58.7 0.7 %shard_map.134 = (bf16[128,512]{1,0:T(8,128)(2,1)}, f32[1,512]{1,0:T(1,128)}, f32[1,512]{1,0:T(1,128)}, f32[1,512]{1,0:T(1,128)}, f32[1,512]{1,0:T(1,128)}) custom-call(f32[2,8,512]{2,1,0:T(8,128)S(1)} %bitcast.16, bf16[128,512]{1,0:T(8,128)(2,1)S(1)} %get-tuple-element.39.result_ref), custom_call_target="tpu_custom_call" | custom-call | flops 2000000000 | bytes 4000000 | tf_op jit(solution)/shard_map/pallas_call | solution.py:806
Async XLA Ops:
  1.6 22.5 %copy-start = (bf16[27,128,512]{2,1,0:T(8,128)(2,1)S(1)}, bf16[27,128,512]{2,1,0:T(8,128)(2,1)}, u32[]{:S(2)}) copy-start(bf16[27,128,512]{2,1,0:T(8,128)(2,1)} %weights.2) | copy-start | bytes 10616836
  1.6 22.5 %copy-start.2 = (f32[512]{0:T(512)S(1)}, f32[512]{0:T(512)}, u32[]{:S(2)}) copy-start(f32[512]{0:T(512)} %param.15) | copy-start | bytes 6148
  1.6 22.5 %copy-start.3 = (f32[512]{0:T(512)S(1)}, f32[512]{0:T(512)}, u32[]{:S(2)}) copy-start(f32[512]{0:T(512)} %param.16) | copy-start | bytes 6148
  1.6 22.5 %copy-start.4 = (f32[512]{0:T(512)S(1)}, f32[512]{0:T(512)}, u32[]{:S(2)}) copy-start(f32[512]{0:T(512)} %param.13) | copy-start | bytes 6148
  1.6 22.5 %copy-start.5 = (f32[512]{0:T(512)S(1)}, f32[512]{0:T(512)}, u32[]{:S(2)}) copy-start(f32[512]{0:T(512)} %param.12) | copy-start | bytes 6148
  30.0 14.3 %copy-start.1 = (bf16[27,128,512]{2,1,0:T(8,128)(2,1)S(1)}, bf16[27,128,512]{2,1,0:T(8,128)(2,1)}, u32[]{:S(2)}) copy-start(bf16[27,128,512]{2,1,0:T(8,128)(2,1)} %weights.3) | copy-start | bytes 10616836

commit v21 on v19

--- a/solution.py
+++ b/solution.py
@@ -322,8 +322,7 @@
         self.chunks = self.channels // 128
         self.acts_at = self.chunks // 2 * self.local
         self.packed_at = self.acts_at + self.sub
-        self.cot_at = self.packed_at + 8
-        self.block_rows = self.cot_at + 8
+        self.block_rows = self.packed_at + 16
         self.fits = (
             self.sub == 32
             and self.slice_width == 128
@@ -372,9 +371,10 @@
     halves = one_hot_dot(acts, orders, ((0,), (0,))).astype(jnp.bfloat16)
     halves = [halves[:, :128], halves[:, 128:]]
     small = one_hot_dot(jnp.concatenate([coarse_ref[...], g_ref[...]], axis=0), repeated, ((0,), (0,)))
-    for k, at in enumerate((plan.packed_at, plan.cot_at)):
-        rows_of = jnp.where(quarter, small[:, k * 128 : (k + 1) * 128], 0.0).reshape(plan.count, 4, 8, 128)
-        out_ref[:, at : at + 8, :] = jnp.sum(rows_of, axis=1).astype(jnp.bfloat16)
+    rows_of = [
+        jnp.sum(jnp.where(quarter, small[:, k : k + 128], 0.0).reshape(plan.count, 4, 8, 128), axis=1) for k in (0, 128)
+    ]
+    out_ref[:, plan.packed_at : plan.block_rows, :] = jnp.concatenate(rows_of, axis=1).astype(jnp.bfloat16)
     low = lanes_at((sub, 128), 1) < 64
     for s_r in range(plan.nr):
         for s_f in range(plan.nf):
@@ -467,12 +467,9 @@
     one, two = total(parts), total([part * part for part in parts])
     stats = terms(as_row(one) + pltpu.roll(as_row(two), 64, 1), 3)
     stats = jnp.concatenate(stats + [jnp.zeros_like(stats[0])] * 5, axis=0).astype(jnp.bfloat16)
-    small = [by_frame_device(plan, got_ref, at, 8) for at in (plan.packed_at, plan.cot_at)]
-    merged = one_hot_dot(jnp.concatenate(small, axis=0), order[...], ((1,), (0,)))
-    rows_of = 8 * nf
-    values, cot = [
-        jnp.concatenate(in_places(plan, merged[k * rows_of : (k + 1) * rows_of], 8), axis=0) for k in range(2)
-    ]
+    merged = one_hot_dot(by_frame_device(plan, got_ref, plan.packed_at, 16), order[...], ((1,), (0,)))
+    unpacked = in_places(plan, merged, 16)
+    values, cot = [jnp.concatenate([part[k : k + 8] for part in unpacked], axis=0) for k in (0, 8)]
     gain, bias = columns[0][0:sub, 0:1], columns[1][0:sub, 0:1]
     entries = plan.places * plan.group_width
     mean, inv_std = statistics(total([values]), total([values * values]), entries, plan.group_width)
@@ -616,8 +613,10 @@
     one = total(pre)
     two = total([a * b for a, b in zip(pre, normed)])
     cot = source[pl.ds(pl.multiple_of(r * plan.slice_width + pair * wide, wide), wide), :].astype(jnp.float32)
-    scale = inv_std * gain
-    stacked = halves_from(plan, [cot + scale * part for part in pre]).astype(jnp.bfloat16)
+    group_one = in_groups(gain * one, plan.group_width) * (2.0 / entries)
+    group_two = in_groups(gain * two, plan.group_width) * (2.0 / entries)
+    grads = [cot + inv_std * (gain * part - group_one - unit * group_two) for part, unit in zip(pre, normed)]
+    stacked = halves_from(plan, grads).astype(jnp.bfloat16)
     sent = one_hot_dot(stacked, order[...], ((1,), (1,))).astype(jnp.bfloat16)
     coarse = sums_ref[0:1] + pltpu.roll(sums_ref[1:2], sub, 1)
     coded = (
@@ -638,18 +637,22 @@
     low_row = lanes_at((1, 128), 1) < 64
     first_row = lanes_at((1, 128), 1) < sub
     source = []
-    fine, coarse, moments = [[], []], [[], []], [[], []]
+    fine, apart, coarse, moments = [[], []], [[], []], [[], []], [[], []]
     for s_r in range(nr):
         ones, twos, c_ones, c_twos, invs, means = [], [], 0.0, 0.0, [], []
+        apart_ones, apart_twos = [], []
         for pair in range(nf // 2):
             at = 2 * pair * nr + s_r
             left, right = [got_ref[at + k * nr, 0:sub, :].astype(jnp.float32) for k in range(2)]
             source.append(jnp.where(low, left, pltpu.roll(right, 64, 1)))
             source.append(jnp.where(low, pltpu.roll(left, 64, 1), right))
             coded = [got_ref[at + k * nr, sub : sub + 8, :].astype(jnp.float32) for k in range(2)]
-            sums = coded[0][0:1] + coded[0][1:2] + coded[1][0:1] + coded[1][1:2]
+            halves = [part[0:1] + part[1:2] for part in coded]
+            sums, differences = halves[0] + halves[1], halves[1] - halves[0]
             ones.append(sums if pair == 0 else pltpu.roll(sums, 64, 1))
             twos.append(pltpu.roll(sums, 64, 1) if pair == 0 else sums)
+            apart_ones.append(differences if pair == 0 else pltpu.roll(differences, 64, 1))
+            apart_twos.append(pltpu.roll(differences, 64, 1) if pair == 0 else differences)
             both = coded[0][4:5] + coded[0][5:6] + coded[0][6:7]
             invs.append(both if pair == 0 else pltpu.roll(both, 64, 1))
             means.append(pltpu.roll(both, 64, 1) if pair == 0 else both)
@@ -662,19 +665,25 @@
                 c_twos = c_twos + (pltpu.roll(c_two, to, 1) if to else c_two)
         fine[0].append(jnp.where(low_row, ones[0], ones[1]))
         fine[1].append(jnp.where(low_row, twos[0], twos[1]))
+        apart[0].append(jnp.where(low_row, apart_ones[0], apart_ones[1]))
+        apart[1].append(jnp.where(low_row, apart_twos[0], apart_twos[1]))
         moments[0].append(jnp.where(low_row, invs[0], invs[1]))
         moments[1].append(jnp.where(low_row, means[0], means[1]))
         coarse[0].append(c_ones)
         coarse[1].append(c_twos)
-    one, two, inv_std, mean, c_one, c_two = [jnp.concatenate(part, axis=1) for part in fine + moments + coarse]
+    one, two, inv_std, mean, c_one, c_two, apart_one, apart_two = [
+        jnp.concatenate(part, axis=1) for part in fine + moments + coarse + apart
+    ]
     source = jnp.concatenate(source, axis=0).astype(jnp.bfloat16)
     result = one_hot_dot(pixel_order(plan, False), source, ((1,), (1,)))
     gain = gain_ref[...]
     entries = 4 * plan.places * plan.group_width
-    group_one = in_lane_groups(gain * one, plan.group_width) / entries
-    group_two = in_lane_groups(gain * two, plan.group_width) / entries
+    group_one = in_lane_groups(gain * apart_one, plan.group_width) / entries
+    group_two = in_lane_groups(gain * apart_two, plan.group_width) / entries
     normed = (acts_ref[...].astype(jnp.float32) - mean) * inv_std
-    out_ref[...] = (result - inv_std * (group_one + normed * group_two)).astype(jnp.bfloat16)
+    half = lanes_at((4 * plan.local, 1), 0) // plan.w % 2
+    signed = jnp.where(half == 0, inv_std, -inv_std)
+    out_ref[...] = (result - signed * (group_one + normed * group_two)).astype(jnp.bfloat16)
     sums_ref[...] = jnp.concatenate([one, two, c_one, c_two] + [jnp.zeros_like(one)] * 4, axis=0)
 
 

time: 59.6 us -> 59.9 us (level)
  no operation moved by 1% of the time
where the time goes in v21:
time: 59.9 us; the launch traced here: 59.6 us
  blocking collectives  52.8 us (88%)
  Pallas kernels  6.02 us (10%)
  between operations  0.74 us (1%)
    all_to_all x1, blocking collectives, fast_shards(): got = lax.all_to_all(packed, BLOCK, 0, 0)  22.1 us
    all_to_all x1, blocking collectives, fast_shards(): spread = lax.all_to_all(quartered, BLOCK, 0, 0)  13 us
    all_to_all x1, blocking collectives, fast_shards(): back = lax.all_to_all(sent, BACK_BLOCK, 0, 0)  11.2 us
    all_gather x1, blocking collectives, fast_shards(): both = lax.all_gather(theirs, 'member')  4.68 us
    pallas_call x1, Pallas kernels, fast_shards(): pl.pallas_call(functools.partial(fine_kernel, plan), out_shape=shape_of((...  1.92 us
    all_gather x1, blocking collectives, fast_shards(): both = lax.all_gather(sums, 'dp')  1.83 us
    pallas_call x1, Pallas kernels, fast_shards(): pl.pallas_call(functools.partial(coarse_kernel, plan), out_shape=(shape_o...  1.25 us

profile of v21, /device:TPU:0, one launch (start us, length us, event | category | flops | bytes accessed | tf_op | source)
XLA Modules:
  0.0 59.6 jit_solution(11042235687965407076)
XLA Ops:
  0.6 0.9 %shard_map.128 = (bf16[32,512]{1,0:T(8,128)(2,1)S(1)}, bf16[32,512]{1,0:T(8,128)(2,1)S(1)}, bf16[128,512]{1,0:T(8,128)(2,1)S(1)}) custom-call(bf16[32,512]{1,0:T(8,128)(2,1)} %bitcast.23, bf16[32,512]{1,0:T(8,128)(2,1)} %bitcast.24, bf16[128,512]{1,0:T(8,128)(2,1)} %bitcast.22), custom_call_target="tpu_custom_call" | custom-call | tf_op jit(solution)/shard_map/pallas_call | solution.py:739
  1.6 0.0 copy-start
  1.6 0.0 copy-start.2
  1.6 0.0 copy-start.3
  1.6 0.0 copy-start.4
  1.6 0.0 copy-start.5
  1.6 0.3 shard_map.129
  2.0 22.1 %all_to_all.15.got_ref = bf16[16,112,128]{2,1,0:T(8,128)(2,1)S(1)} all-to-all(bf16[16,112,128]{2,1,0:T(8,128)(2,1)S(1)} %shard_map.129), channel_id=1, replica_groups=mesh['dp'=2,'pairs'=2,'member'=2,'rows'=4] {'rows','pairs','member'}, dimensions={0} | all-to-all | bytes 917504 | tf_op jit(solution)/shard_map/all_to_all | solution.py:756
  24.1 0.0 copy-done
  24.1 0.0 copy-done.2
  24.1 0.0 copy-done.3
  24.1 0.0 copy-done.4
  24.1 0.0 copy-done.5
  24.1 1.3 %shard_map.130 = (f32[32,512]{1,0:T(8,128)S(1)}, bf16[40,512]{1,0:T(8,128)(2,1)S(1)}, f32[3,32,512]{2,1,0:T(8,128)S(1)}, f32[32,128]{1,0:T(8,128)S(1)}, f32[4,64...) custom-call(bf16[16,112,128]{2,1,0:T(8,128)(2,1)S(1)} %all_to_all.15, ...), custom_call_target="tpu_custom_call" | custom-call | flops 2000000000 | bytes 4000000 | tf_op jit(solution)/shard_map/pallas_call | solution.py:757
  25.4 4.7 %all-gather = bf16[80,512]{1,0:T(8,128)(2,1)S(1)} all-gather(bf16[40,512]{1,0:T(8,128)(2,1)S(1)} %get-tuple-element.29), channel_id=2, replica_groups=mesh['dp'=2,'pairs'=2,'member'=2,'rows'=4] {'member'}, dimensions={0}, use_global_device_ids=true | all-gather | bytes 122880 | tf_op jit(solution)/shard_map/all_gather | solution.py:779
  30.1 0.0 copy-start.1
  30.1 0.4 shard_map.131
  30.5 13.0 %all_to_all.16.got_ref = bf16[16,80,128]{2,1,0:T(8,128)(2,1)S(1)} all-to-all(bf16[16,80,128]{2,1,0:T(8,128)(2,1)S(1)} %get-tuple-element.34), channel_id=1, replica_groups=mesh['dp'=2,'pairs'=2,'member'=2,'rows'=4] {'rows','pairs','member'}, dimensions={0} | all-to-all | bytes 655360 | tf_op jit(solution)/shard_map/all_to_all | solution.py:788
  43.4 0.0 copy-done.1
  43.4 1.9 %shard_map.132 = bf16[16,40,128]{2,1,0:T(8,128)(2,1)S(1)} custom-call(bf16[16,80,128]{2,1,0:T(8,128)(2,1)S(1)} %all_to_all.16.got_ref, f32[4,64,256]{2,1,0:T(8,128)S(1)} %get-tuple-element.35.acts_ref, bf16[2,40,512]{2,1,0:T(8,128)(2,1)S(1)} %bitcast.15, f32[4,64,128]{2,1,0:T(8,128)S(1)} %get-tuple-element.32.columns, ...), custom_call_target="tpu_custom_call" | custom-call | flops 2000000000 | bytes 4000000 | tf_op jit(solution)/shard_map/pallas_call | solution.py:789
  45.4 11.2 %all_to_all.17.got_ref = bf16[16,40,128]{2,1,0:T(8,128)(2,1)S(1)} all-to-all(bf16[16,40,128]{2,1,0:T(8,128)(2,1)S(1)} %shard_map.132), channel_id=1, replica_groups=mesh['dp'=2,'pairs'=2,'member'=2,'rows'=4] {'pairs','member','rows'}, dimensions={0} | all-to-all | bytes 327680 | tf_op jit(solution)/shard_map/all_to_all | solution.py:801
  56.6 0.5 shard_map.133
  57.1 1.8 %all-gather.1 = f32[16,512]{1,0:T(8,128)S(1)} all-gather(f32[8,512]{1,0:T(8,128)S(1)} %get-tuple-element.38), channel_id=3, replica_groups=mesh['dp'=2,'pairs'=2,'member'=2,'rows'=4] {'dp'}, dimensions={0}, use_global_device_ids=true | all-gather | bytes 49152 | tf_op jit(solution)/shard_map/all_gather | solution.py:812
  58.9 0.7 %shard_map.134 = (bf16[128,512]{1,0:T(8,128)(2,1)}, f32[1,512]{1,0:T(1,128)}, f32[1,512]{1,0:T(1,128)}, f32[1,512]{1,0:T(1,128)}, f32[1,512]{1,0:T(1,128)}) custom-call(f32[2,8,512]{2,1,0:T(8,128)S(1)} %bitcast.16, bf16[128,512]{1,0:T(8,128)(2,1)S(1)} %get-tuple-element.39.result_ref), custom_call_target="tpu_custom_call" | custom-call | flops 2000000000 | bytes 4000000 | tf_op jit(solution)/shard_map/pallas_call | solution.py:813
Async XLA Ops:
  1.6 22.5 %copy-start = (bf16[27,128,512]{2,1,0:T(8,128)(2,1)S(1)}, bf16[27,128,512]{2,1,0:T(8,128)(2,1)}, u32[]{:S(2)}) copy-start(bf16[27,128,512]{2,1,0:T(8,128)(2,1)} %weights.2) | copy-start | bytes 10616836
  1.6 22.5 %copy-start.2 = (f32[512]{0:T(512)S(1)}, f32[512]{0:T(512)}, u32[]{:S(2)}) copy-start(f32[512]{0:T(512)} %param.15) | copy-start | bytes 6148
  1.6 22.5 %copy-start.3 = (f32[512]{0:T(512)S(1)}, f32[512]{0:T(512)}, u32[]{:S(2)}) copy-start(f32[512]{0:T(512)} %param.16) | copy-start | bytes 6148
  1.6 22.5 %copy-start.4 = (f32[512]{0:T(512)S(1)}, f32[512]{0:T(512)}, u32[]{:S(2)}) copy-start(f32[512]{0:T(512)} %param.13) | copy-start | bytes 6148
  1.6 22.5 %copy-start.5 = (f32[512]{0:T(512)S(1)}, f32[512]{0:T(512)}, u32[]{:S(2)}) copy-start(f32[512]{0:T(512)} %param.12) | copy-start | bytes 6148
  30.1 13.4 %copy-start.1 = (bf16[27,128,512]{2,1,0:T(8,128)(2,1)S(1)}, bf16[27,128,512]{2,1,0:T(8,128)(2,1)}, u32[]{:S(2)}) copy-start(bf16[27,128,512]{2,1,0:T(8,128)(2,1)} %weights.3) | copy-start | bytes 10616836

commit v22 on v19

--- a/solution.py
+++ b/solution.py
@@ -487,9 +487,9 @@
     conv_ref[...] = by_col[1] + moved(by_col[0], 1, has_right) + moved(by_col[2], -1, has_left)
     mine_ref[...] = conv_ref[pl.ds(pl.multiple_of(member * sub, sub), sub), :]
     theirs = conv_ref[pl.ds(pl.multiple_of((1 - member) * sub, sub), sub), :]
-    sent_ref[0:sub, :] = theirs.astype(jnp.bfloat16)
-    sent_ref[sub:, 0:128] = stats
-    sent_ref[sub:, 128:] = jnp.zeros((8, plan.places - 128), jnp.bfloat16)
+    sent_ref[0, 0:sub, :] = theirs.astype(jnp.bfloat16)
+    sent_ref[0, sub:, 0:128] = stats
+    sent_ref[0, sub:, 128:] = jnp.zeros((8, plan.places - 128), jnp.bfloat16)
 
 
 def quarter_kernel(plan, mine_ref, both_ref, held_ref, inv_ref, columns, by_column, out_ref, sums_ref):
@@ -675,7 +675,7 @@
     group_two = in_lane_groups(gain * two, plan.group_width) / entries
     normed = (acts_ref[...].astype(jnp.float32) - mean) * inv_std
     out_ref[...] = (result - inv_std * (group_one + normed * group_two)).astype(jnp.bfloat16)
-    sums_ref[...] = jnp.concatenate([one, two, c_one, c_two] + [jnp.zeros_like(one)] * 4, axis=0)
+    sums_ref[0] = jnp.concatenate([one, two, c_one, c_two] + [jnp.zeros_like(one)] * 4, axis=0)
 
 
 def total_kernel(scales, both_ref, result_ref, result_hbm, out_hbms, rows_ref, sems):
@@ -749,7 +749,7 @@
         functools.partial(coarse_kernel, plan),
         out_shape=(
             shape_of((sub, places), f32),
-            shape_of((sub + 8, places), bf16),
+            shape_of((1, sub + 8, places), bf16),
             shape_of((3, sub, places), f32),
             shape_of((sub, 128), f32),
             shape_of((4, 2 * sub, places // 2), f32),
@@ -767,7 +767,7 @@
         compiler_params=LIMIT,
         cost_estimate=COST,
     )(got, kernel_coarse, *rows)
-    both = lax.all_gather(theirs, "member")
+    both = lax.all_gather(theirs, "member", axis=0, tiled=True)
     quartered, coarse_sums = pl.pallas_call(
         functools.partial(quarter_kernel, plan),
         out_shape=(shape_of((count, 2 * sub + sub // 2, 128), bf16), shape_of((2, 128), f32)),
@@ -794,13 +794,13 @@
     fine_scale, coarse_scale = 1.0 / math.sqrt(4 * cells), 1.0 / math.sqrt(cells)
     out, sums = pl.pallas_call(
         functools.partial(spread_kernel, plan),
-        out_shape=(pltpu.VMEM((4 * local, channels), bf16), shape_of((8, channels), f32)),
+        out_shape=(pltpu.VMEM((4 * local, channels), bf16), shape_of((1, 8, channels), f32)),
         in_specs=in_vmem(3),
         out_specs=tuple(in_vmem(2)),
         compiler_params=LIMIT,
         cost_estimate=COST,
     )(back, acts, rows[2])
-    both = lax.all_gather(sums, "dp")
+    both = lax.all_gather(sums, "dp", axis=0, tiled=True)
     out, sums = pl.pallas_call(
         functools.partial(total_kernel, (fine_scale, fine_scale, coarse_scale, coarse_scale)),
         out_shape=(pltpu.HBM((4 * local, channels), bf16), (pltpu.HBM((1, channels), f32),) * 4),

time: 59.6 us -> 59.6 us (level)
  no operation moved by 1% of the time
where the time goes in v22:
time: 59.6 us; the launch traced here: 59.3 us
  blocking collectives  52.8 us (89%)
  Pallas kernels  5.71 us (10%)
  between operations  0.74 us (1%)
    all_to_all x1, blocking collectives, fast_shards(): got = lax.all_to_all(packed, BLOCK, 0, 0)  22.1 us
    all_to_all x1, blocking collectives, fast_shards(): spread = lax.all_to_all(quartered, BLOCK, 0, 0)  13 us
    all_to_all x1, blocking collectives, fast_shards(): back = lax.all_to_all(sent, BACK_BLOCK, 0, 0)  11.2 us
    all_gather x1, blocking collectives, fast_shards(): both = lax.all_gather(theirs, 'member', axis=0, tiled=True)  4.68 us
    all_gather x1, blocking collectives, fast_shards(): both = lax.all_gather(sums, 'dp', axis=0, tiled=True)  1.83 us
    pallas_call x1, Pallas kernels, fast_shards(): pl.pallas_call(functools.partial(fine_kernel, plan), out_shape=shape_of((...  1.64 us
    pallas_call x1, Pallas kernels, fast_shards(): pl.pallas_call(functools.partial(coarse_kernel, plan), out_shape=(shape_o...  1.24 us

profile of v22, /device:TPU:0, one launch (start us, length us, event | category | flops | bytes accessed | tf_op | source)
XLA Modules:
  0.0 59.3 jit_solution(13055943464490714167)
XLA Ops:
  0.6 0.9 %shard_map.128 = (bf16[32,512]{1,0:T(8,128)(2,1)S(1)}, bf16[32,512]{1,0:T(8,128)(2,1)S(1)}, bf16[128,512]{1,0:T(8,128)(2,1)S(1)}) custom-call(bf16[32,512]{1,0:T(8,128)(2,1)} %bitcast.18, bf16[32,512]{1,0:T(8,128)(2,1)} %bitcast.19, bf16[128,512]{1,0:T(8,128)(2,1)} %bitcast.17), custom_call_target="tpu_custom_call" | custom-call | tf_op jit(solution)/shard_map/pallas_call | solution.py:730
  1.6 0.0 copy-start
  1.6 0.0 copy-start.2
  1.6 0.0 copy-start.3
  1.6 0.0 copy-start.4
  1.6 0.0 copy-start.5
  1.6 0.3 shard_map.129
  2.0 22.1 %all_to_all.15.got_ref = bf16[16,112,128]{2,1,0:T(8,128)(2,1)S(1)} all-to-all(bf16[16,112,128]{2,1,0:T(8,128)(2,1)S(1)} %shard_map.129), channel_id=1, replica_groups=mesh['dp'=2,'pairs'=2,'member'=2,'rows'=4] {'rows','pairs','member'}, dimensions={0} | all-to-all | bytes 917504 | tf_op jit(solution)/shard_map/all_to_all | solution.py:747
  24.1 0.0 copy-done
  24.1 0.0 copy-done.2
  24.1 0.0 copy-done.3
  24.1 0.0 copy-done.4
  24.1 0.0 copy-done.5
  24.1 1.2 %shard_map.130 = (f32[32,512]{1,0:T(8,128)S(1)}, bf16[1,40,512]{2,1,0:T(8,128)(2,1)S(1)}, f32[3,32,512]{2,1,0:T(8,128)S(1)}, f32[32,128]{1,0:T(8,128)S(1)}, f32[...) custom-call(bf16[16,112,128]{2,1,0:T(8,128)(2,1)S(1)} %all_to_all.15, ...), custom_call_target="tpu_custom_call" | custom-call | flops 2000000000 | bytes 4000000 | tf_op jit(solution)/shard_map/pallas_call | solution.py:748
  25.4 4.7 %all_gather.6.both_ref = bf16[2,40,512]{2,1,0:T(8,128)(2,1)S(1)} all-gather(bf16[1,40,512]{2,1,0:T(8,128)(2,1)S(1)} %get-tuple-element.29), channel_id=1, replica_groups=mesh['dp'=2,'pairs'=2,'member'=2,'rows'=4] {'member'}, dimensions={0}, use_global_device_ids=true | all-gather | bytes 122880 | tf_op jit(solution)/shard_map/all_gather | solution.py:770
  30.0 0.0 copy-start.1
  30.0 0.4 shard_map.131
  30.4 13.0 %all_to_all.16.got_ref = bf16[16,80,128]{2,1,0:T(8,128)(2,1)S(1)} all-to-all(bf16[16,80,128]{2,1,0:T(8,128)(2,1)S(1)} %get-tuple-element.34), channel_id=1, replica_groups=mesh['dp'=2,'pairs'=2,'member'=2,'rows'=4] {'rows','pairs','member'}, dimensions={0} | all-to-all | bytes 655360 | tf_op jit(solution)/shard_map/all_to_all | solution.py:779
  43.4 0.0 copy-done.1
  43.4 1.6 %shard_map.132 = bf16[16,40,128]{2,1,0:T(8,128)(2,1)S(1)} custom-call(bf16[16,80,128]{2,1,0:T(8,128)(2,1)S(1)} %all_to_all.16.got_ref, f32[4,64,256]{2,1,0:T(8,128)S(1)} %get-tuple-element.35.acts_ref, bf16[2,40,512]{2,1,0:T(8,128)(2,1)S(1)} %all_gather.6.both_ref, f32[4,64,128]{2,1,0:T(8,128)S(1)} %get-tuple-element.32.columns, ...), custom_call_target="tpu_custom_call" | custom-call | flops 2000000000 | bytes 4000000 | tf_op jit(solution)/shard_map/pallas_call | solution.py:780
  45.1 11.2 %all_to_all.17.got_ref = bf16[16,40,128]{2,1,0:T(8,128)(2,1)S(1)} all-to-all(bf16[16,40,128]{2,1,0:T(8,128)(2,1)S(1)} %shard_map.132), channel_id=1, replica_groups=mesh['dp'=2,'pairs'=2,'member'=2,'rows'=4] {'pairs','member','rows'}, dimensions={0} | all-to-all | bytes 327680 | tf_op jit(solution)/shard_map/all_to_all | solution.py:792
  56.3 0.5 shard_map.133
  56.8 1.8 %all_gather.7.both_ref = f32[2,8,512]{2,1,0:T(8,128)S(1)} all-gather(f32[1,8,512]{2,1,0:T(8,128)S(1)} %get-tuple-element.38), channel_id=1, replica_groups=mesh['dp'=2,'pairs'=2,'member'=2,'rows'=4] {'dp'}, dimensions={0}, use_global_device_ids=true | all-gather | bytes 49152 | tf_op jit(solution)/shard_map/all_gather | solution.py:803
  58.6 0.7 %shard_map.134 = (bf16[128,512]{1,0:T(8,128)(2,1)}, f32[1,512]{1,0:T(1,128)}, f32[1,512]{1,0:T(1,128)}, f32[1,512]{1,0:T(1,128)}, f32[1,512]{1,0:T(1,128)}) custom-call(f32[2,8,512]{2,1,0:T(8,128)S(1)} %all_gather.7.both_ref, bf16[128,512]{1,0:T(8,128)(2,1)S(1)} %get-tuple-element.39.result_ref), custom_call_target="tpu_custom_call" | custom-call | flops 2000000000 | bytes 4000000 | tf_op jit(solution)/shard_map/pallas_call | solution.py:804
Async XLA Ops:
  1.6 22.5 %copy-start = (bf16[27,128,512]{2,1,0:T(8,128)(2,1)S(1)}, bf16[27,128,512]{2,1,0:T(8,128)(2,1)}, u32[]{:S(2)}) copy-start(bf16[27,128,512]{2,1,0:T(8,128)(2,1)} %weights.2) | copy-start | bytes 10616836
  1.6 22.5 %copy-start.2 = (f32[512]{0:T(512)S(1)}, f32[512]{0:T(512)}, u32[]{:S(2)}) copy-start(f32[512]{0:T(512)} %param.15) | copy-start | bytes 6148
  1.6 22.5 %copy-start.3 = (f32[512]{0:T(512)S(1)}, f32[512]{0:T(512)}, u32[]{:S(2)}) copy-start(f32[512]{0:T(512)} %param.16) | copy-start | bytes 6148
  1.6 22.5 %copy-start.4 = (f32[512]{0:T(512)S(1)}, f32[512]{0:T(512)}, u32[]{:S(2)}) copy-start(f32[512]{0:T(512)} %param.13) | copy-start | bytes 6148
  1.6 22.5 %copy-start.5 = (f32[512]{0:T(512)S(1)}, f32[512]{0:T(512)}, u32[]{:S(2)}) copy-start(f32[512]{0:T(512)} %param.12) | copy-start | bytes 6148
  30.0 13.4 %copy-start.1 = (bf16[27,128,512]{2,1,0:T(8,128)(2,1)S(1)}, bf16[27,128,512]{2,1,0:T(8,128)(2,1)}, u32[]{:S(2)}) copy-start(bf16[27,128,512]{2,1,0:T(8,128)(2,1)} %weights.3) | copy-start | bytes 10616836

commit v23 on v19

--- a/solution.py
+++ b/solution.py
@@ -486,10 +486,10 @@
         by_col.append(parts[1] + moved(parts[0], plan.w, has_down) + moved(parts[2], -plan.w, has_up))
     conv_ref[...] = by_col[1] + moved(by_col[0], 1, has_right) + moved(by_col[2], -1, has_left)
     mine_ref[...] = conv_ref[pl.ds(pl.multiple_of(member * sub, sub), sub), :]
-    theirs = conv_ref[pl.ds(pl.multiple_of((1 - member) * sub, sub), sub), :]
-    sent_ref[0:sub, :] = theirs.astype(jnp.bfloat16)
-    sent_ref[sub:, 0:128] = stats
-    sent_ref[sub:, 128:] = jnp.zeros((8, plan.places - 128), jnp.bfloat16)
+    for k in range(2):
+        sent_ref[k, 0:sub, :] = conv_ref[k * sub : (k + 1) * sub, :].astype(jnp.bfloat16)
+        sent_ref[k, sub:, 0:128] = stats
+        sent_ref[k, sub:, 128:] = jnp.zeros((8, plan.places - 128), jnp.bfloat16)
 
 
 def quarter_kernel(plan, mine_ref, both_ref, held_ref, inv_ref, columns, by_column, out_ref, sums_ref):
@@ -749,7 +749,7 @@
         functools.partial(coarse_kernel, plan),
         out_shape=(
             shape_of((sub, places), f32),
-            shape_of((sub + 8, places), bf16),
+            shape_of((2, sub + 8, places), bf16),
             shape_of((3, sub, places), f32),
             shape_of((sub, 128), f32),
             shape_of((4, 2 * sub, places // 2), f32),
@@ -767,7 +767,7 @@
         compiler_params=LIMIT,
         cost_estimate=COST,
     )(got, kernel_coarse, *rows)
-    both = lax.all_gather(theirs, "member")
+    both = lax.all_to_all(theirs, "member", 0, 0)
     quartered, coarse_sums = pl.pallas_call(
         functools.partial(quarter_kernel, plan),
         out_shape=(shape_of((count, 2 * sub + sub // 2, 128), bf16), shape_of((2, 128), f32)),

time: 59.6 us -> 61.3 us (1.029)
  blocking collectives: 52.8 us -> 54.6 us
    all_to_all x0 -> x1, blocking collectives: none -> 6.55 us  [fast_shards(): both = lax.all_to_all(theirs, 'member', 0, 0)]
    all_gather x1 -> x0, blocking collectives: 4.68 us -> none  [fast_shards(): both = lax.all_gather(theirs, 'member')]
where the time goes in v23:
time: 61.3 us; the launch traced here: 61.1 us
  blocking collectives  54.6 us (89%)
  Pallas kernels  5.71 us (9%)
  between operations  0.74 us (1%)
    all_to_all x1, blocking collectives, fast_shards(): got = lax.all_to_all(packed, BLOCK, 0, 0)  22.1 us
    all_to_all x1, blocking collectives, fast_shards(): spread = lax.all_to_all(quartered, BLOCK, 0, 0)  12.7 us
    all_to_all x1, blocking collectives, fast_shards(): back = lax.all_to_all(sent, BACK_BLOCK, 0, 0)  11.4 us
    all_to_all x1, blocking collectives, fast_shards(): both = lax.all_to_all(theirs, 'member', 0, 0)  6.55 us
    all_gather x1, blocking collectives, fast_shards(): both = lax.all_gather(sums, 'dp')  1.83 us
    pallas_call x1, Pallas kernels, fast_shards(): pl.pallas_call(functools.partial(fine_kernel, plan), out_shape=shape_of((...  1.64 us
    pallas_call x1, Pallas kernels, fast_shards(): pl.pallas_call(functools.partial(coarse_kernel, plan), out_shape=(shape_o...  1.24 us

profile of v23, /device:TPU:0, one launch (start us, length us, event | category | flops | bytes accessed | tf_op | source)
XLA Modules:
  0.0 61.1 jit_solution(668907017773504166)
XLA Ops:
  0.6 0.9 %shard_map.128 = (bf16[32,512]{1,0:T(8,128)(2,1)S(1)}, bf16[32,512]{1,0:T(8,128)(2,1)S(1)}, bf16[128,512]{1,0:T(8,128)(2,1)S(1)}) custom-call(bf16[32,512]{1,0:T(8,128)(2,1)} %bitcast.20, bf16[32,512]{1,0:T(8,128)(2,1)} %bitcast.21, bf16[128,512]{1,0:T(8,128)(2,1)} %bitcast.19), custom_call_target="tpu_custom_call" | custom-call | tf_op jit(solution)/shard_map/pallas_call | solution.py:730
  1.6 0.0 copy-start
  1.6 0.0 copy-start.2
  1.6 0.0 copy-start.3
  1.6 0.0 copy-start.4
  1.6 0.0 copy-start.5
  1.6 0.3 shard_map.129
  2.0 22.1 %all_to_all.20.got_ref = bf16[16,112,128]{2,1,0:T(8,128)(2,1)S(1)} all-to-all(bf16[16,112,128]{2,1,0:T(8,128)(2,1)S(1)} %shard_map.129), channel_id=1, replica_groups=mesh['dp'=2,'pairs'=2,'member'=2,'rows'=4] {'rows','pairs','member'}, dimensions={0} | all-to-all | bytes 917504 | tf_op jit(solution)/shard_map/all_to_all | solution.py:747
  24.1 0.0 copy-done
  24.1 0.0 copy-done.2
  24.1 0.0 copy-done.3
  24.1 0.0 copy-done.4
  24.1 0.0 copy-done.5
  24.1 1.2 %shard_map.130 = (f32[32,512]{1,0:T(8,128)S(1)}, bf16[2,40,512]{2,1,0:T(8,128)(2,1)S(1)}, f32[3,32,512]{2,1,0:T(8,128)S(1)}, f32[32,128]{1,0:T(8,128)S(1)}, f32[...) custom-call(bf16[16,112,128]{2,1,0:T(8,128)(2,1)S(1)} %all_to_all.20, ...), custom_call_target="tpu_custom_call" | custom-call | flops 2000000000 | bytes 4000000 | tf_op jit(solution)/shard_map/pallas_call | solution.py:748
  25.4 6.6 %all_to_all.21.both_ref = bf16[2,40,512]{2,1,0:T(8,128)(2,1)S(1)} all-to-all(bf16[2,40,512]{2,1,0:T(8,128)(2,1)S(1)} %get-tuple-element.29), channel_id=1, replica_groups=mesh['dp'=2,'pairs'=2,'member'=2,'rows'=4] {'member'}, dimensions={0} | all-to-all | bytes 163840 | tf_op jit(solution)/shard_map/all_to_all | solution.py:770
  31.9 0.0 copy-start.1
  31.9 0.4 shard_map.131
  32.3 12.7 %all_to_all.22.got_ref = bf16[16,80,128]{2,1,0:T(8,128)(2,1)S(1)} all-to-all(bf16[16,80,128]{2,1,0:T(8,128)(2,1)S(1)} %get-tuple-element.34), channel_id=1, replica_groups=mesh['dp'=2,'pairs'=2,'member'=2,'rows'=4] {'rows','pairs','member'}, dimensions={0} | all-to-all | bytes 655360 | tf_op jit(solution)/shard_map/all_to_all | solution.py:779
  45.0 0.0 copy-done.1
  45.0 1.6 %shard_map.132 = bf16[16,40,128]{2,1,0:T(8,128)(2,1)S(1)} custom-call(bf16[16,80,128]{2,1,0:T(8,128)(2,1)S(1)} %all_to_all.22.got_ref, f32[4,64,256]{2,1,0:T(8,128)S(1)} %get-tuple-element.35.acts_ref, bf16[2,40,512]{2,1,0:T(8,128)(2,1)S(1)} %all_to_all.21.both_ref, f32[4,64,128]{2,1,0:T(8,128)S(1)} %get-tuple-element.32.columns, ...), custom_call_target="tpu_custom_call" | custom-call | flops 2000000000 | bytes 4000000 | tf_op jit(solution)/shard_map/pallas_call | solution.py:780
  46.7 11.4 %all_to_all.23.got_ref = bf16[16,40,128]{2,1,0:T(8,128)(2,1)S(1)} all-to-all(bf16[16,40,128]{2,1,0:T(8,128)(2,1)S(1)} %shard_map.132), channel_id=1, replica_groups=mesh['dp'=2,'pairs'=2,'member'=2,'rows'=4] {'pairs','member','rows'}, dimensions={0} | all-to-all | bytes 327680 | tf_op jit(solution)/shard_map/all_to_all | solution.py:792
  58.1 0.5 shard_map.133
  58.5 1.8 %all-gather = f32[16,512]{1,0:T(8,128)S(1)} all-gather(f32[8,512]{1,0:T(8,128)S(1)} %get-tuple-element.38), channel_id=2, replica_groups=mesh['dp'=2,'pairs'=2,'member'=2,'rows'=4] {'dp'}, dimensions={0}, use_global_device_ids=true | all-gather | bytes 49152 | tf_op jit(solution)/shard_map/all_gather | solution.py:803
  60.4 0.7 %shard_map.134 = (bf16[128,512]{1,0:T(8,128)(2,1)}, f32[1,512]{1,0:T(1,128)}, f32[1,512]{1,0:T(1,128)}, f32[1,512]{1,0:T(1,128)}, f32[1,512]{1,0:T(1,128)}) custom-call(f32[2,8,512]{2,1,0:T(8,128)S(1)} %bitcast.13, bf16[128,512]{1,0:T(8,128)(2,1)S(1)} %get-tuple-element.39.result_ref), custom_call_target="tpu_custom_call" | custom-call | flops 2000000000 | bytes 4000000 | tf_op jit(solution)/shard_map/pallas_call | solution.py:804
Async XLA Ops:
  1.6 22.5 %copy-start = (bf16[27,128,512]{2,1,0:T(8,128)(2,1)S(1)}, bf16[27,128,512]{2,1,0:T(8,128)(2,1)}, u32[]{:S(2)}) copy-start(bf16[27,128,512]{2,1,0:T(8,128)(2,1)} %weights.2) | copy-start | bytes 10616836
  1.6 22.5 %copy-start.2 = (f32[512]{0:T(512)S(1)}, f32[512]{0:T(512)}, u32[]{:S(2)}) copy-start(f32[512]{0:T(512)} %param.15) | copy-start | bytes 6148
  1.6 22.5 %copy-start.3 = (f32[512]{0:T(512)S(1)}, f32[512]{0:T(512)}, u32[]{:S(2)}) copy-start(f32[512]{0:T(512)} %param.16) | copy-start | bytes 6148
  1.6 22.5 %copy-start.4 = (f32[512]{0:T(512)S(1)}, f32[512]{0:T(512)}, u32[]{:S(2)}) copy-start(f32[512]{0:T(512)} %param.13) | copy-start | bytes 6148
  1.6 22.5 %copy-start.5 = (f32[512]{0:T(512)S(1)}, f32[512]{0:T(512)}, u32[]{:S(2)}) copy-start(f32[512]{0:T(512)} %param.12) | copy-start | bytes 6148
  31.9 13.1 %copy-start.1 = (bf16[27,128,512]{2,1,0:T(8,128)(2,1)S(1)}, bf16[27,128,512]{2,1,0:T(8,128)(2,1)}, u32[]{:S(2)}) copy-start(bf16[27,128,512]{2,1,0:T(8,128)(2,1)} %weights.3) | copy-start | bytes 10616836

commit v24 on v19

--- a/solution.py
+++ b/solution.py
@@ -374,11 +374,13 @@
     small = one_hot_dot(jnp.concatenate([coarse_ref[...], g_ref[...]], axis=0), repeated, ((0,), (0,)))
     for k, at in enumerate((plan.packed_at, plan.cot_at)):
         rows_of = jnp.where(quarter, small[:, k * 128 : (k + 1) * 128], 0.0).reshape(plan.count, 4, 8, 128)
-        out_ref[:, at : at + 8, :] = jnp.sum(rows_of, axis=1).astype(jnp.bfloat16)
+        rows_of = jnp.sum(rows_of, axis=1).astype(jnp.bfloat16)
+        for c in range(plan.count):
+            out_ref[c % plan.nf * plan.nr + c // plan.nf, at : at + 8, :] = rows_of[c]
     low = lanes_at((sub, 128), 1) < 64
     for s_r in range(plan.nr):
         for s_f in range(plan.nf):
-            dest = s_r * plan.nf + s_f
+            dest = s_f * plan.nr + s_r
             first, half = s_r * plan.slice_width + s_f // 2 * 2 * sub, s_f % 2
             for k in range(chunks // 2):
                 at = (half * chunks // 2 + k) * 128
@@ -391,7 +393,7 @@
     return jnp.concatenate(
         [
             jnp.concatenate(
-                [got_ref[r * plan.nf + f, at : at + height, :] for r in range(plan.nr)], axis=1
+                [got_ref[f * plan.nr + r, at : at + height, :] for r in range(plan.nr)], axis=1
             )
             for f in range(plan.nf)
         ],
@@ -449,7 +451,7 @@
                 at = (s_f * tl + t) * plan.image + s_r * cells
                 for k in range(plan.chunks // 2):
                     source[at : at + cells, k * 128 : (k + 1) * 128] = got_ref[
-                        s_r * nf + s_f, k * local + t * cells : k * local + (t + 1) * cells, :
+                        s_f * nr + s_r, k * local + t * cells : k * local + (t + 1) * cells, :
                     ]
     source[plan.places :, :] = jnp.zeros((2 * plan.image, depth), jnp.bfloat16)
     products = sum(
@@ -744,7 +746,7 @@
         compiler_params=LIMIT,
         cost_estimate=COST,
     )(*fetched_of)
-    got = lax.all_to_all(packed, BLOCK, 0, 0)
+    got = lax.all_to_all(packed, BACK_BLOCK, 0, 0)
     mine, theirs, held, inv_std, fine_acts, columns, fine_order, by_column = pl.pallas_call(
         functools.partial(coarse_kernel, plan),
         out_shape=(

time: 59.6 us -> 59.9 us (level)
    all_to_all x1, blocking collectives: 22.1 us -> 23 us  [fast_shards(): got = lax.all_to_all(packed, BACK_BLOCK, 0, 0)]
where the time goes in v24:
time: 59.9 us; the launch traced here: 59.7 us
  blocking collectives  53.2 us (89%)
  Pallas kernels  5.71 us (10%)
  between operations  0.74 us (1%)
    all_to_all x1, blocking collectives, fast_shards(): got = lax.all_to_all(packed, BACK_BLOCK, 0, 0)  23 us
    all_to_all x1, blocking collectives, fast_shards(): spread = lax.all_to_all(quartered, BLOCK, 0, 0)  12.4 us
    all_to_all x1, blocking collectives, fast_shards(): back = lax.all_to_all(sent, BACK_BLOCK, 0, 0)  11.2 us
    all_gather x1, blocking collectives, fast_shards(): both = lax.all_gather(theirs, 'member')  4.68 us
    all_gather x1, blocking collectives, fast_shards(): both = lax.all_gather(sums, 'dp')  1.83 us
    pallas_call x1, Pallas kernels, fast_shards(): pl.pallas_call(functools.partial(fine_kernel, plan), out_shape=shape_of((...  1.64 us
    pallas_call x1, Pallas kernels, fast_shards(): pl.pallas_call(functools.partial(coarse_kernel, plan), out_shape=(shape_o...  1.24 us

profile of v24, /device:TPU:0, one launch (start us, length us, event | category | flops | bytes accessed | tf_op | source)
XLA Modules:
  0.0 59.7 jit_solution(17816404669398224030)
XLA Ops:
  0.6 0.9 %shard_map.128 = (bf16[32,512]{1,0:T(8,128)(2,1)S(1)}, bf16[32,512]{1,0:T(8,128)(2,1)S(1)}, bf16[128,512]{1,0:T(8,128)(2,1)S(1)}) custom-call(bf16[32,512]{1,0:T(8,128)(2,1)} %bitcast.23, bf16[32,512]{1,0:T(8,128)(2,1)} %bitcast.24, bf16[128,512]{1,0:T(8,128)(2,1)} %bitcast.22), custom_call_target="tpu_custom_call" | custom-call | tf_op jit(solution)/shard_map/pallas_call | solution.py:732
  1.6 0.0 copy-start
  1.6 0.0 copy-start.2
  1.6 0.0 copy-start.3
  1.6 0.0 copy-start.4
  1.6 0.0 copy-start.5
  1.6 0.3 shard_map.129
  2.0 23.0 %all_to_all.15.got_ref = bf16[16,112,128]{2,1,0:T(8,128)(2,1)S(1)} all-to-all(bf16[16,112,128]{2,1,0:T(8,128)(2,1)S(1)} %shard_map.129), channel_id=1, replica_groups=mesh['dp'=2,'pairs'=2,'member'=2,'rows'=4] {'pairs','member','rows'}, dimensions={0} | all-to-all | bytes 917504 | tf_op jit(solution)/shard_map/all_to_all | solution.py:749
  25.0 0.0 copy-done
  25.0 0.0 copy-done.2
  25.0 0.0 copy-done.3
  25.0 0.0 copy-done.4
  25.0 0.0 copy-done.5
  25.0 1.2 %shard_map.130 = (f32[32,512]{1,0:T(8,128)S(1)}, bf16[40,512]{1,0:T(8,128)(2,1)S(1)}, f32[3,32,512]{2,1,0:T(8,128)S(1)}, f32[32,128]{1,0:T(8,128)S(1)}, f32[4,64...) custom-call(bf16[16,112,128]{2,1,0:T(8,128)(2,1)S(1)} %all_to_all.15, ...), custom_call_target="tpu_custom_call" | custom-call | flops 2000000000 | bytes 4000000 | tf_op jit(solution)/shard_map/pallas_call | solution.py:750
  26.3 4.7 %all-gather = bf16[80,512]{1,0:T(8,128)(2,1)S(1)} all-gather(bf16[40,512]{1,0:T(8,128)(2,1)S(1)} %get-tuple-element.29), channel_id=2, replica_groups=mesh['dp'=2,'pairs'=2,'member'=2,'rows'=4] {'member'}, dimensions={0}, use_global_device_ids=true | all-gather | bytes 122880 | tf_op jit(solution)/shard_map/all_gather | solution.py:772
  31.0 0.0 copy-start.1
  31.0 0.4 shard_map.131
  31.4 12.4 %all_to_all.16.got_ref = bf16[16,80,128]{2,1,0:T(8,128)(2,1)S(1)} all-to-all(bf16[16,80,128]{2,1,0:T(8,128)(2,1)S(1)} %get-tuple-element.34), channel_id=1, replica_groups=mesh['dp'=2,'pairs'=2,'member'=2,'rows'=4] {'rows','pairs','member'}, dimensions={0} | all-to-all | bytes 655360 | tf_op jit(solution)/shard_map/all_to_all | solution.py:781
  43.8 0.0 copy-done.1
  43.8 1.6 %shard_map.132 = bf16[16,40,128]{2,1,0:T(8,128)(2,1)S(1)} custom-call(bf16[16,80,128]{2,1,0:T(8,128)(2,1)S(1)} %all_to_all.16.got_ref, f32[4,64,256]{2,1,0:T(8,128)S(1)} %get-tuple-element.35.acts_ref, bf16[2,40,512]{2,1,0:T(8,128)(2,1)S(1)} %bitcast.15, f32[4,64,128]{2,1,0:T(8,128)S(1)} %get-tuple-element.32.columns, ...), custom_call_target="tpu_custom_call" | custom-call | flops 2000000000 | bytes 4000000 | tf_op jit(solution)/shard_map/pallas_call | solution.py:782
  45.4 11.2 %all_to_all.17.got_ref = bf16[16,40,128]{2,1,0:T(8,128)(2,1)S(1)} all-to-all(bf16[16,40,128]{2,1,0:T(8,128)(2,1)S(1)} %shard_map.132), channel_id=1, replica_groups=mesh['dp'=2,'pairs'=2,'member'=2,'rows'=4] {'pairs','member','rows'}, dimensions={0} | all-to-all | bytes 327680 | tf_op jit(solution)/shard_map/all_to_all | solution.py:794
  56.6 0.5 shard_map.133
  57.1 1.8 %all-gather.1 = f32[16,512]{1,0:T(8,128)S(1)} all-gather(f32[8,512]{1,0:T(8,128)S(1)} %get-tuple-element.38), channel_id=3, replica_groups=mesh['dp'=2,'pairs'=2,'member'=2,'rows'=4] {'dp'}, dimensions={0}, use_global_device_ids=true | all-gather | bytes 49152 | tf_op jit(solution)/shard_map/all_gather | solution.py:805
  59.0 0.7 %shard_map.134 = (bf16[128,512]{1,0:T(8,128)(2,1)}, f32[1,512]{1,0:T(1,128)}, f32[1,512]{1,0:T(1,128)}, f32[1,512]{1,0:T(1,128)}, f32[1,512]{1,0:T(1,128)}) custom-call(f32[2,8,512]{2,1,0:T(8,128)S(1)} %bitcast.16, bf16[128,512]{1,0:T(8,128)(2,1)S(1)} %get-tuple-element.39.result_ref), custom_call_target="tpu_custom_call" | custom-call | flops 2000000000 | bytes 4000000 | tf_op jit(solution)/shard_map/pallas_call | solution.py:806
Async XLA Ops:
  1.6 23.4 %copy-start = (bf16[27,128,512]{2,1,0:T(8,128)(2,1)S(1)}, bf16[27,128,512]{2,1,0:T(8,128)(2,1)}, u32[]{:S(2)}) copy-start(bf16[27,128,512]{2,1,0:T(8,128)(2,1)} %weights.2) | copy-start | bytes 10616836
  1.6 23.4 %copy-start.2 = (f32[512]{0:T(512)S(1)}, f32[512]{0:T(512)}, u32[]{:S(2)}) copy-start(f32[512]{0:T(512)} %param.15) | copy-start | bytes 6148
  1.6 23.4 %copy-start.3 = (f32[512]{0:T(512)S(1)}, f32[512]{0:T(512)}, u32[]{:S(2)}) copy-start(f32[512]{0:T(512)} %param.16) | copy-start | bytes 6148
  1.6 23.4 %copy-start.4 = (f32[512]{0:T(512)S(1)}, f32[512]{0:T(512)}, u32[]{:S(2)}) copy-start(f32[512]{0:T(512)} %param.13) | copy-start | bytes 6148
  1.6 23.4 %copy-start.5 = (f32[512]{0:T(512)S(1)}, f32[512]{0:T(512)}, u32[]{:S(2)}) copy-start(f32[512]{0:T(512)} %param.12) | copy-start | bytes 6148
  31.0 12.8 %copy-start.1 = (bf16[27,128,512]{2,1,0:T(8,128)(2,1)S(1)}, bf16[27,128,512]{2,1,0:T(8,128)(2,1)}, u32[]{:S(2)}) copy-start(bf16[27,128,512]{2,1,0:T(8,128)(2,1)} %weights.3) | copy-start | bytes 10616836

commit v25 on v19

--- a/solution.py
+++ b/solution.py
@@ -487,15 +487,16 @@
     conv_ref[...] = by_col[1] + moved(by_col[0], 1, has_right) + moved(by_col[2], -1, has_left)
     mine_ref[...] = conv_ref[pl.ds(pl.multiple_of(member * sub, sub), sub), :]
     theirs = conv_ref[pl.ds(pl.multiple_of((1 - member) * sub, sub), sub), :]
-    sent_ref[0:sub, :] = theirs.astype(jnp.bfloat16)
-    sent_ref[sub:, 0:128] = stats
-    sent_ref[sub:, 128:] = jnp.zeros((8, plan.places - 128), jnp.bfloat16)
+    for k in range(plan.places // 128):
+        sent_ref[k * sub : (k + 1) * sub, :] = theirs[:, k * 128 : (k + 1) * 128].astype(jnp.bfloat16)
+    sent_ref[plan.places // 128 * sub :, :] = stats
 
 
 def quarter_kernel(plan, mine_ref, both_ref, held_ref, inv_ref, columns, by_column, out_ref, sums_ref):
     sub = plan.sub
     _, member, _, _ = own_place(plan)
-    conv = mine_ref[...] + both_ref[1 - member, 0:sub, :].astype(jnp.float32)
+    theirs = [both_ref[1 - member, k * sub : (k + 1) * sub, :] for k in range(plan.places // 128)]
+    conv = mine_ref[...] + jnp.concatenate(theirs, axis=1).astype(jnp.float32)
     normed, slope, cot = held_ref[0], held_ref[1], held_ref[2]
     gain, inv_std = columns[0][0:sub, 0:1], inv_ref[:, 0:1]
     entries = plan.places * plan.group_width
@@ -558,7 +559,7 @@
 
 
 def fine_kernel(
-    plan, got_ref, acts_ref, both_ref, columns, order, sums_ref, weights, out_ref, source, border
+    plan, got_ref, acts_ref, both_ref, columns, order, sums_ref, weights, out_ref
 ):
     sub, nr, nf, wide = plan.sub, plan.nr, plan.nf, 2 * plan.sub
     pair, member, r, _ = own_place(plan)
@@ -566,22 +567,22 @@
     w = plan.w // 2
     lines = plan.places // plan.w
     places = lines * w
-    for k in range(2):
-        source[:, k * 128 : (k + 1) * 128] = got_ref[:, k * sub : (k + 1) * sub, :].reshape(plan.channels, 128)
+    source = jnp.concatenate(
+        [got_ref[:, k * sub : (k + 1) * sub, :].reshape(plan.channels, 128) for k in range(2)], axis=1
+    )
     packed = got_ref[:, wide : wide + sub // 2, :].reshape(plan.count * sub // 2, 128)
     shape = (128, places)
     beside = lanes_at(shape, 1) == lanes_at(shape, 0) % lines * w + (1 - member) * (w - 1)
+    border = []
     for k in range(2):
         here = one_hot(beside & (lanes_at(shape, 0) // lines == k))
         found = one_hot_dot(packed, here, ((1,), (0,))).astype(jnp.bfloat16)
-        for s in range(plan.count):
-            border[s * sub + k * (sub // 2) : s * sub + (k + 1) * (sub // 2), :] = found[
-                s * (sub // 2) : (s + 1) * (sub // 2)
-            ]
+        border.append(found.reshape(plan.count, sub // 2, places))
+    border = jnp.concatenate(border, axis=1).reshape(plan.channels, places)
     image = plan.image // 2
     sums, extras = 0.0, 0.0
     for k in (2, 1, 0):
-        here, beside = source[...], border[...]
+        here, beside = source, border
         if k < 2:
             shift = (2 - k) * image
             inside = lanes_at((1, places), 1) < places - shift
@@ -594,7 +595,8 @@
         facing = jnp.concatenate([weights[9 * k + 3 * row + 2 * member, both, :] for row in range(3)], axis=0)
         extras = extras + one_hot_dot(facing, beside, ((1,), (0,)))
     parts = [acts_ref[pq] for pq in range(4)]
-    stats = sum(both_ref[k, sub : sub + 8, 0:128].astype(jnp.float32) for k in range(2))
+    at = plan.places // 128 * sub
+    stats = sum(both_ref[k, at : at + 8, :].astype(jnp.float32) for k in range(2))
     stats = stats[0:1] + stats[1:2] + stats[2:3]
     entries = 4 * plan.places * plan.group_width
     one, two = own_column(stats, 0, wide), own_column(stats, 64, wide)
@@ -615,7 +617,15 @@
     pre = [conv * part for conv, part in zip(convs, slope)]
     one = total(pre)
     two = total([a * b for a, b in zip(pre, normed)])
-    cot = source[pl.ds(pl.multiple_of(r * plan.slice_width + pair * wide, wide), wide), :].astype(jnp.float32)
+    cot = jnp.concatenate(
+        [
+            jnp.concatenate(
+                [got_ref[r * nf + 2 * pair + m, k * sub : (k + 1) * sub, :] for k in range(2)], axis=1
+            )
+            for m in range(2)
+        ],
+        axis=0,
+    ).astype(jnp.float32)
     scale = inv_std * gain
     stacked = halves_from(plan, [cot + scale * part for part in pre]).astype(jnp.bfloat16)
     sent = one_hot_dot(stacked, order[...], ((1,), (1,))).astype(jnp.bfloat16)
@@ -749,7 +759,7 @@
         functools.partial(coarse_kernel, plan),
         out_shape=(
             shape_of((sub, places), f32),
-            shape_of((sub + 8, places), bf16),
+            shape_of((places // 128 * sub + 8, 128), bf16),
             shape_of((3, sub, places), f32),
             shape_of((sub, 128), f32),
             shape_of((4, 2 * sub, places // 2), f32),
@@ -782,10 +792,6 @@
         out_shape=shape_of((count, sub + 8, 128), bf16),
         in_specs=in_vmem(7),
         out_specs=in_vmem(1)[0],
-        scratch_shapes=[
-            pltpu.VMEM((channels, places // 2), bf16),
-            pltpu.VMEM((channels, places // 2), bf16),
-        ],
         compiler_params=LIMIT,
         cost_estimate=COST,
     )(spread, fine_acts, both, columns, fine_order, coarse_sums, kernel_fine)

time: 59.6 us -> 59.5 us (level)
  no operation moved by 1% of the time
where the time goes in v25:
time: 59.5 us; the launch traced here: 59.2 us
  blocking collectives  52.7 us (89%)
  Pallas kernels  5.7 us (10%)
  between operations  0.74 us (1%)
    all_to_all x1, blocking collectives, fast_shards(): got = lax.all_to_all(packed, BLOCK, 0, 0)  22.1 us
    all_to_all x1, blocking collectives, fast_shards(): spread = lax.all_to_all(quartered, BLOCK, 0, 0)  13 us
    all_to_all x1, blocking collectives, fast_shards(): back = lax.all_to_all(sent, BACK_BLOCK, 0, 0)  11.2 us
    all_gather x1, blocking collectives, fast_shards(): both = lax.all_gather(theirs, 'member')  4.61 us
    all_gather x1, blocking collectives, fast_shards(): both = lax.all_gather(sums, 'dp')  1.83 us
    pallas_call x1, Pallas kernels, fast_shards(): pl.pallas_call(functools.partial(fine_kernel, plan), out_shape=shape_of((...  1.62 us
    pallas_call x1, Pallas kernels, fast_shards(): pl.pallas_call(functools.partial(coarse_kernel, plan), out_shape=(shape_o...  1.24 us

profile of v25, /device:TPU:0, one launch (start us, length us, event | category | flops | bytes accessed | tf_op | source)
XLA Modules:
  0.0 59.2 jit_solution(6586062292284628147)
XLA Ops:
  0.6 0.9 %shard_map.128 = (bf16[32,512]{1,0:T(8,128)(2,1)S(1)}, bf16[32,512]{1,0:T(8,128)(2,1)S(1)}, bf16[128,512]{1,0:T(8,128)(2,1)S(1)}) custom-call(bf16[32,512]{1,0:T(8,128)(2,1)} %bitcast.23, bf16[32,512]{1,0:T(8,128)(2,1)} %bitcast.24, bf16[128,512]{1,0:T(8,128)(2,1)} %bitcast.22), custom_call_target="tpu_custom_call" | custom-call | tf_op jit(solution)/shard_map/pallas_call | solution.py:740
  1.6 0.0 copy-start
  1.6 0.0 copy-start.2
  1.6 0.0 copy-start.3
  1.6 0.0 copy-start.4
  1.6 0.0 copy-start.5
  1.6 0.3 shard_map.129
  2.0 22.1 %all_to_all.15.got_ref = bf16[16,112,128]{2,1,0:T(8,128)(2,1)S(1)} all-to-all(bf16[16,112,128]{2,1,0:T(8,128)(2,1)S(1)} %shard_map.129), channel_id=1, replica_groups=mesh['dp'=2,'pairs'=2,'member'=2,'rows'=4] {'rows','pairs','member'}, dimensions={0} | all-to-all | bytes 917504 | tf_op jit(solution)/shard_map/all_to_all | solution.py:757
  24.1 0.0 copy-done
  24.1 0.0 copy-done.2
  24.1 0.0 copy-done.3
  24.1 0.0 copy-done.4
  24.1 0.0 copy-done.5
  24.1 1.2 %shard_map.130 = (f32[32,512]{1,0:T(8,128)S(1)}, bf16[136,128]{1,0:T(8,128)(2,1)S(1)}, f32[3,32,512]{2,1,0:T(8,128)S(1)}, f32[32,128]{1,0:T(8,128)S(1)}, f32[4,6...) custom-call(bf16[16,112,128]{2,1,0:T(8,128)(2,1)S(1)} %all_to_all.15, ...), custom_call_target="tpu_custom_call" | custom-call | flops 2000000000 | bytes 4000000 | tf_op jit(solution)/shard_map/pallas_call | solution.py:758
  25.4 4.6 %all-gather = bf16[272,128]{1,0:T(8,128)(2,1)S(1)} all-gather(bf16[136,128]{1,0:T(8,128)(2,1)S(1)} %get-tuple-element.29), channel_id=2, replica_groups=mesh['dp'=2,'pairs'=2,'member'=2,'rows'=4] {'member'}, dimensions={0}, use_global_device_ids=true | all-gather | bytes 104448 | tf_op jit(solution)/shard_map/all_gather | solution.py:780
  30.0 0.0 copy-start.1
  30.0 0.4 shard_map.131
  30.4 13.0 %all_to_all.16.got_ref = bf16[16,80,128]{2,1,0:T(8,128)(2,1)S(1)} all-to-all(bf16[16,80,128]{2,1,0:T(8,128)(2,1)S(1)} %get-tuple-element.34), channel_id=1, replica_groups=mesh['dp'=2,'pairs'=2,'member'=2,'rows'=4] {'rows','pairs','member'}, dimensions={0} | all-to-all | bytes 655360 | tf_op jit(solution)/shard_map/all_to_all | solution.py:789
  43.3 0.0 copy-done.1
  43.3 1.6 %shard_map.132 = bf16[16,40,128]{2,1,0:T(8,128)(2,1)S(1)} custom-call(bf16[16,80,128]{2,1,0:T(8,128)(2,1)S(1)} %all_to_all.16.got_ref, f32[4,64,256]{2,1,0:T(8,128)S(1)} %get-tuple-element.35.acts_ref, bf16[2,136,128]{2,1,0:T(8,128)(2,1)S(1)} %bitcast.15, f32[4,64,128]{2,1,0:T(8,128)S(1)} %get-tuple-element.32.columns, ...), custom_call_target="tpu_custom_call" | custom-call | flops 2000000000 | bytes 4000000 | tf_op jit(solution)/shard_map/pallas_call | solution.py:790
  45.0 11.2 %all_to_all.17.got_ref = bf16[16,40,128]{2,1,0:T(8,128)(2,1)S(1)} all-to-all(bf16[16,40,128]{2,1,0:T(8,128)(2,1)S(1)} %shard_map.132), channel_id=1, replica_groups=mesh['dp'=2,'pairs'=2,'member'=2,'rows'=4] {'pairs','member','rows'}, dimensions={0} | all-to-all | bytes 327680 | tf_op jit(solution)/shard_map/all_to_all | solution.py:798
  56.2 0.5 shard_map.133
  56.7 1.8 %all-gather.1 = f32[16,512]{1,0:T(8,128)S(1)} all-gather(f32[8,512]{1,0:T(8,128)S(1)} %get-tuple-element.38), channel_id=3, replica_groups=mesh['dp'=2,'pairs'=2,'member'=2,'rows'=4] {'dp'}, dimensions={0}, use_global_device_ids=true | all-gather | bytes 49152 | tf_op jit(solution)/shard_map/all_gather | solution.py:809
  58.5 0.7 %shard_map.134 = (bf16[128,512]{1,0:T(8,128)(2,1)}, f32[1,512]{1,0:T(1,128)}, f32[1,512]{1,0:T(1,128)}, f32[1,512]{1,0:T(1,128)}, f32[1,512]{1,0:T(1,128)}) custom-call(f32[2,8,512]{2,1,0:T(8,128)S(1)} %bitcast.16, bf16[128,512]{1,0:T(8,128)(2,1)S(1)} %get-tuple-element.39.result_ref), custom_call_target="tpu_custom_call" | custom-call | flops 2000000000 | bytes 4000000 | tf_op jit(solution)/shard_map/pallas_call | solution.py:810
Async XLA Ops:
  1.6 22.5 %copy-start = (bf16[27,128,512]{2,1,0:T(8,128)(2,1)S(1)}, bf16[27,128,512]{2,1,0:T(8,128)(2,1)}, u32[]{:S(2)}) copy-start(bf16[27,128,512]{2,1,0:T(8,128)(2,1)} %weights.2) | copy-start | bytes 10616836
  1.6 22.5 %copy-start.2 = (f32[512]{0:T(512)S(1)}, f32[512]{0:T(512)}, u32[]{:S(2)}) copy-start(f32[512]{0:T(512)} %param.15) | copy-start | bytes 6148
  1.6 22.5 %copy-start.3 = (f32[512]{0:T(512)S(1)}, f32[512]{0:T(512)}, u32[]{:S(2)}) copy-start(f32[512]{0:T(512)} %param.16) | copy-start | bytes 6148
  1.6 22.5 %copy-start.4 = (f32[512]{0:T(512)S(1)}, f32[512]{0:T(512)}, u32[]{:S(2)}) copy-start(f32[512]{0:T(512)} %param.13) | copy-start | bytes 6148
  1.6 22.5 %copy-start.5 = (f32[512]{0:T(512)S(1)}, f32[512]{0:T(512)}, u32[]{:S(2)}) copy-start(f32[512]{0:T(512)} %param.12) | copy-start | bytes 6148
  30.0 13.4 %copy-start.1 = (bf16[27,128,512]{2,1,0:T(8,128)(2,1)S(1)}, bf16[27,128,512]{2,1,0:T(8,128)(2,1)}, u32[]{:S(2)}) copy-start(bf16[27,128,512]{2,1,0:T(8,128)(2,1)} %weights.3) | copy-start | bytes 10616836

commit v26 on v19

--- a/solution.py
+++ b/solution.py
@@ -320,8 +320,9 @@
         self.places = self.frames * self.image
         self.group_width = self.channels // GROUPS
         self.chunks = self.channels // 128
-        self.acts_at = self.chunks // 2 * self.local
-        self.packed_at = self.acts_at + self.sub
+        self.packed_at = self.chunks // 2 * self.local
+        self.acts_at = 2 * self.sub + self.sub // 2
+        self.stats_at = self.acts_at + self.sub
         self.cot_at = self.packed_at + 8
         self.block_rows = self.cot_at + 8
         self.fits = (
@@ -360,7 +361,7 @@
         copy.wait()
 
 
-def pack_kernel(plan, g_ref, coarse_ref, fine_ref, out_ref):
+def pack_kernel(plan, g_ref, coarse_ref, fine_ref, out_ref, later_ref):
     sub, chunks, local = plan.sub, plan.chunks, plan.local
     shape = (2 * local, 2 * 128)
     lane = lanes_at((1, 2 * 128), 1)
@@ -371,6 +372,11 @@
     acts = fine_ref[...]
     halves = one_hot_dot(acts, orders, ((0,), (0,))).astype(jnp.bfloat16)
     halves = [halves[:, :128], halves[:, 128:]]
+    values = acts.astype(jnp.float32)
+    one = jnp.sum(values, axis=0, keepdims=True)
+    two = jnp.sum(values * values, axis=0, keepdims=True)
+    stats = terms(one, 3) + terms(two, 3) + [jnp.zeros_like(one)] * 2
+    stats = jnp.concatenate(stats, axis=0).astype(jnp.bfloat16)
     small = one_hot_dot(jnp.concatenate([coarse_ref[...], g_ref[...]], axis=0), repeated, ((0,), (0,)))
     for k, at in enumerate((plan.packed_at, plan.cot_at)):
         rows_of = jnp.where(quarter, small[:, k * 128 : (k + 1) * 128], 0.0).reshape(plan.count, 4, 8, 128)
@@ -384,7 +390,8 @@
                 at = (half * chunks // 2 + k) * 128
                 out_ref[dest, k * local : (k + 1) * local, :] = g_ref[:, at : at + 128]
             upper, lower = halves[half][first : first + sub], halves[1 - half][first + sub : first + 2 * sub]
-            out_ref[dest, plan.acts_at : plan.packed_at, :] = jnp.where(low, upper, lower)
+            later_ref[dest, 0:sub, :] = jnp.where(low, upper, lower)
+            later_ref[dest, sub:, :] = stats[:, s_r * 128 : (s_r + 1) * 128]
 
 
 def by_frame_device(plan, got_ref, at, height):
@@ -422,7 +429,6 @@
     sent_ref,
     held_ref,
     inv_ref,
-    fine_ref,
     columns,
     fine_order,
     by_column,
@@ -460,13 +466,6 @@
         )
         for k in range(3)
     )
-    merged = one_hot_dot(by_frame_device(plan, got_ref, plan.acts_at, sub), fine_order[...], ((1,), (0,)))
-    parts = halves_at(plan, merged)
-    for pq in range(4):
-        fine_ref[pq] = parts[pq]
-    one, two = total(parts), total([part * part for part in parts])
-    stats = terms(as_row(one) + pltpu.roll(as_row(two), 64, 1), 3)
-    stats = jnp.concatenate(stats + [jnp.zeros_like(stats[0])] * 5, axis=0).astype(jnp.bfloat16)
     small = [by_frame_device(plan, got_ref, at, 8) for at in (plan.packed_at, plan.cot_at)]
     merged = one_hot_dot(jnp.concatenate(small, axis=0), order[...], ((1,), (0,)))
     rows_of = 8 * nf
@@ -487,15 +486,13 @@
     conv_ref[...] = by_col[1] + moved(by_col[0], 1, has_right) + moved(by_col[2], -1, has_left)
     mine_ref[...] = conv_ref[pl.ds(pl.multiple_of(member * sub, sub), sub), :]
     theirs = conv_ref[pl.ds(pl.multiple_of((1 - member) * sub, sub), sub), :]
-    sent_ref[0:sub, :] = theirs.astype(jnp.bfloat16)
-    sent_ref[sub:, 0:128] = stats
-    sent_ref[sub:, 128:] = jnp.zeros((8, plan.places - 128), jnp.bfloat16)
-
-
-def quarter_kernel(plan, mine_ref, both_ref, held_ref, inv_ref, columns, by_column, out_ref, sums_ref):
+    sent_ref[...] = theirs.astype(jnp.bfloat16)
+
+
+def quarter_kernel(plan, mine_ref, both_ref, held_ref, inv_ref, columns, by_column, later_ref, out_ref, sums_ref):
     sub = plan.sub
     _, member, _, _ = own_place(plan)
-    conv = mine_ref[...] + both_ref[1 - member, 0:sub, :].astype(jnp.float32)
+    conv = mine_ref[...] + both_ref[1 - member].astype(jnp.float32)
     normed, slope, cot = held_ref[0], held_ref[1], held_ref[2]
     gain, inv_std = columns[0][0:sub, 0:1], inv_ref[:, 0:1]
     entries = plan.places * plan.group_width
@@ -514,7 +511,8 @@
         for dest in range(half, plan.count, 2):
             out_ref[dest, 0:sub, :] = sent[:, at : at + 128]
             out_ref[dest, sub : 2 * sub, :] = sent[:, at + 128 : at + 256]
-            out_ref[dest, 2 * sub : 2 * sub + sub // 2, :] = border
+            out_ref[dest, 2 * sub : plan.acts_at, :] = border
+            out_ref[dest, plan.acts_at :, :] = later_ref[dest]
     sums_ref[...] = jnp.concatenate([as_row(one), as_row(two)], axis=0)
 
 
@@ -558,7 +556,7 @@
 
 
 def fine_kernel(
-    plan, got_ref, acts_ref, both_ref, columns, order, sums_ref, weights, out_ref, source, border
+    plan, got_ref, columns, order, sums_ref, weights, out_ref, source, border
 ):
     sub, nr, nf, wide = plan.sub, plan.nr, plan.nf, 2 * plan.sub
     pair, member, r, _ = own_place(plan)
@@ -593,11 +591,12 @@
         )
         facing = jnp.concatenate([weights[9 * k + 3 * row + 2 * member, both, :] for row in range(3)], axis=0)
         extras = extras + one_hot_dot(facing, beside, ((1,), (0,)))
-    parts = [acts_ref[pq] for pq in range(4)]
-    stats = sum(both_ref[k, sub : sub + 8, 0:128].astype(jnp.float32) for k in range(2))
-    stats = stats[0:1] + stats[1:2] + stats[2:3]
+    merged = one_hot_dot(by_frame_device(plan, got_ref, plan.acts_at, sub), order[...], ((1,), (0,)))
+    parts = halves_at(plan, merged)
+    stats = sum(got_ref[s, plan.stats_at : plan.stats_at + 8, :].astype(jnp.float32) for s in range(plan.count))
     entries = 4 * plan.places * plan.group_width
-    one, two = own_column(stats, 0, wide), own_column(stats, 64, wide)
+    one = own_column(stats[0:1] + stats[1:2] + stats[2:3], pair * wide, wide)
+    two = own_column(stats[3:4] + stats[4:5] + stats[5:6], pair * wide, wide)
     mean, inv_std = statistics(one, two, entries, plan.group_width)
     gain, bias = columns[2][:, 0:1], columns[3][:, 0:1]
     normed, slope = normalised(parts, gain, bias, mean, inv_std)
@@ -736,29 +735,28 @@
         compiler_params=LIMIT,
     )(*[kept(part.reshape(shape)) for part, shape in zip((grad_coarse, acts_coarse, acts_fine), places_of)])
     acts = fetched_of[2]
-    packed = pl.pallas_call(
+    packed, later = pl.pallas_call(
         functools.partial(pack_kernel, plan),
-        out_shape=shape_of((count, plan.block_rows, 128), bf16),
+        out_shape=(shape_of((count, plan.block_rows, 128), bf16), shape_of((count, sub + 8, 128), bf16)),
         in_specs=in_vmem(3),
-        out_specs=in_vmem(1)[0],
+        out_specs=tuple(in_vmem(2)),
         compiler_params=LIMIT,
         cost_estimate=COST,
     )(*fetched_of)
     got = lax.all_to_all(packed, BLOCK, 0, 0)
-    mine, theirs, held, inv_std, fine_acts, columns, fine_order, by_column = pl.pallas_call(
+    mine, theirs, held, inv_std, columns, fine_order, by_column = pl.pallas_call(
         functools.partial(coarse_kernel, plan),
         out_shape=(
             shape_of((sub, places), f32),
-            shape_of((sub + 8, places), bf16),
+            shape_of((sub, places), bf16),
             shape_of((3, sub, places), f32),
             shape_of((sub, 128), f32),
-            shape_of((4, 2 * sub, places // 2), f32),
             shape_of((4, 2 * sub, 128), f32),
             shape_of((4 * plan.nr * local, 4 * plan.nr * local), bf16),
             shape_of((places, places + places // 2), bf16),
         ),
         in_specs=in_vmem(6),
-        out_specs=tuple(in_vmem(8)),
+        out_specs=tuple(in_vmem(7)),
         scratch_shapes=[
             pltpu.VMEM((4 * plan.nr * local, 4 * plan.nr * local), bf16),
             pltpu.VMEM((places + 2 * plan.image, channels // 2), bf16),
@@ -770,17 +768,17 @@
     both = lax.all_gather(theirs, "member")
     quartered, coarse_sums = pl.pallas_call(
         functools.partial(quarter_kernel, plan),
-        out_shape=(shape_of((count, 2 * sub + sub // 2, 128), bf16), shape_of((2, 128), f32)),
-        in_specs=in_vmem(6),
+        out_shape=(shape_of((count, plan.stats_at + 8, 128), bf16), shape_of((2, 128), f32)),
+        in_specs=in_vmem(7),
         out_specs=tuple(in_vmem(2)),
         compiler_params=LIMIT,
         cost_estimate=COST,
-    )(mine, both, held, inv_std, columns, by_column)
+    )(mine, both, held, inv_std, columns, by_column, later)
     spread = lax.all_to_all(quartered, BLOCK, 0, 0)
     sent = pl.pallas_call(
         functools.partial(fine_kernel, plan),
         out_shape=shape_of((count, sub + 8, 128), bf16),
-        in_specs=in_vmem(7),
+        in_specs=in_vmem(5),
         out_specs=in_vmem(1)[0],
         scratch_shapes=[
             pltpu.VMEM((channels, places // 2), bf16),
@@ -788,7 +786,7 @@
         ],
         compiler_params=LIMIT,
         cost_estimate=COST,
-    )(spread, fine_acts, both, columns, fine_order, coarse_sums, kernel_fine)
+    )(spread, columns, fine_order, coarse_sums, kernel_fine)
     back = lax.all_to_all(sent, BACK_BLOCK, 0, 0)
     cells = nd * places
     fine_scale, coarse_scale = 1.0 / math.sqrt(4 * cells), 1.0 / math.sqrt(cells)

time: 59.6 us -> 60.1 us (level)
  blocking collectives: 52.8 us -> 53.5 us
    all_to_all x1, blocking collectives: 13 us -> 16.2 us  [fast_shards(): spread = lax.all_to_all(quartered, BLOCK, 0, 0)]
    all_to_all x1, blocking collectives: 22.1 us -> 19.6 us  [fast_shards(): got = lax.all_to_all(packed, BLOCK, 0, 0)]
where the time goes in v26:
time: 60.1 us; the launch traced here: 59.9 us
  blocking collectives  53.5 us (89%)
  Pallas kernels  5.62 us (9%)
  between operations  0.74 us (1%)
    all_to_all x1, blocking collectives, fast_shards(): got = lax.all_to_all(packed, BLOCK, 0, 0)  19.6 us
    all_to_all x1, blocking collectives, fast_shards(): spread = lax.all_to_all(quartered, BLOCK, 0, 0)  16.2 us
    all_to_all x1, blocking collectives, fast_shards(): back = lax.all_to_all(sent, BACK_BLOCK, 0, 0)  11.3 us
    all_gather x1, blocking collectives, fast_shards(): both = lax.all_gather(theirs, 'member')  4.59 us
    all_gather x1, blocking collectives, fast_shards(): both = lax.all_gather(sums, 'dp')  1.83 us
    pallas_call x1, Pallas kernels, fast_shards(): pl.pallas_call(functools.partial(fine_kernel, plan), out_shape=shape_of((...  1.66 us

profile of v26, /device:TPU:0, one launch (start us, length us, event | category | flops | bytes accessed | tf_op | source)
XLA Modules:
  0.0 59.9 jit_solution(13284012193213405004)
XLA Ops:
  0.6 0.9 %shard_map.128 = (bf16[32,512]{1,0:T(8,128)(2,1)S(1)}, bf16[32,512]{1,0:T(8,128)(2,1)S(1)}, bf16[128,512]{1,0:T(8,128)(2,1)S(1)}) custom-call(bf16[32,512]{1,0:T(8,128)(2,1)} %bitcast.22, bf16[32,512]{1,0:T(8,128)(2,1)} %bitcast.23, bf16[128,512]{1,0:T(8,128)(2,1)} %bitcast.21), custom_call_target="tpu_custom_call" | custom-call | tf_op jit(solution)/shard_map/pallas_call | solution.py:729
  1.6 0.0 copy-start
  1.6 0.0 copy-start.2
  1.6 0.0 copy-start.3
  1.6 0.0 copy-start.4
  1.6 0.0 copy-start.5
  1.6 0.3 shard_map.129
  2.0 19.6 %all_to_all.15.got_ref = bf16[16,80,128]{2,1,0:T(8,128)(2,1)S(1)} all-to-all(bf16[16,80,128]{2,1,0:T(8,128)(2,1)S(1)} %get-tuple-element.29), channel_id=1, replica_groups=mesh['dp'=2,'pairs'=2,'member'=2,'rows'=4] {'rows','pairs','member'}, dimensions={0} | all-to-all | bytes 655360 | tf_op jit(solution)/shard_map/all_to_all | solution.py:746
  21.5 0.0 copy-done
  21.5 0.0 copy-done.2
  21.5 0.0 copy-done.3
  21.6 0.0 copy-done.4
  21.6 0.0 copy-done.5
  21.6 1.1 %shard_map.130 = (f32[32,512]{1,0:T(8,128)S(1)}, bf16[32,512]{1,0:T(8,128)(2,1)S(1)}, f32[3,32,512]{2,1,0:T(8,128)S(1)}, f32[32,128]{1,0:T(8,128)S(1)}, f32[4,64...) custom-call(bf16[16,80,128]{2,1,0:T(8,128)(2,1)S(1)} %all_to_all.15.got_ref, ...), custom_call_target="tpu_custom_call" | custom-call | flops 2000000000 | bytes 4000000 | tf_op jit(solution)/shard_map/pallas_call | solution.py:747
  22.7 4.6 %all-gather = bf16[64,512]{1,0:T(8,128)(2,1)S(1)} all-gather(bf16[32,512]{1,0:T(8,128)(2,1)S(1)} %get-tuple-element.31), channel_id=2, replica_groups=mesh['dp'=2,'pairs'=2,'member'=2,'rows'=4] {'member'}, dimensions={0}, use_global_device_ids=true | all-gather | bytes 98304 | tf_op jit(solution)/shard_map/all_gather | solution.py:768
  27.3 0.0 copy-start.1
  27.3 0.4 shard_map.131
  27.7 16.2 %all_to_all.16.got_ref = bf16[16,120,128]{2,1,0:T(8,128)(2,1)S(1)} all-to-all(bf16[16,120,128]{2,1,0:T(8,128)(2,1)S(1)} %get-tuple-element.37), channel_id=1, replica_groups=mesh['dp'=2,'pairs'=2,'member'=2,'rows'=4] {'rows','pairs','member'}, dimensions={0} | all-to-all | bytes 983040 | tf_op jit(solution)/shard_map/all_to_all | solution.py:777
  43.9 0.0 copy-done.1
  43.9 1.7 %shard_map.132 = bf16[16,40,128]{2,1,0:T(8,128)(2,1)S(1)} custom-call(bf16[16,120,128]{2,1,0:T(8,128)(2,1)S(1)} %all_to_all.16.got_ref, f32[4,64,128]{2,1,0:T(8,128)S(1)} %get-tuple-element.34.columns, bf16[512,512]{1,0:T(8,128)(2,1)S(1)} %get-tuple-element.38.order, f32[2,128]{1,0:T(2,128)S(1)} %get-tuple-element.39.sums_ref, ...), custom_call_target="tpu_custom_call" | custom-call | flops 2000000000 | bytes 4000000 | tf_op jit(solution)/shard_map/pallas_call | solution.py:778
  45.6 11.3 %all_to_all.17.got_ref = bf16[16,40,128]{2,1,0:T(8,128)(2,1)S(1)} all-to-all(bf16[16,40,128]{2,1,0:T(8,128)(2,1)S(1)} %shard_map.132), channel_id=1, replica_groups=mesh['dp'=2,'pairs'=2,'member'=2,'rows'=4] {'pairs','member','rows'}, dimensions={0} | all-to-all | bytes 327680 | tf_op jit(solution)/shard_map/all_to_all | solution.py:790
  56.9 0.5 shard_map.133
  57.4 1.8 %all-gather.1 = f32[16,512]{1,0:T(8,128)S(1)} all-gather(f32[8,512]{1,0:T(8,128)S(1)} %get-tuple-element.40), channel_id=3, replica_groups=mesh['dp'=2,'pairs'=2,'member'=2,'rows'=4] {'dp'}, dimensions={0}, use_global_device_ids=true | all-gather | bytes 49152 | tf_op jit(solution)/shard_map/all_gather | solution.py:801
  59.2 0.7 %shard_map.134 = (bf16[128,512]{1,0:T(8,128)(2,1)}, f32[1,512]{1,0:T(1,128)}, f32[1,512]{1,0:T(1,128)}, f32[1,512]{1,0:T(1,128)}, f32[1,512]{1,0:T(1,128)}) custom-call(f32[2,8,512]{2,1,0:T(8,128)S(1)} %bitcast.15, bf16[128,512]{1,0:T(8,128)(2,1)S(1)} %get-tuple-element.41.result_ref), custom_call_target="tpu_custom_call" | custom-call | flops 2000000000 | bytes 4000000 | tf_op jit(solution)/shard_map/pallas_call | solution.py:802
Async XLA Ops:
  1.6 20.0 %copy-start = (bf16[27,128,512]{2,1,0:T(8,128)(2,1)S(1)}, bf16[27,128,512]{2,1,0:T(8,128)(2,1)}, u32[]{:S(2)}) copy-start(bf16[27,128,512]{2,1,0:T(8,128)(2,1)} %weights.2) | copy-start | bytes 10616836
  1.6 20.0 %copy-start.2 = (f32[512]{0:T(512)S(1)}, f32[512]{0:T(512)}, u32[]{:S(2)}) copy-start(f32[512]{0:T(512)} %param.15) | copy-start | bytes 6148
  1.6 19.9 %copy-start.3 = (f32[512]{0:T(512)S(1)}, f32[512]{0:T(512)}, u32[]{:S(2)}) copy-start(f32[512]{0:T(512)} %param.16) | copy-start | bytes 6148
  1.6 19.9 %copy-start.4 = (f32[512]{0:T(512)S(1)}, f32[512]{0:T(512)}, u32[]{:S(2)}) copy-start(f32[512]{0:T(512)} %param.13) | copy-start | bytes 6148
  1.6 19.9 %copy-start.5 = (f32[512]{0:T(512)S(1)}, f32[512]{0:T(512)}, u32[]{:S(2)}) copy-start(f32[512]{0:T(512)} %param.12) | copy-start | bytes 6148
  27.3 16.6 %copy-start.1 = (bf16[27,128,512]{2,1,0:T(8,128)(2,1)S(1)}, bf16[27,128,512]{2,1,0:T(8,128)(2,1)}, u32[]{:S(2)}) copy-start(bf16[27,128,512]{2,1,0:T(8,128)(2,1)} %weights.3) | copy-start | bytes 10616836

commit v27 on v25

--- a/solution.py
+++ b/solution.py
@@ -642,20 +642,15 @@
             out_ref[s_f * nr + s_r, sub : sub + 8, :] = coded
 
 
-def spread_kernel(plan, got_ref, acts_ref, gain_ref, out_ref, sums_ref):
+def spread_kernel(plan, got_ref, gain_ref, sums_ref, rows_ref):
     sub, nr, nf = plan.sub, plan.nr, plan.nf
-    low = lanes_at((sub, 128), 1) < 64
     low_row = lanes_at((1, 128), 1) < 64
     first_row = lanes_at((1, 128), 1) < sub
-    source = []
     fine, coarse, moments = [[], []], [[], []], [[], []]
     for s_r in range(nr):
         ones, twos, c_ones, c_twos, invs, means = [], [], 0.0, 0.0, [], []
         for pair in range(nf // 2):
             at = 2 * pair * nr + s_r
-            left, right = [got_ref[at + k * nr, 0:sub, :].astype(jnp.float32) for k in range(2)]
-            source.append(jnp.where(low, left, pltpu.roll(right, 64, 1)))
-            source.append(jnp.where(low, pltpu.roll(left, 64, 1), right))
             coded = [got_ref[at + k * nr, sub : sub + 8, :].astype(jnp.float32) for k in range(2)]
             sums = coded[0][0:1] + coded[0][1:2] + coded[1][0:1] + coded[1][1:2]
             ones.append(sums if pair == 0 else pltpu.roll(sums, 64, 1))
@@ -677,24 +672,40 @@
         coarse[0].append(c_ones)
         coarse[1].append(c_twos)
     one, two, inv_std, mean, c_one, c_two = [jnp.concatenate(part, axis=1) for part in fine + moments + coarse]
-    source = jnp.concatenate(source, axis=0).astype(jnp.bfloat16)
-    result = one_hot_dot(pixel_order(plan, False), source, ((1,), (1,)))
     gain = gain_ref[...]
     entries = 4 * plan.places * plan.group_width
     group_one = in_lane_groups(gain * one, plan.group_width) / entries
     group_two = in_lane_groups(gain * two, plan.group_width) / entries
-    normed = (acts_ref[...].astype(jnp.float32) - mean) * inv_std
-    out_ref[...] = (result - inv_std * (group_one + normed * group_two)).astype(jnp.bfloat16)
+    rows_ref[...] = jnp.concatenate([inv_std, mean, group_one, group_two] + [jnp.zeros_like(one)] * 4, axis=0)
     sums_ref[...] = jnp.concatenate([one, two, c_one, c_two] + [jnp.zeros_like(one)] * 4, axis=0)
 
 
-def total_kernel(scales, both_ref, result_ref, result_hbm, out_hbms, rows_ref, sems):
-    copies = fetched([(result_ref, result_hbm)], sems)
-    rows = sum(both_ref[k] for k in range(both_ref.shape[0]))
+def total_kernel(plan, scales, both_ref, got_ref, acts_ref, rows_ref, result_hbm, out_hbms, total_ref, out_ref, sems):
+    sub, nr, nf = plan.sub, plan.nr, plan.nf
+    totals = sum(both_ref[k] for k in range(both_ref.shape[0]))
+    copies = []
     for k in range(4):
-        rows_ref[k] = rows[k : k + 1] * scales[k]
-    for k in range(4):
-        copies.append(pltpu.make_async_copy(rows_ref.at[k], out_hbms[k], sems.at[k + 1]))
+        total_ref[k] = totals[k : k + 1] * scales[k]
+        copies.append(pltpu.make_async_copy(total_ref.at[k], out_hbms[k], sems.at[k]))
+        copies[-1].start()
+    low = lanes_at((sub, 128), 1) < 64
+    source = []
+    for s_r in range(nr):
+        for pair in range(nf // 2):
+            at = 2 * pair * nr + s_r
+            left, right = [got_ref[at + k * nr, 0:sub, :].astype(jnp.float32) for k in range(2)]
+            source.append(jnp.where(low, left, pltpu.roll(right, 64, 1)))
+            source.append(jnp.where(low, pltpu.roll(left, 64, 1), right))
+    source = jnp.concatenate(source, axis=0).astype(jnp.bfloat16)
+    inv_std, mean, group_one, group_two = [rows_ref[k : k + 1] for k in range(4)]
+    pixels = pixel_order(plan, False)
+    height = 2 * plan.local
+    for k in range(2):
+        chunk = pl.ds(k * height, height)
+        result = one_hot_dot(pixels[k * height : (k + 1) * height], source, ((1,), (1,)))
+        normed = (acts_ref[chunk, :].astype(jnp.float32) - mean) * inv_std
+        out_ref[chunk, :] = (result - inv_std * (group_one + normed * group_two)).astype(jnp.bfloat16)
+        copies.append(pltpu.make_async_copy(out_ref.at[chunk], result_hbm.at[chunk], sems.at[4 + k]))
         copies[-1].start()
     for copy in copies:
         copy.wait()
@@ -798,24 +809,28 @@
     back = lax.all_to_all(sent, BACK_BLOCK, 0, 0)
     cells = nd * places
     fine_scale, coarse_scale = 1.0 / math.sqrt(4 * cells), 1.0 / math.sqrt(cells)
-    out, sums = pl.pallas_call(
+    sums, moments = pl.pallas_call(
         functools.partial(spread_kernel, plan),
-        out_shape=(pltpu.VMEM((4 * local, channels), bf16), shape_of((8, channels), f32)),
-        in_specs=in_vmem(3),
+        out_shape=(shape_of((8, channels), f32), shape_of((8, channels), f32)),
+        in_specs=in_vmem(2),
         out_specs=tuple(in_vmem(2)),
         compiler_params=LIMIT,
         cost_estimate=COST,
-    )(back, acts, rows[2])
+    )(back, rows[2])
     both = lax.all_gather(sums, "dp")
     out, sums = pl.pallas_call(
-        functools.partial(total_kernel, (fine_scale, fine_scale, coarse_scale, coarse_scale)),
+        functools.partial(total_kernel, plan, (fine_scale, fine_scale, coarse_scale, coarse_scale)),
         out_shape=(pltpu.HBM((4 * local, channels), bf16), (pltpu.HBM((1, channels), f32),) * 4),
-        in_specs=in_vmem(2),
+        in_specs=in_vmem(4),
         out_specs=(in_hbm(1)[0], tuple(in_hbm(4))),
-        scratch_shapes=[pltpu.VMEM((4, 1, channels), f32), pltpu.SemaphoreType.DMA((5,))],
+        scratch_shapes=[
+            pltpu.VMEM((4, 1, channels), f32),
+            pltpu.VMEM((4 * local, channels), bf16),
+            pltpu.SemaphoreType.DMA((6,)),
+        ],
         compiler_params=LIMIT,
         cost_estimate=COST,
-    )(both, out)
+    )(both, back, acts, moments)
     bias_f, gain_f, bias_c, gain_c = [part.reshape(channels) for part in sums]
     return out.reshape(acts_fine.shape), gain_f, bias_f, gain_c, bias_c
 

time: 59.5 us -> 59.7 us (level)
  no operation moved by 1% of the time
where the time goes in v27:
time: 59.7 us; the launch traced here: 59.4 us
  blocking collectives  52.7 us (88%)
  Pallas kernels  5.91 us (10%)
  between operations  0.74 us (1%)
    all_to_all x1, blocking collectives, fast_shards(): got = lax.all_to_all(packed, BLOCK, 0, 0)  22.1 us
    all_to_all x1, blocking collectives, fast_shards(): spread = lax.all_to_all(quartered, BLOCK, 0, 0)  13 us
    all_to_all x1, blocking collectives, fast_shards(): back = lax.all_to_all(sent, BACK_BLOCK, 0, 0)  11.2 us
    all_gather x1, blocking collectives, fast_shards(): both = lax.all_gather(theirs, 'member')  4.61 us
    all_gather x1, blocking collectives, fast_shards(): both = lax.all_gather(sums, 'dp')  1.83 us
    pallas_call x1, Pallas kernels, fast_shards(): pl.pallas_call(functools.partial(fine_kernel, plan), out_shape=shape_of((...  1.62 us
    pallas_call x1, Pallas kernels, fast_shards(): pl.pallas_call(functools.partial(coarse_kernel, plan), out_shape=(shape_o...  1.24 us

profile of v27, /device:TPU:0, one launch (start us, length us, event | category | flops | bytes accessed | tf_op | source)
XLA Modules:
  0.0 59.4 jit_solution(6757357533851771168)
XLA Ops:
  0.6 0.9 %shard_map.128 = (bf16[32,512]{1,0:T(8,128)(2,1)S(1)}, bf16[32,512]{1,0:T(8,128)(2,1)S(1)}, bf16[128,512]{1,0:T(8,128)(2,1)S(1)}) custom-call(bf16[32,512]{1,0:T(8,128)(2,1)} %bitcast.23, bf16[32,512]{1,0:T(8,128)(2,1)} %bitcast.24, bf16[128,512]{1,0:T(8,128)(2,1)} %bitcast.22), custom_call_target="tpu_custom_call" | custom-call | tf_op jit(solution)/shard_map/pallas_call | solution.py:751
  1.6 0.0 copy-start
  1.6 0.0 copy-start.2
  1.6 0.0 copy-start.3
  1.6 0.0 copy-start.4
  1.6 0.0 copy-start.5
  1.6 0.3 shard_map.129
  2.0 22.1 %all_to_all.15.got_ref = bf16[16,112,128]{2,1,0:T(8,128)(2,1)S(1)} all-to-all(bf16[16,112,128]{2,1,0:T(8,128)(2,1)S(1)} %shard_map.129), channel_id=1, replica_groups=mesh['dp'=2,'pairs'=2,'member'=2,'rows'=4] {'rows','pairs','member'}, dimensions={0} | all-to-all | bytes 917504 | tf_op jit(solution)/shard_map/all_to_all | solution.py:768
  24.1 0.0 copy-done
  24.1 0.0 copy-done.2
  24.1 0.0 copy-done.3
  24.1 0.0 copy-done.4
  24.1 0.0 copy-done.5
  24.1 1.2 %shard_map.130 = (f32[32,512]{1,0:T(8,128)S(1)}, bf16[136,128]{1,0:T(8,128)(2,1)S(1)}, f32[3,32,512]{2,1,0:T(8,128)S(1)}, f32[32,128]{1,0:T(8,128)S(1)}, f32[4,6...) custom-call(bf16[16,112,128]{2,1,0:T(8,128)(2,1)S(1)} %all_to_all.15, ...), custom_call_target="tpu_custom_call" | custom-call | flops 2000000000 | bytes 4000000 | tf_op jit(solution)/shard_map/pallas_call | solution.py:769
  25.4 4.6 %all-gather = bf16[272,128]{1,0:T(8,128)(2,1)S(1)} all-gather(bf16[136,128]{1,0:T(8,128)(2,1)S(1)} %get-tuple-element.29), channel_id=2, replica_groups=mesh['dp'=2,'pairs'=2,'member'=2,'rows'=4] {'member'}, dimensions={0}, use_global_device_ids=true | all-gather | bytes 104448 | tf_op jit(solution)/shard_map/all_gather | solution.py:791
  30.0 0.0 copy-start.1
  30.0 0.4 shard_map.131
  30.4 13.0 %all_to_all.16.got_ref = bf16[16,80,128]{2,1,0:T(8,128)(2,1)S(1)} all-to-all(bf16[16,80,128]{2,1,0:T(8,128)(2,1)S(1)} %get-tuple-element.34), channel_id=1, replica_groups=mesh['dp'=2,'pairs'=2,'member'=2,'rows'=4] {'rows','pairs','member'}, dimensions={0} | all-to-all | bytes 655360 | tf_op jit(solution)/shard_map/all_to_all | solution.py:800
  43.3 0.0 copy-done.1
  43.3 1.6 %shard_map.132 = bf16[16,40,128]{2,1,0:T(8,128)(2,1)S(1)} custom-call(bf16[16,80,128]{2,1,0:T(8,128)(2,1)S(1)} %all_to_all.16.got_ref, f32[4,64,256]{2,1,0:T(8,128)S(1)} %get-tuple-element.35.acts_ref, bf16[2,136,128]{2,1,0:T(8,128)(2,1)S(1)} %bitcast.15, f32[4,64,128]{2,1,0:T(8,128)S(1)} %get-tuple-element.32.columns, ...), custom_call_target="tpu_custom_call" | custom-call | flops 2000000000 | bytes 4000000 | tf_op jit(solution)/shard_map/pallas_call | solution.py:801
  45.0 11.2 %all_to_all.17.got_ref = bf16[16,40,128]{2,1,0:T(8,128)(2,1)S(1)} all-to-all(bf16[16,40,128]{2,1,0:T(8,128)(2,1)S(1)} %shard_map.132), channel_id=1, replica_groups=mesh['dp'=2,'pairs'=2,'member'=2,'rows'=4] {'pairs','member','rows'}, dimensions={0} | all-to-all | bytes 327680 | tf_op jit(solution)/shard_map/all_to_all | solution.py:809
  56.2 0.4 shard_map.133
  56.6 1.8 %all-gather.1 = f32[16,512]{1,0:T(8,128)S(1)} all-gather(f32[8,512]{1,0:T(8,128)S(1)} %get-tuple-element.38), channel_id=3, replica_groups=mesh['dp'=2,'pairs'=2,'member'=2,'rows'=4] {'dp'}, dimensions={0}, use_global_device_ids=true | all-gather | bytes 49152 | tf_op jit(solution)/shard_map/all_gather | solution.py:820
  58.5 1.0 %shard_map.134 = (bf16[128,512]{1,0:T(8,128)(2,1)}, f32[1,512]{1,0:T(1,128)}, f32[1,512]{1,0:T(1,128)}, f32[1,512]{1,0:T(1,128)}, f32[1,512]{1,0:T(1,128)}) custom-call(f32[2,8,512]{2,1,0:T(8,128)S(1)} %bitcast.16, bf16[16,40,128]{2,1,0:T(8,128)(2,1)S(1)} %all_to_all.17.got_ref, bf16[128,512]{1,0:T(8,128)(2,1)S(1)} %get-tuple-element.27.fine_ref.acts_ref, ...), custom_call_target="tpu_custom_call" | custom-call | flops 2000000000 | bytes 4000000 | tf_op jit(solution)/shard_map/pallas_call | solution.py:821
Async XLA Ops:
  1.6 22.5 %copy-start = (bf16[27,128,512]{2,1,0:T(8,128)(2,1)S(1)}, bf16[27,128,512]{2,1,0:T(8,128)(2,1)}, u32[]{:S(2)}) copy-start(bf16[27,128,512]{2,1,0:T(8,128)(2,1)} %weights.2) | copy-start | bytes 10616836
  1.6 22.5 %copy-start.2 = (f32[512]{0:T(512)S(1)}, f32[512]{0:T(512)}, u32[]{:S(2)}) copy-start(f32[512]{0:T(512)} %param.15) | copy-start | bytes 6148
  1.6 22.5 %copy-start.3 = (f32[512]{0:T(512)S(1)}, f32[512]{0:T(512)}, u32[]{:S(2)}) copy-start(f32[512]{0:T(512)} %param.16) | copy-start | bytes 6148
  1.6 22.5 %copy-start.4 = (f32[512]{0:T(512)S(1)}, f32[512]{0:T(512)}, u32[]{:S(2)}) copy-start(f32[512]{0:T(512)} %param.13) | copy-start | bytes 6148
  1.6 22.5 %copy-start.5 = (f32[512]{0:T(512)S(1)}, f32[512]{0:T(512)}, u32[]{:S(2)}) copy-start(f32[512]{0:T(512)} %param.12) | copy-start | bytes 6148
  30.0 13.4 %copy-start.1 = (bf16[27,128,512]{2,1,0:T(8,128)(2,1)S(1)}, bf16[27,128,512]{2,1,0:T(8,128)(2,1)}, u32[]{:S(2)}) copy-start(bf16[27,128,512]{2,1,0:T(8,128)(2,1)} %weights.3) | copy-start | bytes 10616836

commit v28 on v27

--- a/solution.py
+++ b/solution.py
@@ -642,7 +642,7 @@
             out_ref[s_f * nr + s_r, sub : sub + 8, :] = coded
 
 
-def spread_kernel(plan, got_ref, gain_ref, sums_ref, rows_ref):
+def spread_kernel(plan, got_ref, sums_ref, rows_ref):
     sub, nr, nf = plan.sub, plan.nr, plan.nf
     low_row = lanes_at((1, 128), 1) < 64
     first_row = lanes_at((1, 128), 1) < sub
@@ -672,15 +672,11 @@
         coarse[0].append(c_ones)
         coarse[1].append(c_twos)
     one, two, inv_std, mean, c_one, c_two = [jnp.concatenate(part, axis=1) for part in fine + moments + coarse]
-    gain = gain_ref[...]
-    entries = 4 * plan.places * plan.group_width
-    group_one = in_lane_groups(gain * one, plan.group_width) / entries
-    group_two = in_lane_groups(gain * two, plan.group_width) / entries
-    rows_ref[...] = jnp.concatenate([inv_std, mean, group_one, group_two] + [jnp.zeros_like(one)] * 4, axis=0)
+    rows_ref[...] = jnp.concatenate([inv_std, mean, one, two] + [jnp.zeros_like(one)] * 4, axis=0)
     sums_ref[...] = jnp.concatenate([one, two, c_one, c_two] + [jnp.zeros_like(one)] * 4, axis=0)
 
 
-def total_kernel(plan, scales, both_ref, got_ref, acts_ref, rows_ref, result_hbm, out_hbms, total_ref, out_ref, sems):
+def total_kernel(plan, scales, both_ref, got_ref, acts_ref, gain_ref, rows_ref, result_hbm, out_hbms, total_ref, out_ref, sems):
     sub, nr, nf = plan.sub, plan.nr, plan.nf
     totals = sum(both_ref[k] for k in range(both_ref.shape[0]))
     copies = []
@@ -697,7 +693,10 @@
             source.append(jnp.where(low, left, pltpu.roll(right, 64, 1)))
             source.append(jnp.where(low, pltpu.roll(left, 64, 1), right))
     source = jnp.concatenate(source, axis=0).astype(jnp.bfloat16)
-    inv_std, mean, group_one, group_two = [rows_ref[k : k + 1] for k in range(4)]
+    inv_std, mean = rows_ref[0:1], rows_ref[1:2]
+    entries = 4 * plan.places * plan.group_width
+    grouped = in_lane_groups(gain_ref[...] * rows_ref[2:4], plan.group_width) / entries
+    group_one, group_two = grouped[0:1], grouped[1:2]
     pixels = pixel_order(plan, False)
     height = 2 * plan.local
     for k in range(2):
@@ -812,16 +811,16 @@
     sums, moments = pl.pallas_call(
         functools.partial(spread_kernel, plan),
         out_shape=(shape_of((8, channels), f32), shape_of((8, channels), f32)),
-        in_specs=in_vmem(2),
+        in_specs=in_vmem(1),
         out_specs=tuple(in_vmem(2)),
         compiler_params=LIMIT,
         cost_estimate=COST,
-    )(back, rows[2])
+    )(back)
     both = lax.all_gather(sums, "dp")
     out, sums = pl.pallas_call(
         functools.partial(total_kernel, plan, (fine_scale, fine_scale, coarse_scale, coarse_scale)),
         out_shape=(pltpu.HBM((4 * local, channels), bf16), (pltpu.HBM((1, channels), f32),) * 4),
-        in_specs=in_vmem(4),
+        in_specs=in_vmem(5),
         out_specs=(in_hbm(1)[0], tuple(in_hbm(4))),
         scratch_shapes=[
             pltpu.VMEM((4, 1, channels), f32),
@@ -830,7 +829,7 @@
         ],
         compiler_params=LIMIT,
         cost_estimate=COST,
-    )(both, back, acts, moments)
+    )(both, back, acts, rows[2], moments)
     bias_f, gain_f, bias_c, gain_c = [part.reshape(channels) for part in sums]
     return out.reshape(acts_fine.shape), gain_f, bias_f, gain_c, bias_c
 

time: 59.7 us -> 59.5 us (level)
  no operation moved by 1% of the time
where the time goes in v28:
time: 59.5 us; the launch traced here: 59.3 us
  blocking collectives  52.7 us (89%)
  Pallas kernels  5.77 us (10%)
  between operations  0.74 us (1%)
    all_to_all x1, blocking collectives, fast_shards(): got = lax.all_to_all(packed, BLOCK, 0, 0)  22.1 us
    all_to_all x1, blocking collectives, fast_shards(): spread = lax.all_to_all(quartered, BLOCK, 0, 0)  13 us
    all_to_all x1, blocking collectives, fast_shards(): back = lax.all_to_all(sent, BACK_BLOCK, 0, 0)  11.2 us
    all_gather x1, blocking collectives, fast_shards(): both = lax.all_gather(theirs, 'member')  4.61 us
    all_gather x1, blocking collectives, fast_shards(): both = lax.all_gather(sums, 'dp')  1.83 us
    pallas_call x1, Pallas kernels, fast_shards(): pl.pallas_call(functools.partial(fine_kernel, plan), out_shape=shape_of((...  1.62 us
    pallas_call x1, Pallas kernels, fast_shards(): pl.pallas_call(functools.partial(coarse_kernel, plan), out_shape=(shape_o...  1.24 us

profile of v28, /device:TPU:0, one launch (start us, length us, event | category | flops | bytes accessed | tf_op | source)
XLA Modules:
  0.0 59.3 jit_solution(976661101551628736)
XLA Ops:
  0.6 0.9 %shard_map.128 = (bf16[32,512]{1,0:T(8,128)(2,1)S(1)}, bf16[32,512]{1,0:T(8,128)(2,1)S(1)}, bf16[128,512]{1,0:T(8,128)(2,1)S(1)}) custom-call(bf16[32,512]{1,0:T(8,128)(2,1)} %bitcast.23, bf16[32,512]{1,0:T(8,128)(2,1)} %bitcast.24, bf16[128,512]{1,0:T(8,128)(2,1)} %bitcast.22), custom_call_target="tpu_custom_call" | custom-call | tf_op jit(solution)/shard_map/pallas_call | solution.py:750
  1.6 0.0 copy-start
  1.6 0.0 copy-start.2
  1.6 0.0 copy-start.3
  1.6 0.0 copy-start.4
  1.6 0.0 copy-start.5
  1.6 0.3 shard_map.129
  2.0 22.1 %all_to_all.15.got_ref = bf16[16,112,128]{2,1,0:T(8,128)(2,1)S(1)} all-to-all(bf16[16,112,128]{2,1,0:T(8,128)(2,1)S(1)} %shard_map.129), channel_id=1, replica_groups=mesh['dp'=2,'pairs'=2,'member'=2,'rows'=4] {'rows','pairs','member'}, dimensions={0} | all-to-all | bytes 917504 | tf_op jit(solution)/shard_map/all_to_all | solution.py:767
  24.1 0.0 copy-done
  24.1 0.0 copy-done.2
  24.1 0.0 copy-done.3
  24.1 0.0 copy-done.4
  24.1 0.0 copy-done.5
  24.1 1.2 %shard_map.130 = (f32[32,512]{1,0:T(8,128)S(1)}, bf16[136,128]{1,0:T(8,128)(2,1)S(1)}, f32[3,32,512]{2,1,0:T(8,128)S(1)}, f32[32,128]{1,0:T(8,128)S(1)}, f32[4,6...) custom-call(bf16[16,112,128]{2,1,0:T(8,128)(2,1)S(1)} %all_to_all.15, ...), custom_call_target="tpu_custom_call" | custom-call | flops 2000000000 | bytes 4000000 | tf_op jit(solution)/shard_map/pallas_call | solution.py:768
  25.4 4.6 %all-gather = bf16[272,128]{1,0:T(8,128)(2,1)S(1)} all-gather(bf16[136,128]{1,0:T(8,128)(2,1)S(1)} %get-tuple-element.29), channel_id=2, replica_groups=mesh['dp'=2,'pairs'=2,'member'=2,'rows'=4] {'member'}, dimensions={0}, use_global_device_ids=true | all-gather | bytes 104448 | tf_op jit(solution)/shard_map/all_gather | solution.py:790
  30.0 0.0 copy-start.1
  30.0 0.4 shard_map.131
  30.4 13.0 %all_to_all.16.got_ref = bf16[16,80,128]{2,1,0:T(8,128)(2,1)S(1)} all-to-all(bf16[16,80,128]{2,1,0:T(8,128)(2,1)S(1)} %get-tuple-element.34), channel_id=1, replica_groups=mesh['dp'=2,'pairs'=2,'member'=2,'rows'=4] {'rows','pairs','member'}, dimensions={0} | all-to-all | bytes 655360 | tf_op jit(solution)/shard_map/all_to_all | solution.py:799
  43.3 0.0 copy-done.1
  43.3 1.6 %shard_map.132 = bf16[16,40,128]{2,1,0:T(8,128)(2,1)S(1)} custom-call(bf16[16,80,128]{2,1,0:T(8,128)(2,1)S(1)} %all_to_all.16.got_ref, f32[4,64,256]{2,1,0:T(8,128)S(1)} %get-tuple-element.35.acts_ref, bf16[2,136,128]{2,1,0:T(8,128)(2,1)S(1)} %bitcast.15, f32[4,64,128]{2,1,0:T(8,128)S(1)} %get-tuple-element.32.columns, ...), custom_call_target="tpu_custom_call" | custom-call | flops 2000000000 | bytes 4000000 | tf_op jit(solution)/shard_map/pallas_call | solution.py:800
  45.0 11.2 %all_to_all.17.got_ref = bf16[16,40,128]{2,1,0:T(8,128)(2,1)S(1)} all-to-all(bf16[16,40,128]{2,1,0:T(8,128)(2,1)S(1)} %shard_map.132), channel_id=1, replica_groups=mesh['dp'=2,'pairs'=2,'member'=2,'rows'=4] {'pairs','member','rows'}, dimensions={0} | all-to-all | bytes 327680 | tf_op jit(solution)/shard_map/all_to_all | solution.py:808
  56.2 0.2 shard_map.133
  56.4 1.8 %all-gather.1 = f32[16,512]{1,0:T(8,128)S(1)} all-gather(f32[8,512]{1,0:T(8,128)S(1)} %get-tuple-element.38), channel_id=3, replica_groups=mesh['dp'=2,'pairs'=2,'member'=2,'rows'=4] {'dp'}, dimensions={0}, use_global_device_ids=true | all-gather | bytes 49152 | tf_op jit(solution)/shard_map/all_gather | solution.py:819
  58.2 1.1 %shard_map.134 = (bf16[128,512]{1,0:T(8,128)(2,1)}, f32[1,512]{1,0:T(1,128)}, f32[1,512]{1,0:T(1,128)}, f32[1,512]{1,0:T(1,128)}, f32[1,512]{1,0:T(1,128)}) custom-call(f32[2,8,512]{2,1,0:T(8,128)S(1)} %bitcast.16, bf16[16,40,128]{2,1,0:T(8,128)(2,1)S(1)} %all_to_all.17.got_ref, bf16[128,512]{1,0:T(8,128)(2,1)S(1)} %get-tuple-element.27.fine_ref.acts_ref, ...), custom_call_target="tpu_custom_call" | custom-call | flops 2000000000 | bytes 4000000 | tf_op jit(solution)/shard_map/pallas_call | solution.py:820
Async XLA Ops:
  1.6 22.5 %copy-start = (bf16[27,128,512]{2,1,0:T(8,128)(2,1)S(1)}, bf16[27,128,512]{2,1,0:T(8,128)(2,1)}, u32[]{:S(2)}) copy-start(bf16[27,128,512]{2,1,0:T(8,128)(2,1)} %weights.2) | copy-start | bytes 10616836
  1.6 22.5 %copy-start.2 = (f32[512]{0:T(512)S(1)}, f32[512]{0:T(512)}, u32[]{:S(2)}) copy-start(f32[512]{0:T(512)} %param.15) | copy-start | bytes 6148
  1.6 22.5 %copy-start.3 = (f32[512]{0:T(512)S(1)}, f32[512]{0:T(512)}, u32[]{:S(2)}) copy-start(f32[512]{0:T(512)} %param.16) | copy-start | bytes 6148
  1.6 22.5 %copy-start.4 = (f32[512]{0:T(512)S(1)}, f32[512]{0:T(512)}, u32[]{:S(2)}) copy-start(f32[512]{0:T(512)} %param.13) | copy-start | bytes 6148
  1.6 22.5 %copy-start.5 = (f32[512]{0:T(512)S(1)}, f32[512]{0:T(512)}, u32[]{:S(2)}) copy-start(f32[512]{0:T(512)} %param.12) | copy-start | bytes 6148
  30.0 13.4 %copy-start.1 = (bf16[27,128,512]{2,1,0:T(8,128)(2,1)S(1)}, bf16[27,128,512]{2,1,0:T(8,128)(2,1)}, u32[]{:S(2)}) copy-start(bf16[27,128,512]{2,1,0:T(8,128)(2,1)} %weights.3) | copy-start | bytes 10616836

commit v29 on v25

--- a/solution.py
+++ b/solution.py
@@ -272,17 +272,6 @@
     sub = column.shape[0]
     grouped = jnp.sum(column.reshape(sub // group_width, group_width, 1), axis=1, keepdims=True)
     return jnp.broadcast_to(grouped, (sub // group_width, group_width, 1)).reshape(sub, 1)
-
-
-def in_lane_groups(row, group_width):
-    lane = lanes_at(row.shape, 1)
-    size = row.shape[1]
-    step = 1
-    while step < group_width:
-        up, down = pltpu.roll(row, size - step, 1), pltpu.roll(row, step, 1)
-        row = row + jnp.where(lane // step % 2 == 0, up, down)
-        step *= 2
-    return row
 
 
 def total(parts):
@@ -630,27 +619,31 @@
     stacked = halves_from(plan, [cot + scale * part for part in pre]).astype(jnp.bfloat16)
     sent = one_hot_dot(stacked, order[...], ((1,), (1,))).astype(jnp.bfloat16)
     coarse = sums_ref[0:1] + pltpu.roll(sums_ref[1:2], sub, 1)
+    group_one = in_groups(gain * one, plan.group_width) / entries
+    group_two = in_groups(gain * two, plan.group_width) / entries
     coded = (
         terms(as_row(one) + pltpu.roll(as_row(two), 64, 1), 2)
         + terms(coarse, 2)
-        + terms(as_row(inv_std) + pltpu.roll(as_row(mean), 64, 1), 3)
-    )
-    coded = jnp.concatenate(coded + [jnp.zeros_like(coarse)], axis=0).astype(jnp.bfloat16)
+        + terms(as_row(inv_std) + pltpu.roll(as_row(mean), 64, 1), 2)
+        + terms(as_row(group_one) + pltpu.roll(as_row(group_two), 64, 1), 2)
+    )
+    coded = jnp.concatenate(coded, axis=0).astype(jnp.bfloat16)
     for s_r in range(nr):
         for s_f in range(nf):
             out_ref[s_f * nr + s_r, 0:sub, :] = sent[s_f * sub : (s_f + 1) * sub, s_r * 128 : (s_r + 1) * 128]
             out_ref[s_f * nr + s_r, sub : sub + 8, :] = coded
 
 
-def spread_kernel(plan, got_ref, acts_ref, gain_ref, out_ref, sums_ref):
+def spread_kernel(plan, got_ref, acts_ref, out_ref, sums_ref):
     sub, nr, nf = plan.sub, plan.nr, plan.nf
     low = lanes_at((sub, 128), 1) < 64
     low_row = lanes_at((1, 128), 1) < 64
     first_row = lanes_at((1, 128), 1) < sub
     source = []
-    fine, coarse, moments = [[], []], [[], []], [[], []]
+    fine, coarse, moments, groups = [[], []], [[], []], [[], []], [[], []]
     for s_r in range(nr):
         ones, twos, c_ones, c_twos, invs, means = [], [], 0.0, 0.0, [], []
+        g_ones, g_twos = [], []
         for pair in range(nf // 2):
             at = 2 * pair * nr + s_r
             left, right = [got_ref[at + k * nr, 0:sub, :].astype(jnp.float32) for k in range(2)]
@@ -660,7 +653,10 @@
             sums = coded[0][0:1] + coded[0][1:2] + coded[1][0:1] + coded[1][1:2]
             ones.append(sums if pair == 0 else pltpu.roll(sums, 64, 1))
             twos.append(pltpu.roll(sums, 64, 1) if pair == 0 else sums)
-            both = coded[0][4:5] + coded[0][5:6] + coded[0][6:7]
+            grouped = coded[0][6:7] + coded[0][7:8] + coded[1][6:7] + coded[1][7:8]
+            g_ones.append(grouped if pair == 0 else pltpu.roll(grouped, 64, 1))
+            g_twos.append(pltpu.roll(grouped, 64, 1) if pair == 0 else grouped)
+            both = coded[0][4:5] + coded[0][5:6]
             invs.append(both if pair == 0 else pltpu.roll(both, 64, 1))
             means.append(pltpu.roll(both, 64, 1) if pair == 0 else both)
             for k in range(2):
@@ -672,17 +668,17 @@
                 c_twos = c_twos + (pltpu.roll(c_two, to, 1) if to else c_two)
         fine[0].append(jnp.where(low_row, ones[0], ones[1]))
         fine[1].append(jnp.where(low_row, twos[0], twos[1]))
+        groups[0].append(jnp.where(low_row, g_ones[0], g_ones[1]))
+        groups[1].append(jnp.where(low_row, g_twos[0], g_twos[1]))
         moments[0].append(jnp.where(low_row, invs[0], invs[1]))
         moments[1].append(jnp.where(low_row, means[0], means[1]))
         coarse[0].append(c_ones)
         coarse[1].append(c_twos)
-    one, two, inv_std, mean, c_one, c_two = [jnp.concatenate(part, axis=1) for part in fine + moments + coarse]
+    one, two, inv_std, mean, c_one, c_two, group_one, group_two = [
+        jnp.concatenate(part, axis=1) for part in fine + moments + coarse + groups
+    ]
     source = jnp.concatenate(source, axis=0).astype(jnp.bfloat16)
     result = one_hot_dot(pixel_order(plan, False), source, ((1,), (1,)))
-    gain = gain_ref[...]
-    entries = 4 * plan.places * plan.group_width
-    group_one = in_lane_groups(gain * one, plan.group_width) / entries
-    group_two = in_lane_groups(gain * two, plan.group_width) / entries
     normed = (acts_ref[...].astype(jnp.float32) - mean) * inv_std
     out_ref[...] = (result - inv_std * (group_one + normed * group_two)).astype(jnp.bfloat16)
     sums_ref[...] = jnp.concatenate([one, two, c_one, c_two] + [jnp.zeros_like(one)] * 4, axis=0)
@@ -801,11 +797,11 @@
     out, sums = pl.pallas_call(
         functools.partial(spread_kernel, plan),
         out_shape=(pltpu.VMEM((4 * local, channels), bf16), shape_of((8, channels), f32)),
-        in_specs=in_vmem(3),
+        in_specs=in_vmem(2),
         out_specs=tuple(in_vmem(2)),
         compiler_params=LIMIT,
         cost_estimate=COST,
-    )(back, acts, rows[2])
+    )(back, acts)
     both = lax.all_gather(sums, "dp")
     out, sums = pl.pallas_call(
         functools.partial(total_kernel, (fine_scale, fine_scale, coarse_scale, coarse_scale)),

time: 59.5 us -> 59.3 us (level)
  no operation moved by 1% of the time
where the time goes in v29:
time: 59.3 us; the launch traced here: 59 us
  blocking collectives  52.7 us (89%)
  Pallas kernels  5.48 us (9%)
  between operations  0.74 us (1%)
    all_to_all x1, blocking collectives, fast_shards(): got = lax.all_to_all(packed, BLOCK, 0, 0)  22.1 us
    all_to_all x1, blocking collectives, fast_shards(): spread = lax.all_to_all(quartered, BLOCK, 0, 0)  13 us
    all_to_all x1, blocking collectives, fast_shards(): back = lax.all_to_all(sent, BACK_BLOCK, 0, 0)  11.2 us
    all_gather x1, blocking collectives, fast_shards(): both = lax.all_gather(theirs, 'member')  4.61 us
    all_gather x1, blocking collectives, fast_shards(): both = lax.all_gather(sums, 'dp')  1.83 us
    pallas_call x1, Pallas kernels, fast_shards(): pl.pallas_call(functools.partial(fine_kernel, plan), out_shape=shape_of((...  1.61 us
    pallas_call x1, Pallas kernels, fast_shards(): pl.pallas_call(functools.partial(coarse_kernel, plan), out_shape=(shape_o...  1.24 us

profile of v29, /device:TPU:0, one launch (start us, length us, event | category | flops | bytes accessed | tf_op | source)
XLA Modules:
  0.0 59.0 jit_solution(2093996879836615974)
XLA Ops:
  0.6 0.9 %shard_map.128 = (bf16[32,512]{1,0:T(8,128)(2,1)S(1)}, bf16[32,512]{1,0:T(8,128)(2,1)S(1)}, bf16[128,512]{1,0:T(8,128)(2,1)S(1)}) custom-call(bf16[32,512]{1,0:T(8,128)(2,1)} %bitcast.22, bf16[32,512]{1,0:T(8,128)(2,1)} %bitcast.23, bf16[128,512]{1,0:T(8,128)(2,1)} %bitcast.21), custom_call_target="tpu_custom_call" | custom-call | tf_op jit(solution)/shard_map/pallas_call | solution.py:736
  1.6 0.0 copy-start
  1.6 0.0 copy-start.2
  1.6 0.0 copy-start.3
  1.6 0.0 copy-start.4
  1.6 0.0 copy-start.5
  1.6 0.3 shard_map.129
  2.0 22.1 %all_to_all.15.got_ref = bf16[16,112,128]{2,1,0:T(8,128)(2,1)S(1)} all-to-all(bf16[16,112,128]{2,1,0:T(8,128)(2,1)S(1)} %shard_map.129), channel_id=1, replica_groups=mesh['dp'=2,'pairs'=2,'member'=2,'rows'=4] {'rows','pairs','member'}, dimensions={0} | all-to-all | bytes 917504 | tf_op jit(solution)/shard_map/all_to_all | solution.py:753
  24.1 0.0 copy-done
  24.1 0.0 copy-done.2
  24.1 0.0 copy-done.3
  24.1 0.0 copy-done.4
  24.1 0.0 copy-done.5
  24.1 1.2 %shard_map.130 = (f32[32,512]{1,0:T(8,128)S(1)}, bf16[136,128]{1,0:T(8,128)(2,1)S(1)}, f32[3,32,512]{2,1,0:T(8,128)S(1)}, f32[32,128]{1,0:T(8,128)S(1)}, f32[4,6...) custom-call(bf16[16,112,128]{2,1,0:T(8,128)(2,1)S(1)} %all_to_all.15, ...), custom_call_target="tpu_custom_call" | custom-call | flops 2000000000 | bytes 4000000 | tf_op jit(solution)/shard_map/pallas_call | solution.py:754
  25.4 4.6 %all-gather = bf16[272,128]{1,0:T(8,128)(2,1)S(1)} all-gather(bf16[136,128]{1,0:T(8,128)(2,1)S(1)} %get-tuple-element.29), channel_id=2, replica_groups=mesh['dp'=2,'pairs'=2,'member'=2,'rows'=4] {'member'}, dimensions={0}, use_global_device_ids=true | all-gather | bytes 104448 | tf_op jit(solution)/shard_map/all_gather | solution.py:776
  30.0 0.0 copy-start.1
  30.0 0.4 shard_map.131
  30.4 13.0 %all_to_all.16.got_ref = bf16[16,80,128]{2,1,0:T(8,128)(2,1)S(1)} all-to-all(bf16[16,80,128]{2,1,0:T(8,128)(2,1)S(1)} %get-tuple-element.34), channel_id=1, replica_groups=mesh['dp'=2,'pairs'=2,'member'=2,'rows'=4] {'rows','pairs','member'}, dimensions={0} | all-to-all | bytes 655360 | tf_op jit(solution)/shard_map/all_to_all | solution.py:785
  43.3 0.0 copy-done.1
  43.3 1.6 %shard_map.132 = bf16[16,40,128]{2,1,0:T(8,128)(2,1)S(1)} custom-call(bf16[16,80,128]{2,1,0:T(8,128)(2,1)S(1)} %all_to_all.16.got_ref, f32[4,64,256]{2,1,0:T(8,128)S(1)} %get-tuple-element.35.acts_ref, bf16[2,136,128]{2,1,0:T(8,128)(2,1)S(1)} %bitcast.15, f32[4,64,128]{2,1,0:T(8,128)S(1)} %get-tuple-element.32.columns, ...), custom_call_target="tpu_custom_call" | custom-call | flops 2000000000 | bytes 4000000 | tf_op jit(solution)/shard_map/pallas_call | solution.py:786
  45.0 11.2 %all_to_all.17.got_ref = bf16[16,40,128]{2,1,0:T(8,128)(2,1)S(1)} all-to-all(bf16[16,40,128]{2,1,0:T(8,128)(2,1)S(1)} %shard_map.132), channel_id=1, replica_groups=mesh['dp'=2,'pairs'=2,'member'=2,'rows'=4] {'pairs','member','rows'}, dimensions={0} | all-to-all | bytes 327680 | tf_op jit(solution)/shard_map/all_to_all | solution.py:794
  56.2 0.3 shard_map.133
  56.5 1.8 %all-gather.1 = f32[16,512]{1,0:T(8,128)S(1)} all-gather(f32[8,512]{1,0:T(8,128)S(1)} %get-tuple-element.38), channel_id=3, replica_groups=mesh['dp'=2,'pairs'=2,'member'=2,'rows'=4] {'dp'}, dimensions={0}, use_global_device_ids=true | all-gather | bytes 49152 | tf_op jit(solution)/shard_map/all_gather | solution.py:805
  58.3 0.7 %shard_map.134 = (bf16[128,512]{1,0:T(8,128)(2,1)}, f32[1,512]{1,0:T(1,128)}, f32[1,512]{1,0:T(1,128)}, f32[1,512]{1,0:T(1,128)}, f32[1,512]{1,0:T(1,128)}) custom-call(f32[2,8,512]{2,1,0:T(8,128)S(1)} %bitcast.16, bf16[128,512]{1,0:T(8,128)(2,1)S(1)} %get-tuple-element.39.result_ref), custom_call_target="tpu_custom_call" | custom-call | flops 2000000000 | bytes 4000000 | tf_op jit(solution)/shard_map/pallas_call | solution.py:806
Async XLA Ops:
  1.6 22.5 %copy-start = (bf16[27,128,512]{2,1,0:T(8,128)(2,1)S(1)}, bf16[27,128,512]{2,1,0:T(8,128)(2,1)}, u32[]{:S(2)}) copy-start(bf16[27,128,512]{2,1,0:T(8,128)(2,1)} %weights.2) | copy-start | bytes 10616836
  1.6 22.5 %copy-start.2 = (f32[512]{0:T(512)S(1)}, f32[512]{0:T(512)}, u32[]{:S(2)}) copy-start(f32[512]{0:T(512)} %param.15) | copy-start | bytes 6148
  1.6 22.5 %copy-start.3 = (f32[512]{0:T(512)S(1)}, f32[512]{0:T(512)}, u32[]{:S(2)}) copy-start(f32[512]{0:T(512)} %param.16) | copy-start | bytes 6148
  1.6 22.5 %copy-start.4 = (f32[512]{0:T(512)S(1)}, f32[512]{0:T(512)}, u32[]{:S(2)}) copy-start(f32[512]{0:T(512)} %param.12) | copy-start | bytes 6148
  1.6 22.5 %copy-start.5 = (f32[512]{0:T(512)S(1)}, f32[512]{0:T(512)}, u32[]{:S(2)}) copy-start(f32[512]{0:T(512)} %param.13) | copy-start | bytes 6148
  30.0 13.4 %copy-start.1 = (bf16[27,128,512]{2,1,0:T(8,128)(2,1)S(1)}, bf16[27,128,512]{2,1,0:T(8,128)(2,1)}, u32[]{:S(2)}) copy-start(bf16[27,128,512]{2,1,0:T(8,128)(2,1)} %weights.3) | copy-start | bytes 10616836

commit v30 on v29

--- a/solution.py
+++ b/solution.py
@@ -681,7 +681,7 @@
     result = one_hot_dot(pixel_order(plan, False), source, ((1,), (1,)))
     normed = (acts_ref[...].astype(jnp.float32) - mean) * inv_std
     out_ref[...] = (result - inv_std * (group_one + normed * group_two)).astype(jnp.bfloat16)
-    sums_ref[...] = jnp.concatenate([one, two, c_one, c_two] + [jnp.zeros_like(one)] * 4, axis=0)
+    sums_ref[...] = jnp.concatenate([one, two, c_one, c_two], axis=0)
 
 
 def total_kernel(scales, both_ref, result_ref, result_hbm, out_hbms, rows_ref, sems):
@@ -796,7 +796,7 @@
     fine_scale, coarse_scale = 1.0 / math.sqrt(4 * cells), 1.0 / math.sqrt(cells)
     out, sums = pl.pallas_call(
         functools.partial(spread_kernel, plan),
-        out_shape=(pltpu.VMEM((4 * local, channels), bf16), shape_of((8, channels), f32)),
+        out_shape=(pltpu.VMEM((4 * local, channels), bf16), shape_of((4, channels), f32)),
         in_specs=in_vmem(2),
         out_specs=tuple(in_vmem(2)),
         compiler_params=LIMIT,

time: 59.3 us -> 59.2 us (level)
  no operation moved by 1% of the time
where the time goes in v30:
time: 59.2 us; the launch traced here: 59 us
  blocking collectives  52.7 us (89%)
  Pallas kernels  5.48 us (9%)
  between operations  0.74 us (1%)
    all_to_all x1, blocking collectives, fast_shards(): got = lax.all_to_all(packed, BLOCK, 0, 0)  22.1 us
    all_to_all x1, blocking collectives, fast_shards(): spread = lax.all_to_all(quartered, BLOCK, 0, 0)  13 us
    all_to_all x1, blocking collectives, fast_shards(): back = lax.all_to_all(sent, BACK_BLOCK, 0, 0)  11.2 us
    all_gather x1, blocking collectives, fast_shards(): both = lax.all_gather(theirs, 'member')  4.61 us
    all_gather x1, blocking collectives, fast_shards(): both = lax.all_gather(sums, 'dp')  1.81 us
    pallas_call x1, Pallas kernels, fast_shards(): pl.pallas_call(functools.partial(fine_kernel, plan), out_shape=shape_of((...  1.61 us
    pallas_call x1, Pallas kernels, fast_shards(): pl.pallas_call(functools.partial(coarse_kernel, plan), out_shape=(shape_o...  1.24 us

profile of v30, /device:TPU:0, one launch (start us, length us, event | category | flops | bytes accessed | tf_op | source)
XLA Modules:
  0.0 59.0 jit_solution(6671020073298909051)
XLA Ops:
  0.6 0.9 %shard_map.128 = (bf16[32,512]{1,0:T(8,128)(2,1)S(1)}, bf16[32,512]{1,0:T(8,128)(2,1)S(1)}, bf16[128,512]{1,0:T(8,128)(2,1)S(1)}) custom-call(bf16[32,512]{1,0:T(8,128)(2,1)} %bitcast.22, bf16[32,512]{1,0:T(8,128)(2,1)} %bitcast.23, bf16[128,512]{1,0:T(8,128)(2,1)} %bitcast.21), custom_call_target="tpu_custom_call" | custom-call | tf_op jit(solution)/shard_map/pallas_call | solution.py:736
  1.6 0.0 copy-start
  1.6 0.0 copy-start.2
  1.6 0.0 copy-start.3
  1.6 0.0 copy-start.4
  1.6 0.0 copy-start.5
  1.6 0.3 shard_map.129
  2.0 22.1 %all_to_all.15.got_ref = bf16[16,112,128]{2,1,0:T(8,128)(2,1)S(1)} all-to-all(bf16[16,112,128]{2,1,0:T(8,128)(2,1)S(1)} %shard_map.129), channel_id=1, replica_groups=mesh['dp'=2,'pairs'=2,'member'=2,'rows'=4] {'rows','pairs','member'}, dimensions={0} | all-to-all | bytes 917504 | tf_op jit(solution)/shard_map/all_to_all | solution.py:753
  24.1 0.0 copy-done
  24.1 0.0 copy-done.2
  24.1 0.0 copy-done.3
  24.1 0.0 copy-done.4
  24.1 0.0 copy-done.5
  24.1 1.2 %shard_map.130 = (f32[32,512]{1,0:T(8,128)S(1)}, bf16[136,128]{1,0:T(8,128)(2,1)S(1)}, f32[3,32,512]{2,1,0:T(8,128)S(1)}, f32[32,128]{1,0:T(8,128)S(1)}, f32[4,6...) custom-call(bf16[16,112,128]{2,1,0:T(8,128)(2,1)S(1)} %all_to_all.15, ...), custom_call_target="tpu_custom_call" | custom-call | flops 2000000000 | bytes 4000000 | tf_op jit(solution)/shard_map/pallas_call | solution.py:754
  25.4 4.6 %all-gather = bf16[272,128]{1,0:T(8,128)(2,1)S(1)} all-gather(bf16[136,128]{1,0:T(8,128)(2,1)S(1)} %get-tuple-element.29), channel_id=2, replica_groups=mesh['dp'=2,'pairs'=2,'member'=2,'rows'=4] {'member'}, dimensions={0}, use_global_device_ids=true | all-gather | bytes 104448 | tf_op jit(solution)/shard_map/all_gather | solution.py:776
  30.0 0.0 copy-start.1
  30.0 0.4 shard_map.131
  30.4 13.0 %all_to_all.16.got_ref = bf16[16,80,128]{2,1,0:T(8,128)(2,1)S(1)} all-to-all(bf16[16,80,128]{2,1,0:T(8,128)(2,1)S(1)} %get-tuple-element.34), channel_id=1, replica_groups=mesh['dp'=2,'pairs'=2,'member'=2,'rows'=4] {'rows','pairs','member'}, dimensions={0} | all-to-all | bytes 655360 | tf_op jit(solution)/shard_map/all_to_all | solution.py:785
  43.3 0.0 copy-done.1
  43.3 1.6 %shard_map.132 = bf16[16,40,128]{2,1,0:T(8,128)(2,1)S(1)} custom-call(bf16[16,80,128]{2,1,0:T(8,128)(2,1)S(1)} %all_to_all.16.got_ref, f32[4,64,256]{2,1,0:T(8,128)S(1)} %get-tuple-element.35.acts_ref, bf16[2,136,128]{2,1,0:T(8,128)(2,1)S(1)} %bitcast.15, f32[4,64,128]{2,1,0:T(8,128)S(1)} %get-tuple-element.32.columns, ...), custom_call_target="tpu_custom_call" | custom-call | flops 2000000000 | bytes 4000000 | tf_op jit(solution)/shard_map/pallas_call | solution.py:786
  45.0 11.2 %all_to_all.17.got_ref = bf16[16,40,128]{2,1,0:T(8,128)(2,1)S(1)} all-to-all(bf16[16,40,128]{2,1,0:T(8,128)(2,1)S(1)} %shard_map.132), channel_id=1, replica_groups=mesh['dp'=2,'pairs'=2,'member'=2,'rows'=4] {'pairs','member','rows'}, dimensions={0} | all-to-all | bytes 327680 | tf_op jit(solution)/shard_map/all_to_all | solution.py:794
  56.2 0.3 shard_map.133
  56.5 1.8 %all-gather.2.both_ref = f32[2,4,512]{2,1,0:T(4,128)S(1)} all-gather(f32[1,4,512]{2,1,0:T(4,128)S(1)} %bitcast.16), channel_id=3, replica_groups=mesh['dp'=2,'pairs'=2,'member'=2,'rows'=4] {'dp'}, dimensions={0}, use_global_device_ids=true | all-gather | bytes 24576 | tf_op jit(solution)/shard_map/all_gather | solution.py:805
  58.3 0.7 %shard_map.134 = (bf16[128,512]{1,0:T(8,128)(2,1)}, f32[1,512]{1,0:T(1,128)}, f32[1,512]{1,0:T(1,128)}, f32[1,512]{1,0:T(1,128)}, f32[1,512]{1,0:T(1,128)}) custom-call(f32[2,4,512]{2,1,0:T(4,128)S(1)} %all-gather.2.both_ref, bf16[128,512]{1,0:T(8,128)(2,1)S(1)} %get-tuple-element.39.result_ref), custom_call_target="tpu_custom_call" | custom-call | flops 2000000000 | bytes 4000000 | tf_op jit(solution)/shard_map/pallas_call | solution.py:806
Async XLA Ops:
  1.6 22.5 %copy-start = (bf16[27,128,512]{2,1,0:T(8,128)(2,1)S(1)}, bf16[27,128,512]{2,1,0:T(8,128)(2,1)}, u32[]{:S(2)}) copy-start(bf16[27,128,512]{2,1,0:T(8,128)(2,1)} %weights.2) | copy-start | bytes 10616836
  1.6 22.5 %copy-start.2 = (f32[512]{0:T(512)S(1)}, f32[512]{0:T(512)}, u32[]{:S(2)}) copy-start(f32[512]{0:T(512)} %param.15) | copy-start | bytes 6148
  1.6 22.5 %copy-start.3 = (f32[512]{0:T(512)S(1)}, f32[512]{0:T(512)}, u32[]{:S(2)}) copy-start(f32[512]{0:T(512)} %param.16) | copy-start | bytes 6148
  1.6 22.5 %copy-start.4 = (f32[512]{0:T(512)S(1)}, f32[512]{0:T(512)}, u32[]{:S(2)}) copy-start(f32[512]{0:T(512)} %param.12) | copy-start | bytes 6148
  1.6 22.5 %copy-start.5 = (f32[512]{0:T(512)S(1)}, f32[512]{0:T(512)}, u32[]{:S(2)}) copy-start(f32[512]{0:T(512)} %param.13) | copy-start | bytes 6148
  30.0 13.4 %copy-start.1 = (bf16[27,128,512]{2,1,0:T(8,128)(2,1)S(1)}, bf16[27,128,512]{2,1,0:T(8,128)(2,1)}, u32[]{:S(2)}) copy-start(bf16[27,128,512]{2,1,0:T(8,128)(2,1)} %weights.3) | copy-start | bytes 10616836
